TPU v7x, 32 devices: a whole 2x2x4 slice. The times are simulated.
32 devices in a mesh: dp: 32 (over z, y, x, core).
Axes of the slice: x: 2, y: 2, z: 4, core: 2. Of those that a mesh axis runs over, the one named last changes fastest.
Arguments:
- node_feats: bfloat16 [20480, 256], P('dp'), may hold values from -6 to 6
- edge_feats: bfloat16 [20480, 256], P('dp'), may hold values from -6 to 6
- segment_ids: int32 [20480], P('dp'), may hold values from 0 to 4, as said below
- neighbours: int32 [20480, 16], P('dp'), may hold values from 0 to 639, as said below
- nbr_mask: int32 [20480, 16], P('dp'), may hold values from 0 to 1, as said below
- degrees: int32 [20480], P('dp'), may hold values from 1 to 63
- w_edge: bfloat16 [2, 16, 256], replicated, may hold values from -1.5 to 1.5
- w_pre: bfloat16 [2, 768, 256], replicated, may hold values from -0.21875 to 0.21875
- b_pre: float32 [2, 256], replicated, may hold values from -3 to 3
- w_post: bfloat16 [2, 4, 832, 64], replicated, may hold values from -0.21875 to 0.21875
- w_mix: bfloat16 [2, 256, 256], replicated, may hold values from -0.375 to 0.375
- bn_gain: float32 [2, 256], replicated, may hold values from 0.1 to 1.9
- bn_bias: float32 [2, 256], replicated, may hold values from -3 to 3
- readout_grad: float32 [128, 256], P('dp'), may hold values from -6 to 6
Outputs:
- readout: float32 [128, 256], P('dp')
- node_grad: float32 [20480, 256], P('dp')
- edge_grad: float32 [20480, 256], P('dp')
- g_w_edge: float32 [2, 16, 256], replicated
- g_w_pre: float32 [2, 768, 256], replicated
- g_b_pre: float32 [2, 256], replicated
- g_w_post: float32 [2, 4, 832, 64], replicated
- g_w_mix: float32 [2, 256, 256], replicated
- g_bn_gain: float32 [2, 256], replicated
- g_bn_bias: float32 [2, 256], replicated
Inputs may be any that keep to these rules, and one draw needn't show every extreme that they name: `segment_ids`: within each device's block of 640 node slots the ids never fall; each of the 4 subgraphs holds 1 to 160 consecutive nodes and one of them exactly 160; id 4 marks the unused slots at the block's end. `neighbours`: indices count from the first node of the device's block and point into the same subgraph; an unused node slot points at itself. `nbr_mask`: slot k is used exactly when k is below the node's neighbour count: 15 for the first node of a subgraph, 10 for its next 15 nodes, 1 to 4 for the others, 1 for unused node slots.
All inputs are finite; a program needn't handle non-finite values.
Results may differ from a plain program's by a relative error of at most 0.039.
Values sent between devices are 32-bit elements; how exact they have to be, the bound alone decides.
No kernel may reach another device: no remote copies, remote signals or barrier semaphores. Data moves between devices by JAX's collectives and lax.ppermute only.
A program may use at most 128 MiB of HBM per device.

v0:
```python
import jax
import jax.numpy as jnp
from jax import lax
from jax.sharding import PartitionSpec as P

SUB_MAX = 160


DEGREE_CENTER = 2.0
SPREAD_OFFSET = 0.25
STABILITY_FLOOR = 1e-05


def summarize(message, alive, filled_rows):
    weight = alive.astype(message.dtype)[:, :, None]
    live_three = alive[:, :, None]
    average = jnp.sum(weight * message, axis=1) / filled_rows[:, None]
    deviation = message - average[:, None, :]
    spread = jnp.sqrt(
        jnp.sum(weight * deviation * deviation, axis=1) / filled_rows[:, None] + SPREAD_OFFSET
    )
    highest_value = jnp.max(jnp.where(live_three, message, -1e30), axis=1)
    upper_terms = jnp.where(
        live_three, jnp.exp(jnp.where(live_three, message - highest_value[:, None, :], 0.0)), 0.0
    )
    soft_max = highest_value + jnp.log(jnp.sum(upper_terms, axis=1))
    lowest_value = jnp.min(jnp.where(live_three, message, 1e30), axis=1)
    lower_terms = jnp.where(
        live_three, jnp.exp(jnp.where(live_three, lowest_value[:, None, :] - message, 0.0)), 0.0
    )
    soft_min = lowest_value - jnp.log(jnp.sum(lower_terms, axis=1))
    return (average, soft_max, soft_min, spread)


def tower_layout(rounded, stats, amplify_rows, attenuate_rows, towers):
    row_count, feat_width = rounded.shape
    summaries = list(stats)
    grown = [member * amplify_rows[:, None] for member in summaries]
    shrunk = [member * attenuate_rows[:, None] for member in summaries]
    stacked = jnp.stack([rounded] + summaries + grown + shrunk, axis=1)
    split_up = stacked.reshape(row_count, 13, towers, feat_width // towers)
    return jnp.transpose(split_up, (0, 2, 1, 3)).reshape(
        row_count, towers, 13 * (feat_width // towers)
    )


def window_table(neighbour_feature_rows, window_start, window_rows):
    local_index = neighbour_feature_rows.reshape(-1) - window_start
    return (local_index[:, None] == jnp.arange(window_rows, dtype=jnp.int32)[None, :]).astype(
        jnp.bfloat16
    )


def message_block(
    own_rows,
    near_high,
    near_rest,
    window_start,
    edge_rows,
    neighbour_feature_rows,
    w_edge_layer,
    w_term,
    bias_layer,
):
    row_count, slot_count = neighbour_feature_rows.shape
    window_rows = 3 * row_count
    table = window_table(neighbour_feature_rows, window_start, window_rows)
    high_part = lax.dynamic_slice_in_dim(near_high, window_start, window_rows, 0)
    rest_part = lax.dynamic_slice_in_dim(near_rest, window_start, window_rows, 0)
    picked = jnp.dot(table, high_part, preferred_element_type=jnp.float32) + jnp.dot(
        table, rest_part, preferred_element_type=jnp.float32
    )
    picked = picked.reshape(row_count, slot_count, -1)
    edges_three = edge_rows.reshape(row_count, slot_count, -1)
    encoded = jnp.einsum(
        "nke,eh->nkh", edges_three, w_edge_layer, preferred_element_type=jnp.float32
    ).astype(jnp.bfloat16)
    edge_term = jnp.einsum("nkh,hg->nkg", encoded, w_term, preferred_element_type=jnp.float32)
    message = own_rows[:, None, :] + picked + edge_term + bias_layer
    return (edges_three, encoded, message, table)


def on_device(
    node_feats,
    edge_feats,
    segment_ids,
    neighbours,
    nbr_mask,
    degrees,
    w_edge,
    w_pre,
    b_pre,
    w_post,
    w_mix,
    bn_gain,
    bn_bias,
    readout_grad,
):
    node_count, feat_width = node_feats.shape
    towers = w_post.shape[1]
    tower_width = w_post.shape[3]
    layer_count = w_pre.shape[0]
    seed_count = readout_grad.shape[0]
    stride = SUB_MAX
    block_count = node_count // stride
    window_rows = 3 * stride
    window_starts = jnp.clip(
        jnp.arange(block_count, dtype=jnp.int32) * stride - stride, 0, node_count - window_rows
    )
    alive_nodes = (segment_ids < seed_count).astype(jnp.float32)[:, None]
    alive_slots = nbr_mask > 0
    filled = jnp.sum(nbr_mask.astype(jnp.float32), axis=1)
    log_degree = jnp.log(degrees.astype(jnp.float32) + 1.0)
    amplify = log_degree / DEGREE_CENTER
    attenuate = DEGREE_CENTER / log_degree

    def blocked(array):
        return array.reshape((block_count, stride) + array.shape[1:])

    fixed_pieces = (
        window_starts,
        blocked(edge_feats),
        blocked(neighbours),
        blocked(alive_slots),
        blocked(filled),
        blocked(amplify),
        blocked(attenuate),
    )
    stored_depth_slices = []
    hidden_state = node_feats.astype(jnp.float32)
    for layer_index in range(layer_count):
        rounded = hidden_state.astype(jnp.bfloat16)
        w_self = w_pre[layer_index, :feat_width]
        w_near = w_pre[layer_index, feat_width : 2 * feat_width]
        w_term = w_pre[layer_index, 2 * feat_width :]
        own = jnp.dot(rounded, w_self, preferred_element_type=jnp.float32)
        near = jnp.dot(rounded, w_near, preferred_element_type=jnp.float32)
        near_high = near.astype(jnp.bfloat16)
        near_rest = (near - near_high.astype(jnp.float32)).astype(jnp.bfloat16)

        def forward_block(pieces):
            (
                own_rows,
                rounded_rows,
                window_start,
                edge_rows,
                neighbour_feature_rows,
                slot_rows,
                filled_rows,
                amplify_rows,
                attenuate_rows,
            ) = pieces
            row_count = own_rows.shape[0]
            edges_three, encoded, message, table = message_block(
                own_rows,
                near_high,
                near_rest,
                window_start,
                edge_rows,
                neighbour_feature_rows,
                w_edge[layer_index],
                w_term,
                b_pre[layer_index],
            )
            stats = summarize(message, slot_rows, filled_rows)
            tower_in = tower_layout(
                rounded_rows.astype(jnp.float32), stats, amplify_rows, attenuate_rows, towers
            ).astype(jnp.bfloat16)
            mixed_rows = (
                jnp.einsum(
                    "ntk,tko->nto",
                    tower_in,
                    w_post[layer_index],
                    preferred_element_type=jnp.float32,
                )
                .astype(jnp.bfloat16)
                .reshape(row_count, feat_width)
            )
            return (
                jnp.dot(mixed_rows, w_mix[layer_index], preferred_element_type=jnp.float32),
                mixed_rows,
            )

        projected, mixed = lax.map(forward_block, (blocked(own), blocked(rounded)) + fixed_pieces)
        projected = projected.reshape(node_count, feat_width)
        mixed = mixed.reshape(node_count, feat_width)
        total, tallied_entries = lax.psum(
            (jnp.sum(alive_nodes * projected, axis=0), jnp.sum(alive_nodes)), "dp"
        )
        center = total / tallied_entries
        centred = lax.psum(jnp.sum(alive_nodes * (projected - center) ** 2, axis=0), "dp")
        sample_dispersion = centred / tallied_entries
        scale = lax.rsqrt(sample_dispersion + STABILITY_FLOOR)
        normed = (projected - center) * scale
        gated = normed * bn_gain[layer_index] + bn_bias[layer_index]
        stored_depth_slices.append(
            (rounded, own, near_high, near_rest, mixed, normed, gated, scale, tallied_entries)
        )
        hidden_state = hidden_state + jax.nn.silu(gated)
    group_belonging = (segment_ids[None, :] == jnp.arange(seed_count)[:, None]).astype(jnp.float32)
    readout = jnp.dot(group_belonging, hidden_state, precision=lax.Precision.HIGHEST) / SUB_MAX
    grad_hidden = (
        jnp.einsum("sn,sh->nh", group_belonging, readout_grad, precision=lax.Precision.HIGHEST)
        / SUB_MAX
    )
    edge_grad = jnp.zeros(edge_feats.shape, jnp.float32)
    collected = [None] * layer_count
    gain_grads = [None] * layer_count
    bias_grads = [None] * layer_count
    for layer_index in range(layer_count - 1, -1, -1):
        rounded, own, near_high, near_rest, mixed, normed, gated, scale, tallied_entries = (
            stored_depth_slices[layer_index]
        )
        w_self = w_pre[layer_index, :feat_width]
        w_near = w_pre[layer_index, feat_width : 2 * feat_width]
        w_term = w_pre[layer_index, 2 * feat_width :]
        sigmoid_gate = jax.nn.sigmoid(gated)
        d_gated = grad_hidden * sigmoid_gate * (1.0 + gated * (1.0 - sigmoid_gate))
        g_bias, gain_gradient = lax.psum(
            (jnp.sum(d_gated, axis=0), jnp.sum(d_gated * normed, axis=0)), "dp"
        )
        gain_grads[layer_index] = gain_gradient
        bias_grads[layer_index] = g_bias
        d_projected = (
            scale
            * bn_gain[layer_index]
            * (d_gated - alive_nodes * (g_bias + normed * gain_gradient) / tallied_entries)
        )
        d_proj_low = d_projected.astype(jnp.bfloat16)
        g_mix = jnp.einsum("nh,ng->hg", mixed, d_proj_low, preferred_element_type=jnp.float32)
        d_mixed = (
            jnp.einsum(
                "ng,hg->nh", d_proj_low, w_mix[layer_index], preferred_element_type=jnp.float32
            )
            .astype(jnp.bfloat16)
            .reshape(node_count, towers, tower_width)
        )

        def backward_block(carry, pieces):
            near_total, g_term, g_edge, g_bias_pre, g_post = carry
            (
                own_rows,
                rounded_rows,
                window_start,
                edge_rows,
                neighbour_feature_rows,
                slot_rows,
                filled_rows,
                amplify_rows,
                attenuate_rows,
                dmix_rows,
            ) = pieces
            row_count = own_rows.shape[0]
            edges_three, encoded, message, table = message_block(
                own_rows,
                near_high,
                near_rest,
                window_start,
                edge_rows,
                neighbour_feature_rows,
                w_edge[layer_index],
                w_term,
                b_pre[layer_index],
            )
            average, soft_max, soft_min, spread = summarize(message, slot_rows, filled_rows)
            tower_in = tower_layout(
                rounded_rows.astype(jnp.float32),
                (average, soft_max, soft_min, spread),
                amplify_rows,
                attenuate_rows,
                towers,
            ).astype(jnp.bfloat16)
            g_post = g_post + jnp.einsum(
                "ntk,nto->tko", tower_in, dmix_rows, preferred_element_type=jnp.float32
            )
            d_tower = jnp.einsum(
                "nto,tko->ntk", dmix_rows, w_post[layer_index], preferred_element_type=jnp.float32
            )
            d_feats = jnp.transpose(
                d_tower.reshape(row_count, towers, 13, tower_width), (0, 2, 1, 3)
            ).reshape(row_count, 13, feat_width)
            grow_col = amplify_rows[:, None]
            shrink_col = attenuate_rows[:, None]
            d_average = d_feats[:, 1] + grow_col * d_feats[:, 5] + shrink_col * d_feats[:, 9]
            d_upper = d_feats[:, 2] + grow_col * d_feats[:, 6] + shrink_col * d_feats[:, 10]
            d_lower = d_feats[:, 3] + grow_col * d_feats[:, 7] + shrink_col * d_feats[:, 11]
            d_spread = d_feats[:, 4] + grow_col * d_feats[:, 8] + shrink_col * d_feats[:, 12]
            live_three = slot_rows[:, :, None]
            weight = live_three.astype(jnp.float32)
            filled_col = filled_rows[:, None]
            deviation = message - average[:, None, :]
            upper_share = jnp.where(
                live_three, jnp.exp(jnp.where(live_three, message - soft_max[:, None, :], 0.0)), 0.0
            )
            lower_share = jnp.where(
                live_three, jnp.exp(jnp.where(live_three, soft_min[:, None, :] - message, 0.0)), 0.0
            )
            message_gradient = weight * (
                (d_average / filled_col)[:, None, :]
                + deviation * (d_spread / (filled_col * spread))[:, None, :]
            )
            message_gradient = (
                message_gradient
                + d_upper[:, None, :] * upper_share
                + d_lower[:, None, :] * lower_share
            )
            flat_gradient = message_gradient.reshape(-1, feat_width)
            grad_high = flat_gradient.astype(jnp.bfloat16)
            grad_rest = (flat_gradient - grad_high.astype(jnp.float32)).astype(jnp.bfloat16)
            landed = jnp.einsum(
                "rw,rh->wh", table, grad_high, preferred_element_type=jnp.float32
            ) + jnp.einsum("rw,rh->wh", table, grad_rest, preferred_element_type=jnp.float32)
            present = lax.dynamic_slice_in_dim(near_total, window_start, window_rows, 0)
            near_total = lax.dynamic_update_slice_in_dim(
                near_total, present + landed, window_start, 0
            )
            g_bias_pre = g_bias_pre + jnp.sum(message_gradient, axis=(0, 1))
            d_own = jnp.sum(message_gradient, axis=1).astype(jnp.bfloat16)
            d_term = message_gradient.astype(jnp.bfloat16)
            g_term = g_term + jnp.einsum(
                "nkh,nkg->hg", encoded, d_term, preferred_element_type=jnp.float32
            )
            d_encoded = jnp.einsum(
                "nkg,hg->nkh", d_term, w_term, preferred_element_type=jnp.float32
            ).astype(jnp.bfloat16)
            g_edge = g_edge + jnp.einsum(
                "nke,nkh->eh", edges_three, d_encoded, preferred_element_type=jnp.float32
            )
            d_edges = jnp.einsum(
                "nkh,eh->nke", d_encoded, w_edge[layer_index], preferred_element_type=jnp.float32
            ).reshape(row_count, -1)
            return (
                (near_total, g_term, g_edge, g_bias_pre, g_post),
                (d_own, d_feats[:, 0], d_edges),
            )

        start_carry = (
            jnp.zeros((node_count, feat_width), jnp.float32),
            jnp.zeros((feat_width, feat_width), jnp.float32),
            jnp.zeros(w_edge.shape[1:], jnp.float32),
            jnp.zeros((feat_width,), jnp.float32),
            jnp.zeros(w_post.shape[1:], jnp.float32),
        )
        pieces = (blocked(own), blocked(rounded)) + fixed_pieces + (blocked(d_mixed),)
        carry, outputs = lax.scan(backward_block, start_carry, pieces)
        near_total, g_term, g_edge, g_bias_pre, g_post = carry
        d_own = outputs[0].reshape(node_count, feat_width)
        d_self_feat = outputs[1].reshape(node_count, feat_width)
        edge_grad = edge_grad + outputs[2].reshape(edge_feats.shape)
        d_near = near_total.astype(jnp.bfloat16)
        g_self = jnp.einsum("nh,ng->hg", rounded, d_own, preferred_element_type=jnp.float32)
        g_near = jnp.einsum("nh,ng->hg", rounded, d_near, preferred_element_type=jnp.float32)
        g_pre = jnp.concatenate([g_self, g_near, g_term], axis=0)
        grad_hidden = grad_hidden + d_self_feat
        grad_hidden = grad_hidden + jnp.einsum(
            "ng,hg->nh", d_own, w_self, preferred_element_type=jnp.float32
        )
        grad_hidden = grad_hidden + jnp.einsum(
            "ng,hg->nh", d_near, w_near, preferred_element_type=jnp.float32
        )
        collected[layer_index] = (g_edge, g_pre, g_bias_pre, g_post, g_mix)
    lower_set = collected[0]
    upper_set = collected[1]
    summed = lax.psum(
        (
            lower_set[0],
            lower_set[1],
            lower_set[2],
            lower_set[3],
            lower_set[4],
            upper_set[0],
            upper_set[1],
            upper_set[2],
            upper_set[3],
            upper_set[4],
        ),
        "dp",
    )
    collected = [summed[:5], summed[5:]]
    g_w_edge = jnp.stack([collected[0][0], collected[1][0]])
    g_w_pre = jnp.stack([collected[0][1], collected[1][1]])
    g_b_pre = jnp.stack([collected[0][2], collected[1][2]])
    g_w_post = jnp.stack([collected[0][3], collected[1][3]])
    g_w_mix = jnp.stack([collected[0][4], collected[1][4]])
    g_bn_gain = jnp.stack(gain_grads)
    g_bn_bias = jnp.stack(bias_grads)
    return (
        readout,
        grad_hidden,
        edge_grad,
        g_w_edge,
        g_w_pre,
        g_b_pre,
        g_w_post,
        g_w_mix,
        g_bn_gain,
        g_bn_bias,
    )


def solution(mesh):
    in_specs = (
        P("dp", None),
        P("dp", None),
        P("dp"),
        P("dp", None),
        P("dp", None),
        P("dp"),
        P(),
        P(),
        P(),
        P(),
        P(),
        P(),
        P(),
        P("dp", None),
    )
    out_specs = (P("dp", None), P("dp", None), P("dp", None), P(), P(), P(), P(), P(), P(), P())
    return jax.shard_map(
        on_device, mesh=mesh, in_specs=in_specs, out_specs=out_specs, check_vma=False
    )
```

profile of v0, /device:TPU:0, one launch (start us, length us, event | category | flops | bytes accessed | tf_op | source)
XLA Modules:
  0.0 1223.9 jit_solution(613317321664875533)
XLA Ops:
  20.5 119.9 %while.74 = (s32[]{:T(128)}, f32[4,160,256]{2,1,0:T(8,128)}, bf16[4,160,256]{2,1,0:T(8,128)(2,1)}, bf16[4,160,256]{1,2,0:T(8,128)(2,1)}, pred[4,160,16]{2,1,0:T(...) while((s32[]{:T(128)}, f32[4,160,256]{2,1,0:T(8,128)}, ...), condition=%wide.region_8.9_spmd, body=%wide.region_1.8_spmd.sunk | while | flops 1722577920 | bytes 35751232 | solution.py:184
  34.1 4.6 select_reduce_fusion.24
  40.3 4.3 select_reduce_fusion.25
  64.0 4.6 select_reduce_fusion.24
  70.2 4.3 select_reduce_fusion.25
  94.0 4.6 select_reduce_fusion.24
  100.2 4.3 select_reduce_fusion.25
  124.0 4.6 select_reduce_fusion.24
  130.2 4.3 select_reduce_fusion.25
  141.8 42.3 %all-reduce.3 = (f32[256]{0:T(256)S(1)}, f32[]{:T(128)}) all-reduce(f32[256]{0:T(256)S(1)} %multiply_reduce_fusion.9, f32[]{:T(128)} %fusion.209), channel_id=1, replica_groups=mesh['dp'=32] {'dp'}, use_global_device_ids=true, to_apply=%region_10.11 | all-reduce | flops 257 | bytes 2056 | tf_op jit(solution)/shard_map/psum | solution.py:187
  186.0 40.6 %psum.138 = f32[256]{0:T(256)S(1)} all-reduce(f32[256]{0:T(256)S(1)} %multiply_reduce_fusion.8), channel_id=1, replica_groups=mesh['dp'=32] {'dp'}, use_global_device_ids=true, to_apply=%region_14.15 | all-reduce | flops 256 | bytes 2048 | tf_op jit(solution)/shard_map/psum | solution.py:191
  236.6 129.5 %while.75 = (s32[]{:T(128)}, f32[4,160,256]{2,1,0:T(8,128)}, bf16[4,160,256]{2,1,0:T(8,128)(2,1)}, bf16[4,160,256]{1,2,0:T(8,128)(2,1)}, pred[4,160,16]{2,1,0:T(...) while((s32[]{:T(128)}, f32[4,160,256]{2,1,0:T(8,128)}, ...), condition=%wide.region_22.23_spmd, body=%wide.region_15.22_spmd.sunk | while | flops 1722577920 | bytes 36932996 | solution.py:184
  250.2 5.3 select_reduce_fusion.26
  257.1 4.3 select_reduce_fusion.27
  282.6 5.3 select_reduce_fusion.26
  289.5 4.3 select_reduce_fusion.27
  314.9 5.3 select_reduce_fusion.26
  321.9 4.3 select_reduce_fusion.27
  347.3 5.3 select_reduce_fusion.26
  354.2 4.3 select_reduce_fusion.27
  367.4 40.0 %psum.139 = f32[256]{0:T(256)S(1)} all-reduce(f32[256]{0:T(256)S(1)} %multiply_reduce_fusion.7), channel_id=1, replica_groups=mesh['dp'=32] {'dp'}, use_global_device_ids=true, to_apply=%region_24.25 | all-reduce | flops 256 | bytes 2048 | tf_op jit(solution)/shard_map/psum | solution.py:187
  409.3 40.1 %psum.140 = f32[256]{0:T(256)S(1)} all-reduce(f32[256]{0:T(256)S(1)} %multiply_reduce_fusion.6), channel_id=1, replica_groups=mesh['dp'=32] {'dp'}, use_global_device_ids=true, to_apply=%region_26.27 | all-reduce | flops 256 | bytes 2048 | tf_op jit(solution)/shard_map/psum | solution.py:191
  452.0 40.0 %all-reduce.2 = (f32[256]{0:T(256)S(1)}, f32[256]{0:T(256)S(1)}) all-reduce(f32[256]{0:T(256)S(1)} %get-tuple-element.1031, f32[256]{0:T(256)S(1)} %get-tuple-element.1030), channel_id=1, replica_groups=mesh['dp'=32] {'dp'}, use_global_device_ids=true, to_apply=%region_30.31 | all-reduce | flops 512 | bytes 4096 | tf_op jit(solution)/shard_map/psum | solution.py:219
  500.1 248.3 %while.76 = (s32[]{:T(128)}, f32[640,256]{1,0:T(8,128)}, f32[256,256]{1,0:T(8,128)}, f32[16,256]{1,0:T(8,128)}, f32[256]{0:T(256)}, /*index=5*/f32[4,832,64]{1,2...) while((s32[]{:T(128)}, f32[640,256]{1,0:T(8,128)}, ...), condition=%wide.region_40.41_spmd.clone, body=%wide.region_31.40_spmd.clone.sunk | while | flops 3760207104 | bytes 147191344 | solution.py:345
  517.3 3.3 select_reduce_fusion.29
  579.2 3.3 select_reduce_fusion.29
  641.1 3.3 select_reduce_fusion.29
  703.1 3.3 select_reduce_fusion.29
  755.6 40.0 %all-reduce.1 = (f32[256]{0:T(256)S(1)}, f32[256]{0:T(256)S(1)}) all-reduce(f32[256]{0:T(256)S(1)} %get-tuple-element.1033, f32[256]{0:T(256)S(1)} %get-tuple-element.1032), channel_id=1, replica_groups=mesh['dp'=32] {'dp'}, use_global_device_ids=true, to_apply=%region_44.45 | all-reduce | flops 512 | bytes 4096 | tf_op jit(solution)/shard_map/psum | solution.py:219
  802.6 257.4 %while.77 = (s32[]{:T(128)}, f32[640,256]{1,0:T(8,128)}, f32[256,256]{1,0:T(8,128)}, f32[16,256]{1,0:T(8,128)}, f32[256]{0:T(256)}, /*index=5*/f32[4,832,64]{1,2...) while((s32[]{:T(128)}, f32[640,256]{1,0:T(8,128)}, ...), condition=%wide.region_54.55_spmd.clone, body=%wide.region_45.54_spmd.clone.sunk | while | flops 3760207104 | bytes 142990704 | solution.py:345
  1070.0 40.8 %all-reduce = (f32[1,16,256]{2,1,0:T(8,128)S(1)}, f32[1,16,256]{2,1,0:T(8,128)S(1)}, f32[1,256]{1,0:T(1,128)S(1)}, f32[1,256]{1,0:T(1,128)S(1)}) all-reduce(f32[1,16,256]{2,1,0:T(8,128)S(1)} %bitcast.820, f32[1,16,256]{2,1,0:T(8,128)S(1)} %bitcast.819, f32[1,256]{1,0:T(1,128)S(1)} %bitcast.823, ...), channel_id=1, replica_groups=mesh['dp'=32] {'dp'}, use_global_device_ids=true, to_apply=%region_56.57 | all-reduce | flops 8704 | bytes 69632 | tf_op jit(solution)/shard_map/psum | solution.py:364
  1118.0 93.8 %all-reduce.7.cloned.1.call-done = (f32[1,768,256]{2,1,0:T(8,128)}, f32[1,768,256]{2,1,0:T(8,128)}, f32[1,4,832,64]{2,3,1,0:T(8,128)}, f32[1,4,832,64]{2,3,1,0:T...) async-done(((f32[1,768,256]{2,1,0:T(8,128)}, f32[1,768,256]{2,1,0:T(8,128)}, f32[1,4,832,64]{2,3,1,0:T(8,128)}, f32[1,4,832,64]{2,3,1,0:T(8,128)}, ...) | async-done | bytes 3801104 | tf_op jit(solution)/shard_map/psum | solution.py:364
  (1759 shorter events, 703.3 us)
Async XLA Ops:
  7.2 442.9 %copy-start = (f32[4,256]{1,0:T(4,128)S(1)}, f32[4,256]{1,0:T(4,128)}, u32[]{:S(2)}) copy-start(f32[4,256]{1,0:T(4,128)} %param.35) | copy-start | bytes 12292
  7.2 1204.6 %all-reduce.7.cloned.1.call-start = ((), (), s32[]{:S(2)}) async-start(), calls=%async_computation | async-start | bytes 7864320 | tf_op jit(solution)/shard_map/psum | solution.py:364
  13.4 478.5 %copy-start.118 = (f32[640]{0:T(1024)}, f32[640]{0:T(1024)S(1)}, u32[]{:S(2)}) copy-start(f32[640]{0:T(1024)S(1)} %compare_convert_fusion) | copy-start | bytes 7684
  14.0 213.8 %copy-start.137 = (f32[1,256]{1,0:T(1,128)}, f32[1,256]{1,0:T(1,128)S(1)}, u32[]{:S(2)}) copy-start(f32[1,256]{1,0:T(1,128)S(1)} %get-tuple-element.1313) | copy-start | bytes 3076
  14.1 477.9 %copy-start.140 = (f32[1,256]{1,0:T(1,128)}, f32[1,256]{1,0:T(1,128)S(1)}, u32[]{:S(2)}) copy-start(f32[1,256]{1,0:T(1,128)S(1)} %get-tuple-element.1312) | copy-start | bytes 3076
  14.1 213.7 %copy-start.131 = (f32[1,256]{1,0:T(1,128)}, f32[1,256]{1,0:T(1,128)S(1)}, u32[]{:S(2)}) copy-start(f32[1,256]{1,0:T(1,128)S(1)} %get-tuple-element.1311) | copy-start | bytes 3076
  14.1 477.9 %copy-start.135 = (f32[1,256]{1,0:T(1,128)}, f32[1,256]{1,0:T(1,128)S(1)}, u32[]{:S(2)}) copy-start(f32[1,256]{1,0:T(1,128)S(1)} %get-tuple-element.1310) | copy-start | bytes 3076
  140.4 87.5 %copy-start.53 = (f32[4,160,256]{2,1,0:T(8,128)S(1)}, f32[4,160,256]{2,1,0:T(8,128)}, u32[]{:S(2)}) copy-start(f32[4,160,256]{2,1,0:T(8,128)} %get-tuple-element.474) | copy-start | bytes 1966084
  184.7 46.3 %copy-start.129 = (f32[256]{0:T(256)}, f32[256]{0:T(256)S(1)}, u32[]{:S(2)}) copy-start(f32[256]{0:T(256)S(1)} %broadcast_divide_fusion.9) | copy-start | bytes 3076
  451.9 40.0 %copy-start.103 = (f32[640,256]{1,0:T(8,128)}, f32[640,256]{1,0:T(8,128)S(1)}, u32[]{:S(2)}) copy-start(f32[640,256]{1,0:T(8,128)S(1)} %get-tuple-element.1245) | copy-start | bytes 1966084
  452.0 41.1 %copy-start.86 = (f32[640,256]{1,0:T(8,128)}, f32[640,256]{1,0:T(8,128)S(1)}, u32[]{:S(2)}) copy-start(f32[640,256]{1,0:T(8,128)S(1)} %get-tuple-element.1314) | copy-start | bytes 1966084
  753.3 42.3 %copy-start.119 = (f32[640]{0:T(1024)S(1)}, f32[640]{0:T(1024)}, u32[]{:S(2)}) copy-start(f32[640]{0:T(1024)} %copy-done.118) | copy-start | bytes 7684
  753.3 42.3 %copy-start.142 = (f32[256]{0:T(256)S(1)}, f32[256]{0:T(256)}, u32[]{:S(2)}) copy-start(f32[256]{0:T(256)} %get-tuple-element.1240) | copy-start | bytes 3076
  755.6 41.6 %copy-start.62 = (bf16[2,256,256]{2,1,0:T(8,128)(2,1)S(1)}, bf16[2,256,256]{2,1,0:T(8,128)(2,1)}, u32[]{:S(2)}) copy-start(bf16[2,256,256]{2,1,0:T(8,128)(2,1)} %get-tuple-element.2381) | copy-start | bytes 786436
  803.5 17.8 %copy-start.32 = (f32[160,16]{1,0:T(8,128)}, f32[160,16]{1,0:T(8,128)S(1)}, u32[]{:S(2)}) copy-start(f32[160,16]{1,0:T(8,128)S(1)} %get-tuple-element.2008) | copy-start | bytes 30724 | tf_op jit(solution)/shard_map/while
  803.5 17.8 %copy-start.74 = (pred[160,16]{1,0:T(8,128)(4,1)}, pred[160,16]{1,0:T(8,128)(4,1)S(1)}, u32[]{:S(2)}) copy-start(pred[160,16]{1,0:T(8,128)(4,1)S(1)} %get-tuple-element.2007) | copy-start | bytes 7684 | tf_op jit(solution)/shard_map/while
  867.8 17.8 %copy-start.32 = (f32[160,16]{1,0:T(8,128)}, f32[160,16]{1,0:T(8,128)S(1)}, u32[]{:S(2)}) copy-start(f32[160,16]{1,0:T(8,128)S(1)} %get-tuple-element.2008) | copy-start | bytes 30724 | tf_op jit(solution)/shard_map/while
  867.8 17.8 %copy-start.74 = (pred[160,16]{1,0:T(8,128)(4,1)}, pred[160,16]{1,0:T(8,128)(4,1)S(1)}, u32[]{:S(2)}) copy-start(pred[160,16]{1,0:T(8,128)(4,1)S(1)} %get-tuple-element.2007) | copy-start | bytes 7684 | tf_op jit(solution)/shard_map/while
  932.0 17.8 %copy-start.32 = (f32[160,16]{1,0:T(8,128)}, f32[160,16]{1,0:T(8,128)S(1)}, u32[]{:S(2)}) copy-start(f32[160,16]{1,0:T(8,128)S(1)} %get-tuple-element.2008) | copy-start | bytes 30724 | tf_op jit(solution)/shard_map/while
  996.3 17.8 %copy-start.32 = (f32[160,16]{1,0:T(8,128)}, f32[160,16]{1,0:T(8,128)S(1)}, u32[]{:S(2)}) copy-start(f32[160,16]{1,0:T(8,128)S(1)} %get-tuple-element.2008) | copy-start | bytes 30724 | tf_op jit(solution)/shard_map/while
  996.3 17.8 %copy-start.74 = (pred[160,16]{1,0:T(8,128)(4,1)}, pred[160,16]{1,0:T(8,128)(4,1)S(1)}, u32[]{:S(2)}) copy-start(pred[160,16]{1,0:T(8,128)(4,1)S(1)} %get-tuple-element.2007) | copy-start | bytes 7684 | tf_op jit(solution)/shard_map/while
  1068.6 42.8 %copy-start.144 = (f32[256]{0:T(256)S(1)}, f32[256]{0:T(256)}, u32[]{:S(2)}) copy-start(f32[256]{0:T(256)} %copy-done.143) | copy-start | bytes 3076
  1068.6 42.8 %copy-start.146 = (f32[256]{0:T(256)S(1)}, f32[256]{0:T(256)}, u32[]{:S(2)}) copy-start(f32[256]{0:T(256)} %copy-done.145) | copy-start | bytes 3076
  1068.6 42.8 %copy-start.148 = (f32[256]{0:T(256)S(1)}, f32[256]{0:T(256)}, u32[]{:S(2)}) copy-start(f32[256]{0:T(256)} %copy-done.147) | copy-start | bytes 3076
  1068.6 42.8 %copy-start.150 = (f32[256]{0:T(256)S(1)}, f32[256]{0:T(256)}, u32[]{:S(2)}) copy-start(f32[256]{0:T(256)} %copy-done.149) | copy-start | bytes 3076
  1068.8 43.9 %copy-start.104 = (f32[640,256]{1,0:T(8,128)S(1)}, f32[640,256]{1,0:T(8,128)}, u32[]{:S(2)}) copy-start(f32[640,256]{1,0:T(8,128)} %copy-done.103) | copy-start | bytes 1966084
  1068.8 43.9 %copy-start.105 = (f32[640,256]{1,0:T(8,128)S(1)}, f32[640,256]{1,0:T(8,128)}, u32[]{:S(2)}) copy-start(f32[640,256]{1,0:T(8,128)} %get-tuple-element.1249) | copy-start | bytes 1966084
  1068.8 43.8 %copy-start.128 = (s32[640]{0:T(1024)S(1)}, s32[640]{0:T(1024)}, u32[]{:S(2)}) copy-start(s32[640]{0:T(1024)} %param.24) | copy-start | bytes 7684
  1068.8 43.8 %copy-start.136 = (f32[1,256]{1,0:T(1,128)S(1)}, f32[1,256]{1,0:T(1,128)}, u32[]{:S(2)}) copy-start(f32[1,256]{1,0:T(1,128)} %copy-done.135) | copy-start | bytes 3076
  1068.8 43.8 %copy-start.141 = (f32[1,256]{1,0:T(1,128)S(1)}, f32[1,256]{1,0:T(1,128)}, u32[]{:S(2)}) copy-start(f32[1,256]{1,0:T(1,128)} %copy-done.140) | copy-start | bytes 3076
  1070.0 43.8 %copy-start.87 = (f32[4,160,256]{2,1,0:T(8,128)S(1)}, f32[4,160,256]{2,1,0:T(8,128)}, u32[]{:S(2)}) copy-start(f32[4,160,256]{2,1,0:T(8,128)} %get-tuple-element.479) | copy-start | bytes 1966084
  1070.0 43.8 %copy-start.106 = (f32[640,256]{1,0:T(8,128)S(1)}, f32[640,256]{1,0:T(8,128)}, u32[]{:S(2)}) copy-start(f32[640,256]{1,0:T(8,128)} %get-tuple-element.1315) | copy-start | bytes 1966084
  (384 other events, 1335.7 us)
Sparse Core Ops, SparseCore 0:
  1067.2 144.5 all-reduce.6
where the time goes:
time: 1240 us; the launch traced here: 1220 us
  local copies, waits for them, and re-layouts  302 us (24%)
  matrix products  296 us (24%)
  blocking collectives  284 us (23%)
  other arithmetic  192 us (15%)
  waiting for transfers between devices  93.9 us (8%)
  loops' own time  40.8 us (3%)
  between operations  15 us (1%)
    psum x1, waiting for transfers between devices, on_device(): lax.psum((lower_set[0], lower_set[1], lower_set[2], lower_set[3], lower_s...  93.8 us
    while x800, local copies, waits for them, and re-layouts  83.6 us
    psum x2, blocking collectives, on_device(): lax.psum((jnp.sum(alive_nodes * projected, axis=0), jnp.sum(alive_nodes))...  82.2 us
    psum x2, blocking collectives, on_device(): lax.psum(jnp.sum(alive_nodes * (projected - center) ** 2, axis=0), 'dp')  80.7 us
    psum x2, blocking collectives, on_device(): lax.psum((jnp.sum(d_gated, axis=0), jnp.sum(d_gated * normed, axis=0)), '...  80 us
    dynamic_slice x64, local copies, waits for them, and re-layouts, on_device(): lax.map(forward_block, (blocked(own), blocked(rounded)) + fixed_pieces)  60.4 us
    dot_general x16, matrix products, message_block(): jnp.einsum('nkh,hg->nkg', encoded, w_term, preferred_element_type=jnp.flo...  58.1 us
    psum x1, blocking collectives, on_device(): lax.psum((lower_set[0], lower_set[1], lower_set[2], lower_set[3], lower_s...  40.8 us
  transfers between devices with their start and end apart: 1, of which 1 were waited for; matrix products, arithmetic and copies ran while one was open for 1% of the time, Pallas kernels for 0%

commit v1 on v0

v1 whole, which is shorter than its diff:
```python
import functools

import jax
import jax.numpy as jnp
from jax import lax
from jax.experimental import pallas as pl
from jax.experimental.pallas import tpu as pltpu
from jax.sharding import PartitionSpec as P

SUB_MAX = 160
DEGREE_CENTER = 2.0
SPREAD_OFFSET = 0.25
STABILITY_FLOOR = 1e-05

LEAF_SLOTS = 4
HUB_RANK = 16
F32 = jnp.float32
BF16 = jnp.bfloat16
NN = (((1,), (0,)), ((), ()))
NT = (((1,), (1,)), ((), ()))
TN = (((0,), (0,)), ((), ()))
TT = (((0,), (1,)), ((), ()))


def mm(a, b, dims=NN):
    return lax.dot_general(a, b, dims, preferred_element_type=F32)


def iota(shape, dim):
    return lax.broadcasted_iota(jnp.int32, shape, dim)


def to_col(row):
    f = row.shape[1]
    return jnp.sum(jnp.where(iota((f, f), 0) == iota((f, f), 1), row, 0.0), axis=1, keepdims=True)


def to_row(col):
    f = col.shape[0]
    return jnp.sum(jnp.where(iota((f, f), 0) == iota((f, f), 1), col, 0.0), axis=0, keepdims=True)


def fold(value, op):
    return op(value, pltpu.roll(value, 64, 1))


def split_two(value):
    high = value.astype(BF16)
    return high, (value - high.astype(F32)).astype(BF16)


def build_tables(ef_ref, seg_ref, nbr_ref, mask_ref, deg_ref, b_ref, live_ref, rows_ref, g_ref, gt_ref):
    nodes = seg_ref.shape[1]
    seg = seg_ref[...]
    lane_h = iota((1, 128), 1)
    sub_h = iota((128, 1), 0)
    node_row = jnp.zeros((1, 128), jnp.int32)
    node_col = jnp.zeros((128, 1), jnp.int32)
    lane_r, sub_r = lane_h & 15, sub_h & 15
    lane_s, sub_s = (lane_h >> 4) & 3, (sub_h >> 4) & 3
    below = [jnp.sum((seg < s).astype(jnp.int32), axis=1, keepdims=True) for s in range(5)]
    for s in range(4):
        start, size = below[s], below[s + 1] - below[s]
        node_row = jnp.where(lane_s == s, jnp.where(lane_r < size, start + lane_r, -1), node_row)
        node_col = jnp.where(sub_s == s, jnp.where(sub_r < size, start + sub_r, -1), node_col)
    node_col = jnp.where(sub_h < 64, node_col, -1)
    g = (iota((nodes, 128), 0) == node_row).astype(F32).astype(BF16)
    gt = (iota((128, nodes), 1) == node_col).astype(F32).astype(BF16)
    g_ref[...] = g
    gt_ref[...] = gt
    is_hub = jnp.sum(gt.astype(F32), axis=0, keepdims=True)

    nbr = nbr_ref[...]
    mask = (mask_ref[...] > 0).astype(F32)
    nbr_h = (
        mm((nbr >> 3).astype(F32).astype(BF16), g) * 8.0 + mm((nbr & 7).astype(F32).astype(BF16), g)
    ).astype(jnp.int32)
    mask_h = mm(mask.astype(BF16), g)
    valid = (node_row >= 0).astype(F32)
    first = (lane_h < 64).astype(F32)

    def degree_rows(deg):
        log_degree = jnp.log(deg + 1.0)
        return log_degree / DEGREE_CENTER, DEGREE_CENTER / log_degree

    deg = deg_ref[...].astype(F32)
    deg_h = mm(jnp.broadcast_to(deg, (8, nodes)).astype(BF16), g)[0:1]
    deg_h = jnp.where(valid > 0, deg_h, 1.0)
    amp, att = degree_rows(deg)
    amp_h, att_h = degree_rows(deg_h)
    filled = jnp.sum(mask, axis=0, keepdims=True)
    filled_h = jnp.maximum(jnp.sum(mask_h, axis=0, keepdims=True), 1.0)
    rows_ref[...] = jnp.zeros_like(rows_ref)
    for i, (leaf, hub) in enumerate(
        (
            (amp, amp_h),
            (att, att_h),
            (1.0 / filled, 1.0 / filled_h),
            ((seg < 4).astype(F32), None),
            (1.0 - is_hub, valid * first),
            (is_hub, valid),
        )
    ):
        rows_ref[i : i + 1, 0:nodes] = leaf
        if hub is not None:
            rows_ref[i : i + 1, nodes : nodes + 128] = hub

    ef_t = ef_ref[...].T
    ef_h = mm(ef_t, g).astype(BF16)
    node_iota = iota((nodes, nodes), 0)
    hub_iota = iota((nodes, 128), 0)
    zero16 = jnp.zeros((16, nodes), BF16)
    for k in range(LEAF_SLOTS):
        lo = k * nodes
        b_ref[0:nodes, lo : lo + nodes] = (node_iota == nbr[k : k + 1]).astype(F32).astype(BF16)
        piece = ef_t[16 * k : 16 * k + 16]
        for r, part in enumerate((piece, zero16, piece, zero16)):
            b_ref[nodes + 16 * r : nodes + 16 * r + 16, lo : lo + nodes] = part
        live_ref[0:1, lo : lo + nodes] = mask[k : k + 1]
    own_half = (iota((32, 128), 0) < 16) == (iota((32, 128), 1) < 64)
    for j in range(8):
        lo = LEAF_SLOTS * nodes + 128 * j
        index = jnp.where(lane_h < 64, nbr_h[2 * j : 2 * j + 1], nbr_h[2 * j + 1 : 2 * j + 2])
        b_ref[0:nodes, lo : lo + 128] = (hub_iota == index).astype(F32).astype(BF16)
        piece = jnp.where(own_half, ef_h[32 * j : 32 * j + 32].astype(F32), 0.0).astype(BF16)
        b_ref[nodes : nodes + 32, lo : lo + 128] = piece
        b_ref[nodes + 32 : nodes + 64, lo : lo + 128] = piece
        live_ref[0:1, lo : lo + 128] = jnp.where(
            lane_h < 64, mask_h[2 * j : 2 * j + 1], mask_h[2 * j + 1 : 2 * j + 2]
        )


def tower_weights(wpost_ref, layer, t):
    w = wpost_ref[layer, t]
    inner = iota((64, 320), 1) >= 64
    zero = jnp.zeros((64, 320), BF16)
    return jnp.concatenate(
        [w[:, 0:320], jnp.where(inner, w[:, 256:576], zero), jnp.where(inner, w[:, 512:832], zero)], axis=0
    )


def forward_layer(
    layer, x_ref, wedge_ref, wpre_ref, bias, wpost_ref, wmix_ref, b_ref, live_ref, rows_ref, g_ref, gt_ref,
    m_ref, s_ref, z_ref, y_ref, u_ref, part_ref, a_ref, ya_ref,
):
    width, nodes = x_ref.shape
    leaf_cols = LEAF_SLOTS * nodes
    x = x_ref[...]
    g = g_ref[...]
    own = mm(wpre_ref[layer, 0:width], x, TN) + bias
    a_ref[:, 0:nodes] = mm(wpre_ref[layer, width : 2 * width], x, TN).astype(BF16)
    wedge = wedge_ref[layer]
    both = mm(wpre_ref[layer, 2 * width :], jnp.concatenate([wedge] * 4, axis=0), TT)
    high, rest = split_two(both)
    a_ref[:, nodes : nodes + 64] = jnp.where(iota((width, 64), 1) < 32, high, rest)
    own_high, own_rest = split_two(own)
    own_h = mm(own_high, g) + mm(own_rest, g)
    a = a_ref[...]
    for k in range(LEAF_SLOTS):
        lo = k * nodes
        m_ref[:, lo : lo + nodes] = mm(a, b_ref[:, lo : lo + nodes]) + own
    for j in range(8):
        lo = leaf_cols + 128 * j
        m_ref[:, lo : lo + 128] = mm(a, b_ref[:, lo : lo + 128]) + own_h
    x_h = mm(x, g).astype(BF16)
    for t in range(4):
        z_ref[320 * t : 320 * t + 64, 0:nodes] = x[64 * t : 64 * t + 64]
        z_ref[320 * t : 320 * t + 64, nodes:] = x_h[64 * t : 64 * t + 64]

    def summarize(msgs, lives, inv, folded):
        def total(parts, op):
            acc = parts[0]
            for p in parts[1:]:
                acc = op(acc, p)
            return fold(acc, op) if folded else acc

        mean = total([jnp.where(l, m, 0.0) for m, l in zip(msgs, lives)], jnp.add) * inv
        square = total([jnp.where(l, (m - mean) * (m - mean), 0.0) for m, l in zip(msgs, lives)], jnp.add)
        std = jnp.sqrt(square * inv + SPREAD_OFFSET)
        ups = [jnp.where(l, m, -1e30) for m, l in zip(msgs, lives)]
        top = total(ups, jnp.maximum)
        smax = top + jnp.log(total([jnp.exp(m - top) for m in ups], jnp.add))
        downs = [jnp.where(l, m, 1e30) for m, l in zip(msgs, lives)]
        low = total(downs, jnp.minimum)
        smin = low - jnp.log(total([jnp.exp(low - m) for m in downs], jnp.add))
        return mean, smax, smin, std

    def row_step(i, _):
        r = pl.multiple_of(i * 16, 16)
        zr = pl.multiple_of((i // 4) * 320 + 64 + (i % 4) * 16, 16)
        for c in range(nodes // 128 + 1):
            lanes = slice(128 * c, 128 * c + 128)
            if c < nodes // 128:
                cols = [k * nodes + 128 * c for k in range(LEAF_SLOTS)]
            else:
                cols = [leaf_cols + 128 * j for j in range(8)]
            msgs = [m_ref[pl.ds(r, 16), lo : lo + 128] for lo in cols]
            lives = [live_ref[0:1, lo : lo + 128] > 0 for lo in cols]
            stats = summarize(msgs, lives, rows_ref[2:3, lanes], c == nodes // 128)
            if c == nodes // 128:
                stats = [jnp.where(rows_ref[5:6, lanes] > 0, s, 0.0) for s in stats]
            for n, s in enumerate(stats):
                s_ref[n, pl.ds(r, 16), lanes] = s
                z_ref[pl.ds(zr + 64 * n, 16), lanes] = s.astype(BF16)
        return 0

    lax.fori_loop(0, width // 16, row_step, 0)

    amp, att = rows_ref[0:1], rows_ref[1:2]
    for t in range(4):
        r = mm(tower_weights(wpost_ref, layer, t), z_ref[320 * t : 320 * t + 320])
        ya_ref[64 * t : 64 * t + 64] = (r[0:64] + amp * r[64:128] + att * r[128:192]).astype(BF16)
    spread_out = mm(ya_ref[:, nodes:], gt_ref[...])
    y = jnp.where(rows_ref[5:6, 0:nodes] > 0, spread_out, ya_ref[:, 0:nodes].astype(F32)).astype(BF16)
    y_ref[...] = y
    u = mm(wmix_ref[layer], y, TN)
    u_ref[...] = u
    alive = rows_ref[3:4, 0:nodes]
    count = jnp.sum(alive, axis=1, keepdims=True)
    mean = jnp.sum(alive * u, axis=1, keepdims=True) / count
    off = u - mean
    square = jnp.sum(alive * off * off, axis=1, keepdims=True)
    row = jnp.concatenate([to_row(mean), to_row(square), jnp.broadcast_to(count, (1, 128))], axis=1)
    part_ref[...] = jnp.broadcast_to(row[None], part_ref.shape)


def forward_first_kernel(
    layer, nf_ref, ef_ref, seg_ref, nbr_ref, mask_ref, deg_ref, wedge_ref, wpre_ref, bpre_ref, wpost_ref, wmix_ref,
    x_ref, b_ref, live_ref, rows_ref, g_ref, gt_ref, m_ref, s_ref, z_ref, y_ref, u_ref, part_ref,
    a_ref, ya_ref,
):
    build_tables(ef_ref, seg_ref, nbr_ref, mask_ref, deg_ref, b_ref, live_ref, rows_ref, g_ref, gt_ref)
    x_ref[...] = nf_ref[...].T
    forward_layer(
        layer, x_ref, wedge_ref, wpre_ref, to_col(bpre_ref[layer : layer + 1]), wpost_ref, wmix_ref, b_ref, live_ref, rows_ref,
        g_ref, gt_ref, m_ref, s_ref, z_ref, y_ref, u_ref, part_ref, a_ref, ya_ref,
    )


def norm_rows(recv_ref):
    w = (recv_ref.shape[2] - 128) // 2
    recv = recv_ref[...]
    means, squares = recv[:, :, 0:w], recv[:, :, w : 2 * w]
    counts = jnp.concatenate([recv[:, :, 2 * w :]] * (w // 128), axis=2)
    total = jnp.sum(counts, axis=0)
    mean = jnp.sum(counts * means, axis=0) / total
    off = means - mean[None]
    var = jnp.sum(squares + counts * off * off, axis=0) / total
    return mean, lax.rsqrt(var + STABILITY_FLOOR), total


def normed(u, norm_ref, gain_ref, bias_ref, layer):
    xh = (u - to_col(norm_ref[0:1])) * to_col(norm_ref[1:2])
    v = xh * to_col(gain_ref[layer : layer + 1]) + to_col(bias_ref[layer : layer + 1])
    return xh, v


def store_norm(norm_ref, recv_ref):
    mean, scale, total = norm_rows(recv_ref)
    norm_ref[...] = jnp.zeros_like(norm_ref)
    norm_ref[0:1] = mean
    norm_ref[1:2] = scale
    norm_ref[2:3] = total


def forward_next_kernel(
    layer, recv_ref, u0_ref, x0_ref, gain_ref, bias_ref, wedge_ref, wpre_ref, bpre_ref, wpost_ref, wmix_ref,
    b_ref, live_ref, rows_ref, g_ref, gt_ref,
    norm_ref, h_ref, x_ref, m_ref, s_ref, z_ref, y_ref, u_ref, part_ref,
    a_ref, ya_ref,
):
    store_norm(norm_ref, recv_ref)
    _, v = normed(u0_ref[...], norm_ref, gain_ref, bias_ref, layer - 1)
    h = x0_ref[...].astype(F32) + v / (1.0 + jnp.exp(-v))
    h_ref[...] = h
    x_ref[...] = h.astype(BF16)
    forward_layer(
        layer, x_ref, wedge_ref, wpre_ref, to_col(bpre_ref[layer : layer + 1]), wpost_ref, wmix_ref, b_ref, live_ref,
        rows_ref, g_ref, gt_ref, m_ref, s_ref, z_ref, y_ref, u_ref, part_ref, a_ref, ya_ref,
    )


def gate_grad(dh, xh, v, dv_ref, part_ref):
    sig = 1.0 / (1.0 + jnp.exp(-v))
    dv = dh * sig * (1.0 + v * (1.0 - sig))
    dv_ref[...] = dv
    sums = [jnp.sum(p, axis=1, keepdims=True) for p in (dv, dv * xh)]
    row = jnp.concatenate([to_row(s) for s in sums], axis=1)
    part_ref[...] = jnp.broadcast_to(row[None], part_ref.shape)


def readout_kernel(
    layer, recv_ref, u_ref, h_ref, gain_ref, bias_ref, seg_ref, rg_ref,
    norm_ref, readout_ref, dh_ref, dv_ref, part_ref,
):
    store_norm(norm_ref, recv_ref)
    xh, v = normed(u_ref[...], norm_ref, gain_ref, bias_ref, layer)
    h = h_ref[...] + v / (1.0 + jnp.exp(-v))
    nodes = h.shape[1]
    seeds = rg_ref.shape[0]
    belong = (iota((8, nodes), 0) == seg_ref[...]).astype(F32)
    readout = lax.dot_general(belong, h, NT, precision=lax.Precision.HIGHEST, preferred_element_type=F32)
    readout_ref[...] = readout[0:seeds] / SUB_MAX
    dh = jnp.zeros(h.shape, F32)
    for s in range(seeds):
        dh = dh + to_col(rg_ref[s : s + 1]) * belong[s : s + 1]
    dh = dh / SUB_MAX
    dh_ref[...] = dh
    gate_grad(dh, xh, v, dv_ref, part_ref)


def backward_layer(
    layer, recv_ref, dv_ref, dh_ref, u_ref, norm_ref, gain_ref, bias_ref, wmix_ref, wpost_ref, wpre_ref,
    b_ref, live_ref, rows_ref, g_ref, gt_ref, m_ref, s_ref,
    gb_ref, du_ref, d_ref, dm_ref, dcat_ref, et_ref, ds_ref, acc_ref, bd_ref,
):
    width, nodes = dv_ref.shape
    leaf_cols = LEAF_SLOTS * nodes
    sums = jnp.sum(recv_ref[...], axis=0)
    g_bias, g_gain = sums[:, 0:width], sums[:, width:]
    gb_ref[...] = sums
    count = norm_ref[2:3, 0:1]
    xh, _ = normed(u_ref[...], norm_ref, gain_ref, bias_ref, layer)
    alive = rows_ref[3:4, 0:nodes]
    scale = to_col(norm_ref[1:2] * gain_ref[layer : layer + 1])
    du = scale * (dv_ref[...] - alive * (to_col(g_bias) + xh * to_col(g_gain)) / count)
    du = du.astype(BF16)
    du_ref[...] = du
    dy = mm(wmix_ref[layer], du)
    dy_low = dy.astype(BF16)
    dcat_ref[2 * width :] = dy_low
    dy_h = mm(dy_low, g_ref[...])
    keep = rows_ref[4:5]
    amp, att = rows_ref[0:1], rows_ref[1:2]
    dy_all = jnp.concatenate([dy_low.astype(F32), dy_h], axis=1) * keep
    bd_ref[...] = jnp.zeros_like(bd_ref)
    for t in range(4):
        part = dy_all[64 * t : 64 * t + 64]
        d_ref[192 * t : 192 * t + 64] = part.astype(BF16)
        d_ref[192 * t + 64 : 192 * t + 128] = (part * amp).astype(BF16)
        d_ref[192 * t + 128 : 192 * t + 192] = (part * att).astype(BF16)
        w = tower_weights(wpost_ref, layer, t)
        dz = mm(w, d_ref[192 * t : 192 * t + 192], TN)
        for n in range(4):
            rows = slice(64 * t, 64 * t + 64)
            block = dz[64 * (n + 1) : 64 * (n + 2)]
            ds_ref[n, rows, 0:nodes] = block[:, 0:nodes]
            ds_ref[n, rows, nodes:] = fold(block[:, nodes:], jnp.add)
        bd_ref[64 * t : 64 * t + 64, 64 * t : 64 * t + 64] = wpost_ref[layer, t][:, 0:64]

    def row_step(i, _):
        r = pl.multiple_of(i * 16, 16)
        for c in range(nodes // 128 + 1):
            lanes = slice(128 * c, 128 * c + 128)
            if c < nodes // 128:
                cols = [k * nodes + 128 * c for k in range(LEAF_SLOTS)]
            else:
                cols = [leaf_cols + 128 * j for j in range(8)]
            mean, smax, smin, std = (s_ref[n, pl.ds(r, 16), lanes] for n in range(4))
            dmean, dsmax, dsmin, dstd = (ds_ref[n, pl.ds(r, 16), lanes] for n in range(4))
            inv = rows_ref[2:3, lanes]
            c0 = dmean * inv
            c1 = dstd * inv / std
            acc = None
            for lo in cols:
                m = m_ref[pl.ds(r, 16), lo : lo + 128]
                d = c0 + (m - mean) * c1 + dsmax * jnp.exp(m - smax) + dsmin * jnp.exp(smin - m)
                d = jnp.where(live_ref[0:1, lo : lo + 128] > 0, d, 0.0)
                acc = d if acc is None else acc + d
                dm_ref[pl.ds(r, 16), lo : lo + 128] = d.astype(BF16)
            if c == nodes // 128:
                acc = fold(acc, jnp.add)
            acc_ref[pl.ds(r, 16), lanes] = acc
        return 0

    lax.fori_loop(0, width // 16, row_step, 0)

    down = acc_ref[:, 0:nodes] + mm(acc_ref[:, nodes:].astype(BF16), gt_ref[...])
    dcat_ref[0:width] = down.astype(BF16)
    landed = mm(dm_ref[...], b_ref[0 : nodes + 32], NT)
    dcat_ref[width : 2 * width] = landed[:, 0:nodes].astype(BF16)
    et_ref[...] = landed[:, nodes : nodes + 16] + landed[:, nodes + 16 : nodes + 32]
    weights = jnp.concatenate([wpre_ref[layer, 0:width], wpre_ref[layer, width : 2 * width]], axis=1)
    dh = mm(weights, dcat_ref[0 : 2 * width])
    dh = dh + mm(bd_ref[...], dcat_ref[2 * width :], TN)
    return dh_ref[...] + dh


def backward_first_kernel(
    layer, recv_ref, dv_ref, dh_ref, u_ref, norm_ref, gain_ref, bias_ref, wmix_ref, wpost_ref, wpre_ref,
    b_ref, live_ref, rows_ref, g_ref, gt_ref, m_ref, s_ref, u_low_ref, norm_low_ref,
    gb_ref, du_ref, d_ref, dm_ref, dcat_ref, et_ref, acc_ref, dh_out_ref, dv_out_ref, part_ref,
    ds_ref, bd_ref,
):
    dh = backward_layer(
        layer, recv_ref, dv_ref, dh_ref, u_ref, norm_ref, gain_ref, bias_ref, wmix_ref, wpost_ref, wpre_ref,
        b_ref, live_ref, rows_ref, g_ref, gt_ref, m_ref, s_ref,
        gb_ref, du_ref, d_ref, dm_ref, dcat_ref, et_ref, ds_ref, acc_ref, bd_ref,
    )
    dh_out_ref[...] = dh
    xh, v = normed(u_low_ref[...], norm_low_ref, gain_ref, bias_ref, layer - 1)
    gate_grad(dh, xh, v, dv_out_ref, part_ref)


def backward_last_kernel(
    layer, recv_ref, dv_ref, dh_ref, u_ref, norm_ref, gain_ref, bias_ref, wmix_ref, wpost_ref, wpre_ref,
    b_ref, live_ref, rows_ref, g_ref, gt_ref, m_ref, s_ref,
    gb_ref, du_ref, d_ref, dm_ref, dcat_ref, et_ref, acc_ref, node_ref,
    ds_ref, bd_ref,
):
    dh = backward_layer(
        layer, recv_ref, dv_ref, dh_ref, u_ref, norm_ref, gain_ref, bias_ref, wmix_ref, wpost_ref, wpre_ref,
        b_ref, live_ref, rows_ref, g_ref, gt_ref, m_ref, s_ref,
        gb_ref, du_ref, d_ref, dm_ref, dcat_ref, et_ref, ds_ref, acc_ref, bd_ref,
    )
    node_ref[...] = dh.T


def weight_kernel(y_ref, du_ref, d_ref, z_ref, x_ref, dcat_ref, et_ref, acc_ref, grads_ref):
    width, nodes = x_ref.shape
    for t in range(4):
        r = mm(d_ref[192 * t : 192 * t + 192], z_ref[320 * t : 320 * t + 320], NT)
        rows = slice(64 * t, 64 * t + 64)
        inner = iota((64, 320), 1) >= 64
        grads_ref[rows, 0:256] = r[0:64, 0:256]
        grads_ref[rows, 256:512] = jnp.where(
            iota((64, 256), 1) < 64, jnp.concatenate([r[0:64, 256:320]] * 4, axis=1), r[64:128, 0:256]
        )
        grads_ref[rows, 512:768] = jnp.where(
            iota((64, 256), 1) < 64, jnp.concatenate([r[64:128, 256:320]] * 4, axis=1), r[128:192, 0:256]
        )
        grads_ref[rows, 768:832] = r[128:192, 256:320]
    leaf_and_hub = acc_ref[...] * jnp.where(
        iota((1, acc_ref.shape[1]), 1) < nodes + 64, 1.0, 0.0
    )
    bias = jnp.sum(leaf_and_hub, axis=1, keepdims=True)
    grads_ref[:, 832:848] = et_ref[...]
    grads_ref[:, 848:896] = jnp.broadcast_to(bias, (width, 48))
    grads_ref[:, 896:1152] = mm(y_ref[...], du_ref[...], NT)
    both = mm(x_ref[...], dcat_ref[0 : 2 * width], NT)
    grads_ref[:, 1152:1664] = both


def edge_kernel(dm0_ref, dm1_ref, wpre_ref, wedge_ref, gt_ref, out_ref, acc_ref):
    width = dm0_ref.shape[0]
    nodes = gt_ref.shape[1]
    leaf_cols = LEAF_SLOTS * nodes
    total = None
    for layer, dm_ref in ((0, dm0_ref), (1, dm1_ref)):
        w = mm(wedge_ref[layer], wpre_ref[layer, 2 * width :]).astype(BF16)
        part = mm(w, dm_ref[...])
        total = part if total is None else total + part
    hub = total[:, leaf_cols:]
    for j in range(8):
        acc_ref[32 * j : 32 * j + 16] = hub[:, 128 * j : 128 * j + 128]
        acc_ref[32 * j + 16 : 32 * j + 32] = pltpu.roll(hub[:, 128 * j : 128 * j + 128], 64, 1)
    high, rest = split_two(acc_ref[...])
    gt = gt_ref[...]
    spread_out = mm(high, gt) + mm(rest, gt)
    leaf = jnp.concatenate([total[:, k * nodes : (k + 1) * nodes] for k in range(LEAF_SLOTS)], axis=0)
    out = jnp.concatenate([spread_out[0:64] + leaf, spread_out[64:]], axis=0)
    out_ref[...] = out.T


def finish_kernel(g0_ref, g1_ref, wedge_ref, wpre_ref, gedge_ref, gpre_ref, gb_ref, gpost_ref, gmix_ref):
    width = wpre_ref.shape[2]
    for layer, g_ref in ((0, g0_ref), (1, g1_ref)):
        for t in range(4):
            gpost_ref[layer, t] = g_ref[64 * t : 64 * t + 64, 0:832]
        gmix_ref[layer] = g_ref[:, 896:1152]
        gpre_ref[layer, 0:width] = g_ref[:, 1152:1408]
        gpre_ref[layer, width : 2 * width] = g_ref[:, 1408:1664]
        gb_ref[layer : layer + 1] = to_row(g_ref[:, 848:849])
        et = g_ref[:, 832:848]
        wedge = wedge_ref[layer].astype(F32)
        hi = dict(precision=lax.Precision.HIGHEST, preferred_element_type=F32)
        gpre_ref[layer, 2 * width :] = lax.dot_general(wedge, et, TT, **hi)
        gedge_ref[layer] = lax.dot_general(et, wpre_ref[layer, 2 * width :].astype(F32), TT, **hi)


def on_device(
    devices, node_feats, edge_feats, segment_ids, neighbours, nbr_mask, degrees, w_edge, w_pre, b_pre, w_post,
    w_mix, bn_gain, bn_bias, readout_grad,
):
    nodes, width = node_feats.shape
    lanes = nodes + 128
    cols = LEAF_SLOTS * nodes + 1024
    inner = nodes + 64
    seg = segment_ids.reshape(1, nodes)
    deg = degrees.reshape(1, nodes)
    nbr_t = neighbours.T
    mask_t = nbr_mask.T
    wpost_t = jnp.swapaxes(w_post, 2, 3)

    def s(shape, dtype=F32):
        return jax.ShapeDtypeStruct(shape, dtype)

    whole = pl.BlockSpec(memory_space=pltpu.VMEM)

    def call(kernel, args, outs, scratch=(), limit=40):
        return pl.pallas_call(
            kernel,
            in_specs=[whole] * len(args),
            out_specs=[whole] * len(outs),
            out_shape=outs,
            scratch_shapes=list(scratch),
            compiler_params=pltpu.CompilerParams(vmem_limit_bytes=limit * 1024 * 1024),
        )(*args)

    def exchange(part):
        return lax.all_to_all(part, "dp", 0, 0, tiled=True)

    layer_outs = [
        s((width, cols)), s((4, width, lanes)), s((4 * 320, lanes), BF16), s((width, nodes), BF16),
        s((width, nodes)), s((devices, 1, 2 * width + 128)),
    ]
    fwd_scratch = [pltpu.VMEM((width, inner), BF16), pltpu.VMEM((width, lanes), BF16)]
    table_outs = [
        s((inner, cols), BF16), s((1, cols)), s((8, lanes)), s((nodes, 128), BF16), s((128, nodes), BF16),
    ]
    x0, b, live, rows, g, gt, m0, s0, z0, y0, u0, part = call(
        functools.partial(forward_first_kernel, 0),
        [node_feats, edge_feats, seg, nbr_t, mask_t, deg, w_edge, w_pre, b_pre, wpost_t, w_mix],
        [s((width, nodes), BF16)] + table_outs + layer_outs,
        fwd_scratch,
    )
    tables = [b, live, rows, g, gt]
    recv = exchange(part)
    norm0, h1, x1, m1, s1, z1, y1, u1, part = call(
        functools.partial(forward_next_kernel, 1),
        [recv, u0, x0, bn_gain, bn_bias, w_edge, w_pre, b_pre, wpost_t, w_mix] + tables,
        [s((8, width)), s((width, nodes)), s((width, nodes), BF16)] + layer_outs,
        fwd_scratch,
    )
    recv = exchange(part)
    sums_out = s((devices, 1, 2 * width))
    norm1, readout, dh2, dv1, part = call(
        functools.partial(readout_kernel, 1),
        [recv, u1, h1, bn_gain, bn_bias, seg, readout_grad],
        [s((8, width)), s(readout_grad.shape), s((width, nodes)), s((width, nodes)), sums_out],
    )
    back_outs = [
        s((1, 2 * width)), s((width, nodes), BF16), s((4 * 192, lanes), BF16), s((width, cols), BF16),
        s((3 * width, nodes), BF16), s((width, 16)), s((width, lanes)),
    ]
    back_scratch = [pltpu.VMEM((4, width, lanes), F32), pltpu.VMEM((width, width), BF16)]
    recv = exchange(part)
    sums1, du1, d1, dm1, dcat1, et1, acc1, dh1, dv0, part = call(
        functools.partial(backward_first_kernel, 1),
        [recv, dv1, dh2, u1, norm1, bn_gain, bn_bias, w_mix, wpost_t, w_pre] + tables + [m1, s1, u0, norm0],
        back_outs + [s((width, nodes)), s((width, nodes)), sums_out],
        back_scratch,
    )
    recv = exchange(part)
    weight_out = [s((width, 1664))]
    grads1 = call(weight_kernel, [y1, du1, d1, z1, x1, dcat1, et1, acc1], weight_out)[0]
    sums0, du0, d0, dm0, dcat0, et0, acc0, node_grad = call(
        functools.partial(backward_last_kernel, 0),
        [recv, dv0, dh1, u0, norm0, bn_gain, bn_bias, w_mix, wpost_t, w_pre] + tables + [m0, s0],
        back_outs + [s((nodes, width))],
        back_scratch,
    )
    grads0 = call(weight_kernel, [y0, du0, d0, z0, x0, dcat0, et0, acc0], weight_out)[0]
    edge_grad = call(
        edge_kernel, [dm0, dm1, w_pre, w_edge, gt], [s((nodes, width))], [pltpu.VMEM((width, 128), F32)]
    )[0]

    def reduce_all(grads):
        rows_each = width // devices if width >= devices else 1
        pieces = grads.reshape(devices, rows_each, grads.shape[1])
        mine = jnp.sum(lax.all_to_all(pieces, "dp", 0, 0, tiled=True), axis=0)
        spread_out = jnp.broadcast_to(mine[None], pieces.shape)
        return lax.all_to_all(spread_out, "dp", 0, 0, tiled=True).reshape(grads.shape)

    total1 = reduce_all(grads1)
    total0 = reduce_all(grads0)
    layers = w_pre.shape[0]
    g_edge, g_pre, g_b, g_post_t, g_mix = call(
        finish_kernel, [total0, total1, w_edge, w_pre],
        [s(w_edge.shape), s(w_pre.shape), s(b_pre.shape), s((layers, 4, 64, 832)), s(w_mix.shape)],
    )
    sums = jnp.concatenate([sums0, sums1], axis=0)
    return (
        readout, node_grad, edge_grad, g_edge, g_pre, g_b, jnp.swapaxes(g_post_t, 2, 3), g_mix,
        sums[:, width:], sums[:, :width],
    )


def solution(mesh):
    split, split2, full = P("dp"), P("dp", None), P()
    in_specs = (split2, split2, split, split2, split2, split) + (full,) * 7 + (split2,)
    out_specs = (split2, split2, split2) + (full,) * 7
    return jax.shard_map(
        functools.partial(on_device, mesh.shape["dp"]),
        mesh=mesh, in_specs=in_specs, out_specs=out_specs, check_vma=False,
    )
```

time: 1240 us -> 296 us (0.24); the launches traced: 1220 us -> 294 us
  matrix products: 296 us -> 0 us
  local copies, waits for them, and re-layouts: 302 us -> 45.8 us
  blocking collectives: 284 us -> 33.1 us
  other arithmetic: 192 us -> 3.69 us
  Pallas kernels: 0 us -> 55.7 us
  loops' own time: 40.8 us -> 0 us
  waiting for transfers between devices: 93.9 us -> 134 us
  starting transfers between devices: 0.04 us -> 20.5 us
  between operations: 15 us -> 0.87 us
    dot_general x154 -> x0, matrix products: 296 us -> none  [the longest x16 58.1 us: message_block(): jnp.einsum('nkh,hg->nkg', encoded, w_term, preferred_element_type=jnp.flo...]
    psum x7 -> x0, blocking collectives: 284 us -> none  [the longest x2 82.2 us: on_device(): lax.psum((jnp.sum(alive_nodes * projected, axis=0), jnp.sum(alive_nodes))...]
    all_to_all x0 -> x5, waiting for transfers between devices: none -> 134 us  [the longest x2 73.6 us: reduce_all(): lax.all_to_all(spread_out, 'dp', 0, 0, tiled=True).reshape(grads.shape)]
    psum x1 -> x0, waiting for transfers between devices: 93.8 us -> none  [on_device(): lax.psum((lower_set[0], lower_set[1], lower_set[2], lower_set[3], lower_s...]
    while x804 -> x0, local copies, waits for them, and re-layouts: 88.5 us -> none
    reduce_sum x30 -> x2, other arithmetic: 91.1 us -> 3.1 us  [reduce_all(): mine = jnp.sum(lax.all_to_all(pieces, 'dp', 0, 0, tiled=True), axis=0)]
    dynamic_slice x64 -> x0, local copies, waits for them, and re-layouts: 60.4 us -> none  [on_device(): lax.map(forward_block, (blocked(own), blocked(rounded)) + fixed_pieces)]
    pallas_call x0 -> x9, Pallas kernels: none -> 55.7 us  [call(): pl.pallas_call(kernel, in_specs=[whole] * len(args), out_specs=[whole] *...]
  transfers between devices with their start and end apart: 1 -> 5, of which waited for: 1 -> 4; matrix products, arithmetic and copies ran while one was open for 1% -> 1% of each run, Pallas kernels for 0% -> 6%
where the time goes in v1:
time: 296 us; the launch traced here: 294 us
  waiting for transfers between devices  134 us (45%)
  Pallas kernels  55.7 us (19%)
  local copies, waits for them, and re-layouts  45.8 us (15%)
  blocking collectives  33.1 us (11%)
  starting transfers between devices  20.5 us (7%)
  other arithmetic  3.69 us (1%)
    all_to_all x2, waiting for transfers between devices, reduce_all(): lax.all_to_all(spread_out, 'dp', 0, 0, tiled=True).reshape(grads.shape)  73.6 us
    all_to_all x2, waiting for transfers between devices, reduce_all(): mine = jnp.sum(lax.all_to_all(pieces, 'dp', 0, 0, tiled=True), axis=0)  60.9 us
    pallas_call x9, Pallas kernels, call(): pl.pallas_call(kernel, in_specs=[whole] * len(args), out_specs=[whole] *...  55.7 us
    unnamed x100, local copies, waits for them, and re-layouts  41.7 us
    all_to_all x3, blocking collectives, exchange(): return lax.all_to_all(part, 'dp', 0, 0, tiled=True)  33.1 us
    all_to_all x2, starting transfers between devices, reduce_all(): mine = jnp.sum(lax.all_to_all(pieces, 'dp', 0, 0, tiled=True), axis=0)  9.91 us
    all_to_all x2, starting transfers between devices, reduce_all(): lax.all_to_all(spread_out, 'dp', 0, 0, tiled=True).reshape(grads.shape)  8.05 us
  transfers between devices with their start and end apart: 5, of which 4 were waited for; matrix products, arithmetic and copies ran while one was open for 1% of the time, Pallas kernels for 6%

profile of v1, /device:TPU:0, one launch (start us, length us, event | category | flops | bytes accessed | tf_op | source)
XLA Modules:
  0.0 294.1 jit_solution(10204200547649003555)
XLA Ops:
  10.2 10.4 %shard_map.213 = (bf16[256,640]{1,0:T(8,128)(2,1)S(1)}, bf16[704,3584]{1,0:T(8,128)(2,1)}, f32[1,3584]{1,0:T(1,128)S(1)}, f32[8,768]{1,0:T(8,128)S(1)}, bf16[640...) custom-call(bf16[640,256]{1,0:T(8,128)(2,1)S(1)} %copy-done.29, ...), custom_call_target="tpu_custom_call" | custom-call | tf_op jit(solution)/shard_map/pallas_call | solution.py:501
  20.7 1.9 copy-done.6
  22.5 1.6 copy-done.8
  25.5 14.7 %all_to_all.40.recv_ref = f32[32,1,640]{2,1,0:T(1,128)S(1)} all-to-all(f32[32,1,640]{2,1,0:T(1,128)S(1)} %get-tuple-element.59), channel_id=1, replica_groups=mesh['dp'=32] {'dp'}, dimensions={0} | all-to-all | bytes 163840 | tf_op jit(solution)/shard_map/all_to_all | solution.py:511
  40.2 10.5 %shard_map.214 = (f32[8,256]{1,0:T(8,128)S(1)}, f32[256,640]{1,0:T(8,128)S(1)}, bf16[256,640]{1,0:T(8,128)(2,1)S(1)}, f32[256,3584]{1,0:T(8,128)S(1)}, f32[4,256...) custom-call(f32[32,1,640]{2,1,0:T(1,128)S(1)} %all_to_all.40.recv_re, ...), custom_call_target="tpu_custom_call" | custom-call | tf_op jit(solution)/shard_map/pallas_call | solution.py:501
  50.8 1.9 copy-done.7
  52.7 1.7 copy-done.10
  55.7 9.3 %all_to_all.41.recv_ref = f32[32,1,640]{2,1,0:T(1,128)S(1)} all-to-all(f32[32,1,640]{2,1,0:T(1,128)S(1)} %get-tuple-element.67), channel_id=1, replica_groups=mesh['dp'=32] {'dp'}, dimensions={0} | all-to-all | bytes 163840 | tf_op jit(solution)/shard_map/all_to_all | solution.py:511
  65.0 2.1 shard_map.215
  67.1 9.1 %all_to_all.42.recv_ref = f32[32,1,512]{2,1,0:T(1,128)S(1)} all-to-all(f32[32,1,512]{2,1,0:T(1,128)S(1)} %get-tuple-element.71), channel_id=1, replica_groups=mesh['dp'=32] {'dp'}, dimensions={0} | all-to-all | bytes 131072 | tf_op jit(solution)/shard_map/all_to_all | solution.py:511
  76.1 10.7 %shard_map.216 = (f32[1,512]{1,0:T(1,128)S(1)}, bf16[256,640]{1,0:T(8,128)(2,1)S(1)}, bf16[768,768]{1,0:T(8,128)(2,1)S(1)}, bf16[256,3584]{1,0:T(8,128)(2,1)S(1)...) custom-call(f32[32,1,512]{2,1,0:T(1,128)S(1)} %all_to_all.42.recv_re, ...), custom_call_target="tpu_custom_call" | custom-call | tf_op jit(solution)/shard_map/pallas_call | solution.py:501
  94.0 2.6 all-to-all-start.3
  96.5 1.5 copy-done.14
  104.6 2.4 shard_map.220
  107.0 5.9 %all-to-all-start.6 = ((f32[32,8,1664]{2,1,0:T(8,128)}), f32[32,8,1664]{2,1,0:T(8,128)}, u32[]{:S(2)}, u32[]{:S(2)}) async-start(f32[32,8,1664]{2,1,0:T(8,128)} %bitcast.5), calls=%async_computation.6 | async-start | bytes 3407872 | tf_op jit(solution)/shard_map/all_to_all | solution.py:571
  113.0 1.9 copy-done.9
  117.1 10.6 %shard_map.217 = (f32[1,512]{1,0:T(1,128)S(1)}, bf16[256,640]{1,0:T(8,128)(2,1)S(1)}, bf16[768,768]{1,0:T(8,128)(2,1)S(1)}, bf16[256,3584]{1,0:T(8,128)(2,1)S(1)...) custom-call(f32[32,1,512]{2,1,0:T(1,128)S(1)} %all-to-all-done.3.recv_ref,, ...), custom_call_target="tpu_custom_call" | custom-call | tf_op jit(solution)/shard_map/pallas_call | solution.py:501
  128.9 2.4 shard_map.219
  131.4 22.0 %all-to-all-done.6 = f32[32,8,1664]{2,1,0:T(8,128)} async-done(((f32[32,8,1664]{2,1,0:T(8,128)}), f32[32,8,1664]{2,1,0:T(8,128)}, u32[]{:S(2)}, u32[]{:S(2)}) %all-to-all-start.6) | async-done | bytes 1703968 | tf_op jit(solution)/shard_map/all_to_all | solution.py:571
  153.4 4.0 %all-to-all-start.4 = ((f32[32,8,1664]{2,1,0:T(8,128)}), f32[32,8,1664]{2,1,0:T(8,128)S(1)}, u32[]{:S(2)}, u32[]{:S(2)}) async-start(f32[32,8,1664]{2,1,0:T(8,128)} %bitcast.3), calls=%async_computation.4 | async-start | bytes 3407872 | tf_op jit(solution)/shard_map/all_to_all | solution.py:571
  157.4 1.6 reduce_sum.19
  158.9 38.9 %all-to-all-done.4 = f32[32,8,1664]{2,1,0:T(8,128)S(1)} async-done(((f32[32,8,1664]{2,1,0:T(8,128)}), f32[32,8,1664]{2,1,0:T(8,128)S(1)}, u32[]{:S(2)}, u32[]{:S(2)}) %all-to-all-start.4) | async-done | bytes 1703968 | tf_op jit(solution)/shard_map/all_to_all | solution.py:571
  197.8 1.4 broadcast_in_dim.5
  199.5 4.0 %all-to-all-start.7 = ((f32[32,8,1664]{2,1,0:T(8,128)}), f32[32,8,1664]{2,1,0:T(8,128)S(1)}, u32[]{:S(2)}, u32[]{:S(2)}) async-start(f32[32,8,1664]{2,1,0:T(8,128)} %broadcast_in_dim.5), calls=%async_computation.7 | async-start | bytes 3407872 | tf_op jit(solution)/shard_map/all_to_all | solution.py:573
  203.5 1.6 reduce_sum.18
  205.0 38.9 %all-to-all-done.7 = f32[32,8,1664]{2,1,0:T(8,128)S(1)} async-done(((f32[32,8,1664]{2,1,0:T(8,128)}), f32[32,8,1664]{2,1,0:T(8,128)S(1)}, u32[]{:S(2)}, u32[]{:S(2)}) %all-to-all-start.7) | async-done | bytes 1703968 | tf_op jit(solution)/shard_map/all_to_all | solution.py:573
  245.2 4.1 %all-to-all-start.5 = ((f32[32,8,1664]{2,1,0:T(8,128)}), f32[32,8,1664]{2,1,0:T(8,128)}, u32[]{:S(2)}, u32[]{:S(2)}) async-start(f32[32,8,1664]{2,1,0:T(8,128)} %broadcast_in_dim.4), calls=%async_computation.5 | async-start | bytes 3407872 | tf_op jit(solution)/shard_map/all_to_all | solution.py:573
  249.3 1.5 copy-done.16
  250.8 1.5 copy-done.18
  252.3 2.0 shard_map.218
  254.9 34.8 %all-to-all-done.5 = f32[32,8,1664]{2,1,0:T(8,128)} async-done(((f32[32,8,1664]{2,1,0:T(8,128)}), f32[32,8,1664]{2,1,0:T(8,128)}, u32[]{:S(2)}, u32[]{:S(2)}) %all-to-all-start.5) | async-done | bytes 1703968 | tf_op jit(solution)/shard_map/all_to_all | solution.py:573
  289.7 4.4 %shard_map.221 = (f32[2,16,256]{2,1,0:T(8,128)}, f32[2,768,256]{2,1,0:T(8,128)}, f32[2,256]{1,0:T(2,128)}, f32[2,4,64,832]{3,2,1,0:T(8,128)}, f32[2,256,256]{2,1,0:T(8,128)}) custom-call(f32[256,1664]{1,0:T(8,128)} %bitcast.4.g0_ref, f32[256,1664]{1,0:T(8,128)S(1)} %bitcast.12, bf16[2,16,256]{2,1,0:T(8,128)(2,1)S(1)} %copy-done.40, ...), custom_call_target="tpu_custom_call" | custom-call | tf_op jit(solution)/shard_map/pallas_call | solution.py:501
  (97 shorter events, 31.5 us)
Async XLA Ops:
  0.6 39.5 %copy-start.47 = (f32[2,256]{1,0:T(2,128)S(1)}, f32[2,256]{1,0:T(2,128)}, u32[]{:S(2)}) copy-start(f32[2,256]{1,0:T(2,128)} %bpre_ref.3) | copy-start | bytes 6148
  0.7 39.5 %copy-start.45 = (f32[2,256]{1,0:T(2,128)S(1)}, f32[2,256]{1,0:T(2,128)}, u32[]{:S(2)}) copy-start(f32[2,256]{1,0:T(2,128)} %bias_ref.7) | copy-start | bytes 6148
  0.7 39.5 %copy-start.44 = (f32[2,256]{1,0:T(2,128)S(1)}, f32[2,256]{1,0:T(2,128)}, u32[]{:S(2)}) copy-start(f32[2,256]{1,0:T(2,128)} %gain_ref.7) | copy-start | bytes 6148
  10.2 29.9 %copy-start.1 = (bf16[2,768,256]{2,1,0:T(8,128)(2,1)S(1)}, bf16[2,768,256]{2,1,0:T(8,128)(2,1)}, u32[]{:S(2)}) copy-start(bf16[2,768,256]{2,1,0:T(8,128)(2,1)} %wpre_ref.11) | copy-start | bytes 2359300
  10.2 29.9 %copy-start.3 = (bf16[2,4,832,64]{2,3,1,0:T(8,128)(2,1)S(1)}, bf16[2,4,832,64]{2,3,1,0:T(8,128)(2,1)}, u32[]{:S(2)}) copy-start(bf16[2,4,832,64]{2,3,1,0:T(8,128)(2,1)} %param.23) | copy-start | bytes 2555908
  10.2 30.0 %copy-start.5 = (bf16[2,256,256]{2,1,0:T(8,128)(2,1)S(1)}, bf16[2,256,256]{2,1,0:T(8,128)(2,1)}, u32[]{:S(2)}) copy-start(bf16[2,256,256]{2,1,0:T(8,128)(2,1)} %wmix_ref.7) | copy-start | bytes 786436
  20.7 1.9 copy-start.6
  22.5 1.6 copy-start.8
  24.2 1.3 copy-start.11
  25.5 25.3 %copy-start.31 = (bf16[256,640]{1,0:T(8,128)(2,1)}, bf16[256,640]{1,0:T(8,128)(2,1)S(1)}, u32[]{:S(2)}) copy-start(bf16[256,640]{1,0:T(8,128)(2,1)S(1)} %get-tuple-element.86.y_ref) | copy-start | bytes 983044
  40.2 24.8 %copy-start.48 = (f32[4,256]{1,0:T(4,128)S(1)}, f32[4,256]{1,0:T(4,128)}, u32[]{:S(2)}) copy-start(f32[4,256]{1,0:T(4,128)} %rg_ref.1) | copy-start | bytes 12292
  50.8 1.9 copy-start.7
  52.7 1.7 copy-start.10
  54.3 1.3 copy-start.13
  55.7 20.5 %copy-start.33 = (bf16[256,640]{1,0:T(8,128)(2,1)}, bf16[256,640]{1,0:T(8,128)(2,1)S(1)}, u32[]{:S(2)}) copy-start(bf16[256,640]{1,0:T(8,128)(2,1)S(1)} %get-tuple-element.97.x_ref) | copy-start | bytes 983044
  55.7 31.2 %copy-start.35 = (bf16[256,640]{1,0:T(8,128)(2,1)}, bf16[256,640]{1,0:T(8,128)(2,1)S(1)}, u32[]{:S(2)}) copy-start(bf16[256,640]{1,0:T(8,128)(2,1)S(1)} %get-tuple-element.93.y_ref) | copy-start | bytes 983044
  86.8 1.2 copy-start.15
  94.0 13.1 %all-to-all-start.3 = ((f32[32,1,512]{2,1,0:T(1,128)}), f32[32,1,512]{2,1,0:T(1,128)S(1)}, u32[]{:S(2)}, u32[]{:S(2)}) async-start(f32[32,1,512]{2,1,0:T(1,128)} %copy-done.41), calls=%async_computation.3 | async-start | bytes 131072 | tf_op jit(solution)/shard_map/all_to_all | solution.py:511
  96.5 1.5 copy-start.14
  98.1 1.3 copy-start.20
  107.0 46.4 %all-to-all-start.6 = ((f32[32,8,1664]{2,1,0:T(8,128)}), f32[32,8,1664]{2,1,0:T(8,128)}, u32[]{:S(2)}, u32[]{:S(2)}) async-start(f32[32,8,1664]{2,1,0:T(8,128)} %bitcast.5), calls=%async_computation.6 | async-start | bytes 3407872 | tf_op jit(solution)/shard_map/all_to_all | solution.py:571
  113.0 1.9 copy-start.9
  117.1 11.9 %copy-start.12 = (bf16[1280,768]{1,0:T(8,128)(2,1)S(1)}, bf16[1280,768]{1,0:T(8,128)(2,1)}, u32[]{:S(2)}) copy-start(bf16[1280,768]{1,0:T(8,128)(2,1)} %copy-done.11) | copy-start | bytes 5898244
  117.1 11.9 %copy-start.32 = (bf16[256,640]{1,0:T(8,128)(2,1)S(1)}, bf16[256,640]{1,0:T(8,128)(2,1)}, u32[]{:S(2)}) copy-start(bf16[256,640]{1,0:T(8,128)(2,1)} %copy-done.31) | copy-start | bytes 983044
  127.7 1.2 copy-start.17
  153.4 44.4 %all-to-all-start.4 = ((f32[32,8,1664]{2,1,0:T(8,128)}), f32[32,8,1664]{2,1,0:T(8,128)S(1)}, u32[]{:S(2)}, u32[]{:S(2)}) async-start(f32[32,8,1664]{2,1,0:T(8,128)} %bitcast.3), calls=%async_computation.4 | async-start | bytes 3407872 | tf_op jit(solution)/shard_map/all_to_all | solution.py:571
  197.8 1.7 copy-start.49
  199.5 44.4 %all-to-all-start.7 = ((f32[32,8,1664]{2,1,0:T(8,128)}), f32[32,8,1664]{2,1,0:T(8,128)S(1)}, u32[]{:S(2)}, u32[]{:S(2)}) async-start(f32[32,8,1664]{2,1,0:T(8,128)} %broadcast_in_dim.5), calls=%async_computation.7 | async-start | bytes 3407872 | tf_op jit(solution)/shard_map/all_to_all | solution.py:573
  245.2 4.1 %copy-start.40 = (bf16[2,16,256]{2,1,0:T(8,128)(2,1)S(1)}, bf16[2,16,256]{2,1,0:T(8,128)(2,1)}, u32[]{:S(2)}) copy-start(bf16[2,16,256]{2,1,0:T(8,128)(2,1)} %wedge_ref.7) | copy-start | bytes 49156
  245.2 44.5 %all-to-all-start.5 = ((f32[32,8,1664]{2,1,0:T(8,128)}), f32[32,8,1664]{2,1,0:T(8,128)}, u32[]{:S(2)}, u32[]{:S(2)}) async-start(f32[32,8,1664]{2,1,0:T(8,128)} %broadcast_in_dim.4), calls=%async_computation.5 | async-start | bytes 3407872 | tf_op jit(solution)/shard_map/all_to_all | solution.py:573
  249.3 1.5 copy-start.16
  250.8 1.5 copy-start.18
  (23 other events, 21.5 us)

commit v2 on v1

--- a/solution.py
+++ b/solution.py
@@ -47,6 +47,18 @@
 def split_two(value):
     high = value.astype(BF16)
     return high, (value - high.astype(F32)).astype(BF16)
+
+
+def start_copies(pairs, sems):
+    copies = [pltpu.make_async_copy(src, dst, sems.at[i]) for i, (src, dst) in enumerate(pairs)]
+    for copy in copies:
+        copy.start()
+    return copies
+
+
+def wait_all(copies):
+    for copy in copies:
+        copy.wait()
 
 
 def build_tables(ef_ref, seg_ref, nbr_ref, mask_ref, deg_ref, b_ref, live_ref, rows_ref, g_ref, gt_ref):
@@ -141,8 +153,9 @@
 
 def forward_layer(
     layer, x_ref, wedge_ref, wpre_ref, bias, wpost_ref, wmix_ref, b_ref, live_ref, rows_ref, g_ref, gt_ref,
-    m_ref, s_ref, z_ref, y_ref, u_ref, part_ref, a_ref, ya_ref,
-):
+    outs, y_ref, u_ref, part_ref, m_ref, s_ref, z_ref, a_ref, ya_ref, out_sems, ready=lambda: None,
+):
+    m_out, s_out, z_out = outs
     width, nodes = x_ref.shape
     leaf_cols = LEAF_SLOTS * nodes
     x = x_ref[...]
@@ -155,6 +168,7 @@
     a_ref[:, nodes : nodes + 64] = jnp.where(iota((width, 64), 1) < 32, high, rest)
     own_high, own_rest = split_two(own)
     own_h = mm(own_high, g) + mm(own_rest, g)
+    ready()
     a = a_ref[...]
     for k in range(LEAF_SLOTS):
         lo = k * nodes
@@ -162,6 +176,7 @@
     for j in range(8):
         lo = leaf_cols + 128 * j
         m_ref[:, lo : lo + 128] = mm(a, b_ref[:, lo : lo + 128]) + own_h
+    copies = start_copies([(m_ref, m_out)], out_sems)
     x_h = mm(x, g).astype(BF16)
     for t in range(4):
         z_ref[320 * t : 320 * t + 64, 0:nodes] = x[64 * t : 64 * t + 64]
@@ -205,6 +220,7 @@
         return 0
 
     lax.fori_loop(0, width // 16, row_step, 0)
+    copies += start_copies([(s_ref, s_out), (z_ref, z_out)], out_sems.at[1:3])
 
     amp, att = rows_ref[0:1], rows_ref[1:2]
     for t in range(4):
@@ -222,19 +238,33 @@
     square = jnp.sum(alive * off * off, axis=1, keepdims=True)
     row = jnp.concatenate([to_row(mean), to_row(square), jnp.broadcast_to(count, (1, 128))], axis=1)
     part_ref[...] = jnp.broadcast_to(row[None], part_ref.shape)
+    wait_all(copies)
 
 
 def forward_first_kernel(
-    layer, nf_ref, ef_ref, seg_ref, nbr_ref, mask_ref, deg_ref, wedge_ref, wpre_ref, bpre_ref, wpost_ref, wmix_ref,
-    x_ref, b_ref, live_ref, rows_ref, g_ref, gt_ref, m_ref, s_ref, z_ref, y_ref, u_ref, part_ref,
-    a_ref, ya_ref,
-):
+    layer, nf_hbm, ef_hbm, seg_ref, nbr_hbm, mask_hbm, deg_ref, wedge_hbm, wpre_hbm, bpre_hbm, wpost_hbm, wmix_hbm,
+    x_ref, b_out, live_ref, rows_ref, g_ref, gt_ref, m_out, s_out, z_out, y_ref, u_ref, part_ref,
+    m_ref, s_ref, z_ref, a_ref, ya_ref, out_sems, b_ref, nf_ref, ef_ref, nbr_ref, mask_ref, wedge_ref, wpre_ref,
+    bpre_ref, wpost_ref, wmix_ref, in_sems, b_sem,
+):
+    loads = start_copies(
+        [
+            (nbr_hbm, nbr_ref), (mask_hbm, mask_ref), (ef_hbm, ef_ref), (nf_hbm, nf_ref), (wpre_hbm, wpre_ref),
+            (wedge_hbm, wedge_ref), (bpre_hbm, bpre_ref), (wpost_hbm, wpost_ref), (wmix_hbm, wmix_ref),
+        ],
+        in_sems,
+    )
+    wait_all(loads[0:3])
     build_tables(ef_ref, seg_ref, nbr_ref, mask_ref, deg_ref, b_ref, live_ref, rows_ref, g_ref, gt_ref)
+    stores = start_copies([(b_ref, b_out)], b_sem)
+    wait_all(loads[3:])
     x_ref[...] = nf_ref[...].T
     forward_layer(
-        layer, x_ref, wedge_ref, wpre_ref, to_col(bpre_ref[layer : layer + 1]), wpost_ref, wmix_ref, b_ref, live_ref, rows_ref,
-        g_ref, gt_ref, m_ref, s_ref, z_ref, y_ref, u_ref, part_ref, a_ref, ya_ref,
-    )
+        layer, x_ref, wedge_ref, wpre_ref, to_col(bpre_ref[layer : layer + 1]), wpost_ref, wmix_ref, b_ref,
+        live_ref, rows_ref, g_ref, gt_ref, (m_out, s_out, z_out), y_ref, u_ref, part_ref,
+        m_ref, s_ref, z_ref, a_ref, ya_ref, out_sems,
+    )
+    wait_all(stores)
 
 
 def norm_rows(recv_ref):
@@ -265,18 +295,20 @@
 
 def forward_next_kernel(
     layer, recv_ref, u0_ref, x0_ref, gain_ref, bias_ref, wedge_ref, wpre_ref, bpre_ref, wpost_ref, wmix_ref,
-    b_ref, live_ref, rows_ref, g_ref, gt_ref,
-    norm_ref, h_ref, x_ref, m_ref, s_ref, z_ref, y_ref, u_ref, part_ref,
-    a_ref, ya_ref,
-):
+    b_hbm, live_ref, rows_ref, g_ref, gt_ref,
+    norm_ref, h_ref, x_ref, m_out, s_out, z_out, y_ref, u_ref, part_ref,
+    m_ref, s_ref, z_ref, a_ref, ya_ref, out_sems, b_ref, b_sem,
+):
+    loads = start_copies([(b_hbm, b_ref)], b_sem)
     store_norm(norm_ref, recv_ref)
     _, v = normed(u0_ref[...], norm_ref, gain_ref, bias_ref, layer - 1)
     h = x0_ref[...].astype(F32) + v / (1.0 + jnp.exp(-v))
     h_ref[...] = h
     x_ref[...] = h.astype(BF16)
     forward_layer(
-        layer, x_ref, wedge_ref, wpre_ref, to_col(bpre_ref[layer : layer + 1]), wpost_ref, wmix_ref, b_ref, live_ref,
-        rows_ref, g_ref, gt_ref, m_ref, s_ref, z_ref, y_ref, u_ref, part_ref, a_ref, ya_ref,
+        layer, x_ref, wedge_ref, wpre_ref, to_col(bpre_ref[layer : layer + 1]), wpost_ref, wmix_ref, b_ref,
+        live_ref, rows_ref, g_ref, gt_ref, (m_out, s_out, z_out), y_ref, u_ref, part_ref,
+        m_ref, s_ref, z_ref, a_ref, ya_ref, out_sems, lambda: wait_all(loads),
     )
 
 
@@ -311,9 +343,10 @@
 
 def backward_layer(
     layer, recv_ref, dv_ref, dh_ref, u_ref, norm_ref, gain_ref, bias_ref, wmix_ref, wpost_ref, wpre_ref,
-    b_ref, live_ref, rows_ref, g_ref, gt_ref, m_ref, s_ref,
-    gb_ref, du_ref, d_ref, dm_ref, dcat_ref, et_ref, ds_ref, acc_ref, bd_ref,
-):
+    b_hbm, live_ref, rows_ref, g_ref, gt_ref, m_hbm, s_hbm,
+    gb_ref, du_ref, d_ref, dm_ref, dcat_ref, et_ref, ds_ref, acc_ref, bd_ref, m_ref, s_ref, b_ref, in_sems,
+):
+    loads = start_copies([(m_hbm, m_ref), (s_hbm, s_ref), (b_hbm, b_ref)], in_sems)
     width, nodes = dv_ref.shape
     leaf_cols = LEAF_SLOTS * nodes
     sums = jnp.sum(recv_ref[...], axis=0)
@@ -348,6 +381,8 @@
             ds_ref[n, rows, nodes:] = fold(block[:, nodes:], jnp.add)
         bd_ref[64 * t : 64 * t + 64, 64 * t : 64 * t + 64] = wpost_ref[layer, t][:, 0:64]
 
+    wait_all(loads[0:2])
+
     def row_step(i, _):
         r = pl.multiple_of(i * 16, 16)
         for c in range(nodes // 128 + 1):
@@ -377,9 +412,13 @@
 
     down = acc_ref[:, 0:nodes] + mm(acc_ref[:, nodes:].astype(BF16), gt_ref[...])
     dcat_ref[0:width] = down.astype(BF16)
+    wait_all(loads[2:])
     landed = mm(dm_ref[...], b_ref[0 : nodes + 32], NT)
     dcat_ref[width : 2 * width] = landed[:, 0:nodes].astype(BF16)
-    et_ref[...] = landed[:, nodes : nodes + 16] + landed[:, nodes + 16 : nodes + 32]
+    once = jnp.where(iota((1, nodes + 128), 1) < nodes + 64, acc_ref[...], 0.0)
+    bias = jnp.sum(once, axis=1, keepdims=True)
+    factor = landed[:, nodes : nodes + 16] + landed[:, nodes + 16 : nodes + 32]
+    et_ref[...] = jnp.concatenate([factor, jnp.broadcast_to(bias, (width, 48))], axis=1)
     weights = jnp.concatenate([wpre_ref[layer, 0:width], wpre_ref[layer, width : 2 * width]], axis=1)
     dh = mm(weights, dcat_ref[0 : 2 * width])
     dh = dh + mm(bd_ref[...], dcat_ref[2 * width :], TN)
@@ -388,57 +427,83 @@
 
 def backward_first_kernel(
     layer, recv_ref, dv_ref, dh_ref, u_ref, norm_ref, gain_ref, bias_ref, wmix_ref, wpost_ref, wpre_ref,
-    b_ref, live_ref, rows_ref, g_ref, gt_ref, m_ref, s_ref, u_low_ref, norm_low_ref,
-    gb_ref, du_ref, d_ref, dm_ref, dcat_ref, et_ref, acc_ref, dh_out_ref, dv_out_ref, part_ref,
-    ds_ref, bd_ref,
+    b_hbm, live_ref, rows_ref, g_ref, gt_ref, m_hbm, s_hbm, u_low_ref, norm_low_ref,
+    gb_ref, du_out, d_out, dm_out, dcat_out, et_out, dh_out_ref, dv_out_ref, part_ref,
+    du_ref, d_ref, dm_ref, dcat_ref, et_ref, ds_ref, acc_ref, bd_ref, m_ref, s_ref, b_ref, in_sems, out_sems,
 ):
     dh = backward_layer(
         layer, recv_ref, dv_ref, dh_ref, u_ref, norm_ref, gain_ref, bias_ref, wmix_ref, wpost_ref, wpre_ref,
-        b_ref, live_ref, rows_ref, g_ref, gt_ref, m_ref, s_ref,
-        gb_ref, du_ref, d_ref, dm_ref, dcat_ref, et_ref, ds_ref, acc_ref, bd_ref,
+        b_hbm, live_ref, rows_ref, g_ref, gt_ref, m_hbm, s_hbm,
+        gb_ref, du_ref, d_ref, dm_ref, dcat_ref, et_ref, ds_ref, acc_ref, bd_ref, m_ref, s_ref, b_ref, in_sems,
+    )
+    stores = start_copies(
+        [(dcat_ref, dcat_out), (et_ref, et_out), (du_ref, du_out), (d_ref, d_out), (dm_ref, dm_out)], out_sems
     )
     dh_out_ref[...] = dh
     xh, v = normed(u_low_ref[...], norm_low_ref, gain_ref, bias_ref, layer - 1)
     gate_grad(dh, xh, v, dv_out_ref, part_ref)
-
-
-def backward_last_kernel(
-    layer, recv_ref, dv_ref, dh_ref, u_ref, norm_ref, gain_ref, bias_ref, wmix_ref, wpost_ref, wpre_ref,
-    b_ref, live_ref, rows_ref, g_ref, gt_ref, m_ref, s_ref,
-    gb_ref, du_ref, d_ref, dm_ref, dcat_ref, et_ref, acc_ref, node_ref,
-    ds_ref, bd_ref,
-):
-    dh = backward_layer(
-        layer, recv_ref, dv_ref, dh_ref, u_ref, norm_ref, gain_ref, bias_ref, wmix_ref, wpost_ref, wpre_ref,
-        b_ref, live_ref, rows_ref, g_ref, gt_ref, m_ref, s_ref,
-        gb_ref, du_ref, d_ref, dm_ref, dcat_ref, et_ref, ds_ref, acc_ref, bd_ref,
-    )
-    node_ref[...] = dh.T
-
-
-def weight_kernel(y_ref, du_ref, d_ref, z_ref, x_ref, dcat_ref, et_ref, acc_ref, grads_ref):
+    wait_all(stores)
+
+
+def piece_owner(devices, half, place):
+    return half | ((place >> 2) << 1) | ((place & 3) << 3)
+
+
+def put_weight_grads(y_ref, du_ref, d_ref, z_ref, x_ref, dcat_ref, et_ref, grads_ref, keep_ref, send_ref):
     width, nodes = x_ref.shape
     for t in range(4):
         r = mm(d_ref[192 * t : 192 * t + 192], z_ref[320 * t : 320 * t + 320], NT)
         rows = slice(64 * t, 64 * t + 64)
-        inner = iota((64, 320), 1) >= 64
+        first = iota((64, 256), 1) < 64
         grads_ref[rows, 0:256] = r[0:64, 0:256]
-        grads_ref[rows, 256:512] = jnp.where(
-            iota((64, 256), 1) < 64, jnp.concatenate([r[0:64, 256:320]] * 4, axis=1), r[64:128, 0:256]
-        )
+        grads_ref[rows, 256:512] = jnp.where(first, jnp.concatenate([r[0:64, 256:320]] * 4, axis=1), r[64:128, 0:256])
         grads_ref[rows, 512:768] = jnp.where(
-            iota((64, 256), 1) < 64, jnp.concatenate([r[64:128, 256:320]] * 4, axis=1), r[128:192, 0:256]
+            first, jnp.concatenate([r[64:128, 256:320]] * 4, axis=1), r[128:192, 0:256]
         )
         grads_ref[rows, 768:832] = r[128:192, 256:320]
-    leaf_and_hub = acc_ref[...] * jnp.where(
-        iota((1, acc_ref.shape[1]), 1) < nodes + 64, 1.0, 0.0
-    )
-    bias = jnp.sum(leaf_and_hub, axis=1, keepdims=True)
-    grads_ref[:, 832:848] = et_ref[...]
-    grads_ref[:, 848:896] = jnp.broadcast_to(bias, (width, 48))
+    grads_ref[:, 832:896] = et_ref[...]
     grads_ref[:, 896:1152] = mm(y_ref[...], du_ref[...], NT)
-    both = mm(x_ref[...], dcat_ref[0 : 2 * width], NT)
-    grads_ref[:, 1152:1664] = both
+    grads_ref[:, 1152:1664] = mm(x_ref[...], dcat_ref[0 : 2 * width], NT)
+    me = lax.axis_index("dp") & 31
+    for place in range(16):
+        for half, ref in ((0, keep_ref), (1, send_ref)):
+            row = pl.multiple_of((me ^ piece_owner(32, half, place)) * 8, 8)
+            ref[8 * place : 8 * place + 8] = grads_ref[pl.ds(row, 8)]
+
+
+def weight_kernel(
+    y_hbm, du_hbm, d_hbm, z_hbm, x_hbm, dcat_hbm, et_hbm, keep_ref, send_ref,
+    y_ref, du_ref, d_ref, z_ref, x_ref, dcat_ref, et_ref, grads_ref, in_sems,
+):
+    loads = start_copies(
+        [
+            (z_hbm, z_ref), (d_hbm, d_ref), (y_hbm, y_ref), (du_hbm, du_ref), (x_hbm, x_ref),
+            (dcat_hbm, dcat_ref), (et_hbm, et_ref),
+        ],
+        in_sems,
+    )
+    wait_all(loads)
+    put_weight_grads(y_ref, du_ref, d_ref, z_ref, x_ref, dcat_ref, et_ref, grads_ref, keep_ref, send_ref)
+
+
+def backward_last_kernel(
+    layer, recv_ref, dv_ref, dh_ref, u_ref, norm_ref, gain_ref, bias_ref, wmix_ref, wpost_ref, wpre_ref,
+    b_hbm, live_ref, rows_ref, g_ref, gt_ref, m_hbm, s_hbm, z_hbm, y_ref, x_ref,
+    gb_ref, dm_out, node_ref, keep_ref, send_ref,
+    du_ref, d_ref, dm_ref, dcat_ref, et_ref, ds_ref, acc_ref, bd_ref, m_ref, s_ref, b_ref, in_sems, out_sems,
+    z_ref, grads_ref, z_sem,
+):
+    loads = start_copies([(z_hbm, z_ref)], z_sem)
+    dh = backward_layer(
+        layer, recv_ref, dv_ref, dh_ref, u_ref, norm_ref, gain_ref, bias_ref, wmix_ref, wpost_ref, wpre_ref,
+        b_hbm, live_ref, rows_ref, g_ref, gt_ref, m_hbm, s_hbm,
+        gb_ref, du_ref, d_ref, dm_ref, dcat_ref, et_ref, ds_ref, acc_ref, bd_ref, m_ref, s_ref, b_ref, in_sems,
+    )
+    stores = start_copies([(dm_ref, dm_out)], out_sems)
+    node_ref[...] = dh.T
+    wait_all(loads)
+    put_weight_grads(y_ref, du_ref, d_ref, z_ref, x_ref, dcat_ref, et_ref, grads_ref, keep_ref, send_ref)
+    wait_all(stores)
 
 
 def edge_kernel(dm0_ref, dm1_ref, wpre_ref, wedge_ref, gt_ref, out_ref, acc_ref):
@@ -462,16 +527,23 @@
     out_ref[...] = out.T
 
 
-def finish_kernel(g0_ref, g1_ref, wedge_ref, wpre_ref, gedge_ref, gpre_ref, gb_ref, gpost_ref, gmix_ref):
+def finish_kernel(
+    a0_ref, b0_ref, a1_ref, b1_ref, wedge_ref, wpre_ref, gedge_ref, gpre_ref, gb_ref, gpost_ref, gmix_ref, et_ref
+):
     width = wpre_ref.shape[2]
-    for layer, g_ref in ((0, g0_ref), (1, g1_ref)):
-        for t in range(4):
-            gpost_ref[layer, t] = g_ref[64 * t : 64 * t + 64, 0:832]
-        gmix_ref[layer] = g_ref[:, 896:1152]
-        gpre_ref[layer, 0:width] = g_ref[:, 1152:1408]
-        gpre_ref[layer, width : 2 * width] = g_ref[:, 1408:1664]
-        gb_ref[layer : layer + 1] = to_row(g_ref[:, 848:849])
-        et = g_ref[:, 832:848]
+    me = lax.axis_index("dp") & 31
+    for layer, halves in ((0, (a0_ref, b0_ref)), (1, (a1_ref, b1_ref))):
+        for place in range(16):
+            for half in range(2):
+                row = pl.multiple_of((me ^ piece_owner(32, half, place)) * 8, 8)
+                piece = halves[half][8 * place : 8 * place + 8]
+                gpost_ref[layer, pl.ds(row, 8)] = piece[:, 0:832]
+                et_ref[pl.ds(row, 8)] = piece[:, 832:896]
+                gmix_ref[layer, pl.ds(row, 8)] = piece[:, 896:1152]
+                gpre_ref[layer, pl.ds(row, 8)] = piece[:, 1152:1408]
+                gpre_ref[layer, pl.ds(width + row, 8)] = piece[:, 1408:1664]
+        gb_ref[layer : layer + 1] = to_row(et_ref[:, 16:17])
+        et = et_ref[:, 0:16]
         wedge = wedge_ref[layer].astype(F32)
         hi = dict(precision=lax.Precision.HIGHEST, preferred_element_type=F32)
         gpre_ref[layer, 2 * width :] = lax.dot_general(wedge, et, TT, **hi)
@@ -495,94 +567,112 @@
     def s(shape, dtype=F32):
         return jax.ShapeDtypeStruct(shape, dtype)
 
-    whole = pl.BlockSpec(memory_space=pltpu.VMEM)
-
-    def call(kernel, args, outs, scratch=(), limit=40):
+    vmem = pl.BlockSpec(memory_space=pltpu.VMEM)
+    hbm = pl.BlockSpec(memory_space=pltpu.HBM)
+
+    def call(kernel, args, outs, scratch=(), far=(), far_out=(), limit=20):
         return pl.pallas_call(
             kernel,
-            in_specs=[whole] * len(args),
-            out_specs=[whole] * len(outs),
+            in_specs=[hbm if i in far else vmem for i in range(len(args))],
+            out_specs=[hbm if i in far_out else vmem for i in range(len(outs))],
             out_shape=outs,
             scratch_shapes=list(scratch),
             compiler_params=pltpu.CompilerParams(vmem_limit_bytes=limit * 1024 * 1024),
         )(*args)
 
+    def like(shapes):
+        return [pltpu.VMEM(x.shape, x.dtype) for x in shapes]
+
+    def dma(n):
+        return pltpu.SemaphoreType.DMA((n,))
+
     def exchange(part):
         return lax.all_to_all(part, "dp", 0, 0, tiled=True)
 
-    layer_outs = [
-        s((width, cols)), s((4, width, lanes)), s((4 * 320, lanes), BF16), s((width, nodes), BF16),
-        s((width, nodes)), s((devices, 1, 2 * width + 128)),
-    ]
-    fwd_scratch = [pltpu.VMEM((width, inner), BF16), pltpu.VMEM((width, lanes), BF16)]
-    table_outs = [
-        s((inner, cols), BF16), s((1, cols)), s((8, lanes)), s((nodes, 128), BF16), s((128, nodes), BF16),
-    ]
+    m_s, s_s, z_s = s((width, cols)), s((4, width, lanes)), s((4 * 320, lanes), BF16)
+    b_s = s((inner, cols), BF16)
+    row_s, low_s = s((width, nodes)), s((width, nodes), BF16)
+    layer_outs = [m_s, s_s, z_s, low_s, row_s, s((devices, 1, 2 * width + 128))]
+    fwd_scratch = like([m_s, s_s, z_s, s((width, inner), BF16), s((width, lanes), BF16)]) + [dma(3)]
+    table_outs = [b_s, s((1, cols)), s((8, lanes)), s((nodes, 128), BF16), s((128, nodes), BF16)]
+    first_args = [node_feats, edge_feats, seg, nbr_t, mask_t, deg, w_edge, w_pre, b_pre, wpost_t, w_mix]
     x0, b, live, rows, g, gt, m0, s0, z0, y0, u0, part = call(
         functools.partial(forward_first_kernel, 0),
-        [node_feats, edge_feats, seg, nbr_t, mask_t, deg, w_edge, w_pre, b_pre, wpost_t, w_mix],
-        [s((width, nodes), BF16)] + table_outs + layer_outs,
-        fwd_scratch,
+        first_args, [low_s] + table_outs + layer_outs,
+        fwd_scratch + like([b_s] + [a for i, a in enumerate(first_args) if i not in (2, 5)]) + [dma(9), dma(1)],
+        (0, 1, 3, 4, 6, 7, 8, 9, 10), (1, 6, 7, 8), 48,
     )
     tables = [b, live, rows, g, gt]
     recv = exchange(part)
     norm0, h1, x1, m1, s1, z1, y1, u1, part = call(
         functools.partial(forward_next_kernel, 1),
         [recv, u0, x0, bn_gain, bn_bias, w_edge, w_pre, b_pre, wpost_t, w_mix] + tables,
-        [s((8, width)), s((width, nodes)), s((width, nodes), BF16)] + layer_outs,
-        fwd_scratch,
+        [s((8, width)), row_s, low_s] + layer_outs,
+        fwd_scratch + like([b_s]) + [dma(1)], (10,), (3, 4, 5), 40,
     )
     recv = exchange(part)
     sums_out = s((devices, 1, 2 * width))
     norm1, readout, dh2, dv1, part = call(
         functools.partial(readout_kernel, 1),
         [recv, u1, h1, bn_gain, bn_bias, seg, readout_grad],
-        [s((8, width)), s(readout_grad.shape), s((width, nodes)), s((width, nodes)), sums_out],
-    )
-    back_outs = [
-        s((1, 2 * width)), s((width, nodes), BF16), s((4 * 192, lanes), BF16), s((width, cols), BF16),
-        s((3 * width, nodes), BF16), s((width, 16)), s((width, lanes)),
-    ]
-    back_scratch = [pltpu.VMEM((4, width, lanes), F32), pltpu.VMEM((width, width), BF16)]
+        [s((8, width)), s(readout_grad.shape), row_s, row_s, sums_out],
+    )
+    sum_s = s((1, 2 * width))
+    du_s, d_s, dm_s = low_s, s((4 * 192, lanes), BF16), s((width, cols), BF16)
+    dcat_s, et_s, acc_s = s((3 * width, nodes), BF16), s((width, 64)), s((width, lanes))
+    back_scratch = like([du_s, d_s, dm_s, dcat_s, et_s, s_s, acc_s, s((width, width), BF16), m_s, s_s, b_s])
     recv = exchange(part)
-    sums1, du1, d1, dm1, dcat1, et1, acc1, dh1, dv0, part = call(
+    sums1, du1, d1, dm1, dcat1, et1, dh1, dv0, part = call(
         functools.partial(backward_first_kernel, 1),
         [recv, dv1, dh2, u1, norm1, bn_gain, bn_bias, w_mix, wpost_t, w_pre] + tables + [m1, s1, u0, norm0],
-        back_outs + [s((width, nodes)), s((width, nodes)), sums_out],
-        back_scratch,
+        [sum_s, du_s, d_s, dm_s, dcat_s, et_s, row_s, row_s, sums_out],
+        back_scratch + [dma(3), dma(5)], (10, 15, 16), (1, 2, 3, 4, 5), 40,
     )
     recv = exchange(part)
-    weight_out = [s((width, 1664))]
-    grads1 = call(weight_kernel, [y1, du1, d1, z1, x1, dcat1, et1, acc1], weight_out)[0]
-    sums0, du0, d0, dm0, dcat0, et0, acc0, node_grad = call(
+    grad_cols = 1664
+    grad_s, half_s = s((width, grad_cols)), s((width // 2, grad_cols))
+    halves1 = call(
+        weight_kernel, [y1, du1, d1, z1, x1, dcat1, et1], [half_s, half_s],
+        like([low_s, du_s, d_s, z_s, low_s, dcat_s, et_s, grad_s]) + [dma(7)], range(7), (), 20,
+    )
+    sums0, dm0, node_grad, *halves0 = call(
         functools.partial(backward_last_kernel, 0),
-        [recv, dv0, dh1, u0, norm0, bn_gain, bn_bias, w_mix, wpost_t, w_pre] + tables + [m0, s0],
-        back_outs + [s((nodes, width))],
-        back_scratch,
-    )
-    grads0 = call(weight_kernel, [y0, du0, d0, z0, x0, dcat0, et0, acc0], weight_out)[0]
+        [recv, dv0, dh1, u0, norm0, bn_gain, bn_bias, w_mix, wpost_t, w_pre] + tables + [m0, s0, z0, y0, x0],
+        [sum_s, dm_s, s((nodes, width)), half_s, half_s],
+        back_scratch + [dma(3), dma(1)] + like([z_s, grad_s]) + [dma(1)], (10, 15, 16, 17), (1,), 44,
+    )
     edge_grad = call(
         edge_kernel, [dm0, dm1, w_pre, w_edge, gt], [s((nodes, width))], [pltpu.VMEM((width, 128), F32)]
     )[0]
 
-    def reduce_all(grads):
-        rows_each = width // devices if width >= devices else 1
-        pieces = grads.reshape(devices, rows_each, grads.shape[1])
-        mine = jnp.sum(lax.all_to_all(pieces, "dp", 0, 0, tiled=True), axis=0)
-        spread_out = jnp.broadcast_to(mine[None], pieces.shape)
-        return lax.all_to_all(spread_out, "dp", 0, 0, tiled=True).reshape(grads.shape)
-
-    total1 = reduce_all(grads1)
-    total0 = reduce_all(grads0)
+    def swap(value, mask):
+        return lax.ppermute(value, "dp", [(i, i ^ mask) for i in range(devices)])
+
+    def reduce_all(keep, send):
+        part = keep + swap(send, 1)
+        for step, size in ((1, 32), (3, 8)):
+            got = [swap(part[size * i : size * (i + 1)], i << step) for i in range(1, 4)]
+            part = part[0:size] + got[0] + got[1] + got[2]
+        mask = 32
+        while mask < devices:
+            part = part + swap(part, mask)
+            mask *= 2
+        for step in (3, 1):
+            part = jnp.concatenate([part] + [swap(part, i << step) for i in range(1, 4)], axis=0)
+        return part, swap(part, 1)
+
+    total1 = reduce_all(*halves1)
+    total0 = reduce_all(*halves0)
     layers = w_pre.shape[0]
     g_edge, g_pre, g_b, g_post_t, g_mix = call(
-        finish_kernel, [total0, total1, w_edge, w_pre],
-        [s(w_edge.shape), s(w_pre.shape), s(b_pre.shape), s((layers, 4, 64, 832)), s(w_mix.shape)],
-    )
+        finish_kernel, [*total0, *total1, w_edge, w_pre],
+        [s(w_edge.shape), s(w_pre.shape), s(b_pre.shape), s((layers, width, 832)), s(w_mix.shape)],
+        [pltpu.VMEM((width, 64), F32)],
+    )
+    g_post = jnp.swapaxes(g_post_t.reshape(wpost_t.shape), 2, 3)
     sums = jnp.concatenate([sums0, sums1], axis=0)
     return (
-        readout, node_grad, edge_grad, g_edge, g_pre, g_b, jnp.swapaxes(g_post_t, 2, 3), g_mix,
-        sums[:, width:], sums[:, :width],
+        readout, node_grad, edge_grad, g_edge, g_pre, g_b, g_post, g_mix, sums[:, width:], sums[:, :width],
     )
 
 

time: 296 us -> 176 us (0.59)
  waiting for transfers between devices: 134 us -> 35.3 us
  local copies, waits for them, and re-layouts: 45.8 us -> 11.7 us
  blocking collectives: 33.1 us -> 43.6 us
  starting transfers between devices: 20.5 us -> 28.9 us
    all_to_all x5 -> x0, waiting for transfers between devices: 134 us -> none  [the longest x2 73.6 us: reduce_all(): lax.all_to_all(spread_out, 'dp', 0, 0, tiled=True).reshape(grads.shape)]
    ppermute x0 -> x28, waiting for transfers between devices: none -> 35.3 us  [swap(): return lax.ppermute(value, 'dp', [(i, i ^ mask) for i in range(devices)])]
    unnamed x100 -> x42, local copies, waits for them, and re-layouts: 41.7 us -> 10.1 us
    ppermute x0 -> x28, starting transfers between devices: none -> 28.9 us  [swap(): return lax.ppermute(value, 'dp', [(i, i ^ mask) for i in range(devices)])]
    all_to_all x5 -> x0, starting transfers between devices: 20.5 us -> none  [the longest x2 9.91 us: reduce_all(): mine = jnp.sum(lax.all_to_all(pieces, 'dp', 0, 0, tiled=True), axis=0)]
    all_to_all x3 -> x4, blocking collectives: 33.1 us -> 43.6 us  [exchange(): return lax.all_to_all(part, 'dp', 0, 0, tiled=True)]
    reduce_sum x2 -> x0, other arithmetic: 3.1 us -> none  [reduce_all(): mine = jnp.sum(lax.all_to_all(pieces, 'dp', 0, 0, tiled=True), axis=0)]
    pallas_call x9 -> x8, Pallas kernels: 55.7 us -> 53.6 us  [call(): pl.pallas_call(kernel, in_specs=[hbm if i in far else vmem for i in range...]
  transfers between devices with their start and end apart: 5 -> 28, of which waited for: 4 -> 14; matrix products, arithmetic and copies ran while one was open for 1% -> 1% of each run, Pallas kernels for 6% -> 8%
where the time goes in v2:
time: 176 us; the launch traced here: 175 us
  Pallas kernels  53.6 us (30%)
  blocking collectives  43.6 us (25%)
  waiting for transfers between devices  35.3 us (20%)
  starting transfers between devices  28.9 us (16%)
  local copies, waits for them, and re-layouts  11.7 us (7%)
    pallas_call x8, Pallas kernels, call(): pl.pallas_call(kernel, in_specs=[hbm if i in far else vmem for i in range...  53.6 us
    all_to_all x4, blocking collectives, exchange(): return lax.all_to_all(part, 'dp', 0, 0, tiled=True)  43.6 us
    ppermute x28, waiting for transfers between devices, swap(): return lax.ppermute(value, 'dp', [(i, i ^ mask) for i in range(devices)])  35.3 us
    ppermute x28, starting transfers between devices, swap(): return lax.ppermute(value, 'dp', [(i, i ^ mask) for i in range(devices)])  28.9 us
    unnamed x42, local copies, waits for them, and re-layouts  10.1 us
  transfers between devices with their start and end apart: 28, of which 14 were waited for; matrix products, arithmetic and copies ran while one was open for 1% of the time, Pallas kernels for 8%

profile of v2, /device:TPU:0, one launch (start us, length us, event | category | flops | bytes accessed | tf_op | source)
XLA Modules:
  0.0 174.9 jit_solution(14859511172971222992)
XLA Ops:
  10.2 12.3 %shard_map.213 = (bf16[256,640]{1,0:T(8,128)(2,1)S(1)}, bf16[704,3584]{1,0:T(8,128)(2,1)}, f32[1,3584]{1,0:T(1,128)S(1)}, f32[8,768]{1,0:T(8,128)S(1)}, bf16[640...) custom-call(bf16[640,256]{1,0:T(8,128)(2,1)S(1)} %copy-done.7, ...), custom_call_target="tpu_custom_call" | custom-call | tf_op jit(solution)/shard_map/pallas_call | solution.py:574
  22.5 14.7 %all_to_all.20.recv_ref = f32[32,1,640]{2,1,0:T(1,128)S(1)} all-to-all(f32[32,1,640]{2,1,0:T(1,128)S(1)} %get-tuple-element.57), channel_id=1, replica_groups=mesh['dp'=32] {'dp'}, dimensions={0} | all-to-all | bytes 163840 | tf_op jit(solution)/shard_map/all_to_all | solution.py:590
  37.2 11.5 %shard_map.214 = (f32[8,256]{1,0:T(8,128)S(1)}, f32[256,640]{1,0:T(8,128)S(1)}, bf16[256,640]{1,0:T(8,128)(2,1)S(1)}, f32[256,3584]{1,0:T(8,128)S(1)}, f32[4,256...) custom-call(f32[32,1,640]{2,1,0:T(1,128)S(1)} %all_to_all.20.recv_re, ...), custom_call_target="tpu_custom_call" | custom-call | tf_op jit(solution)/shard_map/pallas_call | solution.py:574
  48.8 1.9 %copy-done.6 = f32[256,3584]{1,0:T(8,128)} copy-done((f32[256,3584]{1,0:T(8,128)}, f32[256,3584]{1,0:T(8,128)S(1)}, u32[]{:S(2)}) %copy-start.6) | copy-done | bytes 3670040
  50.6 9.3 %all_to_all.21.recv_ref = f32[32,1,640]{2,1,0:T(1,128)S(1)} all-to-all(f32[32,1,640]{2,1,0:T(1,128)S(1)} %get-tuple-element.65), channel_id=1, replica_groups=mesh['dp'=32] {'dp'}, dimensions={0} | all-to-all | bytes 163840 | tf_op jit(solution)/shard_map/all_to_all | solution.py:590
  59.9 2.1 %shard_map.215 = (f32[8,256]{1,0:T(8,128)S(1)}, f32[4,256]{1,0:T(4,128)}, f32[256,640]{1,0:T(8,128)S(1)}, f32[256,640]{1,0:T(8,128)S(1)}, f32[32,1,512]{2,1,0:T(1,128)S(1)}) custom-call(f32[32,1,640]{2,1,0:T(1,128)S(1)} %all_to_all.21.recv_ref, f32[256,640]{1,0:T(8,128)S(1)} %get-tuple-element.66.u_ref, f32[256,640]{1,0:T(8,128)S(1)} %get-tuple-element.67.h_ref, ...), custom_call_target="tpu_custom_call" | custom-call | tf_op jit(solution)/shard_map/pallas_call | solution.py:574
  62.0 9.1 %all_to_all.22.recv_ref = f32[32,1,512]{2,1,0:T(1,128)S(1)} all-to-all(f32[32,1,512]{2,1,0:T(1,128)S(1)} %get-tuple-element.69), channel_id=1, replica_groups=mesh['dp'=32] {'dp'}, dimensions={0} | all-to-all | bytes 131072 | tf_op jit(solution)/shard_map/all_to_all | solution.py:590
  71.1 8.6 %shard_map.216 = (f32[1,512]{1,0:T(1,128)S(1)}, bf16[256,640]{1,0:T(8,128)(2,1)S(1)}, bf16[768,768]{1,0:T(8,128)(2,1)S(1)}, bf16[256,3584]{1,0:T(8,128)(2,1)S(1)...) custom-call(f32[32,1,512]{2,1,0:T(1,128)S(1)} %all_to_all.22.recv_re, ...), custom_call_target="tpu_custom_call" | custom-call | tf_op jit(solution)/shard_map/pallas_call | solution.py:574
  79.7 2.7 %shard_map.219 = (f32[128,1664]{1,0:T(8,128)S(1)}, f32[128,1664]{1,0:T(8,128)S(1)}) custom-call(bf16[256,640]{1,0:T(8,128)(2,1)S(1)} %get-tuple-element.88.y_hbm, bf16[256,640]{1,0:T(8,128)(2,1)S(1)} %get-tuple-element.89.du_hbm, bf16[768,768]{1,0:T(8,128)(2,1)S(1)} %get-tuple-element.90.d_hbm, bf16[1280,768]{1,0:T(8,128)(2,1)S(1)} %get-tuple-element.91.z_hbm, ...), custom_call_target="tpu_custom_call" | custom-call | tf_op jit(solution)/shard_map/pallas_call | solution.py:574
  82.6 2.3 %collective-permute-done.14 = f32[128,1664]{1,0:T(8,128)S(1)} collective-permute-done((f32[128,1664]{1,0:T(8,128)S(1)}, f32[128,1664]{1,0:T(8,128)S(1)}, u32[]{:S(2)}, u32[]{:S(2)}) %collective-permute-start.14) | collective-permute-done | bytes 852000 | tf_op jit(solution)/shard_map/ppermute | solution.py:649
  85.5 1.6 collective-permute-start.17
  87.1 1.4 collective-permute-start.16
  88.5 10.6 %all_to_all.23.recv_ref = f32[32,1,512]{2,1,0:T(1,128)S(1)} all-to-all(f32[32,1,512]{2,1,0:T(1,128)S(1)} %get-tuple-element.76), channel_id=1, replica_groups=mesh['dp'=32] {'dp'}, dimensions={0} | all-to-all | bytes 131072 | tf_op jit(solution)/shard_map/all_to_all | solution.py:590
  99.1 11.3 %shard_map.217 = (f32[1,512]{1,0:T(1,128)S(1)}, bf16[256,3584]{1,0:T(8,128)(2,1)S(1)}, f32[640,256]{1,0:T(8,128)}, f32[128,1664]{1,0:T(8,128)S(1)}, f32[128,1664]{1,0:T(8,128)S(1)}) custom-call(f32[32,1,512]{2,1,0:T(1,128)S(1)} %all_to_all.23.recv_ref, f32[256,640]{1,0:T(8,128)S(1)} %get-tuple-element.77.dv_ref, f32[256,640]{1,0:T(8,128)S(1)} %get-tuple-element.78.dh_ref, ...), custom_call_target="tpu_custom_call" | custom-call | tf_op jit(solution)/shard_map/pallas_call | solution.py:574
  111.3 1.5 collective-permute-start.20
  114.9 2.8 %collective-permute-done.20 = f32[8,1664]{1,0:T(8,128)S(1)} collective-permute-done((f32[8,1664]{1,0:T(8,128)S(1)}, f32[8,1664]{1,0:T(8,128)S(1)}, u32[]{:S(2)}, u32[]{:S(2)}) %collective-permute-start.20) | collective-permute-done | bytes 53280 | tf_op jit(solution)/shard_map/ppermute | solution.py:649
  117.7 2.0 %collective-permute-done.19 = f32[8,1664]{1,0:T(8,128)S(1)} collective-permute-done((f32[8,1664]{1,0:T(8,128)S(1)}, f32[8,1664]{1,0:T(8,128)S(1)}, u32[]{:S(2)}, u32[]{:S(2)}) %collective-permute-start.19) | collective-permute-done | bytes 53280 | tf_op jit(solution)/shard_map/ppermute | solution.py:649
  121.2 3.1 %collective-permute-start.21 = (f32[8,1664]{1,0:T(8,128)S(1)}, f32[8,1664]{1,0:T(8,128)S(1)}, u32[]{:S(2)}, u32[]{:S(2)}) collective-permute-start(f32[8,1664]{1,0:T(8,128)S(1)} %get-tuple-element.105), channel_id=1, source_target_pairs={{0,8},{1,9},{2,10},{3,11},{4,12},{5,13},{6,14},{7,15},{8,0},{9,1},... | collective-permute-start | bytes 159752 | tf_op jit(solution)/shard_map/ppermute | solution.py:649
  125.0 2.2 %collective-permute-start.3 = (f32[32,1664]{1,0:T(8,128)S(1)}, f32[32,1664]{1,0:T(8,128)S(1)}, u32[]{:S(2)}, u32[]{:S(2)}) collective-permute-start(f32[32,1664]{1,0:T(8,128)S(1)} %get-tuple-element.112), channel_id=1, source_target_pairs={{0,6},{1,7},{2,4},{3,5},{4,2},{5,3},{6,0},{7,1},{8,14},{9,15},{10,... | collective-permute-start | bytes 638984 | tf_op jit(solution)/shard_map/ppermute | solution.py:649
  130.1 2.4 %collective-permute-done.1 = f32[32,1664]{1,0:T(8,128)S(1)} collective-permute-done((f32[32,1664]{1,0:T(8,128)S(1)}, f32[32,1664]{1,0:T(8,128)S(1)}, u32[]{:S(2)}, u32[]{:S(2)}) %collective-permute-start.1) | collective-permute-done | bytes 213024 | tf_op jit(solution)/shard_map/ppermute | solution.py:649
  132.5 5.6 %collective-permute-done.3 = f32[32,1664]{1,0:T(8,128)S(1)} collective-permute-done((f32[32,1664]{1,0:T(8,128)S(1)}, f32[32,1664]{1,0:T(8,128)S(1)}, u32[]{:S(2)}, u32[]{:S(2)}) %collective-permute-start.3) | collective-permute-done | bytes 213024 | tf_op jit(solution)/shard_map/ppermute | solution.py:649
  138.1 5.6 %collective-permute-done.2 = f32[32,1664]{1,0:T(8,128)S(1)} collective-permute-done((f32[32,1664]{1,0:T(8,128)S(1)}, f32[32,1664]{1,0:T(8,128)S(1)}, u32[]{:S(2)}, u32[]{:S(2)}) %collective-permute-start.2) | collective-permute-done | bytes 213024 | tf_op jit(solution)/shard_map/ppermute | solution.py:649
  144.2 1.5 collective-permute-start.6
  145.7 1.7 collective-permute-start.5
  148.0 2.1 %collective-permute-done.6 = f32[8,1664]{1,0:T(8,128)S(1)} collective-permute-done((f32[8,1664]{1,0:T(8,128)S(1)}, f32[8,1664]{1,0:T(8,128)S(1)}, u32[]{:S(2)}, u32[]{:S(2)}) %collective-permute-start.6) | collective-permute-done | bytes 53280 | tf_op jit(solution)/shard_map/ppermute | solution.py:649
  151.3 2.4 %collective-permute-start.9 = (f32[8,1664]{1,0:T(8,128)S(1)}, f32[8,1664]{1,0:T(8,128)S(1)}, u32[]{:S(2)}, u32[]{:S(2)}) collective-permute-start(f32[8,1664]{1,0:T(8,128)S(1)} %get-tuple-element.107), channel_id=1, source_target_pairs={{0,24},{1,25},{2,26},{3,27},{4,28},{5,29},{6,30},{7,31},{8,16},{9,... | collective-permute-start | bytes 159752 | tf_op jit(solution)/shard_map/ppermute | solution.py:649
  153.7 2.1 %collective-permute-start.7 = (f32[8,1664]{1,0:T(8,128)S(1)}, f32[8,1664]{1,0:T(8,128)S(1)}, u32[]{:S(2)}, u32[]{:S(2)}) collective-permute-start(f32[8,1664]{1,0:T(8,128)S(1)} %get-tuple-element.107), channel_id=1, source_target_pairs={{0,8},{1,9},{2,10},{3,11},{4,12},{5,13},{6,14},{7,15},{8,0},{9,1},... | collective-permute-start | bytes 159752 | tf_op jit(solution)/shard_map/ppermute | solution.py:649
  155.8 1.5 collective-permute-done.9
  160.9 2.2 %collective-permute-done.24 = f32[32,1664]{1,0:T(8,128)S(1)} collective-permute-done((f32[32,1664]{1,0:T(8,128)S(1)}, f32[32,1664]{1,0:T(8,128)S(1)}, u32[]{:S(2)}, u32[]{:S(2)}) %collective-permute-start.24) | collective-permute-done | bytes 213024 | tf_op jit(solution)/shard_map/ppermute | solution.py:649
  163.8 5.2 %collective-permute-done.10 = f32[32,1664]{1,0:T(8,128)S(1)} collective-permute-done((f32[32,1664]{1,0:T(8,128)S(1)}, f32[32,1664]{1,0:T(8,128)S(1)}, u32[]{:S(2)}, u32[]{:S(2)}) %collective-permute-start.10) | collective-permute-done | bytes 213024 | tf_op jit(solution)/shard_map/ppermute | solution.py:649
  169.2 2.0 %shard_map.218 = f32[640,256]{1,0:T(8,128)} custom-call(bf16[256,3584]{1,0:T(8,128)(2,1)S(1)} %get-tuple-element.84.dm0_ref, bf16[256,3584]{1,0:T(8,128)(2,1)S(1)} %get-tuple-element.85.dm1_ref, bf16[2,768,256]{2,1,0:T(8,128)(2,1)S(1)} %copy-done.1, bf16[2,16,256]{2,1,0:T(8,128)(2,1)S(1)} %copy-done.9, bf16[128,640]{1,0:T(8,128)(2,1)S(1)} %get-tuple-element.64.gt_ref), custom_call_target="tpu_custom_call" | custom-call | tf_op jit(solution)/shard_map/pallas_call | solution.py:574
  171.8 3.0 %shard_map.220 = (f32[2,16,256]{2,1,0:T(8,128)}, f32[2,768,256]{2,1,0:T(8,128)}, f32[2,256]{1,0:T(2,128)}, f32[2,256,832]{2,1,0:T(8,128)}, f32[2,256,256]{2,1,0:T(8,128)}) custom-call(f32[128,1664]{1,0:T(8,128)S(1)} %constant_dynamic-update-slice_fusion.a0_ref, f32[128,1664]{1,0:T(8,128)S(1)} %collective-permute-done.13.b0_ref, ...), custom_call_target="tpu_custom_call" | custom-call | tf_op jit(solution)/shard_map/pallas_call | solution.py:574
  (95 shorter events, 25.5 us)
Async XLA Ops:
  0.6 36.6 %copy-start.13 = (f32[2,256]{1,0:T(2,128)S(1)}, f32[2,256]{1,0:T(2,128)}, u32[]{:S(2)}) copy-start(f32[2,256]{1,0:T(2,128)} %bias_ref.7) | copy-start | bytes 6148
  0.7 36.6 %copy-start.12 = (f32[2,256]{1,0:T(2,128)S(1)}, f32[2,256]{1,0:T(2,128)}, u32[]{:S(2)}) copy-start(f32[2,256]{1,0:T(2,128)} %gain_ref.7) | copy-start | bytes 6148
  10.2 27.0 %copy-start.3 = (bf16[2,4,832,64]{2,3,1,0:T(8,128)(2,1)S(1)}, bf16[2,4,832,64]{2,3,1,0:T(8,128)(2,1)}, u32[]{:S(2)}) copy-start(bf16[2,4,832,64]{2,3,1,0:T(8,128)(2,1)} %param.23) | copy-start | bytes 2555908
  10.2 27.0 %copy-start.5 = (bf16[2,256,256]{2,1,0:T(8,128)(2,1)S(1)}, bf16[2,256,256]{2,1,0:T(8,128)(2,1)}, u32[]{:S(2)}) copy-start(bf16[2,256,256]{2,1,0:T(8,128)(2,1)} %wmix_ref.5) | copy-start | bytes 786436
  82.4 2.4 %collective-permute-start.14 = (f32[128,1664]{1,0:T(8,128)S(1)}, f32[128,1664]{1,0:T(8,128)S(1)}, u32[]{:S(2)}, u32[]{:S(2)}) collective-permute-start(f32[128,1664]{1,0:T(8,128)S(1)} %get-tuple-element.96), channel_id=1, source_target_pairs={{0,1},{1,0},{2,3},{3,2},{4,5},{5,4},{6,7},{7,6},{8,9},{9,8},{10,11... | collective-permute-start | bytes 2555912 | tf_op jit(solution)/shard_map/ppermute | solution.py:649
  85.0 25.6 %collective-permute-start.15 = (f32[32,1664]{1,0:T(8,128)S(1)}, f32[32,1664]{1,0:T(8,128)S(1)}, u32[]{:S(2)}, u32[]{:S(2)}) collective-permute-start(f32[32,1664]{1,0:T(8,128)S(1)} %get-tuple-element.108), channel_id=1, source_target_pairs={{0,2},{1,3},{2,0},{3,1},{4,6},{5,7},{6,4},{7,5},{8,10},{9,11},{10,... | collective-permute-start | bytes 638984 | tf_op jit(solution)/shard_map/ppermute | solution.py:649
  85.5 25.1 %collective-permute-start.17 = (f32[32,1664]{1,0:T(8,128)S(1)}, f32[32,1664]{1,0:T(8,128)S(1)}, u32[]{:S(2)}, u32[]{:S(2)}) collective-permute-start(f32[32,1664]{1,0:T(8,128)S(1)} %get-tuple-element.109), channel_id=1, source_target_pairs={{0,6},{1,7},{2,4},{3,5},{4,2},{5,3},{6,0},{7,1},{8,14},{9,15},{10,... | collective-permute-start | bytes 638984 | tf_op jit(solution)/shard_map/ppermute | solution.py:649
  87.1 23.5 %collective-permute-start.16 = (f32[32,1664]{1,0:T(8,128)S(1)}, f32[32,1664]{1,0:T(8,128)S(1)}, u32[]{:S(2)}, u32[]{:S(2)}) collective-permute-start(f32[32,1664]{1,0:T(8,128)S(1)} %get-tuple-element.110), channel_id=1, source_target_pairs={{0,4},{1,5},{2,6},{3,7},{4,0},{5,1},{6,2},{7,3},{8,12},{9,13},{10,... | collective-permute-start | bytes 638984 | tf_op jit(solution)/shard_map/ppermute | solution.py:649
  110.4 3.8 %collective-permute-start = (f32[128,1664]{1,0:T(8,128)S(1)}, f32[128,1664]{1,0:T(8,128)S(1)}, u32[]{:S(2)}, u32[]{:S(2)}) collective-permute-start(f32[128,1664]{1,0:T(8,128)S(1)} %get-tuple-element.87), channel_id=1, source_target_pairs={{0,1},{1,0},{2,3},{3,2},{4,5},{5,4},{6,7},{7,6},{8,9},{9,8},{10,11... | collective-permute-start | bytes 2555912 | tf_op jit(solution)/shard_map/ppermute | solution.py:649
  110.7 4.2 %collective-permute-start.18 = (f32[8,1664]{1,0:T(8,128)S(1)}, f32[8,1664]{1,0:T(8,128)S(1)}, u32[]{:S(2)}, u32[]{:S(2)}) collective-permute-start(f32[8,1664]{1,0:T(8,128)S(1)} %get-tuple-element.114), channel_id=1, source_target_pairs={{0,8},{1,9},{2,10},{3,11},{4,12},{5,13},{6,14},{7,15},{8,0},{9,1},... | collective-permute-start | bytes 159752 | tf_op jit(solution)/shard_map/ppermute | solution.py:649
  111.3 6.4 %collective-permute-start.20 = (f32[8,1664]{1,0:T(8,128)S(1)}, f32[8,1664]{1,0:T(8,128)S(1)}, u32[]{:S(2)}, u32[]{:S(2)}) collective-permute-start(f32[8,1664]{1,0:T(8,128)S(1)} %get-tuple-element.115), channel_id=1, source_target_pairs={{0,24},{1,25},{2,26},{3,27},{4,28},{5,29},{6,30},{7,31},{8,16},{9,... | collective-permute-start | bytes 159752 | tf_op jit(solution)/shard_map/ppermute | solution.py:649
  112.9 6.9 %collective-permute-start.19 = (f32[8,1664]{1,0:T(8,128)S(1)}, f32[8,1664]{1,0:T(8,128)S(1)}, u32[]{:S(2)}, u32[]{:S(2)}) collective-permute-start(f32[8,1664]{1,0:T(8,128)S(1)} %get-tuple-element.116), channel_id=1, source_target_pairs={{0,16},{1,17},{2,18},{3,19},{4,20},{5,21},{6,22},{7,23},{8,24},{9,... | collective-permute-start | bytes 159752 | tf_op jit(solution)/shard_map/ppermute | solution.py:649
  119.8 7.5 %collective-permute-start.23 = (f32[8,1664]{1,0:T(8,128)S(1)}, f32[8,1664]{1,0:T(8,128)S(1)}, u32[]{:S(2)}, u32[]{:S(2)}) collective-permute-start(f32[8,1664]{1,0:T(8,128)S(1)} %get-tuple-element.105), channel_id=1, source_target_pairs={{0,24},{1,25},{2,26},{3,27},{4,28},{5,29},{6,30},{7,31},{8,16},{9,... | collective-permute-start | bytes 159752 | tf_op jit(solution)/shard_map/ppermute | solution.py:649
  121.2 6.7 %collective-permute-start.22 = (f32[8,1664]{1,0:T(8,128)S(1)}, f32[8,1664]{1,0:T(8,128)S(1)}, u32[]{:S(2)}, u32[]{:S(2)}) collective-permute-start(f32[8,1664]{1,0:T(8,128)S(1)} %get-tuple-element.105), channel_id=1, source_target_pairs={{0,16},{1,17},{2,18},{3,19},{4,20},{5,21},{6,22},{7,23},{8,24},{9,... | collective-permute-start | bytes 159752 | tf_op jit(solution)/shard_map/ppermute | solution.py:649
  121.2 6.7 %collective-permute-start.21 = (f32[8,1664]{1,0:T(8,128)S(1)}, f32[8,1664]{1,0:T(8,128)S(1)}, u32[]{:S(2)}, u32[]{:S(2)}) collective-permute-start(f32[8,1664]{1,0:T(8,128)S(1)} %get-tuple-element.105), channel_id=1, source_target_pairs={{0,8},{1,9},{2,10},{3,11},{4,12},{5,13},{6,14},{7,15},{8,0},{9,1},... | collective-permute-start | bytes 159752 | tf_op jit(solution)/shard_map/ppermute | solution.py:649
  124.3 8.3 %collective-permute-start.1 = (f32[32,1664]{1,0:T(8,128)S(1)}, f32[32,1664]{1,0:T(8,128)S(1)}, u32[]{:S(2)}, u32[]{:S(2)}) collective-permute-start(f32[32,1664]{1,0:T(8,128)S(1)} %get-tuple-element.111), channel_id=1, source_target_pairs={{0,2},{1,3},{2,0},{3,1},{4,6},{5,7},{6,4},{7,5},{8,10},{9,11},{10,... | collective-permute-start | bytes 638984 | tf_op jit(solution)/shard_map/ppermute | solution.py:649
  125.0 13.1 %collective-permute-start.3 = (f32[32,1664]{1,0:T(8,128)S(1)}, f32[32,1664]{1,0:T(8,128)S(1)}, u32[]{:S(2)}, u32[]{:S(2)}) collective-permute-start(f32[32,1664]{1,0:T(8,128)S(1)} %get-tuple-element.112), channel_id=1, source_target_pairs={{0,6},{1,7},{2,4},{3,5},{4,2},{5,3},{6,0},{7,1},{8,14},{9,15},{10,... | collective-permute-start | bytes 638984 | tf_op jit(solution)/shard_map/ppermute | solution.py:649
  127.3 16.4 %collective-permute-start.2 = (f32[32,1664]{1,0:T(8,128)S(1)}, f32[32,1664]{1,0:T(8,128)S(1)}, u32[]{:S(2)}, u32[]{:S(2)}) collective-permute-start(f32[32,1664]{1,0:T(8,128)S(1)} %get-tuple-element.113), channel_id=1, source_target_pairs={{0,4},{1,5},{2,6},{3,7},{4,0},{5,1},{6,2},{7,3},{8,12},{9,13},{10,... | collective-permute-start | bytes 638984 | tf_op jit(solution)/shard_map/ppermute | solution.py:649
  127.9 35.8 %collective-permute-start.26 = (f32[32,1664]{1,0:T(8,128)S(1)}, f32[32,1664]{1,0:T(8,128)S(1)}, u32[]{:S(2)}, u32[]{:S(2)}) collective-permute-start(f32[32,1664]{1,0:T(8,128)S(1)} %pad_maximum_fusion.1), channel_id=1, source_target_pairs={{0,6},{1,7},{2,4},{3,5},{4,2},{5,3},{6,0},{7,1},{8,14},{9,15},{10,... | collective-permute-start | bytes 638984 | tf_op jit(solution)/shard_map/ppermute | solution.py:649
  129.3 34.3 %collective-permute-start.25 = (f32[32,1664]{1,0:T(8,128)S(1)}, f32[32,1664]{1,0:T(8,128)S(1)}, u32[]{:S(2)}, u32[]{:S(2)}) collective-permute-start(f32[32,1664]{1,0:T(8,128)S(1)} %pad_maximum_fusion.1), channel_id=1, source_target_pairs={{0,4},{1,5},{2,6},{3,7},{4,0},{5,1},{6,2},{7,3},{8,12},{9,13},{10,... | collective-permute-start | bytes 638984 | tf_op jit(solution)/shard_map/ppermute | solution.py:649
  143.8 4.2 %collective-permute-start.4 = (f32[8,1664]{1,0:T(8,128)S(1)}, f32[8,1664]{1,0:T(8,128)S(1)}, u32[]{:S(2)}, u32[]{:S(2)}) collective-permute-start(f32[8,1664]{1,0:T(8,128)S(1)} %get-tuple-element.117), channel_id=1, source_target_pairs={{0,8},{1,9},{2,10},{3,11},{4,12},{5,13},{6,14},{7,15},{8,0},{9,1},... | collective-permute-start | bytes 159752 | tf_op jit(solution)/shard_map/ppermute | solution.py:649
  144.2 5.9 %collective-permute-start.6 = (f32[8,1664]{1,0:T(8,128)S(1)}, f32[8,1664]{1,0:T(8,128)S(1)}, u32[]{:S(2)}, u32[]{:S(2)}) collective-permute-start(f32[8,1664]{1,0:T(8,128)S(1)} %get-tuple-element.118), channel_id=1, source_target_pairs={{0,24},{1,25},{2,26},{3,27},{4,28},{5,29},{6,30},{7,31},{8,16},{9,... | collective-permute-start | bytes 159752 | tf_op jit(solution)/shard_map/ppermute | solution.py:649
  145.7 5.6 %collective-permute-start.5 = (f32[8,1664]{1,0:T(8,128)S(1)}, f32[8,1664]{1,0:T(8,128)S(1)}, u32[]{:S(2)}, u32[]{:S(2)}) collective-permute-start(f32[8,1664]{1,0:T(8,128)S(1)} %get-tuple-element.119), channel_id=1, source_target_pairs={{0,16},{1,17},{2,18},{3,19},{4,20},{5,21},{6,22},{7,23},{8,24},{9,... | collective-permute-start | bytes 159752 | tf_op jit(solution)/shard_map/ppermute | solution.py:649
  151.3 6.0 %collective-permute-start.9 = (f32[8,1664]{1,0:T(8,128)S(1)}, f32[8,1664]{1,0:T(8,128)S(1)}, u32[]{:S(2)}, u32[]{:S(2)}) collective-permute-start(f32[8,1664]{1,0:T(8,128)S(1)} %get-tuple-element.107), channel_id=1, source_target_pairs={{0,24},{1,25},{2,26},{3,27},{4,28},{5,29},{6,30},{7,31},{8,16},{9,... | collective-permute-start | bytes 159752 | tf_op jit(solution)/shard_map/ppermute | solution.py:649
  153.7 5.0 %collective-permute-start.8 = (f32[8,1664]{1,0:T(8,128)S(1)}, f32[8,1664]{1,0:T(8,128)S(1)}, u32[]{:S(2)}, u32[]{:S(2)}) collective-permute-start(f32[8,1664]{1,0:T(8,128)S(1)} %get-tuple-element.107), channel_id=1, source_target_pairs={{0,16},{1,17},{2,18},{3,19},{4,20},{5,21},{6,22},{7,23},{8,24},{9,... | collective-permute-start | bytes 159752 | tf_op jit(solution)/shard_map/ppermute | solution.py:649
  153.7 5.0 %collective-permute-start.7 = (f32[8,1664]{1,0:T(8,128)S(1)}, f32[8,1664]{1,0:T(8,128)S(1)}, u32[]{:S(2)}, u32[]{:S(2)}) collective-permute-start(f32[8,1664]{1,0:T(8,128)S(1)} %get-tuple-element.107), channel_id=1, source_target_pairs={{0,8},{1,9},{2,10},{3,11},{4,12},{5,13},{6,14},{7,15},{8,0},{9,1},... | collective-permute-start | bytes 159752 | tf_op jit(solution)/shard_map/ppermute | solution.py:649
  157.3 5.8 %collective-permute-start.24 = (f32[32,1664]{1,0:T(8,128)S(1)}, f32[32,1664]{1,0:T(8,128)S(1)}, u32[]{:S(2)}, u32[]{:S(2)}) collective-permute-start(f32[32,1664]{1,0:T(8,128)S(1)} %pad_maximum_fusion.1), channel_id=1, source_target_pairs={{0,2},{1,3},{2,0},{3,1},{4,6},{5,7},{6,4},{7,5},{8,10},{9,11},{10,... | collective-permute-start | bytes 638984 | tf_op jit(solution)/shard_map/ppermute | solution.py:649
  158.7 10.3 %collective-permute-start.12 = (f32[32,1664]{1,0:T(8,128)S(1)}, f32[32,1664]{1,0:T(8,128)S(1)}, u32[]{:S(2)}, u32[]{:S(2)}) collective-permute-start(f32[32,1664]{1,0:T(8,128)S(1)} %pad_maximum_fusion), channel_id=1, source_target_pairs={{0,6},{1,7},{2,4},{3,5},{4,2},{5,3},{6,0},{7,1},{8,14},{9,15},{10,... | collective-permute-start | bytes 638984 | tf_op jit(solution)/shard_map/ppermute | solution.py:649
  159.6 9.5 %collective-permute-start.11 = (f32[32,1664]{1,0:T(8,128)S(1)}, f32[32,1664]{1,0:T(8,128)S(1)}, u32[]{:S(2)}, u32[]{:S(2)}) collective-permute-start(f32[32,1664]{1,0:T(8,128)S(1)} %pad_maximum_fusion), channel_id=1, source_target_pairs={{0,4},{1,5},{2,6},{3,7},{4,0},{5,1},{6,2},{7,3},{8,12},{9,13},{10,... | collective-permute-start | bytes 638984 | tf_op jit(solution)/shard_map/ppermute | solution.py:649
  163.2 5.8 %collective-permute-start.10 = (f32[32,1664]{1,0:T(8,128)S(1)}, f32[32,1664]{1,0:T(8,128)S(1)}, u32[]{:S(2)}, u32[]{:S(2)}) collective-permute-start(f32[32,1664]{1,0:T(8,128)S(1)} %pad_maximum_fusion), channel_id=1, source_target_pairs={{0,2},{1,3},{2,0},{3,1},{4,6},{5,7},{6,4},{7,5},{8,10},{9,11},{10,... | collective-permute-start | bytes 638984 | tf_op jit(solution)/shard_map/ppermute | solution.py:649
  163.7 8.1 %collective-permute-start.27 = (f32[128,1664]{1,0:T(8,128)S(1)}, f32[128,1664]{1,0:T(8,128)S(1)}, u32[]{:S(2)}, u32[]{:S(2)}) collective-permute-start(f32[128,1664]{1,0:T(8,128)S(1)} %constant_dynamic-update-slice_fusion.7.a1_ref), channel_id=1, source_target_pairs={{0,1},{1,0},{2,3},{3,2},{4,5},{5,4},{6,7},{7,6},{8,9},{9,8},{10,11... | collective-permute-start | bytes 2555912 | tf_op jit(solution)/shard_map/ppermute | solution.py:649
  169.1 2.7 %collective-permute-start.13 = (f32[128,1664]{1,0:T(8,128)S(1)}, f32[128,1664]{1,0:T(8,128)S(1)}, u32[]{:S(2)}, u32[]{:S(2)}) collective-permute-start(f32[128,1664]{1,0:T(8,128)S(1)} %constant_dynamic-update-slice_fusion.a0_ref), channel_id=1, source_target_pairs={{0,1},{1,0},{2,3},{3,2},{4,5},{5,4},{6,7},{7,6},{8,9},{9,8},{10,11... | collective-permute-start | bytes 2555912 | tf_op jit(solution)/shard_map/ppermute | solution.py:649
  (12 other events, 59.7 us)

commit v3 on v2

v3 whole, which is shorter than its diff:
```python
import functools

import jax
import jax.numpy as jnp
from jax import lax
from jax.experimental import pallas as pl
from jax.experimental.pallas import tpu as pltpu
from jax.sharding import PartitionSpec as P

SUB_MAX = 160
DEGREE_CENTER = 2.0
SPREAD_OFFSET = 0.25
STABILITY_FLOOR = 1e-05

LEAF_SLOTS = 4
HUB_RANK = 16
LOG2E = 1.4426950408889634
LN2 = 0.6931471805599453
ROW_CHUNK = 64
F32 = jnp.float32
BF16 = jnp.bfloat16
NN = (((1,), (0,)), ((), ()))
NT = (((1,), (1,)), ((), ()))
TN = (((0,), (0,)), ((), ()))
TT = (((0,), (1,)), ((), ()))


def mm(a, b, dims=NN):
    return lax.dot_general(a, b, dims, preferred_element_type=F32)


def iota(shape, dim):
    return lax.broadcasted_iota(jnp.int32, shape, dim)


def to_cols(*rows):
    pad = [jnp.zeros((8 - len(rows), rows[0].shape[1]), F32)] if len(rows) < 8 else []
    turned = jnp.concatenate(list(rows) + pad, axis=0).T
    return [turned[:, i : i + 1] for i in range(len(rows))]


def to_rows(*cols):
    wide = jnp.concatenate([jnp.broadcast_to(c, (c.shape[0], 128 // len(cols))) for c in cols], axis=1).T
    step = 128 // len(cols)
    return [wide[i * step : i * step + 1] for i in range(len(cols))]


def fold(value, op):
    return op(value, pltpu.roll(value, 64, 1))


def split_two(value):
    high = value.astype(BF16)
    return high, (value - high.astype(F32)).astype(BF16)


def start_copies(pairs, sems):
    copies = [pltpu.make_async_copy(src, dst, sems.at[i]) for i, (src, dst) in enumerate(pairs)]
    for copy in copies:
        copy.start()
    return copies


def wait_all(copies):
    for copy in copies:
        copy.wait()


def build_tables(ef_ref, seg_ref, nbr_ref, mask_ref, deg_ref, b_ref, live_ref, rows_ref, g_ref, gt_ref):
    nodes = seg_ref.shape[0]
    seg = seg_ref[...].reshape(1, nodes)
    lane_h = iota((1, 128), 1)
    sub_h = iota((128, 1), 0)
    node_row = jnp.zeros((1, 128), jnp.int32)
    node_col = jnp.zeros((128, 1), jnp.int32)
    lane_r, sub_r = lane_h & 15, sub_h & 15
    lane_s, sub_s = (lane_h >> 4) & 3, (sub_h >> 4) & 3
    below = [jnp.sum((seg < s).astype(jnp.int32), axis=1, keepdims=True) for s in range(5)]
    for s in range(4):
        start, size = below[s], below[s + 1] - below[s]
        node_row = jnp.where(lane_s == s, jnp.where(lane_r < size, start + lane_r, -1), node_row)
        node_col = jnp.where(sub_s == s, jnp.where(sub_r < size, start + sub_r, -1), node_col)
    node_col = jnp.where(sub_h < 64, node_col, -1)
    g = (iota((nodes, 128), 0) == node_row).astype(F32).astype(BF16)
    gt = (iota((128, nodes), 1) == node_col).astype(F32).astype(BF16)
    g_ref[...] = g
    gt_ref[...] = gt
    is_hub = jnp.sum(gt.astype(F32), axis=0, keepdims=True)

    nbr = nbr_ref[...]
    mask = (mask_ref[...] > 0).astype(F32)
    nbr_h = (
        mm((nbr >> 3).astype(F32).astype(BF16), g) * 8.0 + mm((nbr & 7).astype(F32).astype(BF16), g)
    ).astype(jnp.int32)
    mask_h = mm(mask.astype(BF16), g)
    valid = (node_row >= 0).astype(F32)
    first = (lane_h < 64).astype(F32)

    def degree_rows(deg):
        log_degree = jnp.log(deg + 1.0)
        return log_degree / DEGREE_CENTER, DEGREE_CENTER / log_degree

    deg = deg_ref[...].reshape(1, nodes).astype(F32)
    deg_h = mm(jnp.broadcast_to(deg, (8, nodes)).astype(BF16), g)[0:1]
    deg_h = jnp.where(valid > 0, deg_h, 1.0)
    amp, att = degree_rows(deg)
    amp_h, att_h = degree_rows(deg_h)
    filled = jnp.sum(mask, axis=0, keepdims=True)
    filled_h = jnp.maximum(jnp.sum(mask_h, axis=0, keepdims=True), 1.0)
    rows_ref[...] = jnp.zeros_like(rows_ref)
    for i, (leaf, hub) in enumerate(
        (
            (amp, amp_h),
            (att, att_h),
            (1.0 / filled, 1.0 / filled_h),
            ((seg < 4).astype(F32), None),
            (1.0 - is_hub, valid * first),
            (is_hub, valid),
            (jnp.sum(mask[1:LEAF_SLOTS], axis=0, keepdims=True) - (LEAF_SLOTS - 2.0), filled_h - 16.0),
            (seg.astype(F32), None),
        )
    ):
        rows_ref[i : i + 1, 0:nodes] = leaf
        if hub is not None:
            rows_ref[i : i + 1, nodes : nodes + 128] = hub

    ef_t = ef_ref[...].T
    ef_h = mm(ef_t, g).astype(BF16)
    node_iota = iota((nodes, nodes), 0)
    hub_iota = iota((nodes, 128), 0)
    zero16 = jnp.zeros((16, nodes), BF16)
    for k in range(LEAF_SLOTS):
        lo = k * nodes
        b_ref[0:nodes, lo : lo + nodes] = (node_iota == nbr[k : k + 1]).astype(F32).astype(BF16)
        piece = ef_t[16 * k : 16 * k + 16]
        for r, part in enumerate((piece, zero16, piece, zero16)):
            b_ref[nodes + 16 * r : nodes + 16 * r + 16, lo : lo + nodes] = part
        live_ref[0:1, lo : lo + nodes] = mask[k : k + 1] * LOG2E
        live_ref[1:2, lo : lo + nodes] = mask[k : k + 1]
    own_half = (iota((32, 128), 0) < 16) == (iota((32, 128), 1) < 64)
    for j in range(8):
        lo = LEAF_SLOTS * nodes + 128 * j
        index = jnp.where(lane_h < 64, nbr_h[2 * j : 2 * j + 1], nbr_h[2 * j + 1 : 2 * j + 2])
        b_ref[0:nodes, lo : lo + 128] = (hub_iota == index).astype(F32).astype(BF16)
        piece = jnp.where(own_half, ef_h[32 * j : 32 * j + 32].astype(F32), 0.0).astype(BF16)
        b_ref[nodes : nodes + 32, lo : lo + 128] = piece
        b_ref[nodes + 32 : nodes + 64, lo : lo + 128] = piece
        live = jnp.where(lane_h < 64, mask_h[2 * j : 2 * j + 1], mask_h[2 * j + 1 : 2 * j + 2])
        live_ref[0:1, lo : lo + 128] = live * LOG2E
        live_ref[1:2, lo : lo + 128] = live


def tower_weights(wpost_ref, layer, t):
    w = wpost_ref[layer, t]
    inner = iota((64, 320), 1) >= 64
    zero = jnp.zeros((64, 320), BF16)
    return jnp.concatenate(
        [w[:, 0:320], jnp.where(inner, w[:, 256:576], zero), jnp.where(inner, w[:, 512:832], zero)], axis=0
    )


def forward_layer(
    layer, x_ref, wedge_ref, wpre_ref, bias, wpost_ref, wmix_ref, b_ref, live_ref, rows_ref, g_ref, gt_ref,
    m_ref, s_ref, z_ref, y_ref, u_ref, part_ref, a_ref, ya_ref, own_ref,
):
    width, nodes = x_ref.shape
    leaf_cols = LEAF_SLOTS * nodes
    x = x_ref[...]
    g = g_ref[...]
    own = mm(wpre_ref[layer, 0:width], x, TN) + bias
    own_ref[:, 0:nodes] = own
    a_ref[:, 0:nodes] = mm(wpre_ref[layer, width : 2 * width], x, TN).astype(BF16)
    wedge = wedge_ref[layer]
    both = mm(wpre_ref[layer, 2 * width :], jnp.concatenate([wedge] * 4, axis=0), TT)
    high, rest = split_two(both)
    a_ref[:, nodes : nodes + 64] = jnp.where(iota((width, 64), 1) < 32, high, rest)
    own_high, own_rest = split_two(own)
    own_ref[:, nodes:] = mm(own_high, g) + mm(own_rest, g)
    a = a_ref[...]

    def messages(lo, hi):
        m_ref[:, lo:hi] = mm(a, b_ref[:, lo:hi])

    x_h = mm(x, g).astype(BF16)
    for t in range(4):
        z_ref[320 * t : 320 * t + 64, 0:nodes] = x[64 * t : 64 * t + 64]
        z_ref[320 * t : 320 * t + 64, nodes:] = x_h[64 * t : 64 * t + 64]

    def summarize(i, tiles):
        per = 64 // ROW_CHUNK
        zr = (i // per) * 320 + 64 + (i % per) * ROW_CHUNK
        rows = pl.ds(i * ROW_CHUNK, ROW_CHUNK)
        for c in tiles:
            hub = c == nodes // 128
            lanes = slice(128 * c, 128 * c + 128)
            if hub:
                cols = [leaf_cols + 128 * j for j in range(8)]
                first = m_ref[rows, leaf_cols : leaf_cols + 128]
                first = jnp.where(iota((1, 128), 1) < 64, first, pltpu.roll(first, 64, 1))
            else:
                cols = [k * nodes + 128 * c for k in range(1, LEAF_SLOTS)]
                first = m_ref[rows, lanes]
            offs = []
            for lo in cols:
                d = (m_ref[rows, lo : lo + 128] - first) * live_ref[0:1, lo : lo + 128]
                m_ref[rows, lo : lo + 128] = d
                offs.append(d)

            def total(parts, op):
                while len(parts) > 1:
                    parts = [op(*parts[i : i + 2]) if i + 1 < len(parts) else parts[i] for i in range(0, len(parts), 2)]
                return fold(parts[0], op) if hub else parts[0]

            inv, missing = rows_ref[2:3, lanes], rows_ref[6:7, lanes]
            mean = total(offs, jnp.add) * inv
            var = total([d * d for d in offs], jnp.add) * inv - mean * mean
            spread = jnp.maximum(var * (LN2 * LN2), 0.0) + SPREAD_OFFSET
            rstd = lax.rsqrt(spread)
            top = jnp.maximum(total(offs, jnp.maximum), 0.0)
            low = jnp.minimum(total(offs, jnp.minimum), 0.0)
            ups = total([jnp.exp2(d - top) for d in offs], jnp.add) + missing * jnp.exp2(-top)
            downs = total([jnp.exp2(low - d) for d in offs], jnp.add) + missing * jnp.exp2(low)
            smax = top + jnp.log2(ups)
            smin = low - jnp.log2(downs)
            base = own_ref[rows, lanes] + first
            for n, stat in enumerate((mean, smax, smin, rstd)):
                s_ref[n, rows, lanes] = stat
                value = base + LN2 * stat if n < 3 else spread * rstd
                z_ref[pl.ds(zr + 64 * n, ROW_CHUNK), lanes] = value.astype(BF16)

    last = nodes // 128
    groups = [range(last, last + 1)] + [range(c, min(c + 2, last)) for c in range(0, last, 2)]
    waiting = None
    for tiles in groups + [None]:
        if tiles is not None:
            if tiles[0] == last:
                messages(leaf_cols, leaf_cols + 1024)
            else:
                for k in range(LEAF_SLOTS):
                    messages(k * nodes + 128 * tiles[0], k * nodes + 128 * (tiles[-1] + 1))
        if waiting is not None:
            for i in range(width // ROW_CHUNK):
                summarize(i, waiting)
        waiting = tiles

    amp, att = rows_ref[0:1], rows_ref[1:2]
    for t in range(4):
        r = mm(tower_weights(wpost_ref, layer, t), z_ref[320 * t : 320 * t + 320])
        ya_ref[64 * t : 64 * t + 64] = (r[0:64] + amp * r[64:128] + att * r[128:192]).astype(BF16)
    spread_out = mm(ya_ref[:, nodes:], gt_ref[...])
    y = jnp.where(rows_ref[5:6, 0:nodes] > 0, spread_out, ya_ref[:, 0:nodes].astype(F32)).astype(BF16)
    y_ref[...] = y
    u = mm(wmix_ref[layer], y, TN)
    u_ref[...] = u
    alive = rows_ref[3:4, 0:nodes]
    count = jnp.sum(alive, axis=1, keepdims=True)
    mean = jnp.sum(alive * u, axis=1, keepdims=True) / count
    off = u - mean
    square = jnp.sum(alive * off * off, axis=1, keepdims=True)
    row = jnp.concatenate(to_rows(mean, square) + [jnp.broadcast_to(count, (1, 128))], axis=1)
    part_ref[...] = jnp.broadcast_to(row[None], part_ref.shape)


def forward_first_kernel(
    layer, nf_hbm, ef_hbm, seg_hbm, nbr_hbm, mask_hbm, deg_hbm, wedge_hbm, wpre_hbm, bpre_hbm, wpost_hbm, wmix_hbm,
    x_ref, b_ref, live_ref, rows_ref, g_ref, gt_ref, m_ref, s_ref, z_ref, y_ref, u_ref, part_ref,
    a_ref, ya_ref, own_ref, nf_ref, ef_ref, seg_ref, nbr_ref, mask_ref, deg_ref, wedge_ref, wpre_ref, bpre_ref, wpost_ref, wmix_ref, in_sems,
):
    loads = start_copies(
        [
            (seg_hbm, seg_ref), (nbr_hbm, nbr_ref), (mask_hbm, mask_ref), (deg_hbm, deg_ref), (ef_hbm, ef_ref), (nf_hbm, nf_ref), (wpre_hbm, wpre_ref),
            (wedge_hbm, wedge_ref), (bpre_hbm, bpre_ref), (wpost_hbm, wpost_ref), (wmix_hbm, wmix_ref),
        ],
        in_sems,
    )
    wait_all(loads[0:5])
    build_tables(ef_ref, seg_ref, nbr_ref, mask_ref, deg_ref, b_ref, live_ref, rows_ref, g_ref, gt_ref)
    wait_all(loads[5:])
    x_ref[...] = nf_ref[...].T
    forward_layer(
        layer, x_ref, wedge_ref, wpre_ref, *to_cols(bpre_ref[layer : layer + 1]), wpost_ref, wmix_ref, b_ref,
        live_ref, rows_ref, g_ref, gt_ref, m_ref, s_ref, z_ref, y_ref, u_ref, part_ref, a_ref, ya_ref, own_ref,
    )


def norm_rows(recv_ref):
    w = (recv_ref.shape[2] - 128) // 2
    recv = recv_ref[...]
    means, squares = recv[:, :, 0:w], recv[:, :, w : 2 * w]
    counts = jnp.concatenate([recv[:, :, 2 * w :]] * (w // 128), axis=2)
    total = jnp.sum(counts, axis=0)
    mean = jnp.sum(counts * means, axis=0) / total
    off = means - mean[None]
    var = jnp.sum(squares + counts * off * off, axis=0) / total
    return mean, lax.rsqrt(var + STABILITY_FLOOR), total


def normed(u, norm_ref, gain_ref, bias_ref, layer):
    mean, scale, gain, bias = to_cols(
        norm_ref[0:1], norm_ref[1:2], gain_ref[layer : layer + 1], bias_ref[layer : layer + 1]
    )
    xh = (u - mean) * scale
    return xh, xh * gain + bias


def store_norm(norm_ref, recv_ref):
    mean, scale, total = norm_rows(recv_ref)
    norm_ref[...] = jnp.zeros_like(norm_ref)
    norm_ref[0:1] = mean
    norm_ref[1:2] = scale
    norm_ref[2:3] = total


def forward_next_kernel(
    layer, recv_ref, u0_ref, x0_ref, gain_ref, bias_ref, wedge_ref, wpre_ref, bpre_ref, wpost_ref, wmix_ref,
    b_ref, live_ref, rows_ref, g_ref, gt_ref,
    norm_ref, h_ref, x_ref, m_ref, s_ref, z_ref, y_ref, u_ref, part_ref, a_ref, ya_ref, own_ref,
):
    store_norm(norm_ref, recv_ref)
    _, v = normed(u0_ref[...], norm_ref, gain_ref, bias_ref, layer - 1)
    h = x0_ref[...].astype(F32) + v / (1.0 + jnp.exp(-v))
    h_ref[...] = h
    x_ref[...] = h.astype(BF16)
    forward_layer(
        layer, x_ref, wedge_ref, wpre_ref, *to_cols(bpre_ref[layer : layer + 1]), wpost_ref, wmix_ref, b_ref,
        live_ref, rows_ref, g_ref, gt_ref, m_ref, s_ref, z_ref, y_ref, u_ref, part_ref, a_ref, ya_ref, own_ref,
    )


def gate_grad(dh, xh, v, dv_ref, part_ref):
    sig = 1.0 / (1.0 + jnp.exp(-v))
    dv = dh * sig * (1.0 + v * (1.0 - sig))
    dv_ref[...] = dv
    sums = [jnp.sum(p, axis=1, keepdims=True) for p in (dv, dv * xh)]
    row = jnp.concatenate(to_rows(*sums), axis=1)
    part_ref[...] = jnp.broadcast_to(row[None], part_ref.shape)


def last_gate_kernel(
    layer, recv_ref, u_ref, h_ref, gain_ref, bias_ref, rows_ref, rg_ref, norm_ref, h_out_ref, dh_ref, dv_ref, part_ref
):
    store_norm(norm_ref, recv_ref)
    xh, v = normed(u_ref[...], norm_ref, gain_ref, bias_ref, layer)
    nodes = v.shape[1]
    seeds = rg_ref.shape[0]
    sig = 1.0 / (1.0 + jnp.exp(-v))
    h_out_ref[...] = h_ref[...] + v * sig
    dh = jnp.zeros(v.shape, F32)
    cols = to_cols(*[rg_ref[s : s + 1] / SUB_MAX for s in range(seeds)])
    for s, col in enumerate(cols):
        dh = jnp.where(rows_ref[7:8, 0:nodes] == s, col, dh)
    dh_ref[...] = dh
    gate_grad(dh, xh, v, dv_ref, part_ref)


def backward_layer(
    layer, recv_ref, dv_ref, dh_ref, u_ref, norm_ref, gain_ref, bias_ref, wmix_ref, wpost_ref, wpre_ref,
    b_ref, live_ref, rows_ref, g_ref, gt_ref, m_ref, s_ref,
    gb_ref, du_ref, d_ref, dm_ref, dcat_ref, et_ref, ds_ref, acc_ref, bd_ref, beside=(),
):
    width, nodes = dv_ref.shape
    leaf_cols = LEAF_SLOTS * nodes
    sums = jnp.sum(recv_ref[...], axis=0)
    g_bias, g_gain = sums[:, 0:width], sums[:, width:]
    gb_ref[...] = sums
    xh, _ = normed(u_ref[...], norm_ref, gain_ref, bias_ref, layer)
    alive = rows_ref[3:4, 0:nodes]
    scale, part_bias, part_gain = to_cols(
        norm_ref[1:2] * gain_ref[layer : layer + 1], g_bias / norm_ref[2:3], g_gain / norm_ref[2:3]
    )
    du = scale * (dv_ref[...] - alive * (part_bias + xh * part_gain))
    du = du.astype(BF16)
    du_ref[...] = du
    dy = mm(wmix_ref[layer], du)
    dy_low = dy.astype(BF16)
    dcat_ref[2 * width :] = dy_low
    dy_h = mm(dy_low, g_ref[...])
    keep = rows_ref[4:5]
    amp, att = rows_ref[0:1], rows_ref[1:2]
    dy_all = jnp.concatenate([dy_low.astype(F32), dy_h], axis=1) * keep
    bd_ref[...] = jnp.zeros_like(bd_ref)
    for t in range(4):
        part = dy_all[64 * t : 64 * t + 64]
        d_ref[192 * t : 192 * t + 64] = part.astype(BF16)
        d_ref[192 * t + 64 : 192 * t + 128] = (part * amp).astype(BF16)
        d_ref[192 * t + 128 : 192 * t + 192] = (part * att).astype(BF16)
        w = tower_weights(wpost_ref, layer, t)
        dz = mm(w, d_ref[192 * t : 192 * t + 192], TN)
        for n in range(4):
            rows = slice(64 * t, 64 * t + 64)
            block = dz[64 * (n + 1) : 64 * (n + 2)]
            ds_ref[n, rows, 0:nodes] = block[:, 0:nodes]
            ds_ref[n, rows, nodes:] = fold(block[:, nodes:], jnp.add)
        bd_ref[64 * t : 64 * t + 64, 64 * t : 64 * t + 64] = wpost_ref[layer, t][:, 0:64]

    def spread_back(i, tiles):
        rows = pl.ds(i * ROW_CHUNK, ROW_CHUNK)
        for c in tiles:
            hub = c == nodes // 128
            lanes = slice(128 * c, 128 * c + 128)
            mean, smax, smin, rstd = (s_ref[n, rows, lanes] for n in range(4))
            dmean, dsmax, dsmin, dstd = (ds_ref[n, rows, lanes] for n in range(4))
            inv = rows_ref[2:3, lanes]
            c1 = dstd * inv * rstd * LN2
            c0 = dmean * inv - mean * c1
            if hub:
                cols = [leaf_cols + 128 * j for j in range(8)]
                acc = None
            else:
                cols = [k * nodes + 128 * c for k in range(1, LEAF_SLOTS)]
                acc = c0 + dsmax * jnp.exp2(-smax) + dsmin * jnp.exp2(smin)
                dm_ref[rows, lanes] = acc.astype(BF16)
            for lo in cols:
                m = m_ref[rows, lo : lo + 128]
                d = c0 + m * c1 + dsmax * jnp.exp2(m - smax) + dsmin * jnp.exp2(smin - m)
                d = d * live_ref[1:2, lo : lo + 128]
                acc = d if acc is None else acc + d
                dm_ref[rows, lo : lo + 128] = d.astype(BF16)
            acc_ref[rows, lanes] = fold(acc, jnp.add) if hub else acc

    def land(lo, hi):
        return mm(dm_ref[:, lo:hi], b_ref[0 : nodes + 32, lo:hi], NT)

    last = nodes // 128
    groups = [range(last, last + 1)] + [range(c, min(c + 2, last)) for c in range(0, last, 2)]
    waiting, landed = None, None
    for step, tiles in enumerate(groups + [None]):
        if tiles is not None:
            for i in range(width // ROW_CHUNK):
                spread_back(i, tiles)
        if step < len(beside):
            beside[step]()
        if waiting is not None:
            if waiting[0] == last:
                landed = land(leaf_cols, leaf_cols + 1024)
            else:
                for k in range(LEAF_SLOTS):
                    landed = landed + land(k * nodes + 128 * waiting[0], k * nodes + 128 * (waiting[-1] + 1))
        waiting = tiles

    down = acc_ref[:, 0:nodes] + mm(acc_ref[:, nodes:].astype(BF16), gt_ref[...])
    dcat_ref[0:width] = down.astype(BF16)
    dcat_ref[width : 2 * width] = landed[:, 0:nodes].astype(BF16)
    once = jnp.where(iota((1, nodes + 128), 1) < nodes + 64, acc_ref[...], 0.0)
    bias = jnp.sum(once, axis=1, keepdims=True)
    factor = landed[:, nodes : nodes + 16] + landed[:, nodes + 16 : nodes + 32]
    et_ref[...] = jnp.concatenate([factor, jnp.broadcast_to(bias, (width, 48))], axis=1)
    weights = jnp.concatenate([wpre_ref[layer, 0:width], wpre_ref[layer, width : 2 * width]], axis=1)
    dh = mm(weights, dcat_ref[0 : 2 * width])
    dh = dh + mm(bd_ref[...], dcat_ref[2 * width :], TN)
    return dh_ref[...] + dh


def backward_first_kernel(
    layer, recv_ref, dv_ref, dh_ref, u_ref, norm_ref, gain_ref, bias_ref, wmix_ref, wpost_ref, wpre_ref,
    b_ref, live_ref, rows_ref, g_ref, gt_ref, m_ref, s_ref, u_low_ref, norm_low_ref,
    gb_ref, du_ref, d_ref, dm_ref, dcat_ref, et_ref, dh_out_ref, dv_out_ref, part_ref,
    ds_ref, acc_ref, bd_ref,
):
    dh = backward_layer(
        layer, recv_ref, dv_ref, dh_ref, u_ref, norm_ref, gain_ref, bias_ref, wmix_ref, wpost_ref, wpre_ref,
        b_ref, live_ref, rows_ref, g_ref, gt_ref, m_ref, s_ref,
        gb_ref, du_ref, d_ref, dm_ref, dcat_ref, et_ref, ds_ref, acc_ref, bd_ref,
    )
    dh_out_ref[...] = dh
    xh, v = normed(u_low_ref[...], norm_low_ref, gain_ref, bias_ref, layer - 1)
    gate_grad(dh, xh, v, dv_out_ref, part_ref)


def piece_owner(core, half, place):
    plane_first = ((place >> 2) << 1) | ((place & 3) << 3)
    line_first = ((place >> 2) << 3) | ((place & 3) << 1)
    return half + jnp.where(core == half, plane_first, line_first)


def put_tower_grad(t, d_ref, z_ref, grads_ref):
    r = mm(d_ref[192 * t : 192 * t + 192], z_ref[320 * t : 320 * t + 320], NT)
    rows = slice(64 * t, 64 * t + 64)
    first = iota((64, 256), 1) < 64
    grads_ref[rows, 0:256] = r[0:64, 0:256]
    grads_ref[rows, 256:512] = jnp.where(first, jnp.concatenate([r[0:64, 256:320]] * 4, axis=1), r[64:128, 0:256])
    grads_ref[rows, 512:768] = jnp.where(first, jnp.concatenate([r[64:128, 256:320]] * 4, axis=1), r[128:192, 0:256])
    grads_ref[rows, 768:832] = r[128:192, 256:320]


def put_mix_grad(y_ref, du_ref, grads_ref):
    grads_ref[:, 896:1152] = mm(y_ref[...], du_ref[...], NT)


def put_message_grads(x_ref, dcat_ref, et_ref, grads_ref, keep_ref, send_ref):
    width = x_ref.shape[0]
    grads_ref[:, 832:896] = et_ref[...]
    grads_ref[:, 1152:1664] = mm(x_ref[...], dcat_ref[0 : 2 * width], NT)
    me = lax.axis_index("dp") & 31
    for place in range(16):
        for half, ref in ((0, keep_ref), (1, send_ref)):
            row = pl.multiple_of((me ^ piece_owner(me & 1, half, place)) * 8, 8)
            ref[8 * place : 8 * place + 8] = grads_ref[pl.ds(row, 8)]


def weight_kernel(
    y_ref, du_ref, d_ref, z_ref, x_ref, dcat_ref, et_ref, keep_ref, send_ref, grads_ref
):
    for t in range(4):
        put_tower_grad(t, d_ref, z_ref, grads_ref)
    put_mix_grad(y_ref, du_ref, grads_ref)
    put_message_grads(x_ref, dcat_ref, et_ref, grads_ref, keep_ref, send_ref)


def backward_last_kernel(
    layer, recv_ref, dv_ref, dh_ref, u_ref, norm_ref, gain_ref, bias_ref, wmix_ref, wpost_ref, wpre_ref,
    b_ref, live_ref, rows_ref, g_ref, gt_ref, m_ref, s_ref, z_ref, y_ref, x_ref,
    gb_ref, dm_ref, node_ref, keep_ref, send_ref,
    du_ref, d_ref, dcat_ref, et_ref, ds_ref, acc_ref, bd_ref, grads_ref,
):
    beside = [functools.partial(put_tower_grad, t, d_ref, z_ref, grads_ref) for t in range(4)]
    beside[3:] = [lambda: put_tower_grad(3, d_ref, z_ref, grads_ref) or put_mix_grad(y_ref, du_ref, grads_ref)]
    dh = backward_layer(
        layer, recv_ref, dv_ref, dh_ref, u_ref, norm_ref, gain_ref, bias_ref, wmix_ref, wpost_ref, wpre_ref,
        b_ref, live_ref, rows_ref, g_ref, gt_ref, m_ref, s_ref,
        gb_ref, du_ref, d_ref, dm_ref, dcat_ref, et_ref, ds_ref, acc_ref, bd_ref, beside,
    )
    put_message_grads(x_ref, dcat_ref, et_ref, grads_ref, keep_ref, send_ref)
    node_ref[...] = dh.T


def edge_kernel(dm0_ref, dm1_ref, wpre_ref, wedge_ref, gt_ref, h_ref, rows_ref, out_ref, readout_ref, acc_ref):
    width = dm0_ref.shape[0]
    nodes = gt_ref.shape[1]
    leaf_cols = LEAF_SLOTS * nodes
    total = None
    for layer, dm_ref in ((0, dm0_ref), (1, dm1_ref)):
        w = mm(wedge_ref[layer], wpre_ref[layer, 2 * width :]).astype(BF16)
        part = mm(w, dm_ref[...])
        total = part if total is None else total + part
    hub = total[:, leaf_cols:]
    for j in range(8):
        acc_ref[32 * j : 32 * j + 16] = hub[:, 128 * j : 128 * j + 128]
        acc_ref[32 * j + 16 : 32 * j + 32] = pltpu.roll(hub[:, 128 * j : 128 * j + 128], 64, 1)
    high, rest = split_two(acc_ref[...])
    gt = gt_ref[...]
    spread_out = mm(high, gt) + mm(rest, gt)
    leaf = jnp.concatenate([total[:, k * nodes : (k + 1) * nodes] for k in range(LEAF_SLOTS)], axis=0)
    out = jnp.concatenate([spread_out[0:64] + leaf, spread_out[64:]], axis=0)
    out_ref[...] = out.T
    belong = (iota((8, nodes), 0).astype(F32) == rows_ref[7:8, 0:nodes]).astype(F32)
    total = lax.dot_general(belong, h_ref[...], NT, precision=lax.Precision.HIGHEST, preferred_element_type=F32)
    readout_ref[...] = total[0 : readout_ref.shape[0]] / SUB_MAX


def finish_half(half, half_ref, outs, bufs, sems):
    me = lax.axis_index("dp") & 31
    core = me & 1
    post, mix, pre, et = bufs
    for layer in range(post.shape[0]):
        cols = 1664 * layer
        for place in range(16):
            block = (me ^ piece_owner(core, half, place)) >> 1
            piece = half_ref[8 * place : 8 * place + 8, cols : cols + 1664]
            post[layer, block] = piece[:, 0:832]
            et[layer, block] = piece[:, 832:896]
            mix[layer, block] = piece[:, 896:1152]
            pre[layer, 0, block] = piece[:, 1152:1408]
            pre[layer, 1, block] = piece[:, 1408:1664]
    side = core ^ half
    post_out, mix_out, pre_out = outs
    pairs = [(post, post_out.at[:, :, side]), (mix, mix_out.at[:, :, side]), (pre, pre_out.at[:, 0:2, :, side])]
    return start_copies(pairs, sems)


def finish_first_kernel(half_ref, post_out, mix_out, pre_out, et, post, mix, pre, sems):
    wait_all(finish_half(0, half_ref, (post_out, mix_out, pre_out), (post, mix, pre, et), sems))


def finish_last_kernel(
    post_in, mix_in, pre_in, other_et, half_ref, wedge_ref, wpre_ref, post_out, mix_out, pre_out, gb_ref, gedge_ref,
    post, mix, pre, et, term, sems,
):
    del post_in, mix_in, pre_in
    copies = finish_half(1, half_ref, (post_out, mix_out, pre_out), (post, mix, pre, et), sems)
    width = wpre_ref.shape[2]
    core = lax.axis_index("dp") & 1
    for layer in range(2):
        mine, other = et[layer], other_et[layer]
        first, second = jnp.where(core == 0, other, mine), jnp.where(core == 0, mine, other)
        both = jnp.concatenate([first[:, None], second[:, None]], axis=1).reshape(width, 64)
        gb_ref[layer : layer + 1] = to_rows(both[:, 16:17])[0]
        factor = both[:, 0:16]
        high, rest = split_two(factor)
        last = (factor - high.astype(F32) - rest.astype(F32)).astype(BF16)
        three = jnp.concatenate([high, rest, last], axis=1)
        grad = mm(jnp.concatenate([wedge_ref[layer]] * 3, axis=0), three, TT)
        term[layer] = grad.reshape(term.shape[1:])
        parts = mm(three, wpre_ref[layer, 2 * width :], TT)
        gedge_ref[layer] = parts[0:16] + parts[16:32] + parts[32:48]
    copies += start_copies([(term, pre_out.at[:, 2])], sems.at[3:4])
    wait_all(copies)


def on_device(
    devices, node_feats, edge_feats, segment_ids, neighbours, nbr_mask, degrees, w_edge, w_pre, b_pre, w_post,
    w_mix, bn_gain, bn_bias, readout_grad,
):
    nodes, width = node_feats.shape
    lanes = nodes + 128
    cols = LEAF_SLOTS * nodes + 1024
    inner = nodes + 64
    nbr_t = neighbours.T
    mask_t = nbr_mask.T
    wpost_t = jnp.swapaxes(w_post, 2, 3)

    def s(shape, dtype=F32):
        return jax.ShapeDtypeStruct(shape, dtype)

    vmem = pl.BlockSpec(memory_space=pltpu.VMEM)
    hbm = pl.BlockSpec(memory_space=pltpu.HBM)

    def call(kernel, args, outs, scratch=(), far=(), free=(), far_out=(), alias={}, cost=0, limit=20):
        args = [pltpu.with_memory_space_constraint(a, pltpu.HBM) if i in far else a for i, a in enumerate(args)]
        return pl.pallas_call(
            kernel,
            in_specs=[hbm if i in far else vmem for i in range(len(args))],
            out_specs=[hbm if i in far_out else vmem for i in range(len(outs))],
            out_shape=[
                o if i in free else (pltpu.HBM if i in far_out else pltpu.VMEM)(o.shape, o.dtype)
                for i, o in enumerate(outs)
            ],
            scratch_shapes=list(scratch),
            input_output_aliases=alias,
            cost_estimate=pl.CostEstimate(flops=int(cost * 1e9), bytes_accessed=0, transcendentals=0) if cost else None,
            compiler_params=pltpu.CompilerParams(vmem_limit_bytes=limit * 1024 * 1024),
        )(*args)

    def like(shapes):
        return [pltpu.VMEM(x.shape, x.dtype) for x in shapes]

    def dma(n):
        return pltpu.SemaphoreType.DMA((n,))

    def exchange(part):
        return lax.all_to_all(part, "dp", 0, 0, tiled=True)

    m_s, s_s, z_s = s((width, cols)), s((4, width, lanes)), s((4 * 320, lanes), BF16)
    b_s = s((inner, cols), BF16)
    row_s, low_s = s((width, nodes)), s((width, nodes), BF16)
    layer_outs = [m_s, s_s, z_s, low_s, row_s, s((devices, 1, 2 * width + 128))]
    fwd_scratch = like([s((width, inner), BF16), s((width, lanes), BF16), s((width, lanes))])
    table_outs = [b_s, s((2, cols)), s((8, lanes)), s((nodes, 128), BF16), s((128, nodes), BF16)]
    first_args = [node_feats, edge_feats, segment_ids, nbr_t, mask_t, degrees, w_edge, w_pre, b_pre, wpost_t, w_mix]
    x0, b, live, rows, g, gt, m0, s0, z0, y0, u0, part = call(
        functools.partial(forward_first_kernel, 0),
        first_args, [low_s] + table_outs + layer_outs,
        fwd_scratch + like(first_args) + [dma(11)], range(11),
    )
    tables = [b, live, rows, g, gt]
    recv = exchange(part)
    norm0, h1, x1, m1, s1, z1, y1, u1, part = call(
        functools.partial(forward_next_kernel, 1),
        [recv, u0, x0, bn_gain, bn_bias, w_edge, w_pre, b_pre, wpost_t, w_mix] + tables,
        [s((8, width)), row_s, low_s] + layer_outs,
        fwd_scratch,
    )
    recv = exchange(part)
    sums_out = s((devices, 1, 2 * width))
    norm1, h2, dh2, dv1, part = call(
        functools.partial(last_gate_kernel, 1),
        [recv, u1, h1, bn_gain, bn_bias, rows, readout_grad],
        [s((8, width)), row_s, row_s, row_s, sums_out],
    )
    sum_s = s((1, 2 * width))
    du_s, d_s, dm_s = low_s, s((4 * 192, lanes), BF16), s((width, cols), BF16)
    dcat_s, et_s, acc_s = s((3 * width, nodes), BF16), s((width, 64)), s((width, lanes))
    back_scratch = like([s_s, acc_s, s((width, width), BF16)])
    recv = exchange(part)
    sums1, du1, d1, dm1, dcat1, et1, dh1, dv0, part = call(
        functools.partial(backward_first_kernel, 1),
        [recv, dv1, dh2, u1, norm1, bn_gain, bn_bias, w_mix, wpost_t, w_pre] + tables + [m1, s1, u0, norm0],
        [sum_s, du_s, d_s, dm_s, dcat_s, et_s, row_s, row_s, sums_out],
        back_scratch,
    )
    recv = exchange(part)
    grad_cols = 1664
    grad_s, half_s = s((width, grad_cols)), s((width // 2, grad_cols))
    sums0, dm0, node_grad, keep0, send0 = call(
        functools.partial(backward_last_kernel, 0),
        [recv, dv0, dh1, u0, norm0, bn_gain, bn_bias, w_mix, wpost_t, w_pre] + tables + [m0, s0, z0, y0, x0],
        [sum_s, dm_s, s((nodes, width)), half_s, half_s],
        like([du_s, d_s, dcat_s, et_s]) + back_scratch + like([grad_s]), free=(2,),
    )

    def swap(value, masks):
        return lax.ppermute(value, "dp", [(i, i ^ masks[i & 1]) for i in range(devices)])

    def after(value, *others):
        return lax.optimization_barrier((value, *others))[0]

    got0 = swap(send0, (1, 1))
    keep1, send1 = call(
        weight_kernel, [y1, after(du1, send0), d1, z1, x1, dcat1, et1], [half_s, half_s], like([grad_s]), cost=1.4
    )
    got1 = swap(send1, (1, 1))
    part = jnp.concatenate([keep0 + got0, keep1 + got1], axis=1)
    plane, line = (2, 4, 6), (8, 16, 24)
    stages = ((list(zip(plane, line)), 32), (list(zip(line, plane)), 8))
    edge_grad, readout = call(
        edge_kernel, [dm0, dm1, w_pre, w_edge, after(gt, part), h2, rows], [s((nodes, width)), s(readout_grad.shape)],
        [pltpu.VMEM((width, 128), F32)], free=(0, 1), cost=2,
    )
    for masks, size in stages:
        got = [swap(part[size * (i + 1) : size * (i + 2)], m) for i, m in enumerate(masks)]
        part = part[0:size] + got[0] + got[1] + got[2]
    mask = 32
    while mask < devices:
        part = part + swap(part, (mask, mask))
        mask *= 2
    for masks, _ in stages[::-1]:
        part = jnp.concatenate([part] + [swap(part, m) for m in masks], axis=0)
    other = swap(part, (1, 1))
    layers, blocks = w_pre.shape[0], width // 16
    finals = [
        s((layers, blocks, 2, 8, 832)), s((layers, blocks, 2, 8, width)), s((layers, 3, blocks, 2, 8, width)),
    ]
    bufs = [s((layers, blocks, 8, 832)), s((layers, blocks, 8, width)), s((layers, 2, blocks, 8, width))]
    ets = s((layers, blocks, 8, 64))
    *finals_in, ets_first = call(
        finish_first_kernel, [part], finals + [ets], like(bufs) + [dma(3)], far_out=(0, 1, 2), cost=2
    )
    g_post_t, g_mix, g_pre, g_b, g_edge = call(
        finish_last_kernel, [*finals_in, ets_first, other, w_edge, w_pre], finals + [s(b_pre.shape), s(w_edge.shape)],
        like(bufs + [ets, s((layers, blocks, 2, 8, width))]) + [dma(4)],
        far=(0, 1, 2), far_out=(0, 1, 2), free=(3, 4), alias={0: 0, 1: 1, 2: 2},
    )
    g_post = jnp.swapaxes(g_post_t.reshape(wpost_t.shape), 2, 3)
    g_mix, g_pre = g_mix.reshape(w_mix.shape), g_pre.reshape(w_pre.shape)
    sums = jnp.concatenate([sums0, sums1], axis=0)
    return (
        readout, node_grad, edge_grad, g_edge, g_pre, g_b, g_post, g_mix, sums[:, width:], sums[:, :width],
    )


def solution(mesh):
    split, split2, full = P("dp"), P("dp", None), P()
    in_specs = (split2, split2, split, split2, split2, split) + (full,) * 7 + (split2,)
    out_specs = (split2, split2, split2) + (full,) * 7
    return jax.shard_map(
        functools.partial(on_device, mesh.shape["dp"]),
        mesh=mesh, in_specs=in_specs, out_specs=out_specs, check_vma=False,
    )
```

time: 176 us -> 139 us (0.79)
  Pallas kernels: 53.6 us -> 34.9 us
  local copies, waits for them, and re-layouts: 11.7 us -> 0.18 us
  starting transfers between devices: 28.9 us -> 24.4 us
    pallas_call x8 -> x9, Pallas kernels: 53.6 us -> 34.9 us  [call(): pl.pallas_call(kernel, in_specs=[hbm if i in far else vmem for i in range...]
    unnamed x42 -> x21, local copies, waits for them, and re-layouts: 10.1 us -> 0.12 us
    ppermute x28 -> x15, starting transfers between devices: 28.9 us -> 24.4 us  [swap(): lax.ppermute(value, 'dp', [(i, i ^ masks[i & 1]) for i in range(devices)])]
    ppermute x28 -> x15, waiting for transfers between devices: 35.3 us -> 35.4 us  [swap(): lax.ppermute(value, 'dp', [(i, i ^ masks[i & 1]) for i in range(devices)])]
  transfers between devices with their start and end apart: 28 -> 15, of which waited for: 14 -> 11; matrix products, arithmetic and copies ran while one was open for 1% -> 1% of each run, Pallas kernels for 8% -> 3%
where the time goes in v3:
time: 139 us
  blocking collectives  42.2 us (30%)
  waiting for transfers between devices  35.4 us (25%)
  Pallas kernels  34.9 us (25%)
  starting transfers between devices  24.4 us (18%)
    all_to_all x4, blocking collectives, exchange(): return lax.all_to_all(part, 'dp', 0, 0, tiled=True)  42.2 us
    ppermute x15, waiting for transfers between devices, swap(): lax.ppermute(value, 'dp', [(i, i ^ masks[i & 1]) for i in range(devices)])  35.4 us
    pallas_call x9, Pallas kernels, call(): pl.pallas_call(kernel, in_specs=[hbm if i in far else vmem for i in range...  34.9 us
    ppermute x15, starting transfers between devices, swap(): lax.ppermute(value, 'dp', [(i, i ^ masks[i & 1]) for i in range(devices)])  24.4 us
  transfers between devices with their start and end apart: 15, of which 11 were waited for; matrix products, arithmetic and copies ran while one was open for 1% of the time, Pallas kernels for 3%

profile of v3, /device:TPU:0, one launch (start us, length us, event | category | flops | bytes accessed | tf_op | source)
XLA Modules:
  0.0 139.1 jit_solution(7445536799071989315)
XLA Ops:
  0.7 8.3 %shard_map.213 = (bf16[256,640]{1,0:T(8,128)(2,1)S(1)}, bf16[704,3584]{1,0:T(8,128)(2,1)S(1)}, f32[2,3584]{1,0:T(2,128)S(1)}, f32[8,768]{1,0:T(8,128)S(1)}, bf16...) custom-call(bf16[640,256]{1,0:T(8,128)(2,1)} %nf_hbm.1, ...), custom_call_target="tpu_custom_call" | custom-call | tf_op jit(solution)/shard_map/pallas_call | solution.py:620
  9.0 14.7 %all_to_all.20.recv_ref = f32[32,1,640]{2,1,0:T(1,128)S(1)} all-to-all(f32[32,1,640]{2,1,0:T(1,128)S(1)} %get-tuple-element.65), channel_id=1, replica_groups=mesh['dp'=32] {'dp'}, dimensions={0} | all-to-all | bytes 163840 | tf_op jit(solution)/shard_map/all_to_all | solution.py:641
  23.7 5.5 %shard_map.214 = (f32[8,256]{1,0:T(8,128)S(1)}, f32[256,640]{1,0:T(8,128)S(1)}, bf16[256,640]{1,0:T(8,128)(2,1)S(1)}, f32[256,3584]{1,0:T(8,128)S(1)}, f32[4,256...) custom-call(f32[32,1,640]{2,1,0:T(1,128)S(1)} %all_to_all.20.recv_re, ...), custom_call_target="tpu_custom_call" | custom-call | tf_op jit(solution)/shard_map/pallas_call | solution.py:620
  29.3 9.3 %all_to_all.21.recv_ref = f32[32,1,640]{2,1,0:T(1,128)S(1)} all-to-all(f32[32,1,640]{2,1,0:T(1,128)S(1)} %get-tuple-element.73), channel_id=1, replica_groups=mesh['dp'=32] {'dp'}, dimensions={0} | all-to-all | bytes 163840 | tf_op jit(solution)/shard_map/all_to_all | solution.py:641
  38.6 1.2 shard_map.215
  39.8 9.1 %all_to_all.22.recv_ref = f32[32,1,512]{2,1,0:T(1,128)S(1)} all-to-all(f32[32,1,512]{2,1,0:T(1,128)S(1)} %get-tuple-element.76), channel_id=1, replica_groups=mesh['dp'=32] {'dp'}, dimensions={0} | all-to-all | bytes 131072 | tf_op jit(solution)/shard_map/all_to_all | solution.py:641
  48.9 5.8 %shard_map.216 = (f32[1,512]{1,0:T(1,128)S(1)}, bf16[256,640]{1,0:T(8,128)(2,1)S(1)}, bf16[768,768]{1,0:T(8,128)(2,1)S(1)}, bf16[256,3584]{1,0:T(8,128)(2,1)S(1)...) custom-call(f32[32,1,512]{2,1,0:T(1,128)S(1)} %all_to_all.22.recv_re, ...), custom_call_target="tpu_custom_call" | custom-call | tf_op jit(solution)/shard_map/pallas_call | solution.py:620
  54.7 9.1 %all_to_all.23.recv_ref = f32[32,1,512]{2,1,0:T(1,128)S(1)} all-to-all(f32[32,1,512]{2,1,0:T(1,128)S(1)} %get-tuple-element.83), channel_id=1, replica_groups=mesh['dp'=32] {'dp'}, dimensions={0} | all-to-all | bytes 131072 | tf_op jit(solution)/shard_map/all_to_all | solution.py:641
  63.8 6.9 %shard_map.217 = (f32[1,512]{1,0:T(1,128)S(1)}, bf16[256,3584]{1,0:T(8,128)(2,1)S(1)}, f32[640,256]{1,0:T(8,128)}, f32[128,1664]{1,0:T(8,128)S(1)}, f32[128,1664]{1,0:T(8,128)S(1)}) custom-call(f32[32,1,512]{2,1,0:T(1,128)S(1)} %all_to_all.23.recv_ref, f32[256,640]{1,0:T(8,128)S(1)} %get-tuple-element.84.dv_ref, f32[256,640]{1,0:T(8,128)S(1)} %get-tuple-element.85.dh_ref, ...), custom_call_target="tpu_custom_call" | custom-call | tf_op jit(solution)/shard_map/pallas_call | solution.py:620
  70.8 1.4 shard_map.218
  72.7 1.9 %collective-permute-done.1 = f32[128,1664]{1,0:T(8,128)S(1)} collective-permute-done((f32[128,1664]{1,0:T(8,128)S(1)}, f32[128,1664]{1,0:T(8,128)S(1)}, u32[]{:S(2)}, u32[]{:S(2)}) %collective-permute-start.1) | collective-permute-done | bytes 852000 | tf_op jit(solution)/shard_map/ppermute | solution.py:692
  74.7 1.1 collective-permute-done
  76.5 0.8 collective-permute-start.3
  77.3 2.2 %collective-permute-start.4 = (f32[32,3328]{1,0:T(8,128)S(1)}, f32[32,3328]{1,0:T(8,128)S(1)}, u32[]{:S(2)}, u32[]{:S(2)}) collective-permute-start(f32[32,3328]{1,0:T(8,128)S(1)} %get-tuple-element.124), channel_id=1, source_target_pairs={{0,6},{1,25},{2,4},{3,27},{4,2},{5,29},{6,0},{7,31},{8,14},{9,17},... | collective-permute-start | bytes 1277960 | tf_op jit(solution)/shard_map/ppermute | solution.py:692
  79.5 4.6 %collective-permute-done.2 = f32[32,3328]{1,0:T(8,128)S(1)} collective-permute-done((f32[32,3328]{1,0:T(8,128)S(1)}, f32[32,3328]{1,0:T(8,128)S(1)}, u32[]{:S(2)}, u32[]{:S(2)}) %collective-permute-start.2) | collective-permute-done | bytes 426016 | tf_op jit(solution)/shard_map/ppermute | solution.py:692
  84.2 5.0 %collective-permute-done.3 = f32[32,3328]{1,0:T(8,128)S(1)} collective-permute-done((f32[32,3328]{1,0:T(8,128)S(1)}, f32[32,3328]{1,0:T(8,128)S(1)}, u32[]{:S(2)}, u32[]{:S(2)}) %collective-permute-start.3) | collective-permute-done | bytes 426016 | tf_op jit(solution)/shard_map/ppermute | solution.py:692
  90.0 1.5 %collective-permute-start.7 = (f32[8,3328]{1,0:T(8,128)S(1)}, f32[8,3328]{1,0:T(8,128)S(1)}, u32[]{:S(2)}, u32[]{:S(2)}) collective-permute-start(f32[8,3328]{1,0:T(8,128)S(1)} %get-tuple-element.126), channel_id=1, source_target_pairs={{0,24},{1,7},{2,26},{3,5},{4,28},{5,3},{6,30},{7,1},{8,16},{9,15},... | collective-permute-start | bytes 319496 | tf_op jit(solution)/shard_map/ppermute | solution.py:692
  91.5 1.4 collective-permute-start.6
  92.9 2.0 %collective-permute-done.5 = f32[8,3328]{1,0:T(8,128)S(1)} collective-permute-done((f32[8,3328]{1,0:T(8,128)S(1)}, f32[8,3328]{1,0:T(8,128)S(1)}, u32[]{:S(2)}, u32[]{:S(2)}) %collective-permute-start.5) | collective-permute-done | bytes 106528 | tf_op jit(solution)/shard_map/ppermute | solution.py:692
  94.9 1.7 %collective-permute-done.7 = f32[8,3328]{1,0:T(8,128)S(1)} collective-permute-done((f32[8,3328]{1,0:T(8,128)S(1)}, f32[8,3328]{1,0:T(8,128)S(1)}, u32[]{:S(2)}, u32[]{:S(2)}) %collective-permute-start.7) | collective-permute-done | bytes 106528 | tf_op jit(solution)/shard_map/ppermute | solution.py:692
  96.6 4.7 %collective-permute-done.6 = f32[8,3328]{1,0:T(8,128)S(1)} collective-permute-done((f32[8,3328]{1,0:T(8,128)S(1)}, f32[8,3328]{1,0:T(8,128)S(1)}, u32[]{:S(2)}, u32[]{:S(2)}) %collective-permute-start.6) | collective-permute-done | bytes 106528 | tf_op jit(solution)/shard_map/ppermute | solution.py:692
  101.3 1.0 collective-permute-start.10
  102.3 3.5 %collective-permute-start.8 = (f32[8,3328]{1,0:T(8,128)S(1)}, f32[8,3328]{1,0:T(8,128)S(1)}, u32[]{:S(2)}, u32[]{:S(2)}) collective-permute-start(f32[8,3328]{1,0:T(8,128)S(1)} %get-tuple-element.121), channel_id=1, source_target_pairs={{0,8},{1,3},{2,10},{3,1},{4,12},{5,7},{6,14},{7,5},{8,0},{9,11},{1... | collective-permute-start | bytes 319496 | tf_op jit(solution)/shard_map/ppermute | solution.py:692
  105.8 2.3 %collective-permute-done.10 = f32[8,3328]{1,0:T(8,128)S(1)} collective-permute-done((f32[8,3328]{1,0:T(8,128)S(1)}, f32[8,3328]{1,0:T(8,128)S(1)}, u32[]{:S(2)}, u32[]{:S(2)}) %collective-permute-start.10) | collective-permute-done | bytes 106528 | tf_op jit(solution)/shard_map/ppermute | solution.py:692
  108.1 2.1 %collective-permute-done.9 = f32[8,3328]{1,0:T(8,128)S(1)} collective-permute-done((f32[8,3328]{1,0:T(8,128)S(1)}, f32[8,3328]{1,0:T(8,128)S(1)}, u32[]{:S(2)}, u32[]{:S(2)}) %collective-permute-start.9) | collective-permute-done | bytes 106528 | tf_op jit(solution)/shard_map/ppermute | solution.py:692
  110.2 1.7 %collective-permute-start.13 = (f32[32,3328]{1,0:T(8,128)S(1)}, f32[32,3328]{1,0:T(8,128)S(1)}, u32[]{:S(2)}, u32[]{:S(2)}) collective-permute-start(f32[32,3328]{1,0:T(8,128)S(1)} %pad_maximum_fusion.1), channel_id=1, source_target_pairs={{0,6},{1,25},{2,4},{3,27},{4,2},{5,29},{6,0},{7,31},{8,14},{9,17},... | collective-permute-start | bytes 1277960 | tf_op jit(solution)/shard_map/ppermute | solution.py:692
  111.9 2.0 %collective-permute-start.12 = (f32[32,3328]{1,0:T(8,128)S(1)}, f32[32,3328]{1,0:T(8,128)S(1)}, u32[]{:S(2)}, u32[]{:S(2)}) collective-permute-start(f32[32,3328]{1,0:T(8,128)S(1)} %pad_maximum_fusion.1), channel_id=1, source_target_pairs={{0,4},{1,17},{2,6},{3,19},{4,0},{5,21},{6,2},{7,23},{8,12},{9,25},... | collective-permute-start | bytes 1277960 | tf_op jit(solution)/shard_map/ppermute | solution.py:692
  114.0 9.5 %collective-permute-done.11 = f32[32,3328]{1,0:T(8,128)S(1)} collective-permute-done((f32[32,3328]{1,0:T(8,128)S(1)}, f32[32,3328]{1,0:T(8,128)S(1)}, u32[]{:S(2)}, u32[]{:S(2)}) %collective-permute-start.11) | collective-permute-done | bytes 426016 | tf_op jit(solution)/shard_map/ppermute | solution.py:692
  124.0 8.5 %collective-permute-start.14 = (f32[128,3328]{1,0:T(8,128)S(1)}, f32[128,3328]{1,0:T(8,128)S(1)}, u32[]{:S(2)}, u32[]{:S(2)}) collective-permute-start(f32[128,3328]{1,0:T(8,128)S(1)} %constant_dynamic-update-slice_fusion.half_ref), channel_id=1, source_target_pairs={{0,1},{1,0},{2,3},{3,2},{4,5},{5,4},{6,7},{7,6},{8,9},{9,8},{10,11... | collective-permute-start | bytes 5111816 | tf_op jit(solution)/shard_map/ppermute | solution.py:692
  133.1 2.4 %shard_map.219 = (f32[640,256]{1,0:T(8,128)}, f32[4,256]{1,0:T(4,128)}) custom-call(bf16[256,3584]{1,0:T(8,128)(2,1)S(1)} %get-tuple-element.90.dm0_ref, bf16[256,3584]{1,0:T(8,128)(2,1)S(1)} %get-tuple-element.91.dm1_ref, bf16[2,768,256]{2,1,0:T(8,128)(2,1)S(1)} %copy-done, bf16[2,16,256]{2,1,0:T(8,128)(2,1)S(1)} %copy-done.3, ...), custom_call_target="tpu_custom_call" | custom-call | flops 2000000000 | tf_op jit(solution)/shard_map/pallas_call | solution.py:620
  135.5 1.3 shard_map.220
  136.8 2.1 %shard_map.221 = (f32[2,16,2,8,832]{4,3,2,1,0:T(8,128)}, f32[2,16,2,8,256]{4,3,2,1,0:T(8,128)}, f32[2,3,16,2,8,256]{5,4,3,2,1,0:T(8,128)}, f32[2,256]{1,0:T(2,128)}, f32[2,16,256]{2,1,0:T(8,128)}) custom-call(f32[2,16,2,8,832]{4,3,2,1,0:T(8,128)} %get-tuple-element.109.post_in, ...), custom_call_target="tpu_custom_call", output_to_operand_aliasing={{0}: (0, {}), {1}: (1, {}), {2}: (2, {})} | custom-call | tf_op jit(solution)/shard_map/pallas_call | solution.py:620
  (41 shorter events, 3.3 us)
Async XLA Ops:
  0.6 23.0 %copy-start = (bf16[2,768,256]{2,1,0:T(8,128)(2,1)S(1)}, bf16[2,768,256]{2,1,0:T(8,128)(2,1)}, u32[]{:S(2)}) copy-start(bf16[2,768,256]{2,1,0:T(8,128)(2,1)} %wpre_ref.9) | copy-start | bytes 2359300
  0.7 23.0 %copy-start.2 = (bf16[2,256,256]{2,1,0:T(8,128)(2,1)S(1)}, bf16[2,256,256]{2,1,0:T(8,128)(2,1)}, u32[]{:S(2)}) copy-start(bf16[2,256,256]{2,1,0:T(8,128)(2,1)} %wmix_ref.5) | copy-start | bytes 786436
  0.7 23.0 %copy-start.3 = (bf16[2,16,256]{2,1,0:T(8,128)(2,1)S(1)}, bf16[2,16,256]{2,1,0:T(8,128)(2,1)}, u32[]{:S(2)}) copy-start(bf16[2,16,256]{2,1,0:T(8,128)(2,1)} %wedge_ref.5) | copy-start | bytes 49156
  0.7 23.0 %copy-start.6 = (f32[2,256]{1,0:T(2,128)S(1)}, f32[2,256]{1,0:T(2,128)}, u32[]{:S(2)}) copy-start(f32[2,256]{1,0:T(2,128)} %bpre_ref.1) | copy-start | bytes 6148
  0.7 23.0 %copy-start.1 = (bf16[2,4,832,64]{2,3,1,0:T(8,128)(2,1)S(1)}, bf16[2,4,832,64]{2,3,1,0:T(8,128)(2,1)}, u32[]{:S(2)}) copy-start(bf16[2,4,832,64]{2,3,1,0:T(8,128)(2,1)} %param.23) | copy-start | bytes 2555908
  0.7 23.0 %copy-start.5 = (f32[2,256]{1,0:T(2,128)S(1)}, f32[2,256]{1,0:T(2,128)}, u32[]{:S(2)}) copy-start(f32[2,256]{1,0:T(2,128)} %bias_ref.7) | copy-start | bytes 6148
  0.7 23.0 %copy-start.4 = (f32[2,256]{1,0:T(2,128)S(1)}, f32[2,256]{1,0:T(2,128)}, u32[]{:S(2)}) copy-start(f32[2,256]{1,0:T(2,128)} %gain_ref.7) | copy-start | bytes 6148
  23.7 14.9 %copy-start.7 = (f32[4,256]{1,0:T(4,128)S(1)}, f32[4,256]{1,0:T(4,128)}, u32[]{:S(2)}) copy-start(f32[4,256]{1,0:T(4,128)} %rg_ref.1) | copy-start | bytes 12292
  72.1 2.4 %collective-permute-start.1 = (f32[128,1664]{1,0:T(8,128)S(1)}, f32[128,1664]{1,0:T(8,128)S(1)}, u32[]{:S(2)}, u32[]{:S(2)}) collective-permute-start(f32[128,1664]{1,0:T(8,128)S(1)} %get-tuple-element.103), channel_id=1, source_target_pairs={{0,1},{1,0},{2,3},{3,2},{4,5},{5,4},{6,7},{7,6},{8,9},{9,8},{10,11... | collective-permute-start | bytes 2555912 | tf_op jit(solution)/shard_map/ppermute | solution.py:692
  72.3 3.5 %collective-permute-start = (f32[128,1664]{1,0:T(8,128)S(1)}, f32[128,1664]{1,0:T(8,128)S(1)}, u32[]{:S(2)}, u32[]{:S(2)}) collective-permute-start(f32[128,1664]{1,0:T(8,128)S(1)} %get-tuple-element.93), channel_id=1, source_target_pairs={{0,1},{1,0},{2,3},{3,2},{4,5},{5,4},{6,7},{7,6},{8,9},{9,8},{10,11... | collective-permute-start | bytes 2555912 | tf_op jit(solution)/shard_map/ppermute | solution.py:692
  76.0 8.2 %collective-permute-start.2 = (f32[32,3328]{1,0:T(8,128)S(1)}, f32[32,3328]{1,0:T(8,128)S(1)}, u32[]{:S(2)}, u32[]{:S(2)}) collective-permute-start(f32[32,3328]{1,0:T(8,128)S(1)} %get-tuple-element.122), channel_id=1, source_target_pairs={{0,2},{1,9},{2,0},{3,11},{4,6},{5,13},{6,4},{7,15},{8,10},{9,1},{1... | collective-permute-start | bytes 1277960 | tf_op jit(solution)/shard_map/ppermute | solution.py:692
  76.5 12.7 %collective-permute-start.3 = (f32[32,3328]{1,0:T(8,128)S(1)}, f32[32,3328]{1,0:T(8,128)S(1)}, u32[]{:S(2)}, u32[]{:S(2)}) collective-permute-start(f32[32,3328]{1,0:T(8,128)S(1)} %get-tuple-element.123), channel_id=1, source_target_pairs={{0,4},{1,17},{2,6},{3,19},{4,0},{5,21},{6,2},{7,23},{8,12},{9,25},... | collective-permute-start | bytes 1277960 | tf_op jit(solution)/shard_map/ppermute | solution.py:692
  77.3 11.8 %collective-permute-start.4 = (f32[32,3328]{1,0:T(8,128)S(1)}, f32[32,3328]{1,0:T(8,128)S(1)}, u32[]{:S(2)}, u32[]{:S(2)}) collective-permute-start(f32[32,3328]{1,0:T(8,128)S(1)} %get-tuple-element.124), channel_id=1, source_target_pairs={{0,6},{1,25},{2,4},{3,27},{4,2},{5,29},{6,0},{7,31},{8,14},{9,17},... | collective-permute-start | bytes 1277960 | tf_op jit(solution)/shard_map/ppermute | solution.py:692
  89.3 5.6 %collective-permute-start.5 = (f32[8,3328]{1,0:T(8,128)S(1)}, f32[8,3328]{1,0:T(8,128)S(1)}, u32[]{:S(2)}, u32[]{:S(2)}) collective-permute-start(f32[8,3328]{1,0:T(8,128)S(1)} %get-tuple-element.125), channel_id=1, source_target_pairs={{0,8},{1,3},{2,10},{3,1},{4,12},{5,7},{6,14},{7,5},{8,0},{9,11},{1... | collective-permute-start | bytes 319496 | tf_op jit(solution)/shard_map/ppermute | solution.py:692
  90.0 6.6 %collective-permute-start.7 = (f32[8,3328]{1,0:T(8,128)S(1)}, f32[8,3328]{1,0:T(8,128)S(1)}, u32[]{:S(2)}, u32[]{:S(2)}) collective-permute-start(f32[8,3328]{1,0:T(8,128)S(1)} %get-tuple-element.126), channel_id=1, source_target_pairs={{0,24},{1,7},{2,26},{3,5},{4,28},{5,3},{6,30},{7,1},{8,16},{9,15},... | collective-permute-start | bytes 319496 | tf_op jit(solution)/shard_map/ppermute | solution.py:692
  91.5 9.8 %collective-permute-start.6 = (f32[8,3328]{1,0:T(8,128)S(1)}, f32[8,3328]{1,0:T(8,128)S(1)}, u32[]{:S(2)}, u32[]{:S(2)}) collective-permute-start(f32[8,3328]{1,0:T(8,128)S(1)} %get-tuple-element.127), channel_id=1, source_target_pairs={{0,16},{1,5},{2,18},{3,7},{4,20},{5,1},{6,22},{7,3},{8,24},{9,13},... | collective-permute-start | bytes 319496 | tf_op jit(solution)/shard_map/ppermute | solution.py:692
  101.3 6.7 %collective-permute-start.10 = (f32[8,3328]{1,0:T(8,128)S(1)}, f32[8,3328]{1,0:T(8,128)S(1)}, u32[]{:S(2)}, u32[]{:S(2)}) collective-permute-start(f32[8,3328]{1,0:T(8,128)S(1)} %get-tuple-element.121), channel_id=1, source_target_pairs={{0,24},{1,7},{2,26},{3,5},{4,28},{5,3},{6,30},{7,1},{8,16},{9,15},... | collective-permute-start | bytes 319496 | tf_op jit(solution)/shard_map/ppermute | solution.py:692
  102.3 7.9 %collective-permute-start.9 = (f32[8,3328]{1,0:T(8,128)S(1)}, f32[8,3328]{1,0:T(8,128)S(1)}, u32[]{:S(2)}, u32[]{:S(2)}) collective-permute-start(f32[8,3328]{1,0:T(8,128)S(1)} %get-tuple-element.121), channel_id=1, source_target_pairs={{0,16},{1,5},{2,18},{3,7},{4,20},{5,1},{6,22},{7,3},{8,24},{9,13},... | collective-permute-start | bytes 319496 | tf_op jit(solution)/shard_map/ppermute | solution.py:692
  102.3 7.9 %collective-permute-start.8 = (f32[8,3328]{1,0:T(8,128)S(1)}, f32[8,3328]{1,0:T(8,128)S(1)}, u32[]{:S(2)}, u32[]{:S(2)}) collective-permute-start(f32[8,3328]{1,0:T(8,128)S(1)} %get-tuple-element.121), channel_id=1, source_target_pairs={{0,8},{1,3},{2,10},{3,1},{4,12},{5,7},{6,14},{7,5},{8,0},{9,11},{1... | collective-permute-start | bytes 319496 | tf_op jit(solution)/shard_map/ppermute | solution.py:692
  110.2 13.7 %collective-permute-start.13 = (f32[32,3328]{1,0:T(8,128)S(1)}, f32[32,3328]{1,0:T(8,128)S(1)}, u32[]{:S(2)}, u32[]{:S(2)}) collective-permute-start(f32[32,3328]{1,0:T(8,128)S(1)} %pad_maximum_fusion.1), channel_id=1, source_target_pairs={{0,6},{1,25},{2,4},{3,27},{4,2},{5,29},{6,0},{7,31},{8,14},{9,17},... | collective-permute-start | bytes 1277960 | tf_op jit(solution)/shard_map/ppermute | solution.py:692
  111.9 12.0 %collective-permute-start.12 = (f32[32,3328]{1,0:T(8,128)S(1)}, f32[32,3328]{1,0:T(8,128)S(1)}, u32[]{:S(2)}, u32[]{:S(2)}) collective-permute-start(f32[32,3328]{1,0:T(8,128)S(1)} %pad_maximum_fusion.1), channel_id=1, source_target_pairs={{0,4},{1,17},{2,6},{3,19},{4,0},{5,21},{6,2},{7,23},{8,12},{9,25},... | collective-permute-start | bytes 1277960 | tf_op jit(solution)/shard_map/ppermute | solution.py:692
  113.9 9.6 %collective-permute-start.11 = (f32[32,3328]{1,0:T(8,128)S(1)}, f32[32,3328]{1,0:T(8,128)S(1)}, u32[]{:S(2)}, u32[]{:S(2)}) collective-permute-start(f32[32,3328]{1,0:T(8,128)S(1)} %pad_maximum_fusion.1), channel_id=1, source_target_pairs={{0,2},{1,9},{2,0},{3,11},{4,6},{5,13},{6,4},{7,15},{8,10},{9,1},{1... | collective-permute-start | bytes 1277960 | tf_op jit(solution)/shard_map/ppermute | solution.py:692
  124.0 12.8 %collective-permute-start.14 = (f32[128,3328]{1,0:T(8,128)S(1)}, f32[128,3328]{1,0:T(8,128)S(1)}, u32[]{:S(2)}, u32[]{:S(2)}) collective-permute-start(f32[128,3328]{1,0:T(8,128)S(1)} %constant_dynamic-update-slice_fusion.half_ref), channel_id=1, source_target_pairs={{0,1},{1,0},{2,3},{3,2},{4,5},{5,4},{6,7},{7,6},{8,9},{9,8},{10,11... | collective-permute-start | bytes 5111816 | tf_op jit(solution)/shard_map/ppermute | solution.py:692

commit v4 on v3

--- a/solution.py
+++ b/solution.py
@@ -47,6 +47,15 @@
 
 def fold(value, op):
     return op(value, pltpu.roll(value, 64, 1))
+
+
+def lane_groups(nodes):
+    return [(lo, min(lo + 256, nodes)) for lo in range(0, nodes, 256)]
+
+
+def leaf_col(nodes, slot, node):
+    lo, hi = next(g for g in lane_groups(nodes) if g[0] <= node < g[1])
+    return LEAF_SLOTS * lo + slot * (hi - lo) + node - lo
 
 
 def split_two(value):
@@ -126,17 +135,21 @@
 
     ef_t = ef_ref[...].T
     ef_h = mm(ef_t, g).astype(BF16)
-    node_iota = iota((nodes, nodes), 0)
     hub_iota = iota((nodes, 128), 0)
-    zero16 = jnp.zeros((16, nodes), BF16)
-    for k in range(LEAF_SLOTS):
-        lo = k * nodes
-        b_ref[0:nodes, lo : lo + nodes] = (node_iota == nbr[k : k + 1]).astype(F32).astype(BF16)
-        piece = ef_t[16 * k : 16 * k + 16]
-        for r, part in enumerate((piece, zero16, piece, zero16)):
-            b_ref[nodes + 16 * r : nodes + 16 * r + 16, lo : lo + nodes] = part
-        live_ref[0:1, lo : lo + nodes] = mask[k : k + 1] * LOG2E
-        live_ref[1:2, lo : lo + nodes] = mask[k : k + 1]
+    for first_node, end_node in lane_groups(nodes):
+        span = slice(first_node, end_node)
+        size = end_node - first_node
+        node_iota = iota((nodes, size), 0)
+        zero16 = jnp.zeros((16, size), BF16)
+        for k in range(LEAF_SLOTS):
+            lo = leaf_col(nodes, k, first_node)
+            cols = slice(lo, lo + size)
+            b_ref[0:nodes, cols] = (node_iota == nbr[k : k + 1, span]).astype(F32).astype(BF16)
+            piece = ef_t[16 * k : 16 * k + 16, span]
+            for r, part in enumerate((piece, zero16, piece, zero16)):
+                b_ref[nodes + 16 * r : nodes + 16 * r + 16, cols] = part
+            live_ref[0:1, cols] = mask[k : k + 1, span] * LOG2E
+            live_ref[1:2, cols] = mask[k : k + 1, span]
     own_half = (iota((32, 128), 0) < 16) == (iota((32, 128), 1) < 64)
     for j in range(8):
         lo = LEAF_SLOTS * nodes + 128 * j
@@ -198,8 +211,8 @@
                 first = m_ref[rows, leaf_cols : leaf_cols + 128]
                 first = jnp.where(iota((1, 128), 1) < 64, first, pltpu.roll(first, 64, 1))
             else:
-                cols = [k * nodes + 128 * c for k in range(1, LEAF_SLOTS)]
-                first = m_ref[rows, lanes]
+                zero, *cols = [leaf_col(nodes, k, 128 * c) for k in range(LEAF_SLOTS)]
+                first = m_ref[rows, zero : zero + 128]
             offs = []
             for lo in cols:
                 d = (m_ref[rows, lo : lo + 128] - first) * live_ref[0:1, lo : lo + 128]
@@ -228,20 +241,17 @@
                 value = base + LN2 * stat if n < 3 else spread * rstd
                 z_ref[pl.ds(zr + 64 * n, ROW_CHUNK), lanes] = value.astype(BF16)
 
-    last = nodes // 128
-    groups = [range(last, last + 1)] + [range(c, min(c + 2, last)) for c in range(0, last, 2)]
+    groups = [(leaf_cols, leaf_cols + 1024, range(nodes // 128, nodes // 128 + 1))]
+    for lo, hi in lane_groups(nodes):
+        groups.append((LEAF_SLOTS * lo, LEAF_SLOTS * hi, range(lo // 128, hi // 128)))
     waiting = None
-    for tiles in groups + [None]:
-        if tiles is not None:
-            if tiles[0] == last:
-                messages(leaf_cols, leaf_cols + 1024)
-            else:
-                for k in range(LEAF_SLOTS):
-                    messages(k * nodes + 128 * tiles[0], k * nodes + 128 * (tiles[-1] + 1))
+    for group in groups + [None]:
+        if group is not None:
+            messages(*group[0:2])
         if waiting is not None:
             for i in range(width // ROW_CHUNK):
-                summarize(i, waiting)
-        waiting = tiles
+                summarize(i, waiting[2])
+        waiting = group
 
     amp, att = rows_ref[0:1], rows_ref[1:2]
     for t in range(4):
@@ -268,14 +278,14 @@
 ):
     loads = start_copies(
         [
-            (seg_hbm, seg_ref), (nbr_hbm, nbr_ref), (mask_hbm, mask_ref), (deg_hbm, deg_ref), (ef_hbm, ef_ref), (nf_hbm, nf_ref), (wpre_hbm, wpre_ref),
-            (wedge_hbm, wedge_ref), (bpre_hbm, bpre_ref), (wpost_hbm, wpost_ref), (wmix_hbm, wmix_ref),
+            (seg_hbm, seg_ref), (nbr_hbm, nbr_ref), (mask_hbm, mask_ref), (deg_hbm, deg_ref), (ef_hbm, ef_ref), (nf_hbm, nf_ref),
+            (wpre_hbm.at[0:1], wpre_ref), (wedge_hbm, wedge_ref), (bpre_hbm, bpre_ref),
+            (wpost_hbm.at[0:1], wpost_ref), (wmix_hbm.at[0:1], wmix_ref),
         ],
         in_sems,
     )
-    wait_all(loads[0:5])
+    wait_all(loads)
     build_tables(ef_ref, seg_ref, nbr_ref, mask_ref, deg_ref, b_ref, live_ref, rows_ref, g_ref, gt_ref)
-    wait_all(loads[5:])
     x_ref[...] = nf_ref[...].T
     forward_layer(
         layer, x_ref, wedge_ref, wpre_ref, *to_cols(bpre_ref[layer : layer + 1]), wpost_ref, wmix_ref, b_ref,
@@ -407,9 +417,9 @@
                 cols = [leaf_cols + 128 * j for j in range(8)]
                 acc = None
             else:
-                cols = [k * nodes + 128 * c for k in range(1, LEAF_SLOTS)]
+                zero, *cols = [leaf_col(nodes, k, 128 * c) for k in range(LEAF_SLOTS)]
                 acc = c0 + dsmax * jnp.exp2(-smax) + dsmin * jnp.exp2(smin)
-                dm_ref[rows, lanes] = acc.astype(BF16)
+                dm_ref[rows, zero : zero + 128] = acc.astype(BF16)
             for lo in cols:
                 m = m_ref[rows, lo : lo + 128]
                 d = c0 + m * c1 + dsmax * jnp.exp2(m - smax) + dsmin * jnp.exp2(smin - m)
@@ -421,22 +431,19 @@
     def land(lo, hi):
         return mm(dm_ref[:, lo:hi], b_ref[0 : nodes + 32, lo:hi], NT)
 
-    last = nodes // 128
-    groups = [range(last, last + 1)] + [range(c, min(c + 2, last)) for c in range(0, last, 2)]
-    waiting, landed = None, None
-    for step, tiles in enumerate(groups + [None]):
-        if tiles is not None:
+    groups = [(leaf_cols, leaf_cols + 1024, range(nodes // 128, nodes // 128 + 1))]
+    for lo, hi in lane_groups(nodes):
+        groups.append((LEAF_SLOTS * lo, LEAF_SLOTS * hi, range(lo // 128, hi // 128)))
+    waiting, landed = None, 0.0
+    for step, group in enumerate(groups + [None]):
+        if group is not None:
             for i in range(width // ROW_CHUNK):
-                spread_back(i, tiles)
+                spread_back(i, group[2])
         if step < len(beside):
             beside[step]()
         if waiting is not None:
-            if waiting[0] == last:
-                landed = land(leaf_cols, leaf_cols + 1024)
-            else:
-                for k in range(LEAF_SLOTS):
-                    landed = landed + land(k * nodes + 128 * waiting[0], k * nodes + 128 * (waiting[-1] + 1))
-        waiting = tiles
+            landed = landed + land(*waiting[0:2])
+        waiting = group
 
     down = acc_ref[:, 0:nodes] + mm(acc_ref[:, nodes:].astype(BF16), gt_ref[...])
     dcat_ref[0:width] = down.astype(BF16)
@@ -451,26 +458,10 @@
     return dh_ref[...] + dh
 
 
-def backward_first_kernel(
-    layer, recv_ref, dv_ref, dh_ref, u_ref, norm_ref, gain_ref, bias_ref, wmix_ref, wpost_ref, wpre_ref,
-    b_ref, live_ref, rows_ref, g_ref, gt_ref, m_ref, s_ref, u_low_ref, norm_low_ref,
-    gb_ref, du_ref, d_ref, dm_ref, dcat_ref, et_ref, dh_out_ref, dv_out_ref, part_ref,
-    ds_ref, acc_ref, bd_ref,
-):
-    dh = backward_layer(
-        layer, recv_ref, dv_ref, dh_ref, u_ref, norm_ref, gain_ref, bias_ref, wmix_ref, wpost_ref, wpre_ref,
-        b_ref, live_ref, rows_ref, g_ref, gt_ref, m_ref, s_ref,
-        gb_ref, du_ref, d_ref, dm_ref, dcat_ref, et_ref, ds_ref, acc_ref, bd_ref,
-    )
-    dh_out_ref[...] = dh
-    xh, v = normed(u_low_ref[...], norm_low_ref, gain_ref, bias_ref, layer - 1)
-    gate_grad(dh, xh, v, dv_out_ref, part_ref)
-
-
-def piece_owner(core, half, place):
+def piece_owner(core, half, place, mixed):
     plane_first = ((place >> 2) << 1) | ((place & 3) << 3)
     line_first = ((place >> 2) << 3) | ((place & 3) << 1)
-    return half + jnp.where(core == half, plane_first, line_first)
+    return half + (jnp.where(core == half, plane_first, line_first) if mixed else plane_first)
 
 
 def put_tower_grad(t, d_ref, z_ref, grads_ref):
@@ -487,41 +478,58 @@
     grads_ref[:, 896:1152] = mm(y_ref[...], du_ref[...], NT)
 
 
-def put_message_grads(x_ref, dcat_ref, et_ref, grads_ref, keep_ref, send_ref):
+def put_message_grads(mixed, x_ref, dcat_ref, et_ref, grads_ref, keep_ref, send_ref):
     width = x_ref.shape[0]
     grads_ref[:, 832:896] = et_ref[...]
     grads_ref[:, 1152:1664] = mm(x_ref[...], dcat_ref[0 : 2 * width], NT)
     me = lax.axis_index("dp") & 31
     for place in range(16):
         for half, ref in ((0, keep_ref), (1, send_ref)):
-            row = pl.multiple_of((me ^ piece_owner(me & 1, half, place)) * 8, 8)
+            row = pl.multiple_of((me ^ piece_owner(me & 1, half, place, mixed)) * 8, 8)
             ref[8 * place : 8 * place + 8] = grads_ref[pl.ds(row, 8)]
 
 
-def weight_kernel(
-    y_ref, du_ref, d_ref, z_ref, x_ref, dcat_ref, et_ref, keep_ref, send_ref, grads_ref
-):
-    for t in range(4):
-        put_tower_grad(t, d_ref, z_ref, grads_ref)
-    put_mix_grad(y_ref, du_ref, grads_ref)
-    put_message_grads(x_ref, dcat_ref, et_ref, grads_ref, keep_ref, send_ref)
+def grad_steps(d_ref, z_ref, y_ref, du_ref, grads_ref):
+    steps = [functools.partial(put_tower_grad, t, d_ref, z_ref, grads_ref) for t in range(4)]
+    return steps + [functools.partial(put_mix_grad, y_ref, du_ref, grads_ref)]
+
+
+def backward_first_kernel(
+    layer, recv_ref, dv_ref, dh_ref, u_ref, norm_ref, gain_ref, bias_ref, wmix_ref, wpost_ref, wpre_ref,
+    b_ref, live_ref, rows_ref, g_ref, gt_ref, m_ref, s_ref, z_ref, y_ref, x_ref, u_low_ref, norm_low_ref,
+    gb_ref, dm_ref, dh_out_ref, dv_out_ref, part_ref, keep_ref, send_ref,
+    du_ref, d_ref, dcat_ref, et_ref, ds_ref, acc_ref, bd_ref, grads_ref,
+):
+    dh = backward_layer(
+        layer, recv_ref, dv_ref, dh_ref, u_ref, norm_ref, gain_ref, bias_ref, wmix_ref, wpost_ref, wpre_ref,
+        b_ref, live_ref, rows_ref, g_ref, gt_ref, m_ref, s_ref,
+        gb_ref, du_ref, d_ref, dm_ref, dcat_ref, et_ref, ds_ref, acc_ref, bd_ref,
+        grad_steps(d_ref, z_ref, y_ref, du_ref, grads_ref),
+    )
+    put_message_grads(False, x_ref, dcat_ref, et_ref, grads_ref, keep_ref, send_ref)
+    dh_out_ref[...] = dh
+    xh, v = normed(u_low_ref[...], norm_low_ref, gain_ref, bias_ref, layer - 1)
+    gate_grad(dh, xh, v, dv_out_ref, part_ref)
 
 
 def backward_last_kernel(
     layer, recv_ref, dv_ref, dh_ref, u_ref, norm_ref, gain_ref, bias_ref, wmix_ref, wpost_ref, wpre_ref,
     b_ref, live_ref, rows_ref, g_ref, gt_ref, m_ref, s_ref, z_ref, y_ref, x_ref,
-    gb_ref, dm_ref, node_ref, keep_ref, send_ref,
-    du_ref, d_ref, dcat_ref, et_ref, ds_ref, acc_ref, bd_ref, grads_ref,
-):
-    beside = [functools.partial(put_tower_grad, t, d_ref, z_ref, grads_ref) for t in range(4)]
-    beside[3:] = [lambda: put_tower_grad(3, d_ref, z_ref, grads_ref) or put_mix_grad(y_ref, du_ref, grads_ref)]
+    sums1_ref, g_gain_ref, g_bias_ref, dm_ref, node_ref, keep_ref, send_ref,
+    gb_ref, du_ref, d_ref, dcat_ref, et_ref, ds_ref, acc_ref, bd_ref, grads_ref,
+):
     dh = backward_layer(
         layer, recv_ref, dv_ref, dh_ref, u_ref, norm_ref, gain_ref, bias_ref, wmix_ref, wpost_ref, wpre_ref,
         b_ref, live_ref, rows_ref, g_ref, gt_ref, m_ref, s_ref,
-        gb_ref, du_ref, d_ref, dm_ref, dcat_ref, et_ref, ds_ref, acc_ref, bd_ref, beside,
-    )
-    put_message_grads(x_ref, dcat_ref, et_ref, grads_ref, keep_ref, send_ref)
+        gb_ref, du_ref, d_ref, dm_ref, dcat_ref, et_ref, ds_ref, acc_ref, bd_ref,
+        grad_steps(d_ref, z_ref, y_ref, du_ref, grads_ref),
+    )
+    put_message_grads(True, x_ref, dcat_ref, et_ref, grads_ref, keep_ref, send_ref)
     node_ref[...] = dh.T
+    width = node_ref.shape[1]
+    for out_ref, cols in ((g_bias_ref, slice(0, width)), (g_gain_ref, slice(width, 2 * width))):
+        out_ref[0:1] = gb_ref[:, cols]
+        out_ref[1:2] = sums1_ref[:, cols]
 
 
 def edge_kernel(dm0_ref, dm1_ref, wpre_ref, wedge_ref, gt_ref, h_ref, rows_ref, out_ref, readout_ref, acc_ref):
@@ -540,7 +548,14 @@
     high, rest = split_two(acc_ref[...])
     gt = gt_ref[...]
     spread_out = mm(high, gt) + mm(rest, gt)
-    leaf = jnp.concatenate([total[:, k * nodes : (k + 1) * nodes] for k in range(LEAF_SLOTS)], axis=0)
+    leaf = []
+    for k in range(LEAF_SLOTS):
+        parts = []
+        for lo, hi in lane_groups(nodes):
+            col = leaf_col(nodes, k, lo)
+            parts.append(total[:, col : col + hi - lo])
+        leaf.append(jnp.concatenate(parts, axis=1))
+    leaf = jnp.concatenate(leaf, axis=0)
     out = jnp.concatenate([spread_out[0:64] + leaf, spread_out[64:]], axis=0)
     out_ref[...] = out.T
     belong = (iota((8, nodes), 0).astype(F32) == rows_ref[7:8, 0:nodes]).astype(F32)
@@ -548,15 +563,14 @@
     readout_ref[...] = total[0 : readout_ref.shape[0]] / SUB_MAX
 
 
-def finish_half(half, half_ref, outs, bufs, sems):
+def finish_half(half, half_refs, outs, bufs, sems):
     me = lax.axis_index("dp") & 31
     core = me & 1
     post, mix, pre, et = bufs
     for layer in range(post.shape[0]):
-        cols = 1664 * layer
         for place in range(16):
-            block = (me ^ piece_owner(core, half, place)) >> 1
-            piece = half_ref[8 * place : 8 * place + 8, cols : cols + 1664]
+            block = (me ^ piece_owner(core, half, place, layer == 0)) >> 1
+            piece = half_refs[layer][8 * place : 8 * place + 8]
             post[layer, block] = piece[:, 0:832]
             et[layer, block] = piece[:, 832:896]
             mix[layer, block] = piece[:, 896:1152]
@@ -568,16 +582,16 @@
     return start_copies(pairs, sems)
 
 
-def finish_first_kernel(half_ref, post_out, mix_out, pre_out, et, post, mix, pre, sems):
-    wait_all(finish_half(0, half_ref, (post_out, mix_out, pre_out), (post, mix, pre, et), sems))
+def finish_first_kernel(half0_ref, half1_ref, post_out, mix_out, pre_out, et, post, mix, pre, sems):
+    wait_all(finish_half(0, (half0_ref, half1_ref), (post_out, mix_out, pre_out), (post, mix, pre, et), sems))
 
 
 def finish_last_kernel(
-    post_in, mix_in, pre_in, other_et, half_ref, wedge_ref, wpre_ref, post_out, mix_out, pre_out, gb_ref, gedge_ref,
+    post_in, mix_in, pre_in, other_et, half0_ref, half1_ref, wedge_ref, wpre_ref, post_out, mix_out, pre_out, gb_ref, gedge_ref,
     post, mix, pre, et, term, sems,
 ):
     del post_in, mix_in, pre_in
-    copies = finish_half(1, half_ref, (post_out, mix_out, pre_out), (post, mix, pre, et), sems)
+    copies = finish_half(1, (half0_ref, half1_ref), (post_out, mix_out, pre_out), (post, mix, pre, et), sems)
     width = wpre_ref.shape[2]
     core = lax.axis_index("dp") & 1
     for layer in range(2):
@@ -650,7 +664,7 @@
     x0, b, live, rows, g, gt, m0, s0, z0, y0, u0, part = call(
         functools.partial(forward_first_kernel, 0),
         first_args, [low_s] + table_outs + layer_outs,
-        fwd_scratch + like(first_args) + [dma(11)], range(11),
+        fwd_scratch + like([a[0:1] if i in (7, 9, 10) else a for i, a in enumerate(first_args)]) + [dma(11)], range(11),
     )
     tables = [b, live, rows, g, gt]
     recv = exchange(part)
@@ -672,50 +686,67 @@
     dcat_s, et_s, acc_s = s((3 * width, nodes), BF16), s((width, 64)), s((width, lanes))
     back_scratch = like([s_s, acc_s, s((width, width), BF16)])
     recv = exchange(part)
-    sums1, du1, d1, dm1, dcat1, et1, dh1, dv0, part = call(
-        functools.partial(backward_first_kernel, 1),
-        [recv, dv1, dh2, u1, norm1, bn_gain, bn_bias, w_mix, wpost_t, w_pre] + tables + [m1, s1, u0, norm0],
-        [sum_s, du_s, d_s, dm_s, dcat_s, et_s, row_s, row_s, sums_out],
-        back_scratch,
-    )
-    recv = exchange(part)
     grad_cols = 1664
     grad_s, half_s = s((width, grad_cols)), s((width // 2, grad_cols))
-    sums0, dm0, node_grad, keep0, send0 = call(
-        functools.partial(backward_last_kernel, 0),
-        [recv, dv0, dh1, u0, norm0, bn_gain, bn_bias, w_mix, wpost_t, w_pre] + tables + [m0, s0, z0, y0, x0],
-        [sum_s, dm_s, s((nodes, width)), half_s, half_s],
-        like([du_s, d_s, dcat_s, et_s]) + back_scratch + like([grad_s]), free=(2,),
+    back_scratch = like([du_s, d_s, dcat_s, et_s]) + back_scratch + like([grad_s])
+    sums1, dm1, dh1, dv0, part, keep1, send1 = call(
+        functools.partial(backward_first_kernel, 1),
+        [recv, dv1, dh2, u1, norm1, bn_gain, bn_bias, w_mix, wpost_t, w_pre] + tables + [m1, s1, z1, y1, x1, u0, norm0],
+        [sum_s, dm_s, row_s, row_s, sums_out, half_s, half_s],
+        back_scratch,
     )
 
     def swap(value, masks):
         return lax.ppermute(value, "dp", [(i, i ^ masks[i & 1]) for i in range(devices)])
 
-    def after(value, *others):
-        return lax.optimization_barrier((value, *others))[0]
-
+    def together(*values):
+        return lax.optimization_barrier(values)
+
+    plane, line = (2, 4, 6), (8, 16, 24)
+    first, second = list(zip(plane, line)), list(zip(line, plane))
+    first1, second1 = list(zip(plane, plane)), list(zip(line, line))
+
+    def relay(value, masks):
+        one, two = swap(value, masks[0]), swap(value, masks[1])
+        return jnp.concatenate([value, one, two, swap(one, masks[1])], axis=0)
+
+    def spread(value):
+        mask = 32
+        while mask < devices:
+            value = value + swap(value, (mask, mask))
+            mask *= 2
+        return value
+
+    def scatter_sum(value, masks, size):
+        got = [swap(value[size * (i + 1) : size * (i + 2)], m) for i, m in enumerate(masks)]
+        return value[0:size] + got[0] + got[1] + got[2]
+
+    def gather(value, masks):
+        return jnp.concatenate([value] + [swap(value, m) for m in masks], axis=0)
+
+    got1 = swap(send1, (1, 1))
+    recv, got1 = together(exchange(part), got1)
+    part1 = scatter_sum(keep1 + got1, first1, 32)
+    g_gain, g_bias, dm0, node_grad, keep0, send0 = call(
+        functools.partial(backward_last_kernel, 0),
+        [recv, dv0, dh1, u0, norm0, bn_gain, bn_bias, w_mix, wpost_t, w_pre] + tables + [m0, s0, z0, y0, x0, sums1],
+        [s(bn_gain.shape), s(bn_bias.shape), dm_s, s((nodes, width)), half_s, half_s],
+        like([sum_s]) + back_scratch, free=(0, 1, 3), cost=8,
+    )
+    edge_grad, readout = call(
+        edge_kernel, [dm0, dm1, w_pre, w_edge, gt, h2, rows],
+        [s((nodes, width)), s(readout_grad.shape)], [pltpu.VMEM((width, 128), F32)], free=(0, 1), cost=2,
+    )
+    send0, part1, edge_grad, readout = together(send0, part1, edge_grad, readout)
     got0 = swap(send0, (1, 1))
-    keep1, send1 = call(
-        weight_kernel, [y1, after(du1, send0), d1, z1, x1, dcat1, et1], [half_s, half_s], like([grad_s]), cost=1.4
-    )
-    got1 = swap(send1, (1, 1))
-    part = jnp.concatenate([keep0 + got0, keep1 + got1], axis=1)
-    plane, line = (2, 4, 6), (8, 16, 24)
-    stages = ((list(zip(plane, line)), 32), (list(zip(line, plane)), 8))
-    edge_grad, readout = call(
-        edge_kernel, [dm0, dm1, w_pre, w_edge, after(gt, part), h2, rows], [s((nodes, width)), s(readout_grad.shape)],
-        [pltpu.VMEM((width, 128), F32)], free=(0, 1), cost=2,
-    )
-    for masks, size in stages:
-        got = [swap(part[size * (i + 1) : size * (i + 2)], m) for i, m in enumerate(masks)]
-        part = part[0:size] + got[0] + got[1] + got[2]
-    mask = 32
-    while mask < devices:
-        part = part + swap(part, (mask, mask))
-        mask *= 2
-    for masks, _ in stages[::-1]:
-        part = jnp.concatenate([part] + [swap(part, m) for m in masks], axis=0)
-    other = swap(part, (1, 1))
+    half0 = keep0 + got0
+    part0 = scatter_sum(half0, first, 32)
+    part1 = gather(spread(scatter_sum(part1, second1, 8)), second1)
+    part1 = relay(together(part1, part0)[0], first1)
+    part0 = spread(scatter_sum(part0, second, 8))
+    part0 = gather(gather(part0, second), first)
+    other1 = swap(part1, (1, 1))
+    other0 = swap(part0, (1, 1))
     layers, blocks = w_pre.shape[0], width // 16
     finals = [
         s((layers, blocks, 2, 8, 832)), s((layers, blocks, 2, 8, width)), s((layers, 3, blocks, 2, 8, width)),
@@ -723,18 +754,17 @@
     bufs = [s((layers, blocks, 8, 832)), s((layers, blocks, 8, width)), s((layers, 2, blocks, 8, width))]
     ets = s((layers, blocks, 8, 64))
     *finals_in, ets_first = call(
-        finish_first_kernel, [part], finals + [ets], like(bufs) + [dma(3)], far_out=(0, 1, 2), cost=2
+        finish_first_kernel, [part0, part1], finals + [ets], like(bufs) + [dma(3)], far_out=(0, 1, 2), cost=2
     )
     g_post_t, g_mix, g_pre, g_b, g_edge = call(
-        finish_last_kernel, [*finals_in, ets_first, other, w_edge, w_pre], finals + [s(b_pre.shape), s(w_edge.shape)],
+        finish_last_kernel, [*finals_in, ets_first, other0, other1, w_edge, w_pre], finals + [s(b_pre.shape), s(w_edge.shape)],
         like(bufs + [ets, s((layers, blocks, 2, 8, width))]) + [dma(4)],
         far=(0, 1, 2), far_out=(0, 1, 2), free=(3, 4), alias={0: 0, 1: 1, 2: 2},
     )
     g_post = jnp.swapaxes(g_post_t.reshape(wpost_t.shape), 2, 3)
     g_mix, g_pre = g_mix.reshape(w_mix.shape), g_pre.reshape(w_pre.shape)
-    sums = jnp.concatenate([sums0, sums1], axis=0)
     return (
-        readout, node_grad, edge_grad, g_edge, g_pre, g_b, g_post, g_mix, sums[:, width:], sums[:, :width],
+        readout, node_grad, edge_grad, g_edge, g_pre, g_b, g_post, g_mix, g_gain, g_bias,
     )
 
 

time: 139 us -> 128 us (0.921)
  waiting for transfers between devices: 35.4 us -> 15.6 us
  starting transfers between devices: 24.4 us -> 35.3 us
  Pallas kernels: 34.9 us -> 32.5 us
    ppermute x15 -> x28, waiting for transfers between devices: 35.4 us -> 15.6 us  [swap(): lax.ppermute(value, 'dp', [(i, i ^ masks[i & 1]) for i in range(devices)])]
    ppermute x15 -> x28, starting transfers between devices: 24.4 us -> 35.3 us  [swap(): lax.ppermute(value, 'dp', [(i, i ^ masks[i & 1]) for i in range(devices)])]
    pallas_call x9 -> x8, Pallas kernels: 34.9 us -> 32.5 us  [call(): pl.pallas_call(kernel, in_specs=[hbm if i in far else vmem for i in range...]
  transfers between devices with their start and end apart: 15 -> 28, of which waited for: 11 -> 12; matrix products, arithmetic and copies ran while one was open for 1% -> 0% of each run, Pallas kernels for 3% -> 8%
where the time goes in v4:
time: 128 us; the launch traced here: 127 us
  blocking collectives  42.2 us (33%)
  starting transfers between devices  35.3 us (28%)
  Pallas kernels  32.5 us (25%)
  waiting for transfers between devices  15.6 us (12%)
    all_to_all x4, blocking collectives, exchange(): return lax.all_to_all(part, 'dp', 0, 0, tiled=True)  42.2 us
    ppermute x28, starting transfers between devices, swap(): lax.ppermute(value, 'dp', [(i, i ^ masks[i & 1]) for i in range(devices)])  35.3 us
    pallas_call x8, Pallas kernels, call(): pl.pallas_call(kernel, in_specs=[hbm if i in far else vmem for i in range...  32.5 us
    ppermute x28, waiting for transfers between devices, swap(): lax.ppermute(value, 'dp', [(i, i ^ masks[i & 1]) for i in range(devices)])  15.6 us
  transfers between devices with their start and end apart: 28, of which 12 were waited for; matrix products, arithmetic and copies ran while one was open for 0% of the time, Pallas kernels for 8%

profile of v4, /device:TPU:0, one launch (start us, length us, event | category | flops | bytes accessed | tf_op | source)
XLA Modules:
  0.0 127.4 jit_solution(13968434769002602081)
XLA Ops:
  0.7 7.2 %shard_map.213 = (bf16[256,640]{1,0:T(8,128)(2,1)S(1)}, bf16[704,3584]{1,0:T(8,128)(2,1)S(1)}, f32[2,3584]{1,0:T(2,128)S(1)}, f32[8,768]{1,0:T(8,128)S(1)}, bf16...) custom-call(bf16[640,256]{1,0:T(8,128)(2,1)} %nf_hbm.1, ...), custom_call_target="tpu_custom_call" | custom-call | tf_op jit(solution)/shard_map/pallas_call | solution.py:634
  7.9 14.7 %all_to_all.20.recv_ref = f32[32,1,640]{2,1,0:T(1,128)S(1)} all-to-all(f32[32,1,640]{2,1,0:T(1,128)S(1)} %get-tuple-element.67), channel_id=1, replica_groups=mesh['dp'=32] {'dp'}, dimensions={0} | all-to-all | bytes 163840 | tf_op jit(solution)/shard_map/all_to_all | solution.py:655
  22.7 5.4 %shard_map.214 = (f32[8,256]{1,0:T(8,128)S(1)}, f32[256,640]{1,0:T(8,128)S(1)}, bf16[256,640]{1,0:T(8,128)(2,1)S(1)}, f32[256,3584]{1,0:T(8,128)S(1)}, f32[4,256...) custom-call(f32[32,1,640]{2,1,0:T(1,128)S(1)} %all_to_all.20.recv_re, ...), custom_call_target="tpu_custom_call" | custom-call | tf_op jit(solution)/shard_map/pallas_call | solution.py:634
  28.1 9.3 %all_to_all.21.recv_ref = f32[32,1,640]{2,1,0:T(1,128)S(1)} all-to-all(f32[32,1,640]{2,1,0:T(1,128)S(1)} %get-tuple-element.75), channel_id=1, replica_groups=mesh['dp'=32] {'dp'}, dimensions={0} | all-to-all | bytes 163840 | tf_op jit(solution)/shard_map/all_to_all | solution.py:655
  38.6 9.1 %all_to_all.22.recv_ref = f32[32,1,512]{2,1,0:T(1,128)S(1)} all-to-all(f32[32,1,512]{2,1,0:T(1,128)S(1)} %get-tuple-element.78), channel_id=1, replica_groups=mesh['dp'=32] {'dp'}, dimensions={0} | all-to-all | bytes 131072 | tf_op jit(solution)/shard_map/all_to_all | solution.py:655
  47.7 6.3 %shard_map.216 = (f32[1,512]{1,0:T(1,128)S(1)}, bf16[256,3584]{1,0:T(8,128)(2,1)S(1)}, f32[256,640]{1,0:T(8,128)S(1)}, f32[256,640]{1,0:T(8,128)S(1)}, f32[32,1,...) custom-call(f32[32,1,512]{2,1,0:T(1,128)S(1)} %all_to_all.22.recv_ref, ...), custom_call_target="tpu_custom_call" | custom-call | tf_op jit(solution)/shard_map/pallas_call | solution.py:634
  54.2 9.1 %all_to_all.23.recv_ref = f32[32,1,512]{2,1,0:T(1,128)S(1)} all-to-all(f32[32,1,512]{2,1,0:T(1,128)S(1)} %get-tuple-element.88), channel_id=1, replica_groups=mesh['dp'=32] {'dp'}, dimensions={0} | all-to-all | bytes 131072 | tf_op jit(solution)/shard_map/all_to_all | solution.py:655
  63.9 1.6 %collective-permute-start.3 = (f32[32,1664]{1,0:T(8,128)S(1)}, f32[32,1664]{1,0:T(8,128)S(1)}, u32[]{:S(2)}, u32[]{:S(2)}) collective-permute-start(f32[32,1664]{1,0:T(8,128)S(1)} %get-tuple-element.130), channel_id=1, source_target_pairs={{0,6},{1,7},{2,4},{3,5},{4,2},{5,3},{6,0},{7,1},{8,14},{9,15},{10,... | collective-permute-start | bytes 638984 | tf_op jit(solution)/shard_map/ppermute | solution.py:700
  65.5 1.4 %collective-permute-start.2 = (f32[32,1664]{1,0:T(8,128)S(1)}, f32[32,1664]{1,0:T(8,128)S(1)}, u32[]{:S(2)}, u32[]{:S(2)}) collective-permute-start(f32[32,1664]{1,0:T(8,128)S(1)} %get-tuple-element.131), channel_id=1, source_target_pairs={{0,4},{1,5},{2,6},{3,7},{4,0},{5,1},{6,2},{7,3},{8,12},{9,13},{10,... | collective-permute-start | bytes 638984 | tf_op jit(solution)/shard_map/ppermute | solution.py:700
  67.0 6.8 %shard_map.217 = (f32[2,256]{1,0:T(2,128)}, f32[2,256]{1,0:T(2,128)}, bf16[256,3584]{1,0:T(8,128)(2,1)S(1)}, f32[640,256]{1,0:T(8,128)}, f32[128,1664]{1,0:T(8,128)S(1)}, /*index=5*/f32[128,1664]{1,0:T(8,128)S(1)}) custom-call(f32[32,1,512]{2,1,0:T(1,128)S(1)} %all_to_all.23.recv_ref, f32[256,640]{1,0:T(8,128)S(1)} %get-tuple-element.91.dv_ref, ...), custom_call_target="tpu_custom_call" | custom-call | flops 8000000000 | tf_op jit(solution)/shard_map/pallas_call | solution.py:634
  73.8 2.3 %shard_map.218 = (f32[640,256]{1,0:T(8,128)}, f32[4,256]{1,0:T(4,128)}) custom-call(bf16[256,3584]{1,0:T(8,128)(2,1)S(1)} %get-tuple-element.101.dm0_ref, bf16[256,3584]{1,0:T(8,128)(2,1)S(1)} %get-tuple-element.102.dm1_ref, bf16[2,768,256]{2,1,0:T(8,128)(2,1)S(1)} %copy-done, bf16[2,16,256]{2,1,0:T(8,128)(2,1)S(1)} %copy-done.3, ...), custom_call_target="tpu_custom_call" | custom-call | flops 2000000000 | tf_op jit(solution)/shard_map/pallas_call | solution.py:634
  77.6 1.5 %collective-permute-start.19 = (f32[8,1664]{1,0:T(8,128)S(1)}, f32[8,1664]{1,0:T(8,128)S(1)}, u32[]{:S(2)}, u32[]{:S(2)}) collective-permute-start(f32[8,1664]{1,0:T(8,128)S(1)} %get-tuple-element.133), channel_id=1, source_target_pairs={{0,24},{1,25},{2,26},{3,27},{4,28},{5,29},{6,30},{7,31},{8,16},{9,... | collective-permute-start | bytes 159752 | tf_op jit(solution)/shard_map/ppermute | solution.py:700
  79.1 1.4 %collective-permute-start.18 = (f32[8,1664]{1,0:T(8,128)S(1)}, f32[8,1664]{1,0:T(8,128)S(1)}, u32[]{:S(2)}, u32[]{:S(2)}) collective-permute-start(f32[8,1664]{1,0:T(8,128)S(1)} %get-tuple-element.134), channel_id=1, source_target_pairs={{0,16},{1,17},{2,18},{3,19},{4,20},{5,21},{6,22},{7,23},{8,24},{9,... | collective-permute-start | bytes 159752 | tf_op jit(solution)/shard_map/ppermute | solution.py:700
  81.3 2.3 %collective-permute-start.7 = (f32[32,1664]{1,0:T(8,128)S(1)}, f32[32,1664]{1,0:T(8,128)S(1)}, u32[]{:S(2)}, u32[]{:S(2)}) collective-permute-start(f32[32,1664]{1,0:T(8,128)S(1)} %get-tuple-element.127), channel_id=1, source_target_pairs={{0,6},{1,25},{2,4},{3,27},{4,2},{5,29},{6,0},{7,31},{8,14},{9,17},... | collective-permute-start | bytes 638984 | tf_op jit(solution)/shard_map/ppermute | solution.py:700
  84.2 2.1 %collective-permute-done.18 = f32[8,1664]{1,0:T(8,128)S(1)} collective-permute-done((f32[8,1664]{1,0:T(8,128)S(1)}, f32[8,1664]{1,0:T(8,128)S(1)}, u32[]{:S(2)}, u32[]{:S(2)}) %collective-permute-start.18) | collective-permute-done | bytes 53280 | tf_op jit(solution)/shard_map/ppermute | solution.py:700
  86.3 1.3 %collective-permute-start.22 = (f32[8,1664]{1,0:T(8,128)S(1)}, f32[8,1664]{1,0:T(8,128)S(1)}, u32[]{:S(2)}, u32[]{:S(2)}) collective-permute-start(f32[8,1664]{1,0:T(8,128)S(1)} %add_add_fusion), channel_id=1, source_target_pairs={{0,24},{1,25},{2,26},{3,27},{4,28},{5,29},{6,30},{7,31},{8,16},{9,... | collective-permute-start | bytes 159752 | tf_op jit(solution)/shard_map/ppermute | solution.py:700
  87.6 3.1 %collective-permute-start.20 = (f32[8,1664]{1,0:T(8,128)S(1)}, f32[8,1664]{1,0:T(8,128)S(1)}, u32[]{:S(2)}, u32[]{:S(2)}) collective-permute-start(f32[8,1664]{1,0:T(8,128)S(1)} %add_add_fusion), channel_id=1, source_target_pairs={{0,8},{1,9},{2,10},{3,11},{4,12},{5,13},{6,14},{7,15},{8,0},{9,1},... | collective-permute-start | bytes 159752 | tf_op jit(solution)/shard_map/ppermute | solution.py:700
  92.9 1.4 %collective-permute-start.10 = (f32[8,1664]{1,0:T(8,128)S(1)}, f32[8,1664]{1,0:T(8,128)S(1)}, u32[]{:S(2)}, u32[]{:S(2)}) collective-permute-start(f32[8,1664]{1,0:T(8,128)S(1)} %get-tuple-element.136), channel_id=1, source_target_pairs={{0,24},{1,7},{2,26},{3,5},{4,28},{5,3},{6,30},{7,1},{8,16},{9,15},... | collective-permute-start | bytes 159752 | tf_op jit(solution)/shard_map/ppermute | solution.py:700
  94.3 1.6 %collective-permute-start.9 = (f32[8,1664]{1,0:T(8,128)S(1)}, f32[8,1664]{1,0:T(8,128)S(1)}, u32[]{:S(2)}, u32[]{:S(2)}) collective-permute-start(f32[8,1664]{1,0:T(8,128)S(1)} %get-tuple-element.137), channel_id=1, source_target_pairs={{0,16},{1,5},{2,18},{3,7},{4,20},{5,1},{6,22},{7,3},{8,24},{9,13},... | collective-permute-start | bytes 159752 | tf_op jit(solution)/shard_map/ppermute | solution.py:700
  96.1 1.4 %collective-permute-start.24 = (f32[32,1664]{1,0:T(8,128)S(1)}, f32[32,1664]{1,0:T(8,128)S(1)}, u32[]{:S(2)}, u32[]{:S(2)}) collective-permute-start(f32[32,1664]{1,0:T(8,128)S(1)} %pad_maximum_fusion.1), channel_id=1, source_target_pairs={{0,4},{1,5},{2,6},{3,7},{4,0},{5,1},{6,2},{7,3},{8,12},{9,13},{10,... | collective-permute-start | bytes 638984 | tf_op jit(solution)/shard_map/ppermute | solution.py:700
  98.9 1.8 %collective-permute-done.9 = f32[8,1664]{1,0:T(8,128)S(1)} collective-permute-done((f32[8,1664]{1,0:T(8,128)S(1)}, f32[8,1664]{1,0:T(8,128)S(1)}, u32[]{:S(2)}, u32[]{:S(2)}) %collective-permute-start.9) | collective-permute-done | bytes 53280 | tf_op jit(solution)/shard_map/ppermute | solution.py:700
  100.7 2.3 %collective-permute-start.13 = (f32[8,1664]{1,0:T(8,128)S(1)}, f32[8,1664]{1,0:T(8,128)S(1)}, u32[]{:S(2)}, u32[]{:S(2)}) collective-permute-start(f32[8,1664]{1,0:T(8,128)S(1)} %get-tuple-element.125), channel_id=1, source_target_pairs={{0,24},{1,7},{2,26},{3,5},{4,28},{5,3},{6,30},{7,1},{8,16},{9,15},... | collective-permute-start | bytes 159752 | tf_op jit(solution)/shard_map/ppermute | solution.py:700
  103.1 2.1 %collective-permute-start.11 = (f32[8,1664]{1,0:T(8,128)S(1)}, f32[8,1664]{1,0:T(8,128)S(1)}, u32[]{:S(2)}, u32[]{:S(2)}) collective-permute-start(f32[8,1664]{1,0:T(8,128)S(1)} %get-tuple-element.125), channel_id=1, source_target_pairs={{0,8},{1,3},{2,10},{3,1},{4,12},{5,7},{6,14},{7,5},{8,0},{9,11},{1... | collective-permute-start | bytes 159752 | tf_op jit(solution)/shard_map/ppermute | solution.py:700
  105.2 1.5 %collective-permute-done.13 = f32[8,1664]{1,0:T(8,128)S(1)} collective-permute-done((f32[8,1664]{1,0:T(8,128)S(1)}, f32[8,1664]{1,0:T(8,128)S(1)}, u32[]{:S(2)}, u32[]{:S(2)}) %collective-permute-start.13) | collective-permute-done | bytes 53280 | tf_op jit(solution)/shard_map/ppermute | solution.py:700
  106.7 1.4 %collective-permute-done.12 = f32[8,1664]{1,0:T(8,128)S(1)} collective-permute-done((f32[8,1664]{1,0:T(8,128)S(1)}, f32[8,1664]{1,0:T(8,128)S(1)}, u32[]{:S(2)}, u32[]{:S(2)}) %collective-permute-start.12) | collective-permute-done | bytes 53280 | tf_op jit(solution)/shard_map/ppermute | solution.py:700
  108.1 1.2 collective-permute-start.16
  110.4 1.3 collective-permute-start.14
  112.9 4.0 %collective-permute-done.14 = f32[32,1664]{1,0:T(8,128)S(1)} collective-permute-done((f32[32,1664]{1,0:T(8,128)S(1)}, f32[32,1664]{1,0:T(8,128)S(1)}, u32[]{:S(2)}, u32[]{:S(2)}) %collective-permute-start.14) | collective-permute-done | bytes 213024 | tf_op jit(solution)/shard_map/ppermute | solution.py:700
  117.3 4.7 %collective-permute-start.26 = (f32[128,1664]{1,0:T(8,128)S(1)}, f32[128,1664]{1,0:T(8,128)S(1)}, u32[]{:S(2)}, u32[]{:S(2)}) collective-permute-start(f32[128,1664]{1,0:T(8,128)S(1)} %constant_dynamic-update-slice_fusion.half0_ref), channel_id=1, source_target_pairs={{0,1},{1,0},{2,3},{3,2},{4,5},{5,4},{6,7},{7,6},{8,9},{9,8},{10,11... | collective-permute-start | bytes 2555912 | tf_op jit(solution)/shard_map/ppermute | solution.py:700
  122.0 1.3 %shard_map.219 = (f32[2,16,2,8,832]{4,3,2,1,0:T(8,128)}, f32[2,16,2,8,256]{4,3,2,1,0:T(8,128)}, f32[2,3,16,2,8,256]{5,4,3,2,1,0:T(8,128)}, f32[2,16,8,64]{3,2,1,0:T(8,128)S(1)}) custom-call(f32[128,1664]{1,0:T(8,128)S(1)} %constant_dynamic-update-slice_fusion.half0_ref, f32[128,1664]{1,0:T(8,128)S(1)} %constant_dynamic-update-slice_fusion.7.half1_ref), custom_call_target="tpu_custom_call" | custom-call | flops 2000000000 | tf_op jit(solution)/shard_map/pallas_call | solution.py:634
  123.9 1.2 collective-permute-done.27.half1_ref
  125.1 2.1 %shard_map.220 = (f32[2,16,2,8,832]{4,3,2,1,0:T(8,128)}, f32[2,16,2,8,256]{4,3,2,1,0:T(8,128)}, f32[2,3,16,2,8,256]{5,4,3,2,1,0:T(8,128)}, f32[2,256]{1,0:T(2,128)}, f32[2,16,256]{2,1,0:T(8,128)}) custom-call(f32[2,16,2,8,832]{4,3,2,1,0:T(8,128)} %get-tuple-element.113.post_in, ...), custom_call_target="tpu_custom_call", output_to_operand_aliasing={{0}: (0, {}), {1}: (1, {}), {2}: (2, {})} | custom-call | tf_op jit(solution)/shard_map/pallas_call | solution.py:634
  (74 shorter events, 12.1 us)
Async XLA Ops:
  0.6 22.0 %copy-start = (bf16[2,768,256]{2,1,0:T(8,128)(2,1)S(1)}, bf16[2,768,256]{2,1,0:T(8,128)(2,1)}, u32[]{:S(2)}) copy-start(bf16[2,768,256]{2,1,0:T(8,128)(2,1)} %wpre_ref.9) | copy-start | bytes 2359300
  0.7 22.0 %copy-start.2 = (bf16[2,256,256]{2,1,0:T(8,128)(2,1)S(1)}, bf16[2,256,256]{2,1,0:T(8,128)(2,1)}, u32[]{:S(2)}) copy-start(bf16[2,256,256]{2,1,0:T(8,128)(2,1)} %wmix_ref.5) | copy-start | bytes 786436
  0.7 22.0 %copy-start.3 = (bf16[2,16,256]{2,1,0:T(8,128)(2,1)S(1)}, bf16[2,16,256]{2,1,0:T(8,128)(2,1)}, u32[]{:S(2)}) copy-start(bf16[2,16,256]{2,1,0:T(8,128)(2,1)} %wedge_ref.5) | copy-start | bytes 49156
  0.7 22.0 %copy-start.6 = (f32[2,256]{1,0:T(2,128)S(1)}, f32[2,256]{1,0:T(2,128)}, u32[]{:S(2)}) copy-start(f32[2,256]{1,0:T(2,128)} %bpre_ref.1) | copy-start | bytes 6148
  54.0 9.3 %collective-permute-start = (f32[128,1664]{1,0:T(8,128)S(1)}, f32[128,1664]{1,0:T(8,128)S(1)}, u32[]{:S(2)}, u32[]{:S(2)}) collective-permute-start(f32[128,1664]{1,0:T(8,128)S(1)} %get-tuple-element.89), channel_id=1, source_target_pairs={{0,1},{1,0},{2,3},{3,2},{4,5},{5,4},{6,7},{7,6},{8,9},{9,8},{10,11... | collective-permute-start | bytes 2555912 | tf_op jit(solution)/shard_map/ppermute | solution.py:700
  63.4 12.7 %collective-permute-start.1 = (f32[32,1664]{1,0:T(8,128)S(1)}, f32[32,1664]{1,0:T(8,128)S(1)}, u32[]{:S(2)}, u32[]{:S(2)}) collective-permute-start(f32[32,1664]{1,0:T(8,128)S(1)} %get-tuple-element.129), channel_id=1, source_target_pairs={{0,2},{1,3},{2,0},{3,1},{4,6},{5,7},{6,4},{7,5},{8,10},{9,11},{10,... | collective-permute-start | bytes 638984 | tf_op jit(solution)/shard_map/ppermute | solution.py:700
  63.9 12.2 %collective-permute-start.3 = (f32[32,1664]{1,0:T(8,128)S(1)}, f32[32,1664]{1,0:T(8,128)S(1)}, u32[]{:S(2)}, u32[]{:S(2)}) collective-permute-start(f32[32,1664]{1,0:T(8,128)S(1)} %get-tuple-element.130), channel_id=1, source_target_pairs={{0,6},{1,7},{2,4},{3,5},{4,2},{5,3},{6,0},{7,1},{8,14},{9,15},{10,... | collective-permute-start | bytes 638984 | tf_op jit(solution)/shard_map/ppermute | solution.py:700
  65.5 11.2 %collective-permute-start.2 = (f32[32,1664]{1,0:T(8,128)S(1)}, f32[32,1664]{1,0:T(8,128)S(1)}, u32[]{:S(2)}, u32[]{:S(2)}) collective-permute-start(f32[32,1664]{1,0:T(8,128)S(1)} %get-tuple-element.131), channel_id=1, source_target_pairs={{0,4},{1,5},{2,6},{3,7},{4,0},{5,1},{6,2},{7,3},{8,12},{9,13},{10,... | collective-permute-start | bytes 638984 | tf_op jit(solution)/shard_map/ppermute | solution.py:700
  76.8 3.7 %collective-permute-start.4 = (f32[128,1664]{1,0:T(8,128)S(1)}, f32[128,1664]{1,0:T(8,128)S(1)}, u32[]{:S(2)}, u32[]{:S(2)}) collective-permute-start(f32[128,1664]{1,0:T(8,128)S(1)} %get-tuple-element.110), channel_id=1, source_target_pairs={{0,1},{1,0},{2,3},{3,2},{4,5},{5,4},{6,7},{7,6},{8,9},{9,8},{10,11... | collective-permute-start | bytes 2555912 | tf_op jit(solution)/shard_map/ppermute | solution.py:700
  76.9 6.7 %collective-permute-start.17 = (f32[8,1664]{1,0:T(8,128)S(1)}, f32[8,1664]{1,0:T(8,128)S(1)}, u32[]{:S(2)}, u32[]{:S(2)}) collective-permute-start(f32[8,1664]{1,0:T(8,128)S(1)} %get-tuple-element.132), channel_id=1, source_target_pairs={{0,8},{1,9},{2,10},{3,11},{4,12},{5,13},{6,14},{7,15},{8,0},{9,1},... | collective-permute-start | bytes 159752 | tf_op jit(solution)/shard_map/ppermute | solution.py:700
  77.6 6.6 %collective-permute-start.19 = (f32[8,1664]{1,0:T(8,128)S(1)}, f32[8,1664]{1,0:T(8,128)S(1)}, u32[]{:S(2)}, u32[]{:S(2)}) collective-permute-start(f32[8,1664]{1,0:T(8,128)S(1)} %get-tuple-element.133), channel_id=1, source_target_pairs={{0,24},{1,25},{2,26},{3,27},{4,28},{5,29},{6,30},{7,31},{8,16},{9,... | collective-permute-start | bytes 159752 | tf_op jit(solution)/shard_map/ppermute | solution.py:700
  79.1 7.1 %collective-permute-start.18 = (f32[8,1664]{1,0:T(8,128)S(1)}, f32[8,1664]{1,0:T(8,128)S(1)}, u32[]{:S(2)}, u32[]{:S(2)}) collective-permute-start(f32[8,1664]{1,0:T(8,128)S(1)} %get-tuple-element.134), channel_id=1, source_target_pairs={{0,16},{1,17},{2,18},{3,19},{4,20},{5,21},{6,22},{7,23},{8,24},{9,... | collective-permute-start | bytes 159752 | tf_op jit(solution)/shard_map/ppermute | solution.py:700
  80.6 7.0 %collective-permute-start.5 = (f32[32,1664]{1,0:T(8,128)S(1)}, f32[32,1664]{1,0:T(8,128)S(1)}, u32[]{:S(2)}, u32[]{:S(2)}) collective-permute-start(f32[32,1664]{1,0:T(8,128)S(1)} %get-tuple-element.126), channel_id=1, source_target_pairs={{0,2},{1,9},{2,0},{3,11},{4,6},{5,13},{6,4},{7,15},{8,10},{9,1},{1... | collective-permute-start | bytes 638984 | tf_op jit(solution)/shard_map/ppermute | solution.py:700
  81.3 9.4 %collective-permute-start.7 = (f32[32,1664]{1,0:T(8,128)S(1)}, f32[32,1664]{1,0:T(8,128)S(1)}, u32[]{:S(2)}, u32[]{:S(2)}) collective-permute-start(f32[32,1664]{1,0:T(8,128)S(1)} %get-tuple-element.127), channel_id=1, source_target_pairs={{0,6},{1,25},{2,4},{3,27},{4,2},{5,29},{6,0},{7,31},{8,14},{9,17},... | collective-permute-start | bytes 638984 | tf_op jit(solution)/shard_map/ppermute | solution.py:700
  83.6 8.1 %collective-permute-start.6 = (f32[32,1664]{1,0:T(8,128)S(1)}, f32[32,1664]{1,0:T(8,128)S(1)}, u32[]{:S(2)}, u32[]{:S(2)}) collective-permute-start(f32[32,1664]{1,0:T(8,128)S(1)} %get-tuple-element.128), channel_id=1, source_target_pairs={{0,4},{1,17},{2,6},{3,19},{4,0},{5,21},{6,2},{7,23},{8,12},{9,25},... | collective-permute-start | bytes 638984 | tf_op jit(solution)/shard_map/ppermute | solution.py:700
  86.3 8.1 %collective-permute-start.22 = (f32[8,1664]{1,0:T(8,128)S(1)}, f32[8,1664]{1,0:T(8,128)S(1)}, u32[]{:S(2)}, u32[]{:S(2)}) collective-permute-start(f32[8,1664]{1,0:T(8,128)S(1)} %add_add_fusion), channel_id=1, source_target_pairs={{0,24},{1,25},{2,26},{3,27},{4,28},{5,29},{6,30},{7,31},{8,16},{9,... | collective-permute-start | bytes 159752 | tf_op jit(solution)/shard_map/ppermute | solution.py:700
  87.6 8.5 %collective-permute-start.21 = (f32[8,1664]{1,0:T(8,128)S(1)}, f32[8,1664]{1,0:T(8,128)S(1)}, u32[]{:S(2)}, u32[]{:S(2)}) collective-permute-start(f32[8,1664]{1,0:T(8,128)S(1)} %add_add_fusion), channel_id=1, source_target_pairs={{0,16},{1,17},{2,18},{3,19},{4,20},{5,21},{6,22},{7,23},{8,24},{9,... | collective-permute-start | bytes 159752 | tf_op jit(solution)/shard_map/ppermute | solution.py:700
  87.6 8.5 %collective-permute-start.20 = (f32[8,1664]{1,0:T(8,128)S(1)}, f32[8,1664]{1,0:T(8,128)S(1)}, u32[]{:S(2)}, u32[]{:S(2)}) collective-permute-start(f32[8,1664]{1,0:T(8,128)S(1)} %add_add_fusion), channel_id=1, source_target_pairs={{0,8},{1,9},{2,10},{3,11},{4,12},{5,13},{6,14},{7,15},{8,0},{9,1},... | collective-permute-start | bytes 159752 | tf_op jit(solution)/shard_map/ppermute | solution.py:700
  91.9 6.3 %collective-permute-start.8 = (f32[8,1664]{1,0:T(8,128)S(1)}, f32[8,1664]{1,0:T(8,128)S(1)}, u32[]{:S(2)}, u32[]{:S(2)}) collective-permute-start(f32[8,1664]{1,0:T(8,128)S(1)} %get-tuple-element.135), channel_id=1, source_target_pairs={{0,8},{1,3},{2,10},{3,1},{4,12},{5,7},{6,14},{7,5},{8,0},{9,11},{1... | collective-permute-start | bytes 159752 | tf_op jit(solution)/shard_map/ppermute | solution.py:700
  92.9 6.0 %collective-permute-start.10 = (f32[8,1664]{1,0:T(8,128)S(1)}, f32[8,1664]{1,0:T(8,128)S(1)}, u32[]{:S(2)}, u32[]{:S(2)}) collective-permute-start(f32[8,1664]{1,0:T(8,128)S(1)} %get-tuple-element.136), channel_id=1, source_target_pairs={{0,24},{1,7},{2,26},{3,5},{4,28},{5,3},{6,30},{7,1},{8,16},{9,15},... | collective-permute-start | bytes 159752 | tf_op jit(solution)/shard_map/ppermute | solution.py:700
  94.3 6.4 %collective-permute-start.9 = (f32[8,1664]{1,0:T(8,128)S(1)}, f32[8,1664]{1,0:T(8,128)S(1)}, u32[]{:S(2)}, u32[]{:S(2)}) collective-permute-start(f32[8,1664]{1,0:T(8,128)S(1)} %get-tuple-element.137), channel_id=1, source_target_pairs={{0,16},{1,5},{2,18},{3,7},{4,20},{5,1},{6,22},{7,3},{8,24},{9,13},... | collective-permute-start | bytes 159752 | tf_op jit(solution)/shard_map/ppermute | solution.py:700
  96.1 16.7 %collective-permute-start.24 = (f32[32,1664]{1,0:T(8,128)S(1)}, f32[32,1664]{1,0:T(8,128)S(1)}, u32[]{:S(2)}, u32[]{:S(2)}) collective-permute-start(f32[32,1664]{1,0:T(8,128)S(1)} %pad_maximum_fusion.1), channel_id=1, source_target_pairs={{0,4},{1,5},{2,6},{3,7},{4,0},{5,1},{6,2},{7,3},{8,12},{9,13},{10,... | collective-permute-start | bytes 638984 | tf_op jit(solution)/shard_map/ppermute | solution.py:700
  97.5 14.2 %collective-permute-start.23 = (f32[32,1664]{1,0:T(8,128)S(1)}, f32[32,1664]{1,0:T(8,128)S(1)}, u32[]{:S(2)}, u32[]{:S(2)}) collective-permute-start(f32[32,1664]{1,0:T(8,128)S(1)} %pad_maximum_fusion.1), channel_id=1, source_target_pairs={{0,2},{1,3},{2,0},{3,1},{4,6},{5,7},{6,4},{7,5},{8,10},{9,11},{10,... | collective-permute-start | bytes 638984 | tf_op jit(solution)/shard_map/ppermute | solution.py:700
  100.7 6.0 %collective-permute-start.13 = (f32[8,1664]{1,0:T(8,128)S(1)}, f32[8,1664]{1,0:T(8,128)S(1)}, u32[]{:S(2)}, u32[]{:S(2)}) collective-permute-start(f32[8,1664]{1,0:T(8,128)S(1)} %get-tuple-element.125), channel_id=1, source_target_pairs={{0,24},{1,7},{2,26},{3,5},{4,28},{5,3},{6,30},{7,1},{8,16},{9,15},... | collective-permute-start | bytes 159752 | tf_op jit(solution)/shard_map/ppermute | solution.py:700
  103.0 5.0 %collective-permute-start.12 = (f32[8,1664]{1,0:T(8,128)S(1)}, f32[8,1664]{1,0:T(8,128)S(1)}, u32[]{:S(2)}, u32[]{:S(2)}) collective-permute-start(f32[8,1664]{1,0:T(8,128)S(1)} %get-tuple-element.125), channel_id=1, source_target_pairs={{0,16},{1,5},{2,18},{3,7},{4,20},{5,1},{6,22},{7,3},{8,24},{9,13},... | collective-permute-start | bytes 159752 | tf_op jit(solution)/shard_map/ppermute | solution.py:700
  103.1 5.0 %collective-permute-start.11 = (f32[8,1664]{1,0:T(8,128)S(1)}, f32[8,1664]{1,0:T(8,128)S(1)}, u32[]{:S(2)}, u32[]{:S(2)}) collective-permute-start(f32[8,1664]{1,0:T(8,128)S(1)} %get-tuple-element.125), channel_id=1, source_target_pairs={{0,8},{1,3},{2,10},{3,1},{4,12},{5,7},{6,14},{7,5},{8,0},{9,11},{1... | collective-permute-start | bytes 159752 | tf_op jit(solution)/shard_map/ppermute | solution.py:700
  108.1 9.1 %collective-permute-start.16 = (f32[32,1664]{1,0:T(8,128)S(1)}, f32[32,1664]{1,0:T(8,128)S(1)}, u32[]{:S(2)}, u32[]{:S(2)}) collective-permute-start(f32[32,1664]{1,0:T(8,128)S(1)} %pad_maximum_fusion), channel_id=1, source_target_pairs={{0,6},{1,25},{2,4},{3,27},{4,2},{5,29},{6,0},{7,31},{8,14},{9,17},... | collective-permute-start | bytes 638984 | tf_op jit(solution)/shard_map/ppermute | solution.py:700
  109.3 7.9 %collective-permute-start.15 = (f32[32,1664]{1,0:T(8,128)S(1)}, f32[32,1664]{1,0:T(8,128)S(1)}, u32[]{:S(2)}, u32[]{:S(2)}) collective-permute-start(f32[32,1664]{1,0:T(8,128)S(1)} %pad_maximum_fusion), channel_id=1, source_target_pairs={{0,4},{1,17},{2,6},{3,19},{4,0},{5,21},{6,2},{7,23},{8,12},{9,25},... | collective-permute-start | bytes 638984 | tf_op jit(solution)/shard_map/ppermute | solution.py:700
  110.4 6.4 %collective-permute-start.14 = (f32[32,1664]{1,0:T(8,128)S(1)}, f32[32,1664]{1,0:T(8,128)S(1)}, u32[]{:S(2)}, u32[]{:S(2)}) collective-permute-start(f32[32,1664]{1,0:T(8,128)S(1)} %pad_maximum_fusion), channel_id=1, source_target_pairs={{0,2},{1,9},{2,0},{3,11},{4,6},{5,13},{6,4},{7,15},{8,10},{9,1},{1... | collective-permute-start | bytes 638984 | tf_op jit(solution)/shard_map/ppermute | solution.py:700
  111.7 10.2 %collective-permute-start.25 = (f32[32,1664]{1,0:T(8,128)S(1)}, f32[32,1664]{1,0:T(8,128)S(1)}, u32[]{:S(2)}, u32[]{:S(2)}) collective-permute-start(f32[32,1664]{1,0:T(8,128)S(1)} %collective-permute-done.23), channel_id=1, source_target_pairs={{0,4},{1,5},{2,6},{3,7},{4,0},{5,1},{6,2},{7,3},{8,12},{9,13},{10,... | collective-permute-start | bytes 638984 | tf_op jit(solution)/shard_map/ppermute | solution.py:700
  117.3 6.7 %collective-permute-start.26 = (f32[128,1664]{1,0:T(8,128)S(1)}, f32[128,1664]{1,0:T(8,128)S(1)}, u32[]{:S(2)}, u32[]{:S(2)}) collective-permute-start(f32[128,1664]{1,0:T(8,128)S(1)} %constant_dynamic-update-slice_fusion.half0_ref), channel_id=1, source_target_pairs={{0,1},{1,0},{2,3},{3,2},{4,5},{5,4},{6,7},{7,6},{8,9},{9,8},{10,11... | collective-permute-start | bytes 2555912 | tf_op jit(solution)/shard_map/ppermute | solution.py:700
  121.9 3.2 %collective-permute-start.27 = (f32[128,1664]{1,0:T(8,128)S(1)}, f32[128,1664]{1,0:T(8,128)S(1)}, u32[]{:S(2)}, u32[]{:S(2)}) collective-permute-start(f32[128,1664]{1,0:T(8,128)S(1)} %constant_dynamic-update-slice_fusion.7.half1_ref), channel_id=1, source_target_pairs={{0,1},{1,0},{2,3},{3,2},{4,5},{5,4},{6,7},{7,6},{8,9},{9,8},{10,11... | collective-permute-start | bytes 2555912 | tf_op jit(solution)/shard_map/ppermute | solution.py:700
  (4 other events, 80.6 us)

commit v5 on v4

--- a/solution.py
+++ b/solution.py
@@ -17,6 +17,10 @@
 LOG2E = 1.4426950408889634
 LN2 = 0.6931471805599453
 ROW_CHUNK = 64
+PLANE, LINE = 0, 1
+MASKS = ((2, 4, 6), (8, 16, 24))
+SUM_KINDS = ((PLANE, LINE), (PLANE, LINE))
+GATHER_KINDS = ((PLANE, LINE), (PLANE, PLANE))
 F32 = jnp.float32
 BF16 = jnp.bfloat16
 NN = (((1,), (0,)), ((), ()))
@@ -134,17 +138,19 @@
             rows_ref[i : i + 1, nodes : nodes + 128] = hub
 
     ef_t = ef_ref[...].T
+    nbr16 = nbr.astype(jnp.int16)
     ef_h = mm(ef_t, g).astype(BF16)
     hub_iota = iota((nodes, 128), 0)
     for first_node, end_node in lane_groups(nodes):
         span = slice(first_node, end_node)
         size = end_node - first_node
-        node_iota = iota((nodes, size), 0)
+        node_iota = iota((nodes, size), 0).astype(jnp.int16)
+        one16, none16 = jnp.ones((nodes, size), BF16), jnp.zeros((nodes, size), BF16)
         zero16 = jnp.zeros((16, size), BF16)
         for k in range(LEAF_SLOTS):
             lo = leaf_col(nodes, k, first_node)
             cols = slice(lo, lo + size)
-            b_ref[0:nodes, cols] = (node_iota == nbr[k : k + 1, span]).astype(F32).astype(BF16)
+            b_ref[0:nodes, cols] = jnp.where(node_iota == nbr16[k : k + 1, span], one16, none16)
             piece = ef_t[16 * k : 16 * k + 16, span]
             for r, part in enumerate((piece, zero16, piece, zero16)):
                 b_ref[nodes + 16 * r : nodes + 16 * r + 16, cols] = part
@@ -366,7 +372,7 @@
 def backward_layer(
     layer, recv_ref, dv_ref, dh_ref, u_ref, norm_ref, gain_ref, bias_ref, wmix_ref, wpost_ref, wpre_ref,
     b_ref, live_ref, rows_ref, g_ref, gt_ref, m_ref, s_ref,
-    gb_ref, du_ref, d_ref, dm_ref, dcat_ref, et_ref, ds_ref, acc_ref, bd_ref, beside=(),
+    gb_ref, du_ref, d_ref, dm_ref, dcat_ref, et_ref, ds_ref, bd_ref, beside=(),
 ):
     width, nodes = dv_ref.shape
     leaf_cols = LEAF_SLOTS * nodes
@@ -403,6 +409,12 @@
             ds_ref[n, rows, nodes:] = fold(block[:, nodes:], jnp.add)
         bd_ref[64 * t : 64 * t + 64, 64 * t : 64 * t + 64] = wpost_ref[layer, t][:, 0:64]
 
+    acc = ds_ref[0] + ds_ref[1] + ds_ref[2]
+    down = acc[:, 0:nodes] + mm(acc[:, nodes:].astype(BF16), gt_ref[...])
+    dcat_ref[0:width] = down.astype(BF16)
+    once = jnp.where(iota((1, nodes + 128), 1) < nodes + 64, acc, 0.0)
+    bias = jnp.sum(once, axis=1, keepdims=True)
+
     def spread_back(i, tiles):
         rows = pl.ds(i * ROW_CHUNK, ROW_CHUNK)
         for c in tiles:
@@ -415,18 +427,15 @@
             c0 = dmean * inv - mean * c1
             if hub:
                 cols = [leaf_cols + 128 * j for j in range(8)]
-                acc = None
             else:
                 zero, *cols = [leaf_col(nodes, k, 128 * c) for k in range(LEAF_SLOTS)]
-                acc = c0 + dsmax * jnp.exp2(-smax) + dsmin * jnp.exp2(smin)
-                dm_ref[rows, zero : zero + 128] = acc.astype(BF16)
+                d = c0 + dsmax * jnp.exp2(-smax) + dsmin * jnp.exp2(smin)
+                dm_ref[rows, zero : zero + 128] = d.astype(BF16)
             for lo in cols:
                 m = m_ref[rows, lo : lo + 128]
                 d = c0 + m * c1 + dsmax * jnp.exp2(m - smax) + dsmin * jnp.exp2(smin - m)
                 d = d * live_ref[1:2, lo : lo + 128]
-                acc = d if acc is None else acc + d
                 dm_ref[rows, lo : lo + 128] = d.astype(BF16)
-            acc_ref[rows, lanes] = fold(acc, jnp.add) if hub else acc
 
     def land(lo, hi):
         return mm(dm_ref[:, lo:hi], b_ref[0 : nodes + 32, lo:hi], NT)
@@ -445,11 +454,7 @@
             landed = landed + land(*waiting[0:2])
         waiting = group
 
-    down = acc_ref[:, 0:nodes] + mm(acc_ref[:, nodes:].astype(BF16), gt_ref[...])
-    dcat_ref[0:width] = down.astype(BF16)
     dcat_ref[width : 2 * width] = landed[:, 0:nodes].astype(BF16)
-    once = jnp.where(iota((1, nodes + 128), 1) < nodes + 64, acc_ref[...], 0.0)
-    bias = jnp.sum(once, axis=1, keepdims=True)
     factor = landed[:, nodes : nodes + 16] + landed[:, nodes + 16 : nodes + 32]
     et_ref[...] = jnp.concatenate([factor, jnp.broadcast_to(bias, (width, 48))], axis=1)
     weights = jnp.concatenate([wpre_ref[layer, 0:width], wpre_ref[layer, width : 2 * width]], axis=1)
@@ -458,10 +463,19 @@
     return dh_ref[...] + dh
 
 
-def piece_owner(core, half, place, mixed):
+def piece_owner(core, half, place, kind):
     plane_first = ((place >> 2) << 1) | ((place & 3) << 3)
     line_first = ((place >> 2) << 3) | ((place & 3) << 1)
-    return half + (jnp.where(core == half, plane_first, line_first) if mixed else plane_first)
+    choice = [plane_first if k == PLANE else line_first for k in kind]
+    return half + jnp.where(core == half, *choice)
+
+
+def larger(kind):
+    return list(zip(*[MASKS[k] for k in kind]))
+
+
+def smaller(kind):
+    return list(zip(*[MASKS[1 - k] for k in kind]))
 
 
 def put_tower_grad(t, d_ref, z_ref, grads_ref):
@@ -478,14 +492,14 @@
     grads_ref[:, 896:1152] = mm(y_ref[...], du_ref[...], NT)
 
 
-def put_message_grads(mixed, x_ref, dcat_ref, et_ref, grads_ref, keep_ref, send_ref):
+def put_message_grads(layer, x_ref, dcat_ref, et_ref, grads_ref, keep_ref, send_ref):
     width = x_ref.shape[0]
     grads_ref[:, 832:896] = et_ref[...]
     grads_ref[:, 1152:1664] = mm(x_ref[...], dcat_ref[0 : 2 * width], NT)
     me = lax.axis_index("dp") & 31
     for place in range(16):
         for half, ref in ((0, keep_ref), (1, send_ref)):
-            row = pl.multiple_of((me ^ piece_owner(me & 1, half, place, mixed)) * 8, 8)
+            row = pl.multiple_of((me ^ piece_owner(me & 1, half, place, SUM_KINDS[layer])) * 8, 8)
             ref[8 * place : 8 * place + 8] = grads_ref[pl.ds(row, 8)]
 
 
@@ -498,15 +512,15 @@
     layer, recv_ref, dv_ref, dh_ref, u_ref, norm_ref, gain_ref, bias_ref, wmix_ref, wpost_ref, wpre_ref,
     b_ref, live_ref, rows_ref, g_ref, gt_ref, m_ref, s_ref, z_ref, y_ref, x_ref, u_low_ref, norm_low_ref,
     gb_ref, dm_ref, dh_out_ref, dv_out_ref, part_ref, keep_ref, send_ref,
-    du_ref, d_ref, dcat_ref, et_ref, ds_ref, acc_ref, bd_ref, grads_ref,
+    du_ref, d_ref, dcat_ref, et_ref, ds_ref, bd_ref, grads_ref,
 ):
     dh = backward_layer(
         layer, recv_ref, dv_ref, dh_ref, u_ref, norm_ref, gain_ref, bias_ref, wmix_ref, wpost_ref, wpre_ref,
         b_ref, live_ref, rows_ref, g_ref, gt_ref, m_ref, s_ref,
-        gb_ref, du_ref, d_ref, dm_ref, dcat_ref, et_ref, ds_ref, acc_ref, bd_ref,
+        gb_ref, du_ref, d_ref, dm_ref, dcat_ref, et_ref, ds_ref, bd_ref,
         grad_steps(d_ref, z_ref, y_ref, du_ref, grads_ref),
     )
-    put_message_grads(False, x_ref, dcat_ref, et_ref, grads_ref, keep_ref, send_ref)
+    put_message_grads(layer, x_ref, dcat_ref, et_ref, grads_ref, keep_ref, send_ref)
     dh_out_ref[...] = dh
     xh, v = normed(u_low_ref[...], norm_low_ref, gain_ref, bias_ref, layer - 1)
     gate_grad(dh, xh, v, dv_out_ref, part_ref)
@@ -515,24 +529,23 @@
 def backward_last_kernel(
     layer, recv_ref, dv_ref, dh_ref, u_ref, norm_ref, gain_ref, bias_ref, wmix_ref, wpost_ref, wpre_ref,
     b_ref, live_ref, rows_ref, g_ref, gt_ref, m_ref, s_ref, z_ref, y_ref, x_ref,
-    sums1_ref, g_gain_ref, g_bias_ref, dm_ref, node_ref, keep_ref, send_ref,
-    gb_ref, du_ref, d_ref, dcat_ref, et_ref, ds_ref, acc_ref, bd_ref, grads_ref,
+    gb_ref, dm_ref, dh_out_ref, keep_ref, send_ref,
+    du_ref, d_ref, dcat_ref, et_ref, ds_ref, bd_ref, grads_ref,
 ):
     dh = backward_layer(
         layer, recv_ref, dv_ref, dh_ref, u_ref, norm_ref, gain_ref, bias_ref, wmix_ref, wpost_ref, wpre_ref,
         b_ref, live_ref, rows_ref, g_ref, gt_ref, m_ref, s_ref,
-        gb_ref, du_ref, d_ref, dm_ref, dcat_ref, et_ref, ds_ref, acc_ref, bd_ref,
+        gb_ref, du_ref, d_ref, dm_ref, dcat_ref, et_ref, ds_ref, bd_ref,
         grad_steps(d_ref, z_ref, y_ref, du_ref, grads_ref),
     )
-    put_message_grads(True, x_ref, dcat_ref, et_ref, grads_ref, keep_ref, send_ref)
-    node_ref[...] = dh.T
-    width = node_ref.shape[1]
-    for out_ref, cols in ((g_bias_ref, slice(0, width)), (g_gain_ref, slice(width, 2 * width))):
-        out_ref[0:1] = gb_ref[:, cols]
-        out_ref[1:2] = sums1_ref[:, cols]
-
-
-def edge_kernel(dm0_ref, dm1_ref, wpre_ref, wedge_ref, gt_ref, h_ref, rows_ref, out_ref, readout_ref, acc_ref):
+    put_message_grads(layer, x_ref, dcat_ref, et_ref, grads_ref, keep_ref, send_ref)
+    dh_out_ref[...] = dh
+
+
+def edge_kernel(
+    dm0_ref, dm1_ref, wpre_ref, wedge_ref, gt_ref, h_ref, rows_ref, dh_ref, sums0_ref, sums1_ref,
+    out_ref, readout_ref, node_ref, g_gain_ref, g_bias_ref, acc_ref,
+):
     width = dm0_ref.shape[0]
     nodes = gt_ref.shape[1]
     leaf_cols = LEAF_SLOTS * nodes
@@ -561,6 +574,10 @@
     belong = (iota((8, nodes), 0).astype(F32) == rows_ref[7:8, 0:nodes]).astype(F32)
     total = lax.dot_general(belong, h_ref[...], NT, precision=lax.Precision.HIGHEST, preferred_element_type=F32)
     readout_ref[...] = total[0 : readout_ref.shape[0]] / SUB_MAX
+    node_ref[...] = dh_ref[...].T
+    for out_ref, cols in ((g_bias_ref, slice(0, width)), (g_gain_ref, slice(width, 2 * width))):
+        out_ref[0:1] = sums0_ref[:, cols]
+        out_ref[1:2] = sums1_ref[:, cols]
 
 
 def finish_half(half, half_refs, outs, bufs, sems):
@@ -569,7 +586,7 @@
     post, mix, pre, et = bufs
     for layer in range(post.shape[0]):
         for place in range(16):
-            block = (me ^ piece_owner(core, half, place, layer == 0)) >> 1
+            block = (me ^ piece_owner(core, half, place, GATHER_KINDS[layer])) >> 1
             piece = half_refs[layer][8 * place : 8 * place + 8]
             post[layer, block] = piece[:, 0:832]
             et[layer, block] = piece[:, 832:896]
@@ -598,14 +615,15 @@
         mine, other = et[layer], other_et[layer]
         first, second = jnp.where(core == 0, other, mine), jnp.where(core == 0, mine, other)
         both = jnp.concatenate([first[:, None], second[:, None]], axis=1).reshape(width, 64)
-        gb_ref[layer : layer + 1] = to_rows(both[:, 16:17])[0]
-        factor = both[:, 0:16]
+        turned = jnp.concatenate([both, both], axis=1).T
+        gb_ref[layer : layer + 1] = turned[16:17]
+        factor = turned[0:16]
         high, rest = split_two(factor)
         last = (factor - high.astype(F32) - rest.astype(F32)).astype(BF16)
-        three = jnp.concatenate([high, rest, last], axis=1)
-        grad = mm(jnp.concatenate([wedge_ref[layer]] * 3, axis=0), three, TT)
+        three = jnp.concatenate([high, rest, last], axis=0)
+        grad = mm(jnp.concatenate([wedge_ref[layer]] * 3, axis=0), three, TN)
         term[layer] = grad.reshape(term.shape[1:])
-        parts = mm(three, wpre_ref[layer, 2 * width :], TT)
+        parts = mm(three, wpre_ref[layer, 2 * width :], NT)
         gedge_ref[layer] = parts[0:16] + parts[16:32] + parts[32:48]
     copies += start_copies([(term, pre_out.at[:, 2])], sems.at[3:4])
     wait_all(copies)
@@ -683,8 +701,8 @@
     )
     sum_s = s((1, 2 * width))
     du_s, d_s, dm_s = low_s, s((4 * 192, lanes), BF16), s((width, cols), BF16)
-    dcat_s, et_s, acc_s = s((3 * width, nodes), BF16), s((width, 64)), s((width, lanes))
-    back_scratch = like([s_s, acc_s, s((width, width), BF16)])
+    dcat_s, et_s = s((3 * width, nodes), BF16), s((width, 64))
+    back_scratch = like([s_s, s((width, width), BF16)])
     recv = exchange(part)
     grad_cols = 1664
     grad_s, half_s = s((width, grad_cols)), s((width // 2, grad_cols))
@@ -702,10 +720,6 @@
     def together(*values):
         return lax.optimization_barrier(values)
 
-    plane, line = (2, 4, 6), (8, 16, 24)
-    first, second = list(zip(plane, line)), list(zip(line, plane))
-    first1, second1 = list(zip(plane, plane)), list(zip(line, line))
-
     def relay(value, masks):
         one, two = swap(value, masks[0]), swap(value, masks[1])
         return jnp.concatenate([value, one, two, swap(one, masks[1])], axis=0)
@@ -726,25 +740,26 @@
 
     got1 = swap(send1, (1, 1))
     recv, got1 = together(exchange(part), got1)
-    part1 = scatter_sum(keep1 + got1, first1, 32)
-    g_gain, g_bias, dm0, node_grad, keep0, send0 = call(
+    part1 = scatter_sum(keep1 + got1, larger(SUM_KINDS[1]), 32)
+    sums0, dm0, dh0, keep0, send0 = call(
         functools.partial(backward_last_kernel, 0),
-        [recv, dv0, dh1, u0, norm0, bn_gain, bn_bias, w_mix, wpost_t, w_pre] + tables + [m0, s0, z0, y0, x0, sums1],
-        [s(bn_gain.shape), s(bn_bias.shape), dm_s, s((nodes, width)), half_s, half_s],
-        like([sum_s]) + back_scratch, free=(0, 1, 3), cost=8,
-    )
-    edge_grad, readout = call(
-        edge_kernel, [dm0, dm1, w_pre, w_edge, gt, h2, rows],
-        [s((nodes, width)), s(readout_grad.shape)], [pltpu.VMEM((width, 128), F32)], free=(0, 1), cost=2,
+        [recv, dv0, dh1, u0, norm0, bn_gain, bn_bias, w_mix, wpost_t, w_pre] + tables + [m0, s0, z0, y0, x0],
+        [sum_s, dm_s, row_s, half_s, half_s],
+        back_scratch, cost=8,
+    )
+    edge_grad, readout, node_grad, g_gain, g_bias = call(
+        edge_kernel, [dm0, dm1, w_pre, w_edge, gt, h2, rows, dh0, sums0, sums1],
+        [s((nodes, width)), s(readout_grad.shape), s((nodes, width)), s(bn_gain.shape), s(bn_bias.shape)],
+        [pltpu.VMEM((width, 128), F32)], free=range(5), cost=2,
     )
     send0, part1, edge_grad, readout = together(send0, part1, edge_grad, readout)
     got0 = swap(send0, (1, 1))
     half0 = keep0 + got0
-    part0 = scatter_sum(half0, first, 32)
-    part1 = gather(spread(scatter_sum(part1, second1, 8)), second1)
-    part1 = relay(together(part1, part0)[0], first1)
-    part0 = spread(scatter_sum(part0, second, 8))
-    part0 = gather(gather(part0, second), first)
+    part0 = scatter_sum(half0, larger(SUM_KINDS[0]), 32)
+    part1 = gather(spread(scatter_sum(part1, smaller(SUM_KINDS[1]), 8)), smaller(GATHER_KINDS[1]))
+    part1 = relay(together(part1, part0)[0], larger(GATHER_KINDS[1]))
+    part0 = spread(scatter_sum(part0, smaller(SUM_KINDS[0]), 8))
+    part0 = gather(gather(part0, smaller(GATHER_KINDS[0])), larger(GATHER_KINDS[0]))
     other1 = swap(part1, (1, 1))
     other0 = swap(part0, (1, 1))
     layers, blocks = w_pre.shape[0], width // 16

time: 128 us -> 125 us (0.977)
  starting transfers between devices: 35.3 us -> 32.3 us
  waiting for transfers between devices: 15.6 us -> 16.9 us
    ppermute x28, starting transfers between devices: 35.3 us -> 32.3 us  [swap(): lax.ppermute(value, 'dp', [(i, i ^ masks[i & 1]) for i in range(devices)])]
    ppermute x28, waiting for transfers between devices: 15.6 us -> 16.9 us  [swap(): lax.ppermute(value, 'dp', [(i, i ^ masks[i & 1]) for i in range(devices)])]
where the time goes in v5:
time: 125 us
  blocking collectives  42.2 us (34%)
  starting transfers between devices  32.3 us (26%)
  Pallas kernels  31.3 us (25%)
  waiting for transfers between devices  16.9 us (14%)
    all_to_all x4, blocking collectives, exchange(): return lax.all_to_all(part, 'dp', 0, 0, tiled=True)  42.2 us
    ppermute x28, starting transfers between devices, swap(): lax.ppermute(value, 'dp', [(i, i ^ masks[i & 1]) for i in range(devices)])  32.3 us
    pallas_call x8, Pallas kernels, call(): pl.pallas_call(kernel, in_specs=[hbm if i in far else vmem for i in range...  31.3 us
    ppermute x28, waiting for transfers between devices, swap(): lax.ppermute(value, 'dp', [(i, i ^ masks[i & 1]) for i in range(devices)])  16.9 us
  transfers between devices with their start and end apart: 28, of which 12 were waited for; matrix products, arithmetic and copies ran while one was open for 0% of the time, Pallas kernels for 8%

profile of v5, /device:TPU:0, one launch (start us, length us, event | category | flops | bytes accessed | tf_op | source)
XLA Modules:
  0.0 124.6 jit_solution(13850874698324643270)
XLA Ops:
  0.7 7.0 %shard_map.213 = (bf16[256,640]{1,0:T(8,128)(2,1)S(1)}, bf16[704,3584]{1,0:T(8,128)(2,1)S(1)}, f32[2,3584]{1,0:T(2,128)S(1)}, f32[8,768]{1,0:T(8,128)S(1)}, bf16...) custom-call(bf16[640,256]{1,0:T(8,128)(2,1)} %nf_hbm.1, ...), custom_call_target="tpu_custom_call" | custom-call | tf_op jit(solution)/shard_map/pallas_call | solution.py:652
  7.7 14.7 %all_to_all.20.recv_ref = f32[32,1,640]{2,1,0:T(1,128)S(1)} all-to-all(f32[32,1,640]{2,1,0:T(1,128)S(1)} %get-tuple-element.69), channel_id=1, replica_groups=mesh['dp'=32] {'dp'}, dimensions={0} | all-to-all | bytes 163840 | tf_op jit(solution)/shard_map/all_to_all | solution.py:673
  22.5 5.4 %shard_map.214 = (f32[8,256]{1,0:T(8,128)S(1)}, f32[256,640]{1,0:T(8,128)S(1)}, bf16[256,640]{1,0:T(8,128)(2,1)S(1)}, f32[256,3584]{1,0:T(8,128)S(1)}, f32[4,256...) custom-call(f32[32,1,640]{2,1,0:T(1,128)S(1)} %all_to_all.20.recv_re, ...), custom_call_target="tpu_custom_call" | custom-call | tf_op jit(solution)/shard_map/pallas_call | solution.py:652
  27.9 9.3 %all_to_all.21.recv_ref = f32[32,1,640]{2,1,0:T(1,128)S(1)} all-to-all(f32[32,1,640]{2,1,0:T(1,128)S(1)} %get-tuple-element.77), channel_id=1, replica_groups=mesh['dp'=32] {'dp'}, dimensions={0} | all-to-all | bytes 163840 | tf_op jit(solution)/shard_map/all_to_all | solution.py:673
  38.4 9.1 %all_to_all.22.recv_ref = f32[32,1,512]{2,1,0:T(1,128)S(1)} all-to-all(f32[32,1,512]{2,1,0:T(1,128)S(1)} %get-tuple-element.80), channel_id=1, replica_groups=mesh['dp'=32] {'dp'}, dimensions={0} | all-to-all | bytes 131072 | tf_op jit(solution)/shard_map/all_to_all | solution.py:673
  47.5 6.2 %shard_map.216 = (f32[1,512]{1,0:T(1,128)S(1)}, bf16[256,3584]{1,0:T(8,128)(2,1)S(1)}, f32[256,640]{1,0:T(8,128)S(1)}, f32[256,640]{1,0:T(8,128)S(1)}, f32[32,1,...) custom-call(f32[32,1,512]{2,1,0:T(1,128)S(1)} %all_to_all.22.recv_ref, ...), custom_call_target="tpu_custom_call" | custom-call | tf_op jit(solution)/shard_map/pallas_call | solution.py:652
  53.8 9.1 %all_to_all.23.recv_ref = f32[32,1,512]{2,1,0:T(1,128)S(1)} all-to-all(f32[32,1,512]{2,1,0:T(1,128)S(1)} %get-tuple-element.90), channel_id=1, replica_groups=mesh['dp'=32] {'dp'}, dimensions={0} | all-to-all | bytes 131072 | tf_op jit(solution)/shard_map/all_to_all | solution.py:673
  63.6 1.6 %collective-permute-start.3 = (f32[32,1664]{1,0:T(8,128)S(1)}, f32[32,1664]{1,0:T(8,128)S(1)}, u32[]{:S(2)}, u32[]{:S(2)}) collective-permute-start(f32[32,1664]{1,0:T(8,128)S(1)} %get-tuple-element.134), channel_id=1, source_target_pairs={{0,6},{1,25},{2,4},{3,27},{4,2},{5,29},{6,0},{7,31},{8,14},{9,17},... | collective-permute-start | bytes 638984 | tf_op jit(solution)/shard_map/ppermute | solution.py:718
  65.2 1.4 %collective-permute-start.2 = (f32[32,1664]{1,0:T(8,128)S(1)}, f32[32,1664]{1,0:T(8,128)S(1)}, u32[]{:S(2)}, u32[]{:S(2)}) collective-permute-start(f32[32,1664]{1,0:T(8,128)S(1)} %get-tuple-element.135), channel_id=1, source_target_pairs={{0,4},{1,17},{2,6},{3,19},{4,0},{5,21},{6,2},{7,23},{8,12},{9,25},... | collective-permute-start | bytes 638984 | tf_op jit(solution)/shard_map/ppermute | solution.py:718
  66.7 5.8 %shard_map.217 = (f32[1,512]{1,0:T(1,128)S(1)}, bf16[256,3584]{1,0:T(8,128)(2,1)S(1)}, f32[256,640]{1,0:T(8,128)S(1)}, f32[128,1664]{1,0:T(8,128)S(1)}, f32[128,1664]{1,0:T(8,128)S(1)}) custom-call(f32[32,1,512]{2,1,0:T(1,128)S(1)} %all_to_all.23.recv_ref, f32[256,640]{1,0:T(8,128)S(1)} %get-tuple-element.93.dv_ref, ...), custom_call_target="tpu_custom_call" | custom-call | flops 8000000000 | tf_op jit(solution)/shard_map/pallas_call | solution.py:652
  72.4 2.5 %shard_map.218 = (f32[640,256]{1,0:T(8,128)}, f32[4,256]{1,0:T(4,128)}, f32[640,256]{1,0:T(8,128)}, f32[2,256]{1,0:T(2,128)}, f32[2,256]{1,0:T(2,128)}) custom-call(bf16[256,3584]{1,0:T(8,128)(2,1)S(1)} %get-tuple-element.102.dm0_ref, bf16[256,3584]{1,0:T(8,128)(2,1)S(1)} %get-tuple-element.103.dm1_ref, bf16[2,768,256]{2,1,0:T(8,128)(2,1)S(1)} %copy-done, ...), custom_call_target="tpu_custom_call" | custom-call | flops 2000000000 | tf_op jit(solution)/shard_map/pallas_call | solution.py:652
  76.2 1.3 %collective-permute-start.19 = (f32[8,1664]{1,0:T(8,128)S(1)}, f32[8,1664]{1,0:T(8,128)S(1)}, u32[]{:S(2)}, u32[]{:S(2)}) collective-permute-start(f32[8,1664]{1,0:T(8,128)S(1)} %get-tuple-element.137), channel_id=1, source_target_pairs={{0,24},{1,7},{2,26},{3,5},{4,28},{5,3},{6,30},{7,1},{8,16},{9,15},... | collective-permute-start | bytes 159752 | tf_op jit(solution)/shard_map/ppermute | solution.py:718
  77.5 2.2 %collective-permute-start.18 = (f32[8,1664]{1,0:T(8,128)S(1)}, f32[8,1664]{1,0:T(8,128)S(1)}, u32[]{:S(2)}, u32[]{:S(2)}) collective-permute-start(f32[8,1664]{1,0:T(8,128)S(1)} %get-tuple-element.138), channel_id=1, source_target_pairs={{0,16},{1,5},{2,18},{3,7},{4,20},{5,1},{6,22},{7,3},{8,24},{9,13},... | collective-permute-start | bytes 159752 | tf_op jit(solution)/shard_map/ppermute | solution.py:718
  80.4 1.6 %collective-permute-start.7 = (f32[32,1664]{1,0:T(8,128)S(1)}, f32[32,1664]{1,0:T(8,128)S(1)}, u32[]{:S(2)}, u32[]{:S(2)}) collective-permute-start(f32[32,1664]{1,0:T(8,128)S(1)} %get-tuple-element.131), channel_id=1, source_target_pairs={{0,6},{1,25},{2,4},{3,27},{4,2},{5,29},{6,0},{7,31},{8,14},{9,17},... | collective-permute-start | bytes 638984 | tf_op jit(solution)/shard_map/ppermute | solution.py:718
  81.9 1.5 %collective-permute-start.6 = (f32[32,1664]{1,0:T(8,128)S(1)}, f32[32,1664]{1,0:T(8,128)S(1)}, u32[]{:S(2)}, u32[]{:S(2)}) collective-permute-start(f32[32,1664]{1,0:T(8,128)S(1)} %get-tuple-element.132), channel_id=1, source_target_pairs={{0,4},{1,17},{2,6},{3,19},{4,0},{5,21},{6,2},{7,23},{8,12},{9,25},... | collective-permute-start | bytes 638984 | tf_op jit(solution)/shard_map/ppermute | solution.py:718
  83.5 2.8 %collective-permute-start.22 = (f32[8,1664]{1,0:T(8,128)S(1)}, f32[8,1664]{1,0:T(8,128)S(1)}, u32[]{:S(2)}, u32[]{:S(2)}) collective-permute-start(f32[8,1664]{1,0:T(8,128)S(1)} %add_add_fusion), channel_id=1, source_target_pairs={{0,24},{1,25},{2,26},{3,27},{4,28},{5,29},{6,30},{7,31},{8,16},{9,... | collective-permute-start | bytes 159752 | tf_op jit(solution)/shard_map/ppermute | solution.py:718
  86.3 1.6 %collective-permute-start.20 = (f32[8,1664]{1,0:T(8,128)S(1)}, f32[8,1664]{1,0:T(8,128)S(1)}, u32[]{:S(2)}, u32[]{:S(2)}) collective-permute-start(f32[8,1664]{1,0:T(8,128)S(1)} %add_add_fusion), channel_id=1, source_target_pairs={{0,8},{1,9},{2,10},{3,11},{4,12},{5,13},{6,14},{7,15},{8,0},{9,1},... | collective-permute-start | bytes 159752 | tf_op jit(solution)/shard_map/ppermute | solution.py:718
  88.1 1.9 %collective-permute-done.6 = f32[32,1664]{1,0:T(8,128)S(1)} collective-permute-done((f32[32,1664]{1,0:T(8,128)S(1)}, f32[32,1664]{1,0:T(8,128)S(1)}, u32[]{:S(2)}, u32[]{:S(2)}) %collective-permute-start.6) | collective-permute-done | bytes 213024 | tf_op jit(solution)/shard_map/ppermute | solution.py:718
  91.2 1.2 collective-permute-start.10
  92.4 1.5 %collective-permute-start.9 = (f32[8,1664]{1,0:T(8,128)S(1)}, f32[8,1664]{1,0:T(8,128)S(1)}, u32[]{:S(2)}, u32[]{:S(2)}) collective-permute-start(f32[8,1664]{1,0:T(8,128)S(1)} %get-tuple-element.141), channel_id=1, source_target_pairs={{0,16},{1,5},{2,18},{3,7},{4,20},{5,1},{6,22},{7,3},{8,24},{9,13},... | collective-permute-start | bytes 159752 | tf_op jit(solution)/shard_map/ppermute | solution.py:718
  94.0 1.3 %collective-permute-start.24 = (f32[32,1664]{1,0:T(8,128)S(1)}, f32[32,1664]{1,0:T(8,128)S(1)}, u32[]{:S(2)}, u32[]{:S(2)}) collective-permute-start(f32[32,1664]{1,0:T(8,128)S(1)} %pad_maximum_fusion.1), channel_id=1, source_target_pairs={{0,4},{1,5},{2,6},{3,7},{4,0},{5,1},{6,2},{7,3},{8,12},{9,13},{10,... | collective-permute-start | bytes 638984 | tf_op jit(solution)/shard_map/ppermute | solution.py:718
  97.2 1.8 %collective-permute-done.9 = f32[8,1664]{1,0:T(8,128)S(1)} collective-permute-done((f32[8,1664]{1,0:T(8,128)S(1)}, f32[8,1664]{1,0:T(8,128)S(1)}, u32[]{:S(2)}, u32[]{:S(2)}) %collective-permute-start.9) | collective-permute-done | bytes 53280 | tf_op jit(solution)/shard_map/ppermute | solution.py:718
  99.0 2.2 %collective-permute-start.13 = (f32[8,1664]{1,0:T(8,128)S(1)}, f32[8,1664]{1,0:T(8,128)S(1)}, u32[]{:S(2)}, u32[]{:S(2)}) collective-permute-start(f32[8,1664]{1,0:T(8,128)S(1)} %get-tuple-element.129), channel_id=1, source_target_pairs={{0,24},{1,7},{2,26},{3,5},{4,28},{5,3},{6,30},{7,1},{8,16},{9,15},... | collective-permute-start | bytes 159752 | tf_op jit(solution)/shard_map/ppermute | solution.py:718
  101.2 2.2 %collective-permute-start.11 = (f32[8,1664]{1,0:T(8,128)S(1)}, f32[8,1664]{1,0:T(8,128)S(1)}, u32[]{:S(2)}, u32[]{:S(2)}) collective-permute-start(f32[8,1664]{1,0:T(8,128)S(1)} %get-tuple-element.129), channel_id=1, source_target_pairs={{0,8},{1,3},{2,10},{3,1},{4,12},{5,7},{6,14},{7,5},{8,0},{9,11},{1... | collective-permute-start | bytes 159752 | tf_op jit(solution)/shard_map/ppermute | solution.py:718
  103.5 1.5 %collective-permute-done.13 = f32[8,1664]{1,0:T(8,128)S(1)} collective-permute-done((f32[8,1664]{1,0:T(8,128)S(1)}, f32[8,1664]{1,0:T(8,128)S(1)}, u32[]{:S(2)}, u32[]{:S(2)}) %collective-permute-start.13) | collective-permute-done | bytes 53280 | tf_op jit(solution)/shard_map/ppermute | solution.py:718
  105.0 1.3 %collective-permute-done.12 = f32[8,1664]{1,0:T(8,128)S(1)} collective-permute-done((f32[8,1664]{1,0:T(8,128)S(1)}, f32[8,1664]{1,0:T(8,128)S(1)}, u32[]{:S(2)}, u32[]{:S(2)}) %collective-permute-start.12) | collective-permute-done | bytes 53280 | tf_op jit(solution)/shard_map/ppermute | solution.py:718
  108.3 1.5 %collective-permute-start.14 = (f32[32,1664]{1,0:T(8,128)S(1)}, f32[32,1664]{1,0:T(8,128)S(1)}, u32[]{:S(2)}, u32[]{:S(2)}) collective-permute-start(f32[32,1664]{1,0:T(8,128)S(1)} %pad_maximum_fusion), channel_id=1, source_target_pairs={{0,2},{1,9},{2,0},{3,11},{4,6},{5,13},{6,4},{7,15},{8,10},{9,1},{1... | collective-permute-start | bytes 638984 | tf_op jit(solution)/shard_map/ppermute | solution.py:718
  110.9 4.0 %collective-permute-done.14 = f32[32,1664]{1,0:T(8,128)S(1)} collective-permute-done((f32[32,1664]{1,0:T(8,128)S(1)}, f32[32,1664]{1,0:T(8,128)S(1)}, u32[]{:S(2)}, u32[]{:S(2)}) %collective-permute-start.14) | collective-permute-done | bytes 213024 | tf_op jit(solution)/shard_map/ppermute | solution.py:718
  114.9 2.6 %collective-permute-done.15 = f32[32,1664]{1,0:T(8,128)S(1)} collective-permute-done((f32[32,1664]{1,0:T(8,128)S(1)}, f32[32,1664]{1,0:T(8,128)S(1)}, u32[]{:S(2)}, u32[]{:S(2)}) %collective-permute-start.15) | collective-permute-done | bytes 213024 | tf_op jit(solution)/shard_map/ppermute | solution.py:718
  117.5 1.3 %collective-permute-start.26 = (f32[128,1664]{1,0:T(8,128)S(1)}, f32[128,1664]{1,0:T(8,128)S(1)}, u32[]{:S(2)}, u32[]{:S(2)}) collective-permute-start(f32[128,1664]{1,0:T(8,128)S(1)} %constant_dynamic-update-slice_fusion.half0_ref), channel_id=1, source_target_pairs={{0,1},{1,0},{2,3},{3,2},{4,5},{5,4},{6,7},{7,6},{8,9},{9,8},{10,11... | collective-permute-start | bytes 2555912 | tf_op jit(solution)/shard_map/ppermute | solution.py:718
  120.0 1.3 %shard_map.219 = (f32[2,16,2,8,832]{4,3,2,1,0:T(8,128)}, f32[2,16,2,8,256]{4,3,2,1,0:T(8,128)}, f32[2,3,16,2,8,256]{5,4,3,2,1,0:T(8,128)}, f32[2,16,8,64]{3,2,1,0:T(8,128)S(1)}) custom-call(f32[128,1664]{1,0:T(8,128)S(1)} %constant_dynamic-update-slice_fusion.half0_ref, f32[128,1664]{1,0:T(8,128)S(1)} %constant_dynamic-update-slice_fusion.7.half1_ref), custom_call_target="tpu_custom_call" | custom-call | flops 2000000000 | tf_op jit(solution)/shard_map/pallas_call | solution.py:652
  122.4 2.1 %shard_map.220 = (f32[2,16,2,8,832]{4,3,2,1,0:T(8,128)}, f32[2,16,2,8,256]{4,3,2,1,0:T(8,128)}, f32[2,3,16,2,8,256]{5,4,3,2,1,0:T(8,128)}, f32[2,256]{1,0:T(2,128)}, f32[2,16,256]{2,1,0:T(8,128)}) custom-call(f32[2,16,2,8,832]{4,3,2,1,0:T(8,128)} %get-tuple-element.117.post_in, ...), custom_call_target="tpu_custom_call", output_to_operand_aliasing={{0}: (0, {}), {1}: (1, {}), {2}: (2, {})} | custom-call | tf_op jit(solution)/shard_map/pallas_call | solution.py:652
  (74 shorter events, 12.8 us)
Async XLA Ops:
  0.6 21.8 %copy-start = (bf16[2,768,256]{2,1,0:T(8,128)(2,1)S(1)}, bf16[2,768,256]{2,1,0:T(8,128)(2,1)}, u32[]{:S(2)}) copy-start(bf16[2,768,256]{2,1,0:T(8,128)(2,1)} %wpre_ref.9) | copy-start | bytes 2359300
  0.7 21.8 %copy-start.2 = (bf16[2,256,256]{2,1,0:T(8,128)(2,1)S(1)}, bf16[2,256,256]{2,1,0:T(8,128)(2,1)}, u32[]{:S(2)}) copy-start(bf16[2,256,256]{2,1,0:T(8,128)(2,1)} %wmix_ref.5) | copy-start | bytes 786436
  0.7 21.8 %copy-start.3 = (bf16[2,16,256]{2,1,0:T(8,128)(2,1)S(1)}, bf16[2,16,256]{2,1,0:T(8,128)(2,1)}, u32[]{:S(2)}) copy-start(bf16[2,16,256]{2,1,0:T(8,128)(2,1)} %wedge_ref.5) | copy-start | bytes 49156
  0.7 21.7 %copy-start.6 = (f32[2,256]{1,0:T(2,128)S(1)}, f32[2,256]{1,0:T(2,128)}, u32[]{:S(2)}) copy-start(f32[2,256]{1,0:T(2,128)} %bpre_ref.1) | copy-start | bytes 6148
  53.6 9.3 %collective-permute-start = (f32[128,1664]{1,0:T(8,128)S(1)}, f32[128,1664]{1,0:T(8,128)S(1)}, u32[]{:S(2)}, u32[]{:S(2)}) collective-permute-start(f32[128,1664]{1,0:T(8,128)S(1)} %get-tuple-element.91), channel_id=1, source_target_pairs={{0,1},{1,0},{2,3},{3,2},{4,5},{5,4},{6,7},{7,6},{8,9},{9,8},{10,11... | collective-permute-start | bytes 2555912 | tf_op jit(solution)/shard_map/ppermute | solution.py:718
  63.1 11.8 %collective-permute-start.1 = (f32[32,1664]{1,0:T(8,128)S(1)}, f32[32,1664]{1,0:T(8,128)S(1)}, u32[]{:S(2)}, u32[]{:S(2)}) collective-permute-start(f32[32,1664]{1,0:T(8,128)S(1)} %get-tuple-element.133), channel_id=1, source_target_pairs={{0,2},{1,9},{2,0},{3,11},{4,6},{5,13},{6,4},{7,15},{8,10},{9,1},{1... | collective-permute-start | bytes 638984 | tf_op jit(solution)/shard_map/ppermute | solution.py:718
  63.6 11.3 %collective-permute-start.3 = (f32[32,1664]{1,0:T(8,128)S(1)}, f32[32,1664]{1,0:T(8,128)S(1)}, u32[]{:S(2)}, u32[]{:S(2)}) collective-permute-start(f32[32,1664]{1,0:T(8,128)S(1)} %get-tuple-element.134), channel_id=1, source_target_pairs={{0,6},{1,25},{2,4},{3,27},{4,2},{5,29},{6,0},{7,31},{8,14},{9,17},... | collective-permute-start | bytes 638984 | tf_op jit(solution)/shard_map/ppermute | solution.py:718
  65.2 9.7 %collective-permute-start.2 = (f32[32,1664]{1,0:T(8,128)S(1)}, f32[32,1664]{1,0:T(8,128)S(1)}, u32[]{:S(2)}, u32[]{:S(2)}) collective-permute-start(f32[32,1664]{1,0:T(8,128)S(1)} %get-tuple-element.135), channel_id=1, source_target_pairs={{0,4},{1,17},{2,6},{3,19},{4,0},{5,21},{6,2},{7,23},{8,12},{9,25},... | collective-permute-start | bytes 638984 | tf_op jit(solution)/shard_map/ppermute | solution.py:718
  75.0 4.7 %collective-permute-start.4 = (f32[128,1664]{1,0:T(8,128)S(1)}, f32[128,1664]{1,0:T(8,128)S(1)}, u32[]{:S(2)}, u32[]{:S(2)}) collective-permute-start(f32[128,1664]{1,0:T(8,128)S(1)} %get-tuple-element.114), channel_id=1, source_target_pairs={{0,1},{1,0},{2,3},{3,2},{4,5},{5,4},{6,7},{7,6},{8,9},{9,8},{10,11... | collective-permute-start | bytes 2555912 | tf_op jit(solution)/shard_map/ppermute | solution.py:718
  76.1 5.8 %collective-permute-start.17 = (f32[8,1664]{1,0:T(8,128)S(1)}, f32[8,1664]{1,0:T(8,128)S(1)}, u32[]{:S(2)}, u32[]{:S(2)}) collective-permute-start(f32[8,1664]{1,0:T(8,128)S(1)} %get-tuple-element.136), channel_id=1, source_target_pairs={{0,8},{1,3},{2,10},{3,1},{4,12},{5,7},{6,14},{7,5},{8,0},{9,11},{1... | collective-permute-start | bytes 159752 | tf_op jit(solution)/shard_map/ppermute | solution.py:718
  76.2 7.2 %collective-permute-start.19 = (f32[8,1664]{1,0:T(8,128)S(1)}, f32[8,1664]{1,0:T(8,128)S(1)}, u32[]{:S(2)}, u32[]{:S(2)}) collective-permute-start(f32[8,1664]{1,0:T(8,128)S(1)} %get-tuple-element.137), channel_id=1, source_target_pairs={{0,24},{1,7},{2,26},{3,5},{4,28},{5,3},{6,30},{7,1},{8,16},{9,15},... | collective-permute-start | bytes 159752 | tf_op jit(solution)/shard_map/ppermute | solution.py:718
  77.5 5.9 %collective-permute-start.18 = (f32[8,1664]{1,0:T(8,128)S(1)}, f32[8,1664]{1,0:T(8,128)S(1)}, u32[]{:S(2)}, u32[]{:S(2)}) collective-permute-start(f32[8,1664]{1,0:T(8,128)S(1)} %get-tuple-element.138), channel_id=1, source_target_pairs={{0,16},{1,5},{2,18},{3,7},{4,20},{5,1},{6,22},{7,3},{8,24},{9,13},... | collective-permute-start | bytes 159752 | tf_op jit(solution)/shard_map/ppermute | solution.py:718
  79.9 6.4 %collective-permute-start.5 = (f32[32,1664]{1,0:T(8,128)S(1)}, f32[32,1664]{1,0:T(8,128)S(1)}, u32[]{:S(2)}, u32[]{:S(2)}) collective-permute-start(f32[32,1664]{1,0:T(8,128)S(1)} %get-tuple-element.130), channel_id=1, source_target_pairs={{0,2},{1,9},{2,0},{3,11},{4,6},{5,13},{6,4},{7,15},{8,10},{9,1},{1... | collective-permute-start | bytes 638984 | tf_op jit(solution)/shard_map/ppermute | solution.py:718
  80.4 7.8 %collective-permute-start.7 = (f32[32,1664]{1,0:T(8,128)S(1)}, f32[32,1664]{1,0:T(8,128)S(1)}, u32[]{:S(2)}, u32[]{:S(2)}) collective-permute-start(f32[32,1664]{1,0:T(8,128)S(1)} %get-tuple-element.131), channel_id=1, source_target_pairs={{0,6},{1,25},{2,4},{3,27},{4,2},{5,29},{6,0},{7,31},{8,14},{9,17},... | collective-permute-start | bytes 638984 | tf_op jit(solution)/shard_map/ppermute | solution.py:718
  81.9 8.1 %collective-permute-start.6 = (f32[32,1664]{1,0:T(8,128)S(1)}, f32[32,1664]{1,0:T(8,128)S(1)}, u32[]{:S(2)}, u32[]{:S(2)}) collective-permute-start(f32[32,1664]{1,0:T(8,128)S(1)} %get-tuple-element.132), channel_id=1, source_target_pairs={{0,4},{1,17},{2,6},{3,19},{4,0},{5,21},{6,2},{7,23},{8,12},{9,25},... | collective-permute-start | bytes 638984 | tf_op jit(solution)/shard_map/ppermute | solution.py:718
  83.5 9.0 %collective-permute-start.22 = (f32[8,1664]{1,0:T(8,128)S(1)}, f32[8,1664]{1,0:T(8,128)S(1)}, u32[]{:S(2)}, u32[]{:S(2)}) collective-permute-start(f32[8,1664]{1,0:T(8,128)S(1)} %add_add_fusion), channel_id=1, source_target_pairs={{0,24},{1,25},{2,26},{3,27},{4,28},{5,29},{6,30},{7,31},{8,16},{9,... | collective-permute-start | bytes 159752 | tf_op jit(solution)/shard_map/ppermute | solution.py:718
  86.3 7.7 %collective-permute-start.21 = (f32[8,1664]{1,0:T(8,128)S(1)}, f32[8,1664]{1,0:T(8,128)S(1)}, u32[]{:S(2)}, u32[]{:S(2)}) collective-permute-start(f32[8,1664]{1,0:T(8,128)S(1)} %add_add_fusion), channel_id=1, source_target_pairs={{0,16},{1,17},{2,18},{3,19},{4,20},{5,21},{6,22},{7,23},{8,24},{9,... | collective-permute-start | bytes 159752 | tf_op jit(solution)/shard_map/ppermute | solution.py:718
  86.3 7.7 %collective-permute-start.20 = (f32[8,1664]{1,0:T(8,128)S(1)}, f32[8,1664]{1,0:T(8,128)S(1)}, u32[]{:S(2)}, u32[]{:S(2)}) collective-permute-start(f32[8,1664]{1,0:T(8,128)S(1)} %add_add_fusion), channel_id=1, source_target_pairs={{0,8},{1,9},{2,10},{3,11},{4,12},{5,13},{6,14},{7,15},{8,0},{9,1},... | collective-permute-start | bytes 159752 | tf_op jit(solution)/shard_map/ppermute | solution.py:718
  90.1 6.3 %collective-permute-start.8 = (f32[8,1664]{1,0:T(8,128)S(1)}, f32[8,1664]{1,0:T(8,128)S(1)}, u32[]{:S(2)}, u32[]{:S(2)}) collective-permute-start(f32[8,1664]{1,0:T(8,128)S(1)} %get-tuple-element.139), channel_id=1, source_target_pairs={{0,8},{1,3},{2,10},{3,1},{4,12},{5,7},{6,14},{7,5},{8,0},{9,11},{1... | collective-permute-start | bytes 159752 | tf_op jit(solution)/shard_map/ppermute | solution.py:718
  91.2 6.0 %collective-permute-start.10 = (f32[8,1664]{1,0:T(8,128)S(1)}, f32[8,1664]{1,0:T(8,128)S(1)}, u32[]{:S(2)}, u32[]{:S(2)}) collective-permute-start(f32[8,1664]{1,0:T(8,128)S(1)} %get-tuple-element.140), channel_id=1, source_target_pairs={{0,24},{1,7},{2,26},{3,5},{4,28},{5,3},{6,30},{7,1},{8,16},{9,15},... | collective-permute-start | bytes 159752 | tf_op jit(solution)/shard_map/ppermute | solution.py:718
  92.4 6.6 %collective-permute-start.9 = (f32[8,1664]{1,0:T(8,128)S(1)}, f32[8,1664]{1,0:T(8,128)S(1)}, u32[]{:S(2)}, u32[]{:S(2)}) collective-permute-start(f32[8,1664]{1,0:T(8,128)S(1)} %get-tuple-element.141), channel_id=1, source_target_pairs={{0,16},{1,5},{2,18},{3,7},{4,20},{5,1},{6,22},{7,3},{8,24},{9,13},... | collective-permute-start | bytes 159752 | tf_op jit(solution)/shard_map/ppermute | solution.py:718
  94.0 16.9 %collective-permute-start.24 = (f32[32,1664]{1,0:T(8,128)S(1)}, f32[32,1664]{1,0:T(8,128)S(1)}, u32[]{:S(2)}, u32[]{:S(2)}) collective-permute-start(f32[32,1664]{1,0:T(8,128)S(1)} %pad_maximum_fusion.1), channel_id=1, source_target_pairs={{0,4},{1,5},{2,6},{3,7},{4,0},{5,1},{6,2},{7,3},{8,12},{9,13},{10,... | collective-permute-start | bytes 638984 | tf_op jit(solution)/shard_map/ppermute | solution.py:718
  95.3 14.6 %collective-permute-start.23 = (f32[32,1664]{1,0:T(8,128)S(1)}, f32[32,1664]{1,0:T(8,128)S(1)}, u32[]{:S(2)}, u32[]{:S(2)}) collective-permute-start(f32[32,1664]{1,0:T(8,128)S(1)} %pad_maximum_fusion.1), channel_id=1, source_target_pairs={{0,2},{1,3},{2,0},{3,1},{4,6},{5,7},{6,4},{7,5},{8,10},{9,11},{10,... | collective-permute-start | bytes 638984 | tf_op jit(solution)/shard_map/ppermute | solution.py:718
  99.0 6.0 %collective-permute-start.13 = (f32[8,1664]{1,0:T(8,128)S(1)}, f32[8,1664]{1,0:T(8,128)S(1)}, u32[]{:S(2)}, u32[]{:S(2)}) collective-permute-start(f32[8,1664]{1,0:T(8,128)S(1)} %get-tuple-element.129), channel_id=1, source_target_pairs={{0,24},{1,7},{2,26},{3,5},{4,28},{5,3},{6,30},{7,1},{8,16},{9,15},... | collective-permute-start | bytes 159752 | tf_op jit(solution)/shard_map/ppermute | solution.py:718
  101.2 5.0 %collective-permute-start.12 = (f32[8,1664]{1,0:T(8,128)S(1)}, f32[8,1664]{1,0:T(8,128)S(1)}, u32[]{:S(2)}, u32[]{:S(2)}) collective-permute-start(f32[8,1664]{1,0:T(8,128)S(1)} %get-tuple-element.129), channel_id=1, source_target_pairs={{0,16},{1,5},{2,18},{3,7},{4,20},{5,1},{6,22},{7,3},{8,24},{9,13},... | collective-permute-start | bytes 159752 | tf_op jit(solution)/shard_map/ppermute | solution.py:718
  101.2 5.0 %collective-permute-start.11 = (f32[8,1664]{1,0:T(8,128)S(1)}, f32[8,1664]{1,0:T(8,128)S(1)}, u32[]{:S(2)}, u32[]{:S(2)}) collective-permute-start(f32[8,1664]{1,0:T(8,128)S(1)} %get-tuple-element.129), channel_id=1, source_target_pairs={{0,8},{1,3},{2,10},{3,1},{4,12},{5,7},{6,14},{7,5},{8,0},{9,11},{1... | collective-permute-start | bytes 159752 | tf_op jit(solution)/shard_map/ppermute | solution.py:718
  106.3 11.2 %collective-permute-start.16 = (f32[32,1664]{1,0:T(8,128)S(1)}, f32[32,1664]{1,0:T(8,128)S(1)}, u32[]{:S(2)}, u32[]{:S(2)}) collective-permute-start(f32[32,1664]{1,0:T(8,128)S(1)} %pad_maximum_fusion), channel_id=1, source_target_pairs={{0,6},{1,25},{2,4},{3,27},{4,2},{5,29},{6,0},{7,31},{8,14},{9,17},... | collective-permute-start | bytes 638984 | tf_op jit(solution)/shard_map/ppermute | solution.py:718
  107.3 10.1 %collective-permute-start.15 = (f32[32,1664]{1,0:T(8,128)S(1)}, f32[32,1664]{1,0:T(8,128)S(1)}, u32[]{:S(2)}, u32[]{:S(2)}) collective-permute-start(f32[32,1664]{1,0:T(8,128)S(1)} %pad_maximum_fusion), channel_id=1, source_target_pairs={{0,4},{1,17},{2,6},{3,19},{4,0},{5,21},{6,2},{7,23},{8,12},{9,25},... | collective-permute-start | bytes 638984 | tf_op jit(solution)/shard_map/ppermute | solution.py:718
  108.3 6.6 %collective-permute-start.14 = (f32[32,1664]{1,0:T(8,128)S(1)}, f32[32,1664]{1,0:T(8,128)S(1)}, u32[]{:S(2)}, u32[]{:S(2)}) collective-permute-start(f32[32,1664]{1,0:T(8,128)S(1)} %pad_maximum_fusion), channel_id=1, source_target_pairs={{0,2},{1,9},{2,0},{3,11},{4,6},{5,13},{6,4},{7,15},{8,10},{9,1},{1... | collective-permute-start | bytes 638984 | tf_op jit(solution)/shard_map/ppermute | solution.py:718
  109.9 10.1 %collective-permute-start.25 = (f32[32,1664]{1,0:T(8,128)S(1)}, f32[32,1664]{1,0:T(8,128)S(1)}, u32[]{:S(2)}, u32[]{:S(2)}) collective-permute-start(f32[32,1664]{1,0:T(8,128)S(1)} %collective-permute-done.23), channel_id=1, source_target_pairs={{0,4},{1,5},{2,6},{3,7},{4,0},{5,1},{6,2},{7,3},{8,12},{9,13},{10,... | collective-permute-start | bytes 638984 | tf_op jit(solution)/shard_map/ppermute | solution.py:718
  117.5 3.8 %collective-permute-start.26 = (f32[128,1664]{1,0:T(8,128)S(1)}, f32[128,1664]{1,0:T(8,128)S(1)}, u32[]{:S(2)}, u32[]{:S(2)}) collective-permute-start(f32[128,1664]{1,0:T(8,128)S(1)} %constant_dynamic-update-slice_fusion.half0_ref), channel_id=1, source_target_pairs={{0,1},{1,0},{2,3},{3,2},{4,5},{5,4},{6,7},{7,6},{8,9},{9,8},{10,11... | collective-permute-start | bytes 2555912 | tf_op jit(solution)/shard_map/ppermute | solution.py:718
  120.0 2.4 %collective-permute-start.27 = (f32[128,1664]{1,0:T(8,128)S(1)}, f32[128,1664]{1,0:T(8,128)S(1)}, u32[]{:S(2)}, u32[]{:S(2)}) collective-permute-start(f32[128,1664]{1,0:T(8,128)S(1)} %constant_dynamic-update-slice_fusion.7.half1_ref), channel_id=1, source_target_pairs={{0,1},{1,0},{2,3},{3,2},{4,5},{5,4},{6,7},{7,6},{8,9},{9,8},{10,11... | collective-permute-start | bytes 2555912 | tf_op jit(solution)/shard_map/ppermute | solution.py:718
  (4 other events, 79.9 us)

commit v6 on v5

--- a/solution.py
+++ b/solution.py
@@ -18,7 +18,7 @@
 LN2 = 0.6931471805599453
 ROW_CHUNK = 64
 PLANE, LINE = 0, 1
-MASKS = ((2, 4, 6), (8, 16, 24))
+MASKS = ((4, 2, 6), (16, 8, 24))
 SUM_KINDS = ((PLANE, LINE), (PLANE, LINE))
 GATHER_KINDS = ((PLANE, LINE), (PLANE, PLANE))
 F32 = jnp.float32
@@ -60,6 +60,14 @@
 def leaf_col(nodes, slot, node):
     lo, hi = next(g for g in lane_groups(nodes) if g[0] <= node < g[1])
     return LEAF_SLOTS * lo + slot * (hi - lo) + node - lo
+
+
+def column_groups(nodes):
+    leaf_cols = LEAF_SLOTS * nodes
+    groups = [(leaf_cols, leaf_cols + 1024, range(nodes // 128, nodes // 128 + 1))]
+    for lo, hi in lane_groups(nodes):
+        groups.append((LEAF_SLOTS * lo, LEAF_SLOTS * hi, range(lo // 128, hi // 128)))
+    return groups
 
 
 def split_two(value):
@@ -140,7 +148,8 @@
     ef_t = ef_ref[...].T
     nbr16 = nbr.astype(jnp.int16)
     ef_h = mm(ef_t, g).astype(BF16)
-    hub_iota = iota((nodes, 128), 0)
+    hub_iota = iota((nodes, 128), 0).astype(jnp.int16)
+    one_h, none_h = jnp.ones((nodes, 128), BF16), jnp.zeros((nodes, 128), BF16)
     for first_node, end_node in lane_groups(nodes):
         span = slice(first_node, end_node)
         size = end_node - first_node
@@ -160,7 +169,7 @@
     for j in range(8):
         lo = LEAF_SLOTS * nodes + 128 * j
         index = jnp.where(lane_h < 64, nbr_h[2 * j : 2 * j + 1], nbr_h[2 * j + 1 : 2 * j + 2])
-        b_ref[0:nodes, lo : lo + 128] = (hub_iota == index).astype(F32).astype(BF16)
+        b_ref[0:nodes, lo : lo + 128] = jnp.where(hub_iota == index.astype(jnp.int16), one_h, none_h)
         piece = jnp.where(own_half, ef_h[32 * j : 32 * j + 32].astype(F32), 0.0).astype(BF16)
         b_ref[nodes : nodes + 32, lo : lo + 128] = piece
         b_ref[nodes + 32 : nodes + 64, lo : lo + 128] = piece
@@ -180,7 +189,7 @@
 
 def forward_layer(
     layer, x_ref, wedge_ref, wpre_ref, bias, wpost_ref, wmix_ref, b_ref, live_ref, rows_ref, g_ref, gt_ref,
-    m_ref, s_ref, z_ref, y_ref, u_ref, part_ref, a_ref, ya_ref, own_ref,
+    m_refs, s_ref, z_ref, y_ref, u_ref, part_ref, a_ref, ya_ref, own_ref,
 ):
     width, nodes = x_ref.shape
     leaf_cols = LEAF_SLOTS * nodes
@@ -197,15 +206,15 @@
     own_ref[:, nodes:] = mm(own_high, g) + mm(own_rest, g)
     a = a_ref[...]
 
-    def messages(lo, hi):
-        m_ref[:, lo:hi] = mm(a, b_ref[:, lo:hi])
+    def messages(m_ref, lo, hi):
+        m_ref[...] = mm(a, b_ref[:, lo:hi])
 
     x_h = mm(x, g).astype(BF16)
     for t in range(4):
         z_ref[320 * t : 320 * t + 64, 0:nodes] = x[64 * t : 64 * t + 64]
         z_ref[320 * t : 320 * t + 64, nodes:] = x_h[64 * t : 64 * t + 64]
 
-    def summarize(i, tiles):
+    def summarize(i, tiles, m_ref, base_col):
         per = 64 // ROW_CHUNK
         zr = (i // per) * 320 + 64 + (i % per) * ROW_CHUNK
         rows = pl.ds(i * ROW_CHUNK, ROW_CHUNK)
@@ -213,15 +222,15 @@
             hub = c == nodes // 128
             lanes = slice(128 * c, 128 * c + 128)
             if hub:
-                cols = [leaf_cols + 128 * j for j in range(8)]
-                first = m_ref[rows, leaf_cols : leaf_cols + 128]
+                cols = [128 * j for j in range(8)]
+                first = m_ref[rows, 0:128]
                 first = jnp.where(iota((1, 128), 1) < 64, first, pltpu.roll(first, 64, 1))
             else:
-                zero, *cols = [leaf_col(nodes, k, 128 * c) for k in range(LEAF_SLOTS)]
+                zero, *cols = [leaf_col(nodes, k, 128 * c) - base_col for k in range(LEAF_SLOTS)]
                 first = m_ref[rows, zero : zero + 128]
             offs = []
             for lo in cols:
-                d = (m_ref[rows, lo : lo + 128] - first) * live_ref[0:1, lo : lo + 128]
+                d = (m_ref[rows, lo : lo + 128] - first) * live_ref[0:1, base_col + lo : base_col + lo + 128]
                 m_ref[rows, lo : lo + 128] = d
                 offs.append(d)
 
@@ -247,16 +256,14 @@
                 value = base + LN2 * stat if n < 3 else spread * rstd
                 z_ref[pl.ds(zr + 64 * n, ROW_CHUNK), lanes] = value.astype(BF16)
 
-    groups = [(leaf_cols, leaf_cols + 1024, range(nodes // 128, nodes // 128 + 1))]
-    for lo, hi in lane_groups(nodes):
-        groups.append((LEAF_SLOTS * lo, LEAF_SLOTS * hi, range(lo // 128, hi // 128)))
+    groups = column_groups(nodes)
     waiting = None
-    for group in groups + [None]:
+    for group in [*zip(m_refs, groups), None]:
         if group is not None:
-            messages(*group[0:2])
+            messages(group[0], *group[1][0:2])
         if waiting is not None:
             for i in range(width // ROW_CHUNK):
-                summarize(i, waiting[2])
+                summarize(i, waiting[1][2], waiting[0], waiting[1][0])
         waiting = group
 
     amp, att = rows_ref[0:1], rows_ref[1:2]
@@ -279,7 +286,8 @@
 
 def forward_first_kernel(
     layer, nf_hbm, ef_hbm, seg_hbm, nbr_hbm, mask_hbm, deg_hbm, wedge_hbm, wpre_hbm, bpre_hbm, wpost_hbm, wmix_hbm,
-    x_ref, b_ref, live_ref, rows_ref, g_ref, gt_ref, m_ref, s_ref, z_ref, y_ref, u_ref, part_ref,
+    x_ref, b_ref, live_ref, rows_ref, g_ref, gt_ref, ma_ref, mb_ref, mc_ref, md_ref,
+    s_ref, z_ref, y_ref, u_ref, part_ref,
     a_ref, ya_ref, own_ref, nf_ref, ef_ref, seg_ref, nbr_ref, mask_ref, deg_ref, wedge_ref, wpre_ref, bpre_ref, wpost_ref, wmix_ref, in_sems,
 ):
     loads = start_copies(
@@ -295,7 +303,8 @@
     x_ref[...] = nf_ref[...].T
     forward_layer(
         layer, x_ref, wedge_ref, wpre_ref, *to_cols(bpre_ref[layer : layer + 1]), wpost_ref, wmix_ref, b_ref,
-        live_ref, rows_ref, g_ref, gt_ref, m_ref, s_ref, z_ref, y_ref, u_ref, part_ref, a_ref, ya_ref, own_ref,
+        live_ref, rows_ref, g_ref, gt_ref, (ma_ref, mb_ref, mc_ref, md_ref), s_ref, z_ref, y_ref, u_ref, part_ref,
+        a_ref, ya_ref, own_ref,
     )
 
 
@@ -330,7 +339,8 @@
 def forward_next_kernel(
     layer, recv_ref, u0_ref, x0_ref, gain_ref, bias_ref, wedge_ref, wpre_ref, bpre_ref, wpost_ref, wmix_ref,
     b_ref, live_ref, rows_ref, g_ref, gt_ref,
-    norm_ref, h_ref, x_ref, m_ref, s_ref, z_ref, y_ref, u_ref, part_ref, a_ref, ya_ref, own_ref,
+    norm_ref, h_ref, x_ref, ma_ref, mb_ref, mc_ref, md_ref, s_ref, z_ref, y_ref, u_ref, part_ref,
+    a_ref, ya_ref, own_ref,
 ):
     store_norm(norm_ref, recv_ref)
     _, v = normed(u0_ref[...], norm_ref, gain_ref, bias_ref, layer - 1)
@@ -339,7 +349,8 @@
     x_ref[...] = h.astype(BF16)
     forward_layer(
         layer, x_ref, wedge_ref, wpre_ref, *to_cols(bpre_ref[layer : layer + 1]), wpost_ref, wmix_ref, b_ref,
-        live_ref, rows_ref, g_ref, gt_ref, m_ref, s_ref, z_ref, y_ref, u_ref, part_ref, a_ref, ya_ref, own_ref,
+        live_ref, rows_ref, g_ref, gt_ref, (ma_ref, mb_ref, mc_ref, md_ref), s_ref, z_ref, y_ref, u_ref, part_ref,
+        a_ref, ya_ref, own_ref,
     )
 
 
@@ -371,8 +382,8 @@
 
 def backward_layer(
     layer, recv_ref, dv_ref, dh_ref, u_ref, norm_ref, gain_ref, bias_ref, wmix_ref, wpost_ref, wpre_ref,
-    b_ref, live_ref, rows_ref, g_ref, gt_ref, m_ref, s_ref,
-    gb_ref, du_ref, d_ref, dm_ref, dcat_ref, et_ref, ds_ref, bd_ref, beside=(),
+    b_ref, live_ref, rows_ref, g_ref, gt_ref, m_refs, s_ref,
+    gb_ref, du_ref, d_ref, dm_refs, dcat_ref, et_ref, ds_ref, bd_ref, beside=(),
 ):
     width, nodes = dv_ref.shape
     leaf_cols = LEAF_SLOTS * nodes
@@ -415,7 +426,7 @@
     once = jnp.where(iota((1, nodes + 128), 1) < nodes + 64, acc, 0.0)
     bias = jnp.sum(once, axis=1, keepdims=True)
 
-    def spread_back(i, tiles):
+    def spread_back(i, tiles, m_ref, dm_ref, base_col):
         rows = pl.ds(i * ROW_CHUNK, ROW_CHUNK)
         for c in tiles:
             hub = c == nodes // 128
@@ -426,32 +437,30 @@
             c1 = dstd * inv * rstd * LN2
             c0 = dmean * inv - mean * c1
             if hub:
-                cols = [leaf_cols + 128 * j for j in range(8)]
+                cols = [128 * j for j in range(8)]
             else:
-                zero, *cols = [leaf_col(nodes, k, 128 * c) for k in range(LEAF_SLOTS)]
+                zero, *cols = [leaf_col(nodes, k, 128 * c) - base_col for k in range(LEAF_SLOTS)]
                 d = c0 + dsmax * jnp.exp2(-smax) + dsmin * jnp.exp2(smin)
                 dm_ref[rows, zero : zero + 128] = d.astype(BF16)
             for lo in cols:
                 m = m_ref[rows, lo : lo + 128]
                 d = c0 + m * c1 + dsmax * jnp.exp2(m - smax) + dsmin * jnp.exp2(smin - m)
-                d = d * live_ref[1:2, lo : lo + 128]
+                d = d * live_ref[1:2, base_col + lo : base_col + lo + 128]
                 dm_ref[rows, lo : lo + 128] = d.astype(BF16)
 
-    def land(lo, hi):
-        return mm(dm_ref[:, lo:hi], b_ref[0 : nodes + 32, lo:hi], NT)
-
-    groups = [(leaf_cols, leaf_cols + 1024, range(nodes // 128, nodes // 128 + 1))]
-    for lo, hi in lane_groups(nodes):
-        groups.append((LEAF_SLOTS * lo, LEAF_SLOTS * hi, range(lo // 128, hi // 128)))
+    def land(dm_ref, lo, hi):
+        return mm(dm_ref[...], b_ref[0 : nodes + 32, lo:hi], NT)
+
+    groups = column_groups(nodes)
     waiting, landed = None, 0.0
-    for step, group in enumerate(groups + [None]):
+    for step, group in enumerate([*zip(m_refs, dm_refs, groups), None]):
         if group is not None:
             for i in range(width // ROW_CHUNK):
-                spread_back(i, group[2])
+                spread_back(i, group[2][2], group[0], group[1], group[2][0])
         if step < len(beside):
             beside[step]()
         if waiting is not None:
-            landed = landed + land(*waiting[0:2])
+            landed = landed + land(waiting[1], *waiting[2][0:2])
         waiting = group
 
     dcat_ref[width : 2 * width] = landed[:, 0:nodes].astype(BF16)
@@ -464,9 +473,7 @@
 
 
 def piece_owner(core, half, place, kind):
-    plane_first = ((place >> 2) << 1) | ((place & 3) << 3)
-    line_first = ((place >> 2) << 3) | ((place & 3) << 1)
-    choice = [plane_first if k == PLANE else line_first for k in kind]
+    choice = [((0,) + MASKS[k])[place >> 2] | ((0,) + MASKS[1 - k])[place & 3] for k in kind]
     return half + jnp.where(core == half, *choice)
 
 
@@ -510,14 +517,14 @@
 
 def backward_first_kernel(
     layer, recv_ref, dv_ref, dh_ref, u_ref, norm_ref, gain_ref, bias_ref, wmix_ref, wpost_ref, wpre_ref,
-    b_ref, live_ref, rows_ref, g_ref, gt_ref, m_ref, s_ref, z_ref, y_ref, x_ref, u_low_ref, norm_low_ref,
-    gb_ref, dm_ref, dh_out_ref, dv_out_ref, part_ref, keep_ref, send_ref,
+    b_ref, live_ref, rows_ref, g_ref, gt_ref, ma_ref, mb_ref, mc_ref, md_ref, s_ref, z_ref, y_ref, x_ref, u_low_ref, norm_low_ref,
+    gb_ref, dma_ref, dmb_ref, dmc_ref, dmd_ref, dh_out_ref, dv_out_ref, part_ref, keep_ref, send_ref,
     du_ref, d_ref, dcat_ref, et_ref, ds_ref, bd_ref, grads_ref,
 ):
     dh = backward_layer(
         layer, recv_ref, dv_ref, dh_ref, u_ref, norm_ref, gain_ref, bias_ref, wmix_ref, wpost_ref, wpre_ref,
-        b_ref, live_ref, rows_ref, g_ref, gt_ref, m_ref, s_ref,
-        gb_ref, du_ref, d_ref, dm_ref, dcat_ref, et_ref, ds_ref, bd_ref,
+        b_ref, live_ref, rows_ref, g_ref, gt_ref, (ma_ref, mb_ref, mc_ref, md_ref), s_ref,
+        gb_ref, du_ref, d_ref, (dma_ref, dmb_ref, dmc_ref, dmd_ref), dcat_ref, et_ref, ds_ref, bd_ref,
         grad_steps(d_ref, z_ref, y_ref, du_ref, grads_ref),
     )
     put_message_grads(layer, x_ref, dcat_ref, et_ref, grads_ref, keep_ref, send_ref)
@@ -528,14 +535,14 @@
 
 def backward_last_kernel(
     layer, recv_ref, dv_ref, dh_ref, u_ref, norm_ref, gain_ref, bias_ref, wmix_ref, wpost_ref, wpre_ref,
-    b_ref, live_ref, rows_ref, g_ref, gt_ref, m_ref, s_ref, z_ref, y_ref, x_ref,
-    gb_ref, dm_ref, dh_out_ref, keep_ref, send_ref,
+    b_ref, live_ref, rows_ref, g_ref, gt_ref, ma_ref, mb_ref, mc_ref, md_ref, s_ref, z_ref, y_ref, x_ref,
+    gb_ref, dma_ref, dmb_ref, dmc_ref, dmd_ref, dh_out_ref, keep_ref, send_ref,
     du_ref, d_ref, dcat_ref, et_ref, ds_ref, bd_ref, grads_ref,
 ):
     dh = backward_layer(
         layer, recv_ref, dv_ref, dh_ref, u_ref, norm_ref, gain_ref, bias_ref, wmix_ref, wpost_ref, wpre_ref,
-        b_ref, live_ref, rows_ref, g_ref, gt_ref, m_ref, s_ref,
-        gb_ref, du_ref, d_ref, dm_ref, dcat_ref, et_ref, ds_ref, bd_ref,
+        b_ref, live_ref, rows_ref, g_ref, gt_ref, (ma_ref, mb_ref, mc_ref, md_ref), s_ref,
+        gb_ref, du_ref, d_ref, (dma_ref, dmb_ref, dmc_ref, dmd_ref), dcat_ref, et_ref, ds_ref, bd_ref,
         grad_steps(d_ref, z_ref, y_ref, du_ref, grads_ref),
     )
     put_message_grads(layer, x_ref, dcat_ref, et_ref, grads_ref, keep_ref, send_ref)
@@ -543,18 +550,16 @@
 
 
 def edge_kernel(
-    dm0_ref, dm1_ref, wpre_ref, wedge_ref, gt_ref, h_ref, rows_ref, dh_ref, sums0_ref, sums1_ref,
+    a0_ref, b0_ref, c0_ref, d0_ref, a1_ref, b1_ref, c1_ref, d1_ref, wpre_ref, wedge_ref, gt_ref, h_ref, rows_ref, dh_ref, sums0_ref, sums1_ref,
     out_ref, readout_ref, node_ref, g_gain_ref, g_bias_ref, acc_ref,
 ):
-    width = dm0_ref.shape[0]
+    width = a0_ref.shape[0]
     nodes = gt_ref.shape[1]
     leaf_cols = LEAF_SLOTS * nodes
-    total = None
-    for layer, dm_ref in ((0, dm0_ref), (1, dm1_ref)):
-        w = mm(wedge_ref[layer], wpre_ref[layer, 2 * width :]).astype(BF16)
-        part = mm(w, dm_ref[...])
-        total = part if total is None else total + part
-    hub = total[:, leaf_cols:]
+    w0, w1 = (mm(wedge_ref[layer], wpre_ref[layer, 2 * width :]).astype(BF16) for layer in range(2))
+    pairs = ((a0_ref, a1_ref), (b0_ref, b1_ref), (c0_ref, c1_ref), (d0_ref, d1_ref))
+    hub, *groups = [mm(w0, lower[...]) + mm(w1, upper[...]) for lower, upper in pairs]
+    total = jnp.concatenate(groups, axis=1)
     for j in range(8):
         acc_ref[32 * j : 32 * j + 16] = hub[:, 128 * j : 128 * j + 128]
         acc_ref[32 * j + 16 : 32 * j + 32] = pltpu.roll(hub[:, 128 * j : 128 * j + 128], 64, 1)
@@ -604,8 +609,8 @@
 
 
 def finish_last_kernel(
-    post_in, mix_in, pre_in, other_et, half0_ref, half1_ref, wedge_ref, wpre_ref, post_out, mix_out, pre_out, gb_ref, gedge_ref,
-    post, mix, pre, et, term, sems,
+    post_in, mix_in, pre_in, other_et, half0_ref, half1_ref, wedge_ref, wpre_ref,
+    post_out, mix_out, pre_out, gb_out, gedge_out, post, mix, pre, et, term, gb_ref, gedge_ref, sems,
 ):
     del post_in, mix_in, pre_in
     copies = finish_half(1, (half0_ref, half1_ref), (post_out, mix_out, pre_out), (post, mix, pre, et), sems)
@@ -625,7 +630,8 @@
         term[layer] = grad.reshape(term.shape[1:])
         parts = mm(three, wpre_ref[layer, 2 * width :], NT)
         gedge_ref[layer] = parts[0:16] + parts[16:32] + parts[32:48]
-    copies += start_copies([(term, pre_out.at[:, 2])], sems.at[3:4])
+    pairs = [(term, pre_out.at[:, 2]), (gedge_ref, gedge_out), (gb_ref, gb_out)]
+    copies += start_copies(pairs, sems.at[3:6])
     wait_all(copies)
 
 
@@ -672,21 +678,22 @@
     def exchange(part):
         return lax.all_to_all(part, "dp", 0, 0, tiled=True)
 
-    m_s, s_s, z_s = s((width, cols)), s((4, width, lanes)), s((4 * 320, lanes), BF16)
+    spans = [hi - lo for lo, hi, _ in column_groups(nodes)]
+    m_s, s_s, z_s = [s((width, n)) for n in spans], s((4, width, lanes)), s((4 * 320, lanes), BF16)
     b_s = s((inner, cols), BF16)
     row_s, low_s = s((width, nodes)), s((width, nodes), BF16)
-    layer_outs = [m_s, s_s, z_s, low_s, row_s, s((devices, 1, 2 * width + 128))]
+    layer_outs = [*m_s, s_s, z_s, low_s, row_s, s((devices, 1, 2 * width + 128))]
     fwd_scratch = like([s((width, inner), BF16), s((width, lanes), BF16), s((width, lanes))])
     table_outs = [b_s, s((2, cols)), s((8, lanes)), s((nodes, 128), BF16), s((128, nodes), BF16)]
     first_args = [node_feats, edge_feats, segment_ids, nbr_t, mask_t, degrees, w_edge, w_pre, b_pre, wpost_t, w_mix]
-    x0, b, live, rows, g, gt, m0, s0, z0, y0, u0, part = call(
+    x0, b, live, rows, g, gt, *m0, s0, z0, y0, u0, part = call(
         functools.partial(forward_first_kernel, 0),
         first_args, [low_s] + table_outs + layer_outs,
         fwd_scratch + like([a[0:1] if i in (7, 9, 10) else a for i, a in enumerate(first_args)]) + [dma(11)], range(11),
     )
     tables = [b, live, rows, g, gt]
     recv = exchange(part)
-    norm0, h1, x1, m1, s1, z1, y1, u1, part = call(
+    norm0, h1, x1, *m1, s1, z1, y1, u1, part = call(
         functools.partial(forward_next_kernel, 1),
         [recv, u0, x0, bn_gain, bn_bias, w_edge, w_pre, b_pre, wpost_t, w_mix] + tables,
         [s((8, width)), row_s, low_s] + layer_outs,
@@ -700,17 +707,17 @@
         [s((8, width)), row_s, row_s, row_s, sums_out],
     )
     sum_s = s((1, 2 * width))
-    du_s, d_s, dm_s = low_s, s((4 * 192, lanes), BF16), s((width, cols), BF16)
+    du_s, d_s, dm_s = low_s, s((4 * 192, lanes), BF16), [s((width, n), BF16) for n in spans]
     dcat_s, et_s = s((3 * width, nodes), BF16), s((width, 64))
     back_scratch = like([s_s, s((width, width), BF16)])
     recv = exchange(part)
     grad_cols = 1664
     grad_s, half_s = s((width, grad_cols)), s((width // 2, grad_cols))
     back_scratch = like([du_s, d_s, dcat_s, et_s]) + back_scratch + like([grad_s])
-    sums1, dm1, dh1, dv0, part, keep1, send1 = call(
+    sums1, *dm1, dh1, dv0, part, keep1, send1 = call(
         functools.partial(backward_first_kernel, 1),
-        [recv, dv1, dh2, u1, norm1, bn_gain, bn_bias, w_mix, wpost_t, w_pre] + tables + [m1, s1, z1, y1, x1, u0, norm0],
-        [sum_s, dm_s, row_s, row_s, sums_out, half_s, half_s],
+        [recv, dv1, dh2, u1, norm1, bn_gain, bn_bias, w_mix, wpost_t, w_pre] + tables + [*m1, s1, z1, y1, x1, u0, norm0],
+        [sum_s, *dm_s, row_s, row_s, sums_out, half_s, half_s],
         back_scratch,
     )
 
@@ -741,22 +748,24 @@
     got1 = swap(send1, (1, 1))
     recv, got1 = together(exchange(part), got1)
     part1 = scatter_sum(keep1 + got1, larger(SUM_KINDS[1]), 32)
-    sums0, dm0, dh0, keep0, send0 = call(
+    sums0, *dm0, dh0, keep0, send0 = call(
         functools.partial(backward_last_kernel, 0),
-        [recv, dv0, dh1, u0, norm0, bn_gain, bn_bias, w_mix, wpost_t, w_pre] + tables + [m0, s0, z0, y0, x0],
-        [sum_s, dm_s, row_s, half_s, half_s],
+        [recv, dv0, dh1, u0, norm0, bn_gain, bn_bias, w_mix, wpost_t, w_pre] + tables + [*m0, s0, z0, y0, x0],
+        [sum_s, *dm_s, row_s, half_s, half_s],
         back_scratch, cost=8,
     )
     edge_grad, readout, node_grad, g_gain, g_bias = call(
-        edge_kernel, [dm0, dm1, w_pre, w_edge, gt, h2, rows, dh0, sums0, sums1],
+        edge_kernel, [*dm0, *dm1, w_pre, w_edge, gt, h2, rows, dh0, sums0, sums1],
         [s((nodes, width)), s(readout_grad.shape), s((nodes, width)), s(bn_gain.shape), s(bn_bias.shape)],
         [pltpu.VMEM((width, 128), F32)], free=range(5), cost=2,
     )
     send0, part1, edge_grad, readout = together(send0, part1, edge_grad, readout)
     got0 = swap(send0, (1, 1))
     half0 = keep0 + got0
-    part0 = scatter_sum(half0, larger(SUM_KINDS[0]), 32)
-    part1 = gather(spread(scatter_sum(part1, smaller(SUM_KINDS[1]), 8)), smaller(GATHER_KINDS[1]))
+    outer = [swap(half0[32 * (i + 1) : 32 * (i + 2)], m) for i, m in enumerate(larger(SUM_KINDS[0]))]
+    part0 = half0[0:32] + outer[0] + outer[1] + outer[2]
+    part1 = spread(scatter_sum(part1, smaller(SUM_KINDS[1]), 8))
+    part1 = gather(together(part1, outer[0])[0], smaller(GATHER_KINDS[1]))
     part1 = relay(together(part1, part0)[0], larger(GATHER_KINDS[1]))
     part0 = spread(scatter_sum(part0, smaller(SUM_KINDS[0]), 8))
     part0 = gather(gather(part0, smaller(GATHER_KINDS[0])), larger(GATHER_KINDS[0]))
@@ -773,8 +782,8 @@
     )
     g_post_t, g_mix, g_pre, g_b, g_edge = call(
         finish_last_kernel, [*finals_in, ets_first, other0, other1, w_edge, w_pre], finals + [s(b_pre.shape), s(w_edge.shape)],
-        like(bufs + [ets, s((layers, blocks, 2, 8, width))]) + [dma(4)],
-        far=(0, 1, 2), far_out=(0, 1, 2), free=(3, 4), alias={0: 0, 1: 1, 2: 2},
+        like(bufs + [ets, s((layers, blocks, 2, 8, width)), s(b_pre.shape), s(w_edge.shape)]) + [dma(6)],
+        far=(0, 1, 2), far_out=range(5), alias={0: 0, 1: 1, 2: 2},
     )
     g_post = jnp.swapaxes(g_post_t.reshape(wpost_t.shape), 2, 3)
     g_mix, g_pre = g_mix.reshape(w_mix.shape), g_pre.reshape(w_pre.shape)

time: 125 us -> 124 us (level)
  starting transfers between devices: 32.3 us -> 28.9 us
  waiting for transfers between devices: 16.9 us -> 19.8 us
    ppermute x28, starting transfers between devices: 32.3 us -> 28.9 us  [swap(): lax.ppermute(value, 'dp', [(i, i ^ masks[i & 1]) for i in range(devices)])]
    ppermute x28, waiting for transfers between devices: 16.9 us -> 19.8 us  [swap(): lax.ppermute(value, 'dp', [(i, i ^ masks[i & 1]) for i in range(devices)])]
where the time goes in v6:
time: 124 us
  blocking collectives  42.2 us (34%)
  Pallas kernels  30.9 us (25%)
  starting transfers between devices  28.9 us (23%)
  waiting for transfers between devices  19.8 us (16%)
    all_to_all x4, blocking collectives, exchange(): return lax.all_to_all(part, 'dp', 0, 0, tiled=True)  42.2 us
    pallas_call x8, Pallas kernels, call(): pl.pallas_call(kernel, in_specs=[hbm if i in far else vmem for i in range...  30.9 us
    ppermute x28, starting transfers between devices, swap(): lax.ppermute(value, 'dp', [(i, i ^ masks[i & 1]) for i in range(devices)])  28.9 us
    ppermute x28, waiting for transfers between devices, swap(): lax.ppermute(value, 'dp', [(i, i ^ masks[i & 1]) for i in range(devices)])  19.8 us
  transfers between devices with their start and end apart: 28, of which 12 were waited for; matrix products, arithmetic and copies ran while one was open for 0% of the time, Pallas kernels for 8%

profile of v6, /device:TPU:0, one launch (start us, length us, event | category | flops | bytes accessed | tf_op | source)
XLA Modules:
  0.0 123.6 jit_solution(17348755315861711416)
XLA Ops:
  0.7 7.0 %shard_map.213 = (bf16[256,640]{1,0:T(8,128)(2,1)S(1)}, bf16[704,3584]{1,0:T(8,128)(2,1)S(1)}, f32[2,3584]{1,0:T(2,128)S(1)}, f32[8,768]{1,0:T(8,128)S(1)}, bf16...) custom-call(bf16[640,256]{1,0:T(8,128)(2,1)} %nf_hbm.1, ...), custom_call_target="tpu_custom_call" | custom-call | tf_op jit(solution)/shard_map/pallas_call | solution.py:658
  7.7 14.7 %all_to_all.20.recv_ref = f32[32,1,640]{2,1,0:T(1,128)S(1)} all-to-all(f32[32,1,640]{2,1,0:T(1,128)S(1)} %get-tuple-element.82), channel_id=1, replica_groups=mesh['dp'=32] {'dp'}, dimensions={0} | all-to-all | bytes 163840 | tf_op jit(solution)/shard_map/all_to_all | solution.py:679
  22.5 5.6 %shard_map.214 = (f32[8,256]{1,0:T(8,128)S(1)}, f32[256,640]{1,0:T(8,128)S(1)}, bf16[256,640]{1,0:T(8,128)(2,1)S(1)}, f32[256,1024]{1,0:T(8,128)S(1)}, f32[256,1...) custom-call(f32[32,1,640]{2,1,0:T(1,128)S(1)} %all_to_all.20.recv_re, ...), custom_call_target="tpu_custom_call" | custom-call | tf_op jit(solution)/shard_map/pallas_call | solution.py:658
  28.0 9.3 %all_to_all.21.recv_ref = f32[32,1,640]{2,1,0:T(1,128)S(1)} all-to-all(f32[32,1,640]{2,1,0:T(1,128)S(1)} %get-tuple-element.90), channel_id=1, replica_groups=mesh['dp'=32] {'dp'}, dimensions={0} | all-to-all | bytes 163840 | tf_op jit(solution)/shard_map/all_to_all | solution.py:679
  37.3 1.2 shard_map.215
  38.5 9.1 %all_to_all.22.recv_ref = f32[32,1,512]{2,1,0:T(1,128)S(1)} all-to-all(f32[32,1,512]{2,1,0:T(1,128)S(1)} %get-tuple-element.93), channel_id=1, replica_groups=mesh['dp'=32] {'dp'}, dimensions={0} | all-to-all | bytes 131072 | tf_op jit(solution)/shard_map/all_to_all | solution.py:679
  47.7 6.2 %shard_map.216 = (f32[1,512]{1,0:T(1,128)S(1)}, bf16[256,1024]{1,0:T(8,128)(2,1)S(1)}, bf16[256,1024]{1,0:T(8,128)(2,1)S(1)}, bf16[256,1024]{1,0:T(8,128)(2,1)S(...) custom-call(f32[32,1,512]{2,1,0:T(1,128)S(1)} %all_to_all.22.recv_re, ...), custom_call_target="tpu_custom_call" | custom-call | tf_op jit(solution)/shard_map/pallas_call | solution.py:658
  54.1 9.1 %all_to_all.23.recv_ref = f32[32,1,512]{2,1,0:T(1,128)S(1)} all-to-all(f32[32,1,512]{2,1,0:T(1,128)S(1)} %get-tuple-element.106), channel_id=1, replica_groups=mesh['dp'=32] {'dp'}, dimensions={0} | all-to-all | bytes 131072 | tf_op jit(solution)/shard_map/all_to_all | solution.py:679
  64.0 1.3 %collective-permute-start.3 = (f32[32,1664]{1,0:T(8,128)S(1)}, f32[32,1664]{1,0:T(8,128)S(1)}, u32[]{:S(2)}, u32[]{:S(2)}) collective-permute-start(f32[32,1664]{1,0:T(8,128)S(1)} %get-tuple-element.160), channel_id=1, source_target_pairs={{0,6},{1,25},{2,4},{3,27},{4,2},{5,29},{6,0},{7,31},{8,14},{9,17},... | collective-permute-start | bytes 638984 | tf_op jit(solution)/shard_map/ppermute | solution.py:725
  65.3 1.6 %collective-permute-start.2 = (f32[32,1664]{1,0:T(8,128)S(1)}, f32[32,1664]{1,0:T(8,128)S(1)}, u32[]{:S(2)}, u32[]{:S(2)}) collective-permute-start(f32[32,1664]{1,0:T(8,128)S(1)} %get-tuple-element.161), channel_id=1, source_target_pairs={{0,2},{1,9},{2,0},{3,11},{4,6},{5,13},{6,4},{7,15},{8,10},{9,1},{1... | collective-permute-start | bytes 638984 | tf_op jit(solution)/shard_map/ppermute | solution.py:725
  66.9 5.8 %shard_map.217 = (f32[1,512]{1,0:T(1,128)S(1)}, bf16[256,1024]{1,0:T(8,128)(2,1)S(1)}, bf16[256,1024]{1,0:T(8,128)(2,1)S(1)}, bf16[256,1024]{1,0:T(8,128)(2,1)S(...) custom-call(f32[32,1,512]{2,1,0:T(1,128)S(1)} %all_to_all.23.recv_re, ...), custom_call_target="tpu_custom_call" | custom-call | flops 8000000000 | tf_op jit(solution)/shard_map/pallas_call | solution.py:658
  72.7 2.4 %shard_map.218 = (f32[640,256]{1,0:T(8,128)}, f32[4,256]{1,0:T(4,128)}, f32[640,256]{1,0:T(8,128)}, f32[2,256]{1,0:T(2,128)}, f32[2,256]{1,0:T(2,128)}) custom-call(bf16[256,1024]{1,0:T(8,128)(2,1)S(1)} %get-tuple-element.121.a0_ref, bf16[256,1024]{1,0:T(8,128)(2,1)S(1)} %get-tuple-element.122.b0_ref, bf16[256,1024]{1,0:T(8,128)(2,1)S(1)} %get-tuple-element.123.c0_ref, ...), custom_call_target="tpu_custom_call" | custom-call | flops 2000000000 | tf_op jit(solution)/shard_map/pallas_call | solution.py:658
  76.0 2.5 %collective-permute-start.19 = (f32[8,1664]{1,0:T(8,128)S(1)}, f32[8,1664]{1,0:T(8,128)S(1)}, u32[]{:S(2)}, u32[]{:S(2)}) collective-permute-start(f32[8,1664]{1,0:T(8,128)S(1)} %get-tuple-element.163), channel_id=1, source_target_pairs={{0,24},{1,7},{2,26},{3,5},{4,28},{5,3},{6,30},{7,1},{8,16},{9,15},... | collective-permute-start | bytes 159752 | tf_op jit(solution)/shard_map/ppermute | solution.py:725
  79.9 1.4 %collective-permute-start.7 = (f32[32,1664]{1,0:T(8,128)S(1)}, f32[32,1664]{1,0:T(8,128)S(1)}, u32[]{:S(2)}, u32[]{:S(2)}) collective-permute-start(f32[32,1664]{1,0:T(8,128)S(1)} %get-tuple-element.157), channel_id=1, source_target_pairs={{0,6},{1,25},{2,4},{3,27},{4,2},{5,29},{6,0},{7,31},{8,14},{9,17},... | collective-permute-start | bytes 638984 | tf_op jit(solution)/shard_map/ppermute | solution.py:725
  81.2 1.3 %collective-permute-start.6 = (f32[32,1664]{1,0:T(8,128)S(1)}, f32[32,1664]{1,0:T(8,128)S(1)}, u32[]{:S(2)}, u32[]{:S(2)}) collective-permute-start(f32[32,1664]{1,0:T(8,128)S(1)} %get-tuple-element.158), channel_id=1, source_target_pairs={{0,2},{1,9},{2,0},{3,11},{4,6},{5,13},{6,4},{7,15},{8,10},{9,1},{1... | collective-permute-start | bytes 638984 | tf_op jit(solution)/shard_map/ppermute | solution.py:725
  83.0 4.2 %collective-permute-done.5 = f32[32,1664]{1,0:T(8,128)S(1)} collective-permute-done((f32[32,1664]{1,0:T(8,128)S(1)}, f32[32,1664]{1,0:T(8,128)S(1)}, u32[]{:S(2)}, u32[]{:S(2)}) %collective-permute-start.5) | collective-permute-done | bytes 213024 | tf_op jit(solution)/shard_map/ppermute | solution.py:725
  88.2 1.1 collective-permute-start.21
  89.3 2.3 %collective-permute-start.20 = (f32[8,1664]{1,0:T(8,128)S(1)}, f32[8,1664]{1,0:T(8,128)S(1)}, u32[]{:S(2)}, u32[]{:S(2)}) collective-permute-start(f32[8,1664]{1,0:T(8,128)S(1)} %add_add_fusion), channel_id=1, source_target_pairs={{0,16},{1,17},{2,18},{3,19},{4,20},{5,21},{6,22},{7,23},{8,24},{9,... | collective-permute-start | bytes 159752 | tf_op jit(solution)/shard_map/ppermute | solution.py:725
  92.4 2.5 %collective-permute-start.10 = (f32[8,1664]{1,0:T(8,128)S(1)}, f32[8,1664]{1,0:T(8,128)S(1)}, u32[]{:S(2)}, u32[]{:S(2)}) collective-permute-start(f32[8,1664]{1,0:T(8,128)S(1)} %get-tuple-element.166), channel_id=1, source_target_pairs={{0,24},{1,7},{2,26},{3,5},{4,28},{5,3},{6,30},{7,1},{8,16},{9,15},... | collective-permute-start | bytes 159752 | tf_op jit(solution)/shard_map/ppermute | solution.py:725
  95.2 1.2 collective-permute-done.20
  99.1 1.9 %collective-permute-start.13 = (f32[8,1664]{1,0:T(8,128)S(1)}, f32[8,1664]{1,0:T(8,128)S(1)}, u32[]{:S(2)}, u32[]{:S(2)}) collective-permute-start(f32[8,1664]{1,0:T(8,128)S(1)} %get-tuple-element.155), channel_id=1, source_target_pairs={{0,24},{1,7},{2,26},{3,5},{4,28},{5,3},{6,30},{7,1},{8,16},{9,15},... | collective-permute-start | bytes 159752 | tf_op jit(solution)/shard_map/ppermute | solution.py:725
  101.0 2.5 %collective-permute-start.11 = (f32[8,1664]{1,0:T(8,128)S(1)}, f32[8,1664]{1,0:T(8,128)S(1)}, u32[]{:S(2)}, u32[]{:S(2)}) collective-permute-start(f32[8,1664]{1,0:T(8,128)S(1)} %get-tuple-element.155), channel_id=1, source_target_pairs={{0,16},{1,5},{2,18},{3,7},{4,20},{5,1},{6,22},{7,3},{8,24},{9,13},... | collective-permute-start | bytes 159752 | tf_op jit(solution)/shard_map/ppermute | solution.py:725
  103.5 1.6 %collective-permute-done.13 = f32[8,1664]{1,0:T(8,128)S(1)} collective-permute-done((f32[8,1664]{1,0:T(8,128)S(1)}, f32[8,1664]{1,0:T(8,128)S(1)}, u32[]{:S(2)}, u32[]{:S(2)}) %collective-permute-start.13) | collective-permute-done | bytes 53280 | tf_op jit(solution)/shard_map/ppermute | solution.py:725
  105.1 1.1 collective-permute-done.12
  106.2 1.4 %collective-permute-start.16 = (f32[32,1664]{1,0:T(8,128)S(1)}, f32[32,1664]{1,0:T(8,128)S(1)}, u32[]{:S(2)}, u32[]{:S(2)}) collective-permute-start(f32[32,1664]{1,0:T(8,128)S(1)} %pad_maximum_fusion), channel_id=1, source_target_pairs={{0,6},{1,25},{2,4},{3,27},{4,2},{5,29},{6,0},{7,31},{8,14},{9,17},... | collective-permute-start | bytes 638984 | tf_op jit(solution)/shard_map/ppermute | solution.py:725
  107.7 1.2 collective-permute-start.15
  109.8 1.1 collective-permute-start.25
  111.0 4.4 %collective-permute-done.14 = f32[32,1664]{1,0:T(8,128)S(1)} collective-permute-done((f32[32,1664]{1,0:T(8,128)S(1)}, f32[32,1664]{1,0:T(8,128)S(1)}, u32[]{:S(2)}, u32[]{:S(2)}) %collective-permute-start.14) | collective-permute-done | bytes 213024 | tf_op jit(solution)/shard_map/ppermute | solution.py:725
  115.4 1.9 %collective-permute-done.15 = f32[32,1664]{1,0:T(8,128)S(1)} collective-permute-done((f32[32,1664]{1,0:T(8,128)S(1)}, f32[32,1664]{1,0:T(8,128)S(1)}, u32[]{:S(2)}, u32[]{:S(2)}) %collective-permute-start.15) | collective-permute-done | bytes 213024 | tf_op jit(solution)/shard_map/ppermute | solution.py:725
  117.4 2.1 %collective-permute-done.25 = f32[32,1664]{1,0:T(8,128)S(1)} collective-permute-done((f32[32,1664]{1,0:T(8,128)S(1)}, f32[32,1664]{1,0:T(8,128)S(1)}, u32[]{:S(2)}, u32[]{:S(2)}) %collective-permute-start.25) | collective-permute-done | bytes 213024 | tf_op jit(solution)/shard_map/ppermute | solution.py:725
  119.6 1.3 %shard_map.219 = (f32[2,16,2,8,832]{4,3,2,1,0:T(8,128)}, f32[2,16,2,8,256]{4,3,2,1,0:T(8,128)}, f32[2,3,16,2,8,256]{5,4,3,2,1,0:T(8,128)}, f32[2,16,8,64]{3,2,1,0:T(8,128)S(1)}) custom-call(f32[128,1664]{1,0:T(8,128)S(1)} %constant_dynamic-update-slice_fusion.half0_ref, f32[128,1664]{1,0:T(8,128)S(1)} %constant_dynamic-update-slice_fusion.7.half1_ref), custom_call_target="tpu_custom_call" | custom-call | flops 2000000000 | tf_op jit(solution)/shard_map/pallas_call | solution.py:658
  122.0 1.5 %shard_map.220 = (f32[2,16,2,8,832]{4,3,2,1,0:T(8,128)}, f32[2,16,2,8,256]{4,3,2,1,0:T(8,128)}, f32[2,3,16,2,8,256]{5,4,3,2,1,0:T(8,128)}, f32[2,256]{1,0:T(2,128)}, f32[2,16,256]{2,1,0:T(8,128)}) custom-call(f32[2,16,2,8,832]{4,3,2,1,0:T(8,128)} %get-tuple-element.143.post_in, ...), custom_call_target="tpu_custom_call", output_to_operand_aliasing={{0}: (0, {}), {1}: (1, {}), {2}: (2, {})} | custom-call | tf_op jit(solution)/shard_map/pallas_call | solution.py:658
  (74 shorter events, 10.7 us)
Async XLA Ops:
  0.6 21.8 %copy-start = (bf16[2,768,256]{2,1,0:T(8,128)(2,1)S(1)}, bf16[2,768,256]{2,1,0:T(8,128)(2,1)}, u32[]{:S(2)}) copy-start(bf16[2,768,256]{2,1,0:T(8,128)(2,1)} %wpre_ref.9) | copy-start | bytes 2359300
  0.7 21.8 %copy-start.2 = (bf16[2,256,256]{2,1,0:T(8,128)(2,1)S(1)}, bf16[2,256,256]{2,1,0:T(8,128)(2,1)}, u32[]{:S(2)}) copy-start(bf16[2,256,256]{2,1,0:T(8,128)(2,1)} %wmix_ref.5) | copy-start | bytes 786436
  0.7 21.8 %copy-start.3 = (bf16[2,16,256]{2,1,0:T(8,128)(2,1)S(1)}, bf16[2,16,256]{2,1,0:T(8,128)(2,1)}, u32[]{:S(2)}) copy-start(bf16[2,16,256]{2,1,0:T(8,128)(2,1)} %wedge_ref.5) | copy-start | bytes 49156
  0.7 21.8 %copy-start.6 = (f32[2,256]{1,0:T(2,128)S(1)}, f32[2,256]{1,0:T(2,128)}, u32[]{:S(2)}) copy-start(f32[2,256]{1,0:T(2,128)} %bpre_ref.1) | copy-start | bytes 6148
  53.9 9.3 %collective-permute-start = (f32[128,1664]{1,0:T(8,128)S(1)}, f32[128,1664]{1,0:T(8,128)S(1)}, u32[]{:S(2)}, u32[]{:S(2)}) collective-permute-start(f32[128,1664]{1,0:T(8,128)S(1)} %get-tuple-element.107), channel_id=1, source_target_pairs={{0,1},{1,0},{2,3},{3,2},{4,5},{5,4},{6,7},{7,6},{8,9},{9,8},{10,11... | collective-permute-start | bytes 2555912 | tf_op jit(solution)/shard_map/ppermute | solution.py:725
  63.3 11.8 %collective-permute-start.1 = (f32[32,1664]{1,0:T(8,128)S(1)}, f32[32,1664]{1,0:T(8,128)S(1)}, u32[]{:S(2)}, u32[]{:S(2)}) collective-permute-start(f32[32,1664]{1,0:T(8,128)S(1)} %get-tuple-element.159), channel_id=1, source_target_pairs={{0,4},{1,17},{2,6},{3,19},{4,0},{5,21},{6,2},{7,23},{8,12},{9,25},... | collective-permute-start | bytes 638984 | tf_op jit(solution)/shard_map/ppermute | solution.py:725
  64.0 11.1 %collective-permute-start.3 = (f32[32,1664]{1,0:T(8,128)S(1)}, f32[32,1664]{1,0:T(8,128)S(1)}, u32[]{:S(2)}, u32[]{:S(2)}) collective-permute-start(f32[32,1664]{1,0:T(8,128)S(1)} %get-tuple-element.160), channel_id=1, source_target_pairs={{0,6},{1,25},{2,4},{3,27},{4,2},{5,29},{6,0},{7,31},{8,14},{9,17},... | collective-permute-start | bytes 638984 | tf_op jit(solution)/shard_map/ppermute | solution.py:725
  65.3 9.8 %collective-permute-start.2 = (f32[32,1664]{1,0:T(8,128)S(1)}, f32[32,1664]{1,0:T(8,128)S(1)}, u32[]{:S(2)}, u32[]{:S(2)}) collective-permute-start(f32[32,1664]{1,0:T(8,128)S(1)} %get-tuple-element.161), channel_id=1, source_target_pairs={{0,2},{1,9},{2,0},{3,11},{4,6},{5,13},{6,4},{7,15},{8,10},{9,1},{1... | collective-permute-start | bytes 638984 | tf_op jit(solution)/shard_map/ppermute | solution.py:725
  75.1 3.7 %collective-permute-start.4 = (f32[128,1664]{1,0:T(8,128)S(1)}, f32[128,1664]{1,0:T(8,128)S(1)}, u32[]{:S(2)}, u32[]{:S(2)}) collective-permute-start(f32[128,1664]{1,0:T(8,128)S(1)} %get-tuple-element.139), channel_id=1, source_target_pairs={{0,1},{1,0},{2,3},{3,2},{4,5},{5,4},{6,7},{7,6},{8,9},{9,8},{10,11... | collective-permute-start | bytes 2555912 | tf_op jit(solution)/shard_map/ppermute | solution.py:725
  75.2 6.0 %collective-permute-start.17 = (f32[8,1664]{1,0:T(8,128)S(1)}, f32[8,1664]{1,0:T(8,128)S(1)}, u32[]{:S(2)}, u32[]{:S(2)}) collective-permute-start(f32[8,1664]{1,0:T(8,128)S(1)} %get-tuple-element.162), channel_id=1, source_target_pairs={{0,16},{1,5},{2,18},{3,7},{4,20},{5,1},{6,22},{7,3},{8,24},{9,13},... | collective-permute-start | bytes 159752 | tf_op jit(solution)/shard_map/ppermute | solution.py:725
  76.0 6.6 %collective-permute-start.19 = (f32[8,1664]{1,0:T(8,128)S(1)}, f32[8,1664]{1,0:T(8,128)S(1)}, u32[]{:S(2)}, u32[]{:S(2)}) collective-permute-start(f32[8,1664]{1,0:T(8,128)S(1)} %get-tuple-element.163), channel_id=1, source_target_pairs={{0,24},{1,7},{2,26},{3,5},{4,28},{5,3},{6,30},{7,1},{8,16},{9,15},... | collective-permute-start | bytes 159752 | tf_op jit(solution)/shard_map/ppermute | solution.py:725
  78.5 4.4 %collective-permute-start.18 = (f32[8,1664]{1,0:T(8,128)S(1)}, f32[8,1664]{1,0:T(8,128)S(1)}, u32[]{:S(2)}, u32[]{:S(2)}) collective-permute-start(f32[8,1664]{1,0:T(8,128)S(1)} %get-tuple-element.164), channel_id=1, source_target_pairs={{0,8},{1,3},{2,10},{3,1},{4,12},{5,7},{6,14},{7,5},{8,0},{9,11},{1... | collective-permute-start | bytes 159752 | tf_op jit(solution)/shard_map/ppermute | solution.py:725
  79.0 8.2 %collective-permute-start.5 = (f32[32,1664]{1,0:T(8,128)S(1)}, f32[32,1664]{1,0:T(8,128)S(1)}, u32[]{:S(2)}, u32[]{:S(2)}) collective-permute-start(f32[32,1664]{1,0:T(8,128)S(1)} %get-tuple-element.156), channel_id=1, source_target_pairs={{0,4},{1,17},{2,6},{3,19},{4,0},{5,21},{6,2},{7,23},{8,12},{9,25},... | collective-permute-start | bytes 638984 | tf_op jit(solution)/shard_map/ppermute | solution.py:725
  79.9 11.7 %collective-permute-start.7 = (f32[32,1664]{1,0:T(8,128)S(1)}, f32[32,1664]{1,0:T(8,128)S(1)}, u32[]{:S(2)}, u32[]{:S(2)}) collective-permute-start(f32[32,1664]{1,0:T(8,128)S(1)} %get-tuple-element.157), channel_id=1, source_target_pairs={{0,6},{1,25},{2,4},{3,27},{4,2},{5,29},{6,0},{7,31},{8,14},{9,17},... | collective-permute-start | bytes 638984 | tf_op jit(solution)/shard_map/ppermute | solution.py:725
  81.2 10.3 %collective-permute-start.6 = (f32[32,1664]{1,0:T(8,128)S(1)}, f32[32,1664]{1,0:T(8,128)S(1)}, u32[]{:S(2)}, u32[]{:S(2)}) collective-permute-start(f32[32,1664]{1,0:T(8,128)S(1)} %get-tuple-element.158), channel_id=1, source_target_pairs={{0,2},{1,9},{2,0},{3,11},{4,6},{5,13},{6,4},{7,15},{8,10},{9,1},{1... | collective-permute-start | bytes 638984 | tf_op jit(solution)/shard_map/ppermute | solution.py:725
  87.2 7.7 %collective-permute-start.22 = (f32[8,1664]{1,0:T(8,128)S(1)}, f32[8,1664]{1,0:T(8,128)S(1)}, u32[]{:S(2)}, u32[]{:S(2)}) collective-permute-start(f32[8,1664]{1,0:T(8,128)S(1)} %add_add_fusion), channel_id=1, source_target_pairs={{0,24},{1,25},{2,26},{3,27},{4,28},{5,29},{6,30},{7,31},{8,16},{9,... | collective-permute-start | bytes 159752 | tf_op jit(solution)/shard_map/ppermute | solution.py:725
  88.2 7.0 %collective-permute-start.21 = (f32[8,1664]{1,0:T(8,128)S(1)}, f32[8,1664]{1,0:T(8,128)S(1)}, u32[]{:S(2)}, u32[]{:S(2)}) collective-permute-start(f32[8,1664]{1,0:T(8,128)S(1)} %add_add_fusion), channel_id=1, source_target_pairs={{0,8},{1,9},{2,10},{3,11},{4,12},{5,13},{6,14},{7,15},{8,0},{9,1},... | collective-permute-start | bytes 159752 | tf_op jit(solution)/shard_map/ppermute | solution.py:725
  89.3 7.1 %collective-permute-start.20 = (f32[8,1664]{1,0:T(8,128)S(1)}, f32[8,1664]{1,0:T(8,128)S(1)}, u32[]{:S(2)}, u32[]{:S(2)}) collective-permute-start(f32[8,1664]{1,0:T(8,128)S(1)} %add_add_fusion), channel_id=1, source_target_pairs={{0,16},{1,17},{2,18},{3,19},{4,20},{5,21},{6,22},{7,23},{8,24},{9,... | collective-permute-start | bytes 159752 | tf_op jit(solution)/shard_map/ppermute | solution.py:725
  91.6 5.9 %collective-permute-start.8 = (f32[8,1664]{1,0:T(8,128)S(1)}, f32[8,1664]{1,0:T(8,128)S(1)}, u32[]{:S(2)}, u32[]{:S(2)}) collective-permute-start(f32[8,1664]{1,0:T(8,128)S(1)} %get-tuple-element.165), channel_id=1, source_target_pairs={{0,16},{1,5},{2,18},{3,7},{4,20},{5,1},{6,22},{7,3},{8,24},{9,13},... | collective-permute-start | bytes 159752 | tf_op jit(solution)/shard_map/ppermute | solution.py:725
  92.4 6.0 %collective-permute-start.10 = (f32[8,1664]{1,0:T(8,128)S(1)}, f32[8,1664]{1,0:T(8,128)S(1)}, u32[]{:S(2)}, u32[]{:S(2)}) collective-permute-start(f32[8,1664]{1,0:T(8,128)S(1)} %get-tuple-element.166), channel_id=1, source_target_pairs={{0,24},{1,7},{2,26},{3,5},{4,28},{5,3},{6,30},{7,1},{8,16},{9,15},... | collective-permute-start | bytes 159752 | tf_op jit(solution)/shard_map/ppermute | solution.py:725
  94.9 4.1 %collective-permute-start.9 = (f32[8,1664]{1,0:T(8,128)S(1)}, f32[8,1664]{1,0:T(8,128)S(1)}, u32[]{:S(2)}, u32[]{:S(2)}) collective-permute-start(f32[8,1664]{1,0:T(8,128)S(1)} %get-tuple-element.167), channel_id=1, source_target_pairs={{0,8},{1,3},{2,10},{3,1},{4,12},{5,7},{6,14},{7,5},{8,0},{9,11},{1... | collective-permute-start | bytes 159752 | tf_op jit(solution)/shard_map/ppermute | solution.py:725
  96.4 14.5 %collective-permute-start.24 = (f32[32,1664]{1,0:T(8,128)S(1)}, f32[32,1664]{1,0:T(8,128)S(1)}, u32[]{:S(2)}, u32[]{:S(2)}) collective-permute-start(f32[32,1664]{1,0:T(8,128)S(1)} %pad_maximum_fusion.1), channel_id=1, source_target_pairs={{0,2},{1,3},{2,0},{3,1},{4,6},{5,7},{6,4},{7,5},{8,10},{9,11},{10,... | collective-permute-start | bytes 638984 | tf_op jit(solution)/shard_map/ppermute | solution.py:725
  97.0 12.8 %collective-permute-start.23 = (f32[32,1664]{1,0:T(8,128)S(1)}, f32[32,1664]{1,0:T(8,128)S(1)}, u32[]{:S(2)}, u32[]{:S(2)}) collective-permute-start(f32[32,1664]{1,0:T(8,128)S(1)} %pad_maximum_fusion.1), channel_id=1, source_target_pairs={{0,4},{1,5},{2,6},{3,7},{4,0},{5,1},{6,2},{7,3},{8,12},{9,13},{10,... | collective-permute-start | bytes 638984 | tf_op jit(solution)/shard_map/ppermute | solution.py:725
  99.1 6.0 %collective-permute-start.13 = (f32[8,1664]{1,0:T(8,128)S(1)}, f32[8,1664]{1,0:T(8,128)S(1)}, u32[]{:S(2)}, u32[]{:S(2)}) collective-permute-start(f32[8,1664]{1,0:T(8,128)S(1)} %get-tuple-element.155), channel_id=1, source_target_pairs={{0,24},{1,7},{2,26},{3,5},{4,28},{5,3},{6,30},{7,1},{8,16},{9,15},... | collective-permute-start | bytes 159752 | tf_op jit(solution)/shard_map/ppermute | solution.py:725
  101.0 5.2 %collective-permute-start.12 = (f32[8,1664]{1,0:T(8,128)S(1)}, f32[8,1664]{1,0:T(8,128)S(1)}, u32[]{:S(2)}, u32[]{:S(2)}) collective-permute-start(f32[8,1664]{1,0:T(8,128)S(1)} %get-tuple-element.155), channel_id=1, source_target_pairs={{0,8},{1,3},{2,10},{3,1},{4,12},{5,7},{6,14},{7,5},{8,0},{9,11},{1... | collective-permute-start | bytes 159752 | tf_op jit(solution)/shard_map/ppermute | solution.py:725
  101.0 5.2 %collective-permute-start.11 = (f32[8,1664]{1,0:T(8,128)S(1)}, f32[8,1664]{1,0:T(8,128)S(1)}, u32[]{:S(2)}, u32[]{:S(2)}) collective-permute-start(f32[8,1664]{1,0:T(8,128)S(1)} %get-tuple-element.155), channel_id=1, source_target_pairs={{0,16},{1,5},{2,18},{3,7},{4,20},{5,1},{6,22},{7,3},{8,24},{9,13},... | collective-permute-start | bytes 159752 | tf_op jit(solution)/shard_map/ppermute | solution.py:725
  106.2 11.0 %collective-permute-start.16 = (f32[32,1664]{1,0:T(8,128)S(1)}, f32[32,1664]{1,0:T(8,128)S(1)}, u32[]{:S(2)}, u32[]{:S(2)}) collective-permute-start(f32[32,1664]{1,0:T(8,128)S(1)} %pad_maximum_fusion), channel_id=1, source_target_pairs={{0,6},{1,25},{2,4},{3,27},{4,2},{5,29},{6,0},{7,31},{8,14},{9,17},... | collective-permute-start | bytes 638984 | tf_op jit(solution)/shard_map/ppermute | solution.py:725
  107.7 9.6 %collective-permute-start.15 = (f32[32,1664]{1,0:T(8,128)S(1)}, f32[32,1664]{1,0:T(8,128)S(1)}, u32[]{:S(2)}, u32[]{:S(2)}) collective-permute-start(f32[32,1664]{1,0:T(8,128)S(1)} %pad_maximum_fusion), channel_id=1, source_target_pairs={{0,2},{1,9},{2,0},{3,11},{4,6},{5,13},{6,4},{7,15},{8,10},{9,1},{1... | collective-permute-start | bytes 638984 | tf_op jit(solution)/shard_map/ppermute | solution.py:725
  108.9 6.5 %collective-permute-start.14 = (f32[32,1664]{1,0:T(8,128)S(1)}, f32[32,1664]{1,0:T(8,128)S(1)}, u32[]{:S(2)}, u32[]{:S(2)}) collective-permute-start(f32[32,1664]{1,0:T(8,128)S(1)} %pad_maximum_fusion), channel_id=1, source_target_pairs={{0,4},{1,17},{2,6},{3,19},{4,0},{5,21},{6,2},{7,23},{8,12},{9,25},... | collective-permute-start | bytes 638984 | tf_op jit(solution)/shard_map/ppermute | solution.py:725
  109.8 9.7 %collective-permute-start.25 = (f32[32,1664]{1,0:T(8,128)S(1)}, f32[32,1664]{1,0:T(8,128)S(1)}, u32[]{:S(2)}, u32[]{:S(2)}) collective-permute-start(f32[32,1664]{1,0:T(8,128)S(1)} %collective-permute-done.23), channel_id=1, source_target_pairs={{0,2},{1,3},{2,0},{3,1},{4,6},{5,7},{6,4},{7,5},{8,10},{9,11},{10,... | collective-permute-start | bytes 638984 | tf_op jit(solution)/shard_map/ppermute | solution.py:725
  117.3 3.6 %collective-permute-start.26 = (f32[128,1664]{1,0:T(8,128)S(1)}, f32[128,1664]{1,0:T(8,128)S(1)}, u32[]{:S(2)}, u32[]{:S(2)}) collective-permute-start(f32[128,1664]{1,0:T(8,128)S(1)} %constant_dynamic-update-slice_fusion.half0_ref), channel_id=1, source_target_pairs={{0,1},{1,0},{2,3},{3,2},{4,5},{5,4},{6,7},{7,6},{8,9},{9,8},{10,11... | collective-permute-start | bytes 2555912 | tf_op jit(solution)/shard_map/ppermute | solution.py:725
  119.5 2.4 %collective-permute-start.27 = (f32[128,1664]{1,0:T(8,128)S(1)}, f32[128,1664]{1,0:T(8,128)S(1)}, u32[]{:S(2)}, u32[]{:S(2)}) collective-permute-start(f32[128,1664]{1,0:T(8,128)S(1)} %constant_dynamic-update-slice_fusion.7.half1_ref), channel_id=1, source_target_pairs={{0,1},{1,0},{2,3},{3,2},{4,5},{5,4},{6,7},{7,6},{8,9},{9,8},{10,11... | collective-permute-start | bytes 2555912 | tf_op jit(solution)/shard_map/ppermute | solution.py:725
  (4 other events, 80.2 us)

commit v7 on v6

--- a/solution.py
+++ b/solution.py
@@ -729,7 +729,7 @@
 
     def relay(value, masks):
         one, two = swap(value, masks[0]), swap(value, masks[1])
-        return jnp.concatenate([value, one, two, swap(one, masks[1])], axis=0)
+        return jnp.concatenate([value, one, two, swap(two, masks[0])], axis=0)
 
     def spread(value):
         mask = 32
@@ -765,7 +765,7 @@
     outer = [swap(half0[32 * (i + 1) : 32 * (i + 2)], m) for i, m in enumerate(larger(SUM_KINDS[0]))]
     part0 = half0[0:32] + outer[0] + outer[1] + outer[2]
     part1 = spread(scatter_sum(part1, smaller(SUM_KINDS[1]), 8))
-    part1 = gather(together(part1, outer[0])[0], smaller(GATHER_KINDS[1]))
+    part1 = gather(part1, smaller(GATHER_KINDS[1]))
     part1 = relay(together(part1, part0)[0], larger(GATHER_KINDS[1]))
     part0 = spread(scatter_sum(part0, smaller(SUM_KINDS[0]), 8))
     part0 = gather(gather(part0, smaller(GATHER_KINDS[0])), larger(GATHER_KINDS[0]))

time: 124 us -> 123 us (level)
  waiting for transfers between devices: 19.8 us -> 15.5 us
  starting transfers between devices: 28.9 us -> 32.3 us
    ppermute x28, waiting for transfers between devices: 19.8 us -> 15.5 us  [swap(): lax.ppermute(value, 'dp', [(i, i ^ masks[i & 1]) for i in range(devices)])]
    ppermute x28, starting transfers between devices: 28.9 us -> 32.3 us  [swap(): lax.ppermute(value, 'dp', [(i, i ^ masks[i & 1]) for i in range(devices)])]
  transfers between devices with their start and end apart: 28 -> 28, of which waited for: 12 -> 10; matrix products, arithmetic and copies ran while one was open for 0% -> 0% of each run, Pallas kernels for 8% -> 8%
where the time goes in v7:
time: 123 us
  blocking collectives  42.2 us (34%)
  starting transfers between devices  32.3 us (26%)
  Pallas kernels  30.9 us (25%)
  waiting for transfers between devices  15.5 us (13%)
    all_to_all x4, blocking collectives, exchange(): return lax.all_to_all(part, 'dp', 0, 0, tiled=True)  42.2 us
    ppermute x28, starting transfers between devices, swap(): lax.ppermute(value, 'dp', [(i, i ^ masks[i & 1]) for i in range(devices)])  32.3 us
    pallas_call x8, Pallas kernels, call(): pl.pallas_call(kernel, in_specs=[hbm if i in far else vmem for i in range...  30.9 us
    ppermute x28, waiting for transfers between devices, swap(): lax.ppermute(value, 'dp', [(i, i ^ masks[i & 1]) for i in range(devices)])  15.5 us
  transfers between devices with their start and end apart: 28, of which 10 were waited for; matrix products, arithmetic and copies ran while one was open for 0% of the time, Pallas kernels for 8%

profile of v7, /device:TPU:0, one launch (start us, length us, event | category | flops | bytes accessed | tf_op | source)
XLA Modules:
  0.0 122.8 jit_solution(4312811955985525360)
XLA Ops:
  0.7 7.0 %shard_map.213 = (bf16[256,640]{1,0:T(8,128)(2,1)S(1)}, bf16[704,3584]{1,0:T(8,128)(2,1)S(1)}, f32[2,3584]{1,0:T(2,128)S(1)}, f32[8,768]{1,0:T(8,128)S(1)}, bf16...) custom-call(bf16[640,256]{1,0:T(8,128)(2,1)} %nf_hbm.1, ...), custom_call_target="tpu_custom_call" | custom-call | tf_op jit(solution)/shard_map/pallas_call | solution.py:658
  7.7 14.7 %all_to_all.20.recv_ref = f32[32,1,640]{2,1,0:T(1,128)S(1)} all-to-all(f32[32,1,640]{2,1,0:T(1,128)S(1)} %get-tuple-element.81), channel_id=1, replica_groups=mesh['dp'=32] {'dp'}, dimensions={0} | all-to-all | bytes 163840 | tf_op jit(solution)/shard_map/all_to_all | solution.py:679
  22.5 5.6 %shard_map.214 = (f32[8,256]{1,0:T(8,128)S(1)}, f32[256,640]{1,0:T(8,128)S(1)}, bf16[256,640]{1,0:T(8,128)(2,1)S(1)}, f32[256,1024]{1,0:T(8,128)S(1)}, f32[256,1...) custom-call(f32[32,1,640]{2,1,0:T(1,128)S(1)} %all_to_all.20.recv_re, ...), custom_call_target="tpu_custom_call" | custom-call | tf_op jit(solution)/shard_map/pallas_call | solution.py:658
  28.0 9.3 %all_to_all.21.recv_ref = f32[32,1,640]{2,1,0:T(1,128)S(1)} all-to-all(f32[32,1,640]{2,1,0:T(1,128)S(1)} %get-tuple-element.89), channel_id=1, replica_groups=mesh['dp'=32] {'dp'}, dimensions={0} | all-to-all | bytes 163840 | tf_op jit(solution)/shard_map/all_to_all | solution.py:679
  37.3 1.2 shard_map.215
  38.5 9.1 %all_to_all.22.recv_ref = f32[32,1,512]{2,1,0:T(1,128)S(1)} all-to-all(f32[32,1,512]{2,1,0:T(1,128)S(1)} %get-tuple-element.92), channel_id=1, replica_groups=mesh['dp'=32] {'dp'}, dimensions={0} | all-to-all | bytes 131072 | tf_op jit(solution)/shard_map/all_to_all | solution.py:679
  47.7 6.2 %shard_map.216 = (f32[1,512]{1,0:T(1,128)S(1)}, bf16[256,1024]{1,0:T(8,128)(2,1)S(1)}, bf16[256,1024]{1,0:T(8,128)(2,1)S(1)}, bf16[256,1024]{1,0:T(8,128)(2,1)S(...) custom-call(f32[32,1,512]{2,1,0:T(1,128)S(1)} %all_to_all.22.recv_re, ...), custom_call_target="tpu_custom_call" | custom-call | tf_op jit(solution)/shard_map/pallas_call | solution.py:658
  54.1 9.1 %all_to_all.23.recv_ref = f32[32,1,512]{2,1,0:T(1,128)S(1)} all-to-all(f32[32,1,512]{2,1,0:T(1,128)S(1)} %get-tuple-element.105), channel_id=1, replica_groups=mesh['dp'=32] {'dp'}, dimensions={0} | all-to-all | bytes 131072 | tf_op jit(solution)/shard_map/all_to_all | solution.py:679
  64.0 1.3 %collective-permute-start.3 = (f32[32,1664]{1,0:T(8,128)S(1)}, f32[32,1664]{1,0:T(8,128)S(1)}, u32[]{:S(2)}, u32[]{:S(2)}) collective-permute-start(f32[32,1664]{1,0:T(8,128)S(1)} %get-tuple-element.158), channel_id=1, source_target_pairs={{0,6},{1,25},{2,4},{3,27},{4,2},{5,29},{6,0},{7,31},{8,14},{9,17},... | collective-permute-start | bytes 638984 | tf_op jit(solution)/shard_map/ppermute | solution.py:725
  65.3 1.6 %collective-permute-start.2 = (f32[32,1664]{1,0:T(8,128)S(1)}, f32[32,1664]{1,0:T(8,128)S(1)}, u32[]{:S(2)}, u32[]{:S(2)}) collective-permute-start(f32[32,1664]{1,0:T(8,128)S(1)} %get-tuple-element.159), channel_id=1, source_target_pairs={{0,2},{1,9},{2,0},{3,11},{4,6},{5,13},{6,4},{7,15},{8,10},{9,1},{1... | collective-permute-start | bytes 638984 | tf_op jit(solution)/shard_map/ppermute | solution.py:725
  66.9 5.8 %shard_map.217 = (f32[1,512]{1,0:T(1,128)S(1)}, bf16[256,1024]{1,0:T(8,128)(2,1)S(1)}, bf16[256,1024]{1,0:T(8,128)(2,1)S(1)}, bf16[256,1024]{1,0:T(8,128)(2,1)S(...) custom-call(f32[32,1,512]{2,1,0:T(1,128)S(1)} %all_to_all.23.recv_re, ...), custom_call_target="tpu_custom_call" | custom-call | flops 8000000000 | tf_op jit(solution)/shard_map/pallas_call | solution.py:658
  72.7 2.4 %shard_map.218 = (f32[640,256]{1,0:T(8,128)}, f32[4,256]{1,0:T(4,128)}, f32[640,256]{1,0:T(8,128)}, f32[2,256]{1,0:T(2,128)}, f32[2,256]{1,0:T(2,128)}) custom-call(bf16[256,1024]{1,0:T(8,128)(2,1)S(1)} %get-tuple-element.120.a0_ref, bf16[256,1024]{1,0:T(8,128)(2,1)S(1)} %get-tuple-element.121.b0_ref, bf16[256,1024]{1,0:T(8,128)(2,1)S(1)} %get-tuple-element.122.c0_ref, ...), custom_call_target="tpu_custom_call" | custom-call | flops 2000000000 | tf_op jit(solution)/shard_map/pallas_call | solution.py:658
  76.0 2.5 %collective-permute-start.19 = (f32[8,1664]{1,0:T(8,128)S(1)}, f32[8,1664]{1,0:T(8,128)S(1)}, u32[]{:S(2)}, u32[]{:S(2)}) collective-permute-start(f32[8,1664]{1,0:T(8,128)S(1)} %get-tuple-element.161), channel_id=1, source_target_pairs={{0,24},{1,7},{2,26},{3,5},{4,28},{5,3},{6,30},{7,1},{8,16},{9,15},... | collective-permute-start | bytes 159752 | tf_op jit(solution)/shard_map/ppermute | solution.py:725
  79.9 1.4 %collective-permute-start.7 = (f32[32,1664]{1,0:T(8,128)S(1)}, f32[32,1664]{1,0:T(8,128)S(1)}, u32[]{:S(2)}, u32[]{:S(2)}) collective-permute-start(f32[32,1664]{1,0:T(8,128)S(1)} %get-tuple-element.155), channel_id=1, source_target_pairs={{0,6},{1,25},{2,4},{3,27},{4,2},{5,29},{6,0},{7,31},{8,14},{9,17},... | collective-permute-start | bytes 638984 | tf_op jit(solution)/shard_map/ppermute | solution.py:725
  81.2 1.3 %collective-permute-start.6 = (f32[32,1664]{1,0:T(8,128)S(1)}, f32[32,1664]{1,0:T(8,128)S(1)}, u32[]{:S(2)}, u32[]{:S(2)}) collective-permute-start(f32[32,1664]{1,0:T(8,128)S(1)} %get-tuple-element.156), channel_id=1, source_target_pairs={{0,2},{1,9},{2,0},{3,11},{4,6},{5,13},{6,4},{7,15},{8,10},{9,1},{1... | collective-permute-start | bytes 638984 | tf_op jit(solution)/shard_map/ppermute | solution.py:725
  83.0 2.2 %collective-permute-start.22 = (f32[8,1664]{1,0:T(8,128)S(1)}, f32[8,1664]{1,0:T(8,128)S(1)}, u32[]{:S(2)}, u32[]{:S(2)}) collective-permute-start(f32[8,1664]{1,0:T(8,128)S(1)} %add_add_fusion), channel_id=1, source_target_pairs={{0,24},{1,25},{2,26},{3,27},{4,28},{5,29},{6,30},{7,31},{8,16},{9,... | collective-permute-start | bytes 159752 | tf_op jit(solution)/shard_map/ppermute | solution.py:725
  85.2 2.0 %collective-permute-done.5 = f32[32,1664]{1,0:T(8,128)S(1)} collective-permute-done((f32[32,1664]{1,0:T(8,128)S(1)}, f32[32,1664]{1,0:T(8,128)S(1)}, u32[]{:S(2)}, u32[]{:S(2)}) %collective-permute-start.5) | collective-permute-done | bytes 213024 | tf_op jit(solution)/shard_map/ppermute | solution.py:725
  87.2 1.6 %collective-permute-start.20 = (f32[8,1664]{1,0:T(8,128)S(1)}, f32[8,1664]{1,0:T(8,128)S(1)}, u32[]{:S(2)}, u32[]{:S(2)}) collective-permute-start(f32[8,1664]{1,0:T(8,128)S(1)} %add_add_fusion), channel_id=1, source_target_pairs={{0,16},{1,17},{2,18},{3,19},{4,20},{5,21},{6,22},{7,23},{8,24},{9,... | collective-permute-start | bytes 159752 | tf_op jit(solution)/shard_map/ppermute | solution.py:725
  88.8 1.5 %collective-permute-start.8 = (f32[8,1664]{1,0:T(8,128)S(1)}, f32[8,1664]{1,0:T(8,128)S(1)}, u32[]{:S(2)}, u32[]{:S(2)}) collective-permute-start(f32[8,1664]{1,0:T(8,128)S(1)} %get-tuple-element.163), channel_id=1, source_target_pairs={{0,16},{1,5},{2,18},{3,7},{4,20},{5,1},{6,22},{7,3},{8,24},{9,13},... | collective-permute-start | bytes 159752 | tf_op jit(solution)/shard_map/ppermute | solution.py:725
  90.3 2.6 %collective-permute-start.10 = (f32[8,1664]{1,0:T(8,128)S(1)}, f32[8,1664]{1,0:T(8,128)S(1)}, u32[]{:S(2)}, u32[]{:S(2)}) collective-permute-start(f32[8,1664]{1,0:T(8,128)S(1)} %get-tuple-element.164), channel_id=1, source_target_pairs={{0,24},{1,7},{2,26},{3,5},{4,28},{5,3},{6,30},{7,1},{8,16},{9,15},... | collective-permute-start | bytes 159752 | tf_op jit(solution)/shard_map/ppermute | solution.py:725
  93.0 1.8 %collective-permute-start.24 = (f32[32,1664]{1,0:T(8,128)S(1)}, f32[32,1664]{1,0:T(8,128)S(1)}, u32[]{:S(2)}, u32[]{:S(2)}) collective-permute-start(f32[32,1664]{1,0:T(8,128)S(1)} %pad_maximum_fusion.1), channel_id=1, source_target_pairs={{0,2},{1,3},{2,0},{3,1},{4,6},{5,7},{6,4},{7,5},{8,10},{9,11},{10,... | collective-permute-start | bytes 638984 | tf_op jit(solution)/shard_map/ppermute | solution.py:725
  97.1 2.0 %collective-permute-start.13 = (f32[8,1664]{1,0:T(8,128)S(1)}, f32[8,1664]{1,0:T(8,128)S(1)}, u32[]{:S(2)}, u32[]{:S(2)}) collective-permute-start(f32[8,1664]{1,0:T(8,128)S(1)} %get-tuple-element.153), channel_id=1, source_target_pairs={{0,24},{1,7},{2,26},{3,5},{4,28},{5,3},{6,30},{7,1},{8,16},{9,15},... | collective-permute-start | bytes 159752 | tf_op jit(solution)/shard_map/ppermute | solution.py:725
  99.0 2.5 %collective-permute-start.11 = (f32[8,1664]{1,0:T(8,128)S(1)}, f32[8,1664]{1,0:T(8,128)S(1)}, u32[]{:S(2)}, u32[]{:S(2)}) collective-permute-start(f32[8,1664]{1,0:T(8,128)S(1)} %get-tuple-element.153), channel_id=1, source_target_pairs={{0,16},{1,5},{2,18},{3,7},{4,20},{5,1},{6,22},{7,3},{8,24},{9,13},... | collective-permute-start | bytes 159752 | tf_op jit(solution)/shard_map/ppermute | solution.py:725
  101.5 1.6 %collective-permute-done.13 = f32[8,1664]{1,0:T(8,128)S(1)} collective-permute-done((f32[8,1664]{1,0:T(8,128)S(1)}, f32[8,1664]{1,0:T(8,128)S(1)}, u32[]{:S(2)}, u32[]{:S(2)}) %collective-permute-start.13) | collective-permute-done | bytes 53280 | tf_op jit(solution)/shard_map/ppermute | solution.py:725
  104.2 1.2 %collective-permute-start.16 = (f32[32,1664]{1,0:T(8,128)S(1)}, f32[32,1664]{1,0:T(8,128)S(1)}, u32[]{:S(2)}, u32[]{:S(2)}) collective-permute-start(f32[32,1664]{1,0:T(8,128)S(1)} %pad_maximum_fusion), channel_id=1, source_target_pairs={{0,6},{1,25},{2,4},{3,27},{4,2},{5,29},{6,0},{7,31},{8,14},{9,17},... | collective-permute-start | bytes 638984 | tf_op jit(solution)/shard_map/ppermute | solution.py:725
  105.5 1.4 %collective-permute-start.15 = (f32[32,1664]{1,0:T(8,128)S(1)}, f32[32,1664]{1,0:T(8,128)S(1)}, u32[]{:S(2)}, u32[]{:S(2)}) collective-permute-start(f32[32,1664]{1,0:T(8,128)S(1)} %pad_maximum_fusion), channel_id=1, source_target_pairs={{0,2},{1,9},{2,0},{3,11},{4,6},{5,13},{6,4},{7,15},{8,10},{9,1},{1... | collective-permute-start | bytes 638984 | tf_op jit(solution)/shard_map/ppermute | solution.py:725
  107.8 1.2 collective-permute-start.25
  109.0 6.5 %collective-permute-done.14 = f32[32,1664]{1,0:T(8,128)S(1)} collective-permute-done((f32[32,1664]{1,0:T(8,128)S(1)}, f32[32,1664]{1,0:T(8,128)S(1)}, u32[]{:S(2)}, u32[]{:S(2)}) %collective-permute-start.14) | collective-permute-done | bytes 213024 | tf_op jit(solution)/shard_map/ppermute | solution.py:725
  115.6 2.3 %collective-permute-start.26 = (f32[128,1664]{1,0:T(8,128)S(1)}, f32[128,1664]{1,0:T(8,128)S(1)}, u32[]{:S(2)}, u32[]{:S(2)}) collective-permute-start(f32[128,1664]{1,0:T(8,128)S(1)} %constant_dynamic-update-slice_fusion.half0_ref), channel_id=1, source_target_pairs={{0,1},{1,0},{2,3},{3,2},{4,5},{5,4},{6,7},{7,6},{8,9},{9,8},{10,11... | collective-permute-start | bytes 2555912 | tf_op jit(solution)/shard_map/ppermute | solution.py:725
  118.0 1.3 %shard_map.219 = (f32[2,16,2,8,832]{4,3,2,1,0:T(8,128)}, f32[2,16,2,8,256]{4,3,2,1,0:T(8,128)}, f32[2,3,16,2,8,256]{5,4,3,2,1,0:T(8,128)}, f32[2,16,8,64]{3,2,1,0:T(8,128)S(1)}) custom-call(f32[128,1664]{1,0:T(8,128)S(1)} %constant_dynamic-update-slice_fusion.half0_ref, f32[128,1664]{1,0:T(8,128)S(1)} %constant_dynamic-update-slice_fusion.7.half1_ref), custom_call_target="tpu_custom_call" | custom-call | flops 2000000000 | tf_op jit(solution)/shard_map/pallas_call | solution.py:658
  119.9 1.2 collective-permute-done.27.half1_ref
  121.1 1.5 %shard_map.220 = (f32[2,16,2,8,832]{4,3,2,1,0:T(8,128)}, f32[2,16,2,8,256]{4,3,2,1,0:T(8,128)}, f32[2,3,16,2,8,256]{5,4,3,2,1,0:T(8,128)}, f32[2,256]{1,0:T(2,128)}, f32[2,16,256]{2,1,0:T(8,128)}) custom-call(f32[2,16,2,8,832]{4,3,2,1,0:T(8,128)} %get-tuple-element.141.post_in, ...), custom_call_target="tpu_custom_call", output_to_operand_aliasing={{0}: (0, {}), {1}: (1, {}), {2}: (2, {})} | custom-call | tf_op jit(solution)/shard_map/pallas_call | solution.py:658
  (74 shorter events, 8.9 us)
Async XLA Ops:
  0.6 21.8 %copy-start = (bf16[2,768,256]{2,1,0:T(8,128)(2,1)S(1)}, bf16[2,768,256]{2,1,0:T(8,128)(2,1)}, u32[]{:S(2)}) copy-start(bf16[2,768,256]{2,1,0:T(8,128)(2,1)} %wpre_ref.9) | copy-start | bytes 2359300
  0.7 21.8 %copy-start.2 = (bf16[2,256,256]{2,1,0:T(8,128)(2,1)S(1)}, bf16[2,256,256]{2,1,0:T(8,128)(2,1)}, u32[]{:S(2)}) copy-start(bf16[2,256,256]{2,1,0:T(8,128)(2,1)} %wmix_ref.5) | copy-start | bytes 786436
  0.7 21.8 %copy-start.3 = (bf16[2,16,256]{2,1,0:T(8,128)(2,1)S(1)}, bf16[2,16,256]{2,1,0:T(8,128)(2,1)}, u32[]{:S(2)}) copy-start(bf16[2,16,256]{2,1,0:T(8,128)(2,1)} %wedge_ref.5) | copy-start | bytes 49156
  0.7 21.8 %copy-start.6 = (f32[2,256]{1,0:T(2,128)S(1)}, f32[2,256]{1,0:T(2,128)}, u32[]{:S(2)}) copy-start(f32[2,256]{1,0:T(2,128)} %bpre_ref.1) | copy-start | bytes 6148
  53.9 9.3 %collective-permute-start = (f32[128,1664]{1,0:T(8,128)S(1)}, f32[128,1664]{1,0:T(8,128)S(1)}, u32[]{:S(2)}, u32[]{:S(2)}) collective-permute-start(f32[128,1664]{1,0:T(8,128)S(1)} %get-tuple-element.106), channel_id=1, source_target_pairs={{0,1},{1,0},{2,3},{3,2},{4,5},{5,4},{6,7},{7,6},{8,9},{9,8},{10,11... | collective-permute-start | bytes 2555912 | tf_op jit(solution)/shard_map/ppermute | solution.py:725
  63.3 11.8 %collective-permute-start.1 = (f32[32,1664]{1,0:T(8,128)S(1)}, f32[32,1664]{1,0:T(8,128)S(1)}, u32[]{:S(2)}, u32[]{:S(2)}) collective-permute-start(f32[32,1664]{1,0:T(8,128)S(1)} %get-tuple-element.157), channel_id=1, source_target_pairs={{0,4},{1,17},{2,6},{3,19},{4,0},{5,21},{6,2},{7,23},{8,12},{9,25},... | collective-permute-start | bytes 638984 | tf_op jit(solution)/shard_map/ppermute | solution.py:725
  64.0 11.1 %collective-permute-start.3 = (f32[32,1664]{1,0:T(8,128)S(1)}, f32[32,1664]{1,0:T(8,128)S(1)}, u32[]{:S(2)}, u32[]{:S(2)}) collective-permute-start(f32[32,1664]{1,0:T(8,128)S(1)} %get-tuple-element.158), channel_id=1, source_target_pairs={{0,6},{1,25},{2,4},{3,27},{4,2},{5,29},{6,0},{7,31},{8,14},{9,17},... | collective-permute-start | bytes 638984 | tf_op jit(solution)/shard_map/ppermute | solution.py:725
  65.3 9.8 %collective-permute-start.2 = (f32[32,1664]{1,0:T(8,128)S(1)}, f32[32,1664]{1,0:T(8,128)S(1)}, u32[]{:S(2)}, u32[]{:S(2)}) collective-permute-start(f32[32,1664]{1,0:T(8,128)S(1)} %get-tuple-element.159), channel_id=1, source_target_pairs={{0,2},{1,9},{2,0},{3,11},{4,6},{5,13},{6,4},{7,15},{8,10},{9,1},{1... | collective-permute-start | bytes 638984 | tf_op jit(solution)/shard_map/ppermute | solution.py:725
  75.1 3.7 %collective-permute-start.4 = (f32[128,1664]{1,0:T(8,128)S(1)}, f32[128,1664]{1,0:T(8,128)S(1)}, u32[]{:S(2)}, u32[]{:S(2)}) collective-permute-start(f32[128,1664]{1,0:T(8,128)S(1)} %get-tuple-element.138), channel_id=1, source_target_pairs={{0,1},{1,0},{2,3},{3,2},{4,5},{5,4},{6,7},{7,6},{8,9},{9,8},{10,11... | collective-permute-start | bytes 2555912 | tf_op jit(solution)/shard_map/ppermute | solution.py:725
  75.2 6.0 %collective-permute-start.17 = (f32[8,1664]{1,0:T(8,128)S(1)}, f32[8,1664]{1,0:T(8,128)S(1)}, u32[]{:S(2)}, u32[]{:S(2)}) collective-permute-start(f32[8,1664]{1,0:T(8,128)S(1)} %get-tuple-element.160), channel_id=1, source_target_pairs={{0,16},{1,5},{2,18},{3,7},{4,20},{5,1},{6,22},{7,3},{8,24},{9,13},... | collective-permute-start | bytes 159752 | tf_op jit(solution)/shard_map/ppermute | solution.py:725
  76.0 6.6 %collective-permute-start.19 = (f32[8,1664]{1,0:T(8,128)S(1)}, f32[8,1664]{1,0:T(8,128)S(1)}, u32[]{:S(2)}, u32[]{:S(2)}) collective-permute-start(f32[8,1664]{1,0:T(8,128)S(1)} %get-tuple-element.161), channel_id=1, source_target_pairs={{0,24},{1,7},{2,26},{3,5},{4,28},{5,3},{6,30},{7,1},{8,16},{9,15},... | collective-permute-start | bytes 159752 | tf_op jit(solution)/shard_map/ppermute | solution.py:725
  78.5 4.4 %collective-permute-start.18 = (f32[8,1664]{1,0:T(8,128)S(1)}, f32[8,1664]{1,0:T(8,128)S(1)}, u32[]{:S(2)}, u32[]{:S(2)}) collective-permute-start(f32[8,1664]{1,0:T(8,128)S(1)} %get-tuple-element.162), channel_id=1, source_target_pairs={{0,8},{1,3},{2,10},{3,1},{4,12},{5,7},{6,14},{7,5},{8,0},{9,11},{1... | collective-permute-start | bytes 159752 | tf_op jit(solution)/shard_map/ppermute | solution.py:725
  79.0 8.2 %collective-permute-start.5 = (f32[32,1664]{1,0:T(8,128)S(1)}, f32[32,1664]{1,0:T(8,128)S(1)}, u32[]{:S(2)}, u32[]{:S(2)}) collective-permute-start(f32[32,1664]{1,0:T(8,128)S(1)} %get-tuple-element.154), channel_id=1, source_target_pairs={{0,4},{1,17},{2,6},{3,19},{4,0},{5,21},{6,2},{7,23},{8,12},{9,25},... | collective-permute-start | bytes 638984 | tf_op jit(solution)/shard_map/ppermute | solution.py:725
  79.9 8.9 %collective-permute-start.7 = (f32[32,1664]{1,0:T(8,128)S(1)}, f32[32,1664]{1,0:T(8,128)S(1)}, u32[]{:S(2)}, u32[]{:S(2)}) collective-permute-start(f32[32,1664]{1,0:T(8,128)S(1)} %get-tuple-element.155), channel_id=1, source_target_pairs={{0,6},{1,25},{2,4},{3,27},{4,2},{5,29},{6,0},{7,31},{8,14},{9,17},... | collective-permute-start | bytes 638984 | tf_op jit(solution)/shard_map/ppermute | solution.py:725
  81.2 7.5 %collective-permute-start.6 = (f32[32,1664]{1,0:T(8,128)S(1)}, f32[32,1664]{1,0:T(8,128)S(1)}, u32[]{:S(2)}, u32[]{:S(2)}) collective-permute-start(f32[32,1664]{1,0:T(8,128)S(1)} %get-tuple-element.156), channel_id=1, source_target_pairs={{0,2},{1,9},{2,0},{3,11},{4,6},{5,13},{6,4},{7,15},{8,10},{9,1},{1... | collective-permute-start | bytes 638984 | tf_op jit(solution)/shard_map/ppermute | solution.py:725
  83.0 9.9 %collective-permute-start.22 = (f32[8,1664]{1,0:T(8,128)S(1)}, f32[8,1664]{1,0:T(8,128)S(1)}, u32[]{:S(2)}, u32[]{:S(2)}) collective-permute-start(f32[8,1664]{1,0:T(8,128)S(1)} %add_add_fusion), channel_id=1, source_target_pairs={{0,24},{1,25},{2,26},{3,27},{4,28},{5,29},{6,30},{7,31},{8,16},{9,... | collective-permute-start | bytes 159752 | tf_op jit(solution)/shard_map/ppermute | solution.py:725
  85.2 7.7 %collective-permute-start.21 = (f32[8,1664]{1,0:T(8,128)S(1)}, f32[8,1664]{1,0:T(8,128)S(1)}, u32[]{:S(2)}, u32[]{:S(2)}) collective-permute-start(f32[8,1664]{1,0:T(8,128)S(1)} %add_add_fusion), channel_id=1, source_target_pairs={{0,8},{1,9},{2,10},{3,11},{4,12},{5,13},{6,14},{7,15},{8,0},{9,1},... | collective-permute-start | bytes 159752 | tf_op jit(solution)/shard_map/ppermute | solution.py:725
  87.2 5.8 %collective-permute-start.20 = (f32[8,1664]{1,0:T(8,128)S(1)}, f32[8,1664]{1,0:T(8,128)S(1)}, u32[]{:S(2)}, u32[]{:S(2)}) collective-permute-start(f32[8,1664]{1,0:T(8,128)S(1)} %add_add_fusion), channel_id=1, source_target_pairs={{0,16},{1,17},{2,18},{3,19},{4,20},{5,21},{6,22},{7,23},{8,24},{9,... | collective-permute-start | bytes 159752 | tf_op jit(solution)/shard_map/ppermute | solution.py:725
  88.8 6.9 %collective-permute-start.8 = (f32[8,1664]{1,0:T(8,128)S(1)}, f32[8,1664]{1,0:T(8,128)S(1)}, u32[]{:S(2)}, u32[]{:S(2)}) collective-permute-start(f32[8,1664]{1,0:T(8,128)S(1)} %get-tuple-element.163), channel_id=1, source_target_pairs={{0,16},{1,5},{2,18},{3,7},{4,20},{5,1},{6,22},{7,3},{8,24},{9,13},... | collective-permute-start | bytes 159752 | tf_op jit(solution)/shard_map/ppermute | solution.py:725
  90.3 6.0 %collective-permute-start.10 = (f32[8,1664]{1,0:T(8,128)S(1)}, f32[8,1664]{1,0:T(8,128)S(1)}, u32[]{:S(2)}, u32[]{:S(2)}) collective-permute-start(f32[8,1664]{1,0:T(8,128)S(1)} %get-tuple-element.164), channel_id=1, source_target_pairs={{0,24},{1,7},{2,26},{3,5},{4,28},{5,3},{6,30},{7,1},{8,16},{9,15},... | collective-permute-start | bytes 159752 | tf_op jit(solution)/shard_map/ppermute | solution.py:725
  92.9 4.1 %collective-permute-start.9 = (f32[8,1664]{1,0:T(8,128)S(1)}, f32[8,1664]{1,0:T(8,128)S(1)}, u32[]{:S(2)}, u32[]{:S(2)}) collective-permute-start(f32[8,1664]{1,0:T(8,128)S(1)} %get-tuple-element.165), channel_id=1, source_target_pairs={{0,8},{1,3},{2,10},{3,1},{4,12},{5,7},{6,14},{7,5},{8,0},{9,11},{1... | collective-permute-start | bytes 159752 | tf_op jit(solution)/shard_map/ppermute | solution.py:725
  93.0 14.9 %collective-permute-start.24 = (f32[32,1664]{1,0:T(8,128)S(1)}, f32[32,1664]{1,0:T(8,128)S(1)}, u32[]{:S(2)}, u32[]{:S(2)}) collective-permute-start(f32[32,1664]{1,0:T(8,128)S(1)} %pad_maximum_fusion.1), channel_id=1, source_target_pairs={{0,2},{1,3},{2,0},{3,1},{4,6},{5,7},{6,4},{7,5},{8,10},{9,11},{10,... | collective-permute-start | bytes 638984 | tf_op jit(solution)/shard_map/ppermute | solution.py:725
  94.8 14.2 %collective-permute-start.23 = (f32[32,1664]{1,0:T(8,128)S(1)}, f32[32,1664]{1,0:T(8,128)S(1)}, u32[]{:S(2)}, u32[]{:S(2)}) collective-permute-start(f32[32,1664]{1,0:T(8,128)S(1)} %pad_maximum_fusion.1), channel_id=1, source_target_pairs={{0,4},{1,5},{2,6},{3,7},{4,0},{5,1},{6,2},{7,3},{8,12},{9,13},{10,... | collective-permute-start | bytes 638984 | tf_op jit(solution)/shard_map/ppermute | solution.py:725
  97.1 6.0 %collective-permute-start.13 = (f32[8,1664]{1,0:T(8,128)S(1)}, f32[8,1664]{1,0:T(8,128)S(1)}, u32[]{:S(2)}, u32[]{:S(2)}) collective-permute-start(f32[8,1664]{1,0:T(8,128)S(1)} %get-tuple-element.153), channel_id=1, source_target_pairs={{0,24},{1,7},{2,26},{3,5},{4,28},{5,3},{6,30},{7,1},{8,16},{9,15},... | collective-permute-start | bytes 159752 | tf_op jit(solution)/shard_map/ppermute | solution.py:725
  99.0 5.2 %collective-permute-start.12 = (f32[8,1664]{1,0:T(8,128)S(1)}, f32[8,1664]{1,0:T(8,128)S(1)}, u32[]{:S(2)}, u32[]{:S(2)}) collective-permute-start(f32[8,1664]{1,0:T(8,128)S(1)} %get-tuple-element.153), channel_id=1, source_target_pairs={{0,8},{1,3},{2,10},{3,1},{4,12},{5,7},{6,14},{7,5},{8,0},{9,11},{1... | collective-permute-start | bytes 159752 | tf_op jit(solution)/shard_map/ppermute | solution.py:725
  99.0 5.2 %collective-permute-start.11 = (f32[8,1664]{1,0:T(8,128)S(1)}, f32[8,1664]{1,0:T(8,128)S(1)}, u32[]{:S(2)}, u32[]{:S(2)}) collective-permute-start(f32[8,1664]{1,0:T(8,128)S(1)} %get-tuple-element.153), channel_id=1, source_target_pairs={{0,16},{1,5},{2,18},{3,7},{4,20},{5,1},{6,22},{7,3},{8,24},{9,13},... | collective-permute-start | bytes 159752 | tf_op jit(solution)/shard_map/ppermute | solution.py:725
  104.2 11.4 %collective-permute-start.16 = (f32[32,1664]{1,0:T(8,128)S(1)}, f32[32,1664]{1,0:T(8,128)S(1)}, u32[]{:S(2)}, u32[]{:S(2)}) collective-permute-start(f32[32,1664]{1,0:T(8,128)S(1)} %pad_maximum_fusion), channel_id=1, source_target_pairs={{0,6},{1,25},{2,4},{3,27},{4,2},{5,29},{6,0},{7,31},{8,14},{9,17},... | collective-permute-start | bytes 638984 | tf_op jit(solution)/shard_map/ppermute | solution.py:725
  105.5 10.1 %collective-permute-start.15 = (f32[32,1664]{1,0:T(8,128)S(1)}, f32[32,1664]{1,0:T(8,128)S(1)}, u32[]{:S(2)}, u32[]{:S(2)}) collective-permute-start(f32[32,1664]{1,0:T(8,128)S(1)} %pad_maximum_fusion), channel_id=1, source_target_pairs={{0,2},{1,9},{2,0},{3,11},{4,6},{5,13},{6,4},{7,15},{8,10},{9,1},{1... | collective-permute-start | bytes 638984 | tf_op jit(solution)/shard_map/ppermute | solution.py:725
  106.9 8.7 %collective-permute-start.14 = (f32[32,1664]{1,0:T(8,128)S(1)}, f32[32,1664]{1,0:T(8,128)S(1)}, u32[]{:S(2)}, u32[]{:S(2)}) collective-permute-start(f32[32,1664]{1,0:T(8,128)S(1)} %pad_maximum_fusion), channel_id=1, source_target_pairs={{0,4},{1,17},{2,6},{3,19},{4,0},{5,21},{6,2},{7,23},{8,12},{9,25},... | collective-permute-start | bytes 638984 | tf_op jit(solution)/shard_map/ppermute | solution.py:725
  107.8 10.1 %collective-permute-start.25 = (f32[32,1664]{1,0:T(8,128)S(1)}, f32[32,1664]{1,0:T(8,128)S(1)}, u32[]{:S(2)}, u32[]{:S(2)}) collective-permute-start(f32[32,1664]{1,0:T(8,128)S(1)} %collective-permute-done.24), channel_id=1, source_target_pairs={{0,4},{1,5},{2,6},{3,7},{4,0},{5,1},{6,2},{7,3},{8,12},{9,13},{10,... | collective-permute-start | bytes 638984 | tf_op jit(solution)/shard_map/ppermute | solution.py:725
  115.6 4.3 %collective-permute-start.26 = (f32[128,1664]{1,0:T(8,128)S(1)}, f32[128,1664]{1,0:T(8,128)S(1)}, u32[]{:S(2)}, u32[]{:S(2)}) collective-permute-start(f32[128,1664]{1,0:T(8,128)S(1)} %constant_dynamic-update-slice_fusion.half0_ref), channel_id=1, source_target_pairs={{0,1},{1,0},{2,3},{3,2},{4,5},{5,4},{6,7},{7,6},{8,9},{9,8},{10,11... | collective-permute-start | bytes 2555912 | tf_op jit(solution)/shard_map/ppermute | solution.py:725
  117.9 3.2 %collective-permute-start.27 = (f32[128,1664]{1,0:T(8,128)S(1)}, f32[128,1664]{1,0:T(8,128)S(1)}, u32[]{:S(2)}, u32[]{:S(2)}) collective-permute-start(f32[128,1664]{1,0:T(8,128)S(1)} %constant_dynamic-update-slice_fusion.7.half1_ref), channel_id=1, source_target_pairs={{0,1},{1,0},{2,3},{3,2},{4,5},{5,4},{6,7},{7,6},{8,9},{9,8},{10,11... | collective-permute-start | bytes 2555912 | tf_op jit(solution)/shard_map/ppermute | solution.py:725
  (4 other events, 80.2 us)

commit v8 on v7

--- a/solution.py
+++ b/solution.py
@@ -759,7 +759,7 @@
         [s((nodes, width)), s(readout_grad.shape), s((nodes, width)), s(bn_gain.shape), s(bn_bias.shape)],
         [pltpu.VMEM((width, 128), F32)], free=range(5), cost=2,
     )
-    send0, part1, edge_grad, readout = together(send0, part1, edge_grad, readout)
+    part1, edge_grad, readout = together(part1, edge_grad, readout)
     got0 = swap(send0, (1, 1))
     half0 = keep0 + got0
     outer = [swap(half0[32 * (i + 1) : 32 * (i + 2)], m) for i, m in enumerate(larger(SUM_KINDS[0]))]

time: 123 us -> 123 us (level)
  starting transfers between devices: 32.3 us -> 30.8 us
  waiting for transfers between devices: 15.5 us -> 16.9 us
    ppermute x28, starting transfers between devices: 32.3 us -> 30.8 us  [swap(): lax.ppermute(value, 'dp', [(i, i ^ masks[i & 1]) for i in range(devices)])]
    ppermute x28, waiting for transfers between devices: 15.5 us -> 16.9 us  [swap(): lax.ppermute(value, 'dp', [(i, i ^ masks[i & 1]) for i in range(devices)])]
  transfers between devices with their start and end apart: 28 -> 28, of which waited for: 10 -> 11; matrix products, arithmetic and copies ran while one was open for 0% -> 0% of each run, Pallas kernels for 8% -> 8%
where the time goes in v8:
time: 123 us
  blocking collectives  42.2 us (34%)
  Pallas kernels  30.9 us (25%)
  starting transfers between devices  30.8 us (25%)
  waiting for transfers between devices  16.9 us (14%)
    all_to_all x4, blocking collectives, exchange(): return lax.all_to_all(part, 'dp', 0, 0, tiled=True)  42.2 us
    pallas_call x8, Pallas kernels, call(): pl.pallas_call(kernel, in_specs=[hbm if i in far else vmem for i in range...  30.9 us
    ppermute x28, starting transfers between devices, swap(): lax.ppermute(value, 'dp', [(i, i ^ masks[i & 1]) for i in range(devices)])  30.8 us
    ppermute x28, waiting for transfers between devices, swap(): lax.ppermute(value, 'dp', [(i, i ^ masks[i & 1]) for i in range(devices)])  16.9 us
  transfers between devices with their start and end apart: 28, of which 11 were waited for; matrix products, arithmetic and copies ran while one was open for 0% of the time, Pallas kernels for 8%

profile of v8, /device:TPU:0, one launch (start us, length us, event | category | flops | bytes accessed | tf_op | source)
XLA Modules:
  0.0 122.7 jit_solution(15519499603952527697)
XLA Ops:
  0.7 7.0 %shard_map.213 = (bf16[256,640]{1,0:T(8,128)(2,1)S(1)}, bf16[704,3584]{1,0:T(8,128)(2,1)S(1)}, f32[2,3584]{1,0:T(2,128)S(1)}, f32[8,768]{1,0:T(8,128)S(1)}, bf16...) custom-call(bf16[640,256]{1,0:T(8,128)(2,1)} %nf_hbm.1, ...), custom_call_target="tpu_custom_call" | custom-call | tf_op jit(solution)/shard_map/pallas_call | solution.py:658
  7.7 14.7 %all_to_all.20.recv_ref = f32[32,1,640]{2,1,0:T(1,128)S(1)} all-to-all(f32[32,1,640]{2,1,0:T(1,128)S(1)} %get-tuple-element.80), channel_id=1, replica_groups=mesh['dp'=32] {'dp'}, dimensions={0} | all-to-all | bytes 163840 | tf_op jit(solution)/shard_map/all_to_all | solution.py:679
  22.5 5.6 %shard_map.214 = (f32[8,256]{1,0:T(8,128)S(1)}, f32[256,640]{1,0:T(8,128)S(1)}, bf16[256,640]{1,0:T(8,128)(2,1)S(1)}, f32[256,1024]{1,0:T(8,128)S(1)}, f32[256,1...) custom-call(f32[32,1,640]{2,1,0:T(1,128)S(1)} %all_to_all.20.recv_re, ...), custom_call_target="tpu_custom_call" | custom-call | tf_op jit(solution)/shard_map/pallas_call | solution.py:658
  28.0 9.3 %all_to_all.21.recv_ref = f32[32,1,640]{2,1,0:T(1,128)S(1)} all-to-all(f32[32,1,640]{2,1,0:T(1,128)S(1)} %get-tuple-element.88), channel_id=1, replica_groups=mesh['dp'=32] {'dp'}, dimensions={0} | all-to-all | bytes 163840 | tf_op jit(solution)/shard_map/all_to_all | solution.py:679
  37.3 1.2 shard_map.215
  38.5 9.1 %all_to_all.22.recv_ref = f32[32,1,512]{2,1,0:T(1,128)S(1)} all-to-all(f32[32,1,512]{2,1,0:T(1,128)S(1)} %get-tuple-element.91), channel_id=1, replica_groups=mesh['dp'=32] {'dp'}, dimensions={0} | all-to-all | bytes 131072 | tf_op jit(solution)/shard_map/all_to_all | solution.py:679
  47.7 6.2 %shard_map.216 = (f32[1,512]{1,0:T(1,128)S(1)}, bf16[256,1024]{1,0:T(8,128)(2,1)S(1)}, bf16[256,1024]{1,0:T(8,128)(2,1)S(1)}, bf16[256,1024]{1,0:T(8,128)(2,1)S(...) custom-call(f32[32,1,512]{2,1,0:T(1,128)S(1)} %all_to_all.22.recv_re, ...), custom_call_target="tpu_custom_call" | custom-call | tf_op jit(solution)/shard_map/pallas_call | solution.py:658
  54.1 9.1 %all_to_all.23.recv_ref = f32[32,1,512]{2,1,0:T(1,128)S(1)} all-to-all(f32[32,1,512]{2,1,0:T(1,128)S(1)} %get-tuple-element.105), channel_id=1, replica_groups=mesh['dp'=32] {'dp'}, dimensions={0} | all-to-all | bytes 131072 | tf_op jit(solution)/shard_map/all_to_all | solution.py:679
  64.0 1.3 %collective-permute-start.3 = (f32[32,1664]{1,0:T(8,128)S(1)}, f32[32,1664]{1,0:T(8,128)S(1)}, u32[]{:S(2)}, u32[]{:S(2)}) collective-permute-start(f32[32,1664]{1,0:T(8,128)S(1)} %get-tuple-element.156), channel_id=1, source_target_pairs={{0,6},{1,25},{2,4},{3,27},{4,2},{5,29},{6,0},{7,31},{8,14},{9,17},... | collective-permute-start | bytes 638984 | tf_op jit(solution)/shard_map/ppermute | solution.py:725
  65.3 1.6 %collective-permute-start.2 = (f32[32,1664]{1,0:T(8,128)S(1)}, f32[32,1664]{1,0:T(8,128)S(1)}, u32[]{:S(2)}, u32[]{:S(2)}) collective-permute-start(f32[32,1664]{1,0:T(8,128)S(1)} %get-tuple-element.157), channel_id=1, source_target_pairs={{0,2},{1,9},{2,0},{3,11},{4,6},{5,13},{6,4},{7,15},{8,10},{9,1},{1... | collective-permute-start | bytes 638984 | tf_op jit(solution)/shard_map/ppermute | solution.py:725
  66.9 5.8 %shard_map.217 = (f32[1,512]{1,0:T(1,128)S(1)}, bf16[256,1024]{1,0:T(8,128)(2,1)S(1)}, bf16[256,1024]{1,0:T(8,128)(2,1)S(1)}, bf16[256,1024]{1,0:T(8,128)(2,1)S(...) custom-call(f32[32,1,512]{2,1,0:T(1,128)S(1)} %all_to_all.23.recv_re, ...), custom_call_target="tpu_custom_call" | custom-call | flops 8000000000 | tf_op jit(solution)/shard_map/pallas_call | solution.py:658
  72.8 2.4 %shard_map.218 = (f32[640,256]{1,0:T(8,128)}, f32[4,256]{1,0:T(4,128)}, f32[640,256]{1,0:T(8,128)}, f32[2,256]{1,0:T(2,128)}, f32[2,256]{1,0:T(2,128)}) custom-call(bf16[256,1024]{1,0:T(8,128)(2,1)S(1)} %get-tuple-element.118.a0_ref, bf16[256,1024]{1,0:T(8,128)(2,1)S(1)} %get-tuple-element.119.b0_ref, bf16[256,1024]{1,0:T(8,128)(2,1)S(1)} %get-tuple-element.120.c0_ref, ...), custom_call_target="tpu_custom_call" | custom-call | flops 2000000000 | tf_op jit(solution)/shard_map/pallas_call | solution.py:658
  76.0 2.3 %collective-permute-start.19 = (f32[8,1664]{1,0:T(8,128)S(1)}, f32[8,1664]{1,0:T(8,128)S(1)}, u32[]{:S(2)}, u32[]{:S(2)}) collective-permute-start(f32[8,1664]{1,0:T(8,128)S(1)} %get-tuple-element.159), channel_id=1, source_target_pairs={{0,24},{1,7},{2,26},{3,5},{4,28},{5,3},{6,30},{7,1},{8,16},{9,15},... | collective-permute-start | bytes 159752 | tf_op jit(solution)/shard_map/ppermute | solution.py:725
  79.6 1.3 %collective-permute-start.7 = (f32[32,1664]{1,0:T(8,128)S(1)}, f32[32,1664]{1,0:T(8,128)S(1)}, u32[]{:S(2)}, u32[]{:S(2)}) collective-permute-start(f32[32,1664]{1,0:T(8,128)S(1)} %get-tuple-element.153), channel_id=1, source_target_pairs={{0,6},{1,25},{2,4},{3,27},{4,2},{5,29},{6,0},{7,31},{8,14},{9,17},... | collective-permute-start | bytes 638984 | tf_op jit(solution)/shard_map/ppermute | solution.py:725
  80.9 1.6 %collective-permute-start.6 = (f32[32,1664]{1,0:T(8,128)S(1)}, f32[32,1664]{1,0:T(8,128)S(1)}, u32[]{:S(2)}, u32[]{:S(2)}) collective-permute-start(f32[32,1664]{1,0:T(8,128)S(1)} %get-tuple-element.154), channel_id=1, source_target_pairs={{0,2},{1,9},{2,0},{3,11},{4,6},{5,13},{6,4},{7,15},{8,10},{9,1},{1... | collective-permute-start | bytes 638984 | tf_op jit(solution)/shard_map/ppermute | solution.py:725
  82.9 2.0 %collective-permute-start.22 = (f32[8,1664]{1,0:T(8,128)S(1)}, f32[8,1664]{1,0:T(8,128)S(1)}, u32[]{:S(2)}, u32[]{:S(2)}) collective-permute-start(f32[8,1664]{1,0:T(8,128)S(1)} %add_add_fusion), channel_id=1, source_target_pairs={{0,24},{1,25},{2,26},{3,27},{4,28},{5,29},{6,30},{7,31},{8,16},{9,... | collective-permute-start | bytes 159752 | tf_op jit(solution)/shard_map/ppermute | solution.py:725
  84.9 2.3 %collective-permute-done.5 = f32[32,1664]{1,0:T(8,128)S(1)} collective-permute-done((f32[32,1664]{1,0:T(8,128)S(1)}, f32[32,1664]{1,0:T(8,128)S(1)}, u32[]{:S(2)}, u32[]{:S(2)}) %collective-permute-start.5) | collective-permute-done | bytes 213024 | tf_op jit(solution)/shard_map/ppermute | solution.py:725
  87.2 1.6 %collective-permute-start.20 = (f32[8,1664]{1,0:T(8,128)S(1)}, f32[8,1664]{1,0:T(8,128)S(1)}, u32[]{:S(2)}, u32[]{:S(2)}) collective-permute-start(f32[8,1664]{1,0:T(8,128)S(1)} %add_add_fusion), channel_id=1, source_target_pairs={{0,16},{1,17},{2,18},{3,19},{4,20},{5,21},{6,22},{7,23},{8,24},{9,... | collective-permute-start | bytes 159752 | tf_op jit(solution)/shard_map/ppermute | solution.py:725
  88.8 1.5 %collective-permute-start.8 = (f32[8,1664]{1,0:T(8,128)S(1)}, f32[8,1664]{1,0:T(8,128)S(1)}, u32[]{:S(2)}, u32[]{:S(2)}) collective-permute-start(f32[8,1664]{1,0:T(8,128)S(1)} %get-tuple-element.161), channel_id=1, source_target_pairs={{0,16},{1,5},{2,18},{3,7},{4,20},{5,1},{6,22},{7,3},{8,24},{9,13},... | collective-permute-start | bytes 159752 | tf_op jit(solution)/shard_map/ppermute | solution.py:725
  90.3 2.3 %collective-permute-start.10 = (f32[8,1664]{1,0:T(8,128)S(1)}, f32[8,1664]{1,0:T(8,128)S(1)}, u32[]{:S(2)}, u32[]{:S(2)}) collective-permute-start(f32[8,1664]{1,0:T(8,128)S(1)} %get-tuple-element.162), channel_id=1, source_target_pairs={{0,24},{1,7},{2,26},{3,5},{4,28},{5,3},{6,30},{7,1},{8,16},{9,15},... | collective-permute-start | bytes 159752 | tf_op jit(solution)/shard_map/ppermute | solution.py:725
  92.6 1.3 %collective-permute-done.20 = f32[8,1664]{1,0:T(8,128)S(1)} collective-permute-done((f32[8,1664]{1,0:T(8,128)S(1)}, f32[8,1664]{1,0:T(8,128)S(1)}, u32[]{:S(2)}, u32[]{:S(2)}) %collective-permute-start.20) | collective-permute-done | bytes 53280 | tf_op jit(solution)/shard_map/ppermute | solution.py:725
  97.0 2.0 %collective-permute-start.13 = (f32[8,1664]{1,0:T(8,128)S(1)}, f32[8,1664]{1,0:T(8,128)S(1)}, u32[]{:S(2)}, u32[]{:S(2)}) collective-permute-start(f32[8,1664]{1,0:T(8,128)S(1)} %get-tuple-element.151), channel_id=1, source_target_pairs={{0,24},{1,7},{2,26},{3,5},{4,28},{5,3},{6,30},{7,1},{8,16},{9,15},... | collective-permute-start | bytes 159752 | tf_op jit(solution)/shard_map/ppermute | solution.py:725
  99.0 2.5 %collective-permute-start.11 = (f32[8,1664]{1,0:T(8,128)S(1)}, f32[8,1664]{1,0:T(8,128)S(1)}, u32[]{:S(2)}, u32[]{:S(2)}) collective-permute-start(f32[8,1664]{1,0:T(8,128)S(1)} %get-tuple-element.151), channel_id=1, source_target_pairs={{0,16},{1,5},{2,18},{3,7},{4,20},{5,1},{6,22},{7,3},{8,24},{9,13},... | collective-permute-start | bytes 159752 | tf_op jit(solution)/shard_map/ppermute | solution.py:725
  101.4 1.6 %collective-permute-done.13 = f32[8,1664]{1,0:T(8,128)S(1)} collective-permute-done((f32[8,1664]{1,0:T(8,128)S(1)}, f32[8,1664]{1,0:T(8,128)S(1)}, u32[]{:S(2)}, u32[]{:S(2)}) %collective-permute-start.13) | collective-permute-done | bytes 53280 | tf_op jit(solution)/shard_map/ppermute | solution.py:725
  103.0 1.1 collective-permute-done.12
  104.8 1.5 %collective-permute-start.15 = (f32[32,1664]{1,0:T(8,128)S(1)}, f32[32,1664]{1,0:T(8,128)S(1)}, u32[]{:S(2)}, u32[]{:S(2)}) collective-permute-start(f32[32,1664]{1,0:T(8,128)S(1)} %pad_maximum_fusion), channel_id=1, source_target_pairs={{0,2},{1,9},{2,0},{3,11},{4,6},{5,13},{6,4},{7,15},{8,10},{9,1},{1... | collective-permute-start | bytes 638984 | tf_op jit(solution)/shard_map/ppermute | solution.py:725
  106.4 1.3 %collective-permute-start.14 = (f32[32,1664]{1,0:T(8,128)S(1)}, f32[32,1664]{1,0:T(8,128)S(1)}, u32[]{:S(2)}, u32[]{:S(2)}) collective-permute-start(f32[32,1664]{1,0:T(8,128)S(1)} %pad_maximum_fusion), channel_id=1, source_target_pairs={{0,4},{1,17},{2,6},{3,19},{4,0},{5,21},{6,2},{7,23},{8,12},{9,25},... | collective-permute-start | bytes 638984 | tf_op jit(solution)/shard_map/ppermute | solution.py:725
  108.6 6.9 %collective-permute-done.14 = f32[32,1664]{1,0:T(8,128)S(1)} collective-permute-done((f32[32,1664]{1,0:T(8,128)S(1)}, f32[32,1664]{1,0:T(8,128)S(1)}, u32[]{:S(2)}, u32[]{:S(2)}) %collective-permute-start.14) | collective-permute-done | bytes 213024 | tf_op jit(solution)/shard_map/ppermute | solution.py:725
  115.5 2.3 %collective-permute-start.26 = (f32[128,1664]{1,0:T(8,128)S(1)}, f32[128,1664]{1,0:T(8,128)S(1)}, u32[]{:S(2)}, u32[]{:S(2)}) collective-permute-start(f32[128,1664]{1,0:T(8,128)S(1)} %constant_dynamic-update-slice_fusion.half0_ref), channel_id=1, source_target_pairs={{0,1},{1,0},{2,3},{3,2},{4,5},{5,4},{6,7},{7,6},{8,9},{9,8},{10,11... | collective-permute-start | bytes 2555912 | tf_op jit(solution)/shard_map/ppermute | solution.py:725
  117.9 1.3 %shard_map.219 = (f32[2,16,2,8,832]{4,3,2,1,0:T(8,128)}, f32[2,16,2,8,256]{4,3,2,1,0:T(8,128)}, f32[2,3,16,2,8,256]{5,4,3,2,1,0:T(8,128)}, f32[2,16,8,64]{3,2,1,0:T(8,128)S(1)}) custom-call(f32[128,1664]{1,0:T(8,128)S(1)} %constant_dynamic-update-slice_fusion.half0_ref, f32[128,1664]{1,0:T(8,128)S(1)} %constant_dynamic-update-slice_fusion.7.half1_ref), custom_call_target="tpu_custom_call" | custom-call | flops 2000000000 | tf_op jit(solution)/shard_map/pallas_call | solution.py:658
  119.8 1.2 collective-permute-done.27.half1_ref
  121.0 1.5 %shard_map.220 = (f32[2,16,2,8,832]{4,3,2,1,0:T(8,128)}, f32[2,16,2,8,256]{4,3,2,1,0:T(8,128)}, f32[2,3,16,2,8,256]{5,4,3,2,1,0:T(8,128)}, f32[2,256]{1,0:T(2,128)}, f32[2,16,256]{2,1,0:T(8,128)}) custom-call(f32[2,16,2,8,832]{4,3,2,1,0:T(8,128)} %get-tuple-element.139.post_in, ...), custom_call_target="tpu_custom_call", output_to_operand_aliasing={{0}: (0, {}), {1}: (1, {}), {2}: (2, {})} | custom-call | tf_op jit(solution)/shard_map/pallas_call | solution.py:658
  (74 shorter events, 9.0 us)
Async XLA Ops:
  0.6 21.8 %copy-start = (bf16[2,768,256]{2,1,0:T(8,128)(2,1)S(1)}, bf16[2,768,256]{2,1,0:T(8,128)(2,1)}, u32[]{:S(2)}) copy-start(bf16[2,768,256]{2,1,0:T(8,128)(2,1)} %wpre_ref.9) | copy-start | bytes 2359300
  0.7 21.8 %copy-start.2 = (bf16[2,256,256]{2,1,0:T(8,128)(2,1)S(1)}, bf16[2,256,256]{2,1,0:T(8,128)(2,1)}, u32[]{:S(2)}) copy-start(bf16[2,256,256]{2,1,0:T(8,128)(2,1)} %wmix_ref.5) | copy-start | bytes 786436
  0.7 21.8 %copy-start.3 = (bf16[2,16,256]{2,1,0:T(8,128)(2,1)S(1)}, bf16[2,16,256]{2,1,0:T(8,128)(2,1)}, u32[]{:S(2)}) copy-start(bf16[2,16,256]{2,1,0:T(8,128)(2,1)} %wedge_ref.5) | copy-start | bytes 49156
  0.7 21.8 %copy-start.6 = (f32[2,256]{1,0:T(2,128)S(1)}, f32[2,256]{1,0:T(2,128)}, u32[]{:S(2)}) copy-start(f32[2,256]{1,0:T(2,128)} %bpre_ref.1) | copy-start | bytes 6148
  53.9 9.3 %collective-permute-start = (f32[128,1664]{1,0:T(8,128)S(1)}, f32[128,1664]{1,0:T(8,128)S(1)}, u32[]{:S(2)}, u32[]{:S(2)}) collective-permute-start(f32[128,1664]{1,0:T(8,128)S(1)} %get-tuple-element.106), channel_id=1, source_target_pairs={{0,1},{1,0},{2,3},{3,2},{4,5},{5,4},{6,7},{7,6},{8,9},{9,8},{10,11... | collective-permute-start | bytes 2555912 | tf_op jit(solution)/shard_map/ppermute | solution.py:725
  63.3 11.8 %collective-permute-start.1 = (f32[32,1664]{1,0:T(8,128)S(1)}, f32[32,1664]{1,0:T(8,128)S(1)}, u32[]{:S(2)}, u32[]{:S(2)}) collective-permute-start(f32[32,1664]{1,0:T(8,128)S(1)} %get-tuple-element.155), channel_id=1, source_target_pairs={{0,4},{1,17},{2,6},{3,19},{4,0},{5,21},{6,2},{7,23},{8,12},{9,25},... | collective-permute-start | bytes 638984 | tf_op jit(solution)/shard_map/ppermute | solution.py:725
  64.0 11.2 %collective-permute-start.3 = (f32[32,1664]{1,0:T(8,128)S(1)}, f32[32,1664]{1,0:T(8,128)S(1)}, u32[]{:S(2)}, u32[]{:S(2)}) collective-permute-start(f32[32,1664]{1,0:T(8,128)S(1)} %get-tuple-element.156), channel_id=1, source_target_pairs={{0,6},{1,25},{2,4},{3,27},{4,2},{5,29},{6,0},{7,31},{8,14},{9,17},... | collective-permute-start | bytes 638984 | tf_op jit(solution)/shard_map/ppermute | solution.py:725
  65.3 9.9 %collective-permute-start.2 = (f32[32,1664]{1,0:T(8,128)S(1)}, f32[32,1664]{1,0:T(8,128)S(1)}, u32[]{:S(2)}, u32[]{:S(2)}) collective-permute-start(f32[32,1664]{1,0:T(8,128)S(1)} %get-tuple-element.157), channel_id=1, source_target_pairs={{0,2},{1,9},{2,0},{3,11},{4,6},{5,13},{6,4},{7,15},{8,10},{9,1},{1... | collective-permute-start | bytes 638984 | tf_op jit(solution)/shard_map/ppermute | solution.py:725
  72.7 6.1 %collective-permute-start.4 = (f32[128,1664]{1,0:T(8,128)S(1)}, f32[128,1664]{1,0:T(8,128)S(1)}, u32[]{:S(2)}, u32[]{:S(2)}) collective-permute-start(f32[128,1664]{1,0:T(8,128)S(1)} %get-tuple-element.136), channel_id=1, source_target_pairs={{0,1},{1,0},{2,3},{3,2},{4,5},{5,4},{6,7},{7,6},{8,9},{9,8},{10,11... | collective-permute-start | bytes 2555912 | tf_op jit(solution)/shard_map/ppermute | solution.py:725
  75.2 5.7 %collective-permute-start.17 = (f32[8,1664]{1,0:T(8,128)S(1)}, f32[8,1664]{1,0:T(8,128)S(1)}, u32[]{:S(2)}, u32[]{:S(2)}) collective-permute-start(f32[8,1664]{1,0:T(8,128)S(1)} %get-tuple-element.158), channel_id=1, source_target_pairs={{0,16},{1,5},{2,18},{3,7},{4,20},{5,1},{6,22},{7,3},{8,24},{9,13},... | collective-permute-start | bytes 159752 | tf_op jit(solution)/shard_map/ppermute | solution.py:725
  76.0 6.6 %collective-permute-start.19 = (f32[8,1664]{1,0:T(8,128)S(1)}, f32[8,1664]{1,0:T(8,128)S(1)}, u32[]{:S(2)}, u32[]{:S(2)}) collective-permute-start(f32[8,1664]{1,0:T(8,128)S(1)} %get-tuple-element.159), channel_id=1, source_target_pairs={{0,24},{1,7},{2,26},{3,5},{4,28},{5,3},{6,30},{7,1},{8,16},{9,15},... | collective-permute-start | bytes 159752 | tf_op jit(solution)/shard_map/ppermute | solution.py:725
  78.3 4.6 %collective-permute-start.18 = (f32[8,1664]{1,0:T(8,128)S(1)}, f32[8,1664]{1,0:T(8,128)S(1)}, u32[]{:S(2)}, u32[]{:S(2)}) collective-permute-start(f32[8,1664]{1,0:T(8,128)S(1)} %get-tuple-element.160), channel_id=1, source_target_pairs={{0,8},{1,3},{2,10},{3,1},{4,12},{5,7},{6,14},{7,5},{8,0},{9,11},{1... | collective-permute-start | bytes 159752 | tf_op jit(solution)/shard_map/ppermute | solution.py:725
  79.0 8.2 %collective-permute-start.5 = (f32[32,1664]{1,0:T(8,128)S(1)}, f32[32,1664]{1,0:T(8,128)S(1)}, u32[]{:S(2)}, u32[]{:S(2)}) collective-permute-start(f32[32,1664]{1,0:T(8,128)S(1)} %get-tuple-element.152), channel_id=1, source_target_pairs={{0,4},{1,17},{2,6},{3,19},{4,0},{5,21},{6,2},{7,23},{8,12},{9,25},... | collective-permute-start | bytes 638984 | tf_op jit(solution)/shard_map/ppermute | solution.py:725
  79.6 9.1 %collective-permute-start.7 = (f32[32,1664]{1,0:T(8,128)S(1)}, f32[32,1664]{1,0:T(8,128)S(1)}, u32[]{:S(2)}, u32[]{:S(2)}) collective-permute-start(f32[32,1664]{1,0:T(8,128)S(1)} %get-tuple-element.153), channel_id=1, source_target_pairs={{0,6},{1,25},{2,4},{3,27},{4,2},{5,29},{6,0},{7,31},{8,14},{9,17},... | collective-permute-start | bytes 638984 | tf_op jit(solution)/shard_map/ppermute | solution.py:725
  80.9 7.8 %collective-permute-start.6 = (f32[32,1664]{1,0:T(8,128)S(1)}, f32[32,1664]{1,0:T(8,128)S(1)}, u32[]{:S(2)}, u32[]{:S(2)}) collective-permute-start(f32[32,1664]{1,0:T(8,128)S(1)} %get-tuple-element.154), channel_id=1, source_target_pairs={{0,2},{1,9},{2,0},{3,11},{4,6},{5,13},{6,4},{7,15},{8,10},{9,1},{1... | collective-permute-start | bytes 638984 | tf_op jit(solution)/shard_map/ppermute | solution.py:725
  82.9 9.7 %collective-permute-start.22 = (f32[8,1664]{1,0:T(8,128)S(1)}, f32[8,1664]{1,0:T(8,128)S(1)}, u32[]{:S(2)}, u32[]{:S(2)}) collective-permute-start(f32[8,1664]{1,0:T(8,128)S(1)} %add_add_fusion), channel_id=1, source_target_pairs={{0,24},{1,25},{2,26},{3,27},{4,28},{5,29},{6,30},{7,31},{8,16},{9,... | collective-permute-start | bytes 159752 | tf_op jit(solution)/shard_map/ppermute | solution.py:725
  84.9 7.7 %collective-permute-start.21 = (f32[8,1664]{1,0:T(8,128)S(1)}, f32[8,1664]{1,0:T(8,128)S(1)}, u32[]{:S(2)}, u32[]{:S(2)}) collective-permute-start(f32[8,1664]{1,0:T(8,128)S(1)} %add_add_fusion), channel_id=1, source_target_pairs={{0,8},{1,9},{2,10},{3,11},{4,12},{5,13},{6,14},{7,15},{8,0},{9,1},... | collective-permute-start | bytes 159752 | tf_op jit(solution)/shard_map/ppermute | solution.py:725
  87.2 6.8 %collective-permute-start.20 = (f32[8,1664]{1,0:T(8,128)S(1)}, f32[8,1664]{1,0:T(8,128)S(1)}, u32[]{:S(2)}, u32[]{:S(2)}) collective-permute-start(f32[8,1664]{1,0:T(8,128)S(1)} %add_add_fusion), channel_id=1, source_target_pairs={{0,16},{1,17},{2,18},{3,19},{4,20},{5,21},{6,22},{7,23},{8,24},{9,... | collective-permute-start | bytes 159752 | tf_op jit(solution)/shard_map/ppermute | solution.py:725
  88.8 6.9 %collective-permute-start.8 = (f32[8,1664]{1,0:T(8,128)S(1)}, f32[8,1664]{1,0:T(8,128)S(1)}, u32[]{:S(2)}, u32[]{:S(2)}) collective-permute-start(f32[8,1664]{1,0:T(8,128)S(1)} %get-tuple-element.161), channel_id=1, source_target_pairs={{0,16},{1,5},{2,18},{3,7},{4,20},{5,1},{6,22},{7,3},{8,24},{9,13},... | collective-permute-start | bytes 159752 | tf_op jit(solution)/shard_map/ppermute | solution.py:725
  90.3 6.1 %collective-permute-start.10 = (f32[8,1664]{1,0:T(8,128)S(1)}, f32[8,1664]{1,0:T(8,128)S(1)}, u32[]{:S(2)}, u32[]{:S(2)}) collective-permute-start(f32[8,1664]{1,0:T(8,128)S(1)} %get-tuple-element.162), channel_id=1, source_target_pairs={{0,24},{1,7},{2,26},{3,5},{4,28},{5,3},{6,30},{7,1},{8,16},{9,15},... | collective-permute-start | bytes 159752 | tf_op jit(solution)/shard_map/ppermute | solution.py:725
  92.6 4.3 %collective-permute-start.9 = (f32[8,1664]{1,0:T(8,128)S(1)}, f32[8,1664]{1,0:T(8,128)S(1)}, u32[]{:S(2)}, u32[]{:S(2)}) collective-permute-start(f32[8,1664]{1,0:T(8,128)S(1)} %get-tuple-element.163), channel_id=1, source_target_pairs={{0,8},{1,3},{2,10},{3,1},{4,12},{5,7},{6,14},{7,5},{8,0},{9,11},{1... | collective-permute-start | bytes 159752 | tf_op jit(solution)/shard_map/ppermute | solution.py:725
  94.0 13.7 %collective-permute-start.24 = (f32[32,1664]{1,0:T(8,128)S(1)}, f32[32,1664]{1,0:T(8,128)S(1)}, u32[]{:S(2)}, u32[]{:S(2)}) collective-permute-start(f32[32,1664]{1,0:T(8,128)S(1)} %pad_maximum_fusion.1), channel_id=1, source_target_pairs={{0,2},{1,3},{2,0},{3,1},{4,6},{5,7},{6,4},{7,5},{8,10},{9,11},{10,... | collective-permute-start | bytes 638984 | tf_op jit(solution)/shard_map/ppermute | solution.py:725
  94.5 14.0 %collective-permute-start.23 = (f32[32,1664]{1,0:T(8,128)S(1)}, f32[32,1664]{1,0:T(8,128)S(1)}, u32[]{:S(2)}, u32[]{:S(2)}) collective-permute-start(f32[32,1664]{1,0:T(8,128)S(1)} %pad_maximum_fusion.1), channel_id=1, source_target_pairs={{0,4},{1,5},{2,6},{3,7},{4,0},{5,1},{6,2},{7,3},{8,12},{9,13},{10,... | collective-permute-start | bytes 638984 | tf_op jit(solution)/shard_map/ppermute | solution.py:725
  97.0 6.0 %collective-permute-start.13 = (f32[8,1664]{1,0:T(8,128)S(1)}, f32[8,1664]{1,0:T(8,128)S(1)}, u32[]{:S(2)}, u32[]{:S(2)}) collective-permute-start(f32[8,1664]{1,0:T(8,128)S(1)} %get-tuple-element.151), channel_id=1, source_target_pairs={{0,24},{1,7},{2,26},{3,5},{4,28},{5,3},{6,30},{7,1},{8,16},{9,15},... | collective-permute-start | bytes 159752 | tf_op jit(solution)/shard_map/ppermute | solution.py:725
  99.0 5.1 %collective-permute-start.12 = (f32[8,1664]{1,0:T(8,128)S(1)}, f32[8,1664]{1,0:T(8,128)S(1)}, u32[]{:S(2)}, u32[]{:S(2)}) collective-permute-start(f32[8,1664]{1,0:T(8,128)S(1)} %get-tuple-element.151), channel_id=1, source_target_pairs={{0,8},{1,3},{2,10},{3,1},{4,12},{5,7},{6,14},{7,5},{8,0},{9,11},{1... | collective-permute-start | bytes 159752 | tf_op jit(solution)/shard_map/ppermute | solution.py:725
  99.0 5.1 %collective-permute-start.11 = (f32[8,1664]{1,0:T(8,128)S(1)}, f32[8,1664]{1,0:T(8,128)S(1)}, u32[]{:S(2)}, u32[]{:S(2)}) collective-permute-start(f32[8,1664]{1,0:T(8,128)S(1)} %get-tuple-element.151), channel_id=1, source_target_pairs={{0,16},{1,5},{2,18},{3,7},{4,20},{5,1},{6,22},{7,3},{8,24},{9,13},... | collective-permute-start | bytes 159752 | tf_op jit(solution)/shard_map/ppermute | solution.py:725
  104.1 11.3 %collective-permute-start.16 = (f32[32,1664]{1,0:T(8,128)S(1)}, f32[32,1664]{1,0:T(8,128)S(1)}, u32[]{:S(2)}, u32[]{:S(2)}) collective-permute-start(f32[32,1664]{1,0:T(8,128)S(1)} %pad_maximum_fusion), channel_id=1, source_target_pairs={{0,6},{1,25},{2,4},{3,27},{4,2},{5,29},{6,0},{7,31},{8,14},{9,17},... | collective-permute-start | bytes 638984 | tf_op jit(solution)/shard_map/ppermute | solution.py:725
  104.8 10.6 %collective-permute-start.15 = (f32[32,1664]{1,0:T(8,128)S(1)}, f32[32,1664]{1,0:T(8,128)S(1)}, u32[]{:S(2)}, u32[]{:S(2)}) collective-permute-start(f32[32,1664]{1,0:T(8,128)S(1)} %pad_maximum_fusion), channel_id=1, source_target_pairs={{0,2},{1,9},{2,0},{3,11},{4,6},{5,13},{6,4},{7,15},{8,10},{9,1},{1... | collective-permute-start | bytes 638984 | tf_op jit(solution)/shard_map/ppermute | solution.py:725
  106.4 9.0 %collective-permute-start.14 = (f32[32,1664]{1,0:T(8,128)S(1)}, f32[32,1664]{1,0:T(8,128)S(1)}, u32[]{:S(2)}, u32[]{:S(2)}) collective-permute-start(f32[32,1664]{1,0:T(8,128)S(1)} %pad_maximum_fusion), channel_id=1, source_target_pairs={{0,4},{1,17},{2,6},{3,19},{4,0},{5,21},{6,2},{7,23},{8,12},{9,25},... | collective-permute-start | bytes 638984 | tf_op jit(solution)/shard_map/ppermute | solution.py:725
  107.7 10.1 %collective-permute-start.25 = (f32[32,1664]{1,0:T(8,128)S(1)}, f32[32,1664]{1,0:T(8,128)S(1)}, u32[]{:S(2)}, u32[]{:S(2)}) collective-permute-start(f32[32,1664]{1,0:T(8,128)S(1)} %collective-permute-done.24), channel_id=1, source_target_pairs={{0,4},{1,5},{2,6},{3,7},{4,0},{5,1},{6,2},{7,3},{8,12},{9,13},{10,... | collective-permute-start | bytes 638984 | tf_op jit(solution)/shard_map/ppermute | solution.py:725
  115.5 4.3 %collective-permute-start.26 = (f32[128,1664]{1,0:T(8,128)S(1)}, f32[128,1664]{1,0:T(8,128)S(1)}, u32[]{:S(2)}, u32[]{:S(2)}) collective-permute-start(f32[128,1664]{1,0:T(8,128)S(1)} %constant_dynamic-update-slice_fusion.half0_ref), channel_id=1, source_target_pairs={{0,1},{1,0},{2,3},{3,2},{4,5},{5,4},{6,7},{7,6},{8,9},{9,8},{10,11... | collective-permute-start | bytes 2555912 | tf_op jit(solution)/shard_map/ppermute | solution.py:725
  117.8 3.2 %collective-permute-start.27 = (f32[128,1664]{1,0:T(8,128)S(1)}, f32[128,1664]{1,0:T(8,128)S(1)}, u32[]{:S(2)}, u32[]{:S(2)}) collective-permute-start(f32[128,1664]{1,0:T(8,128)S(1)} %constant_dynamic-update-slice_fusion.7.half1_ref), channel_id=1, source_target_pairs={{0,1},{1,0},{2,3},{3,2},{4,5},{5,4},{6,7},{7,6},{8,9},{9,8},{10,11... | collective-permute-start | bytes 2555912 | tf_op jit(solution)/shard_map/ppermute | solution.py:725
  (4 other events, 80.2 us)
